TPU v7x, 512 devices: a whole 4x8x8 slice. The times are simulated.
512 devices in a mesh: tok: 32 (over y_hi, x, core), feat: 16 (over y_lo, z).
Axes of the slice: x: 4, y: 8 (y_hi: 4, y_lo: 2; y = y_hi * 2 + y_lo), z: 8, core: 2. Of those that a mesh axis runs over, the one named last changes fastest.
Arguments:
- entering: bfloat16 [2560, 32768], P('feat', 'tok'), may hold values from -210 to 210
- leaving: bfloat16 [2560, 32768], P('feat', 'tok'), may hold values from -280 to 280
Outputs:
- transform: float32 [2560, 2560], P('feat', 'tok')
All inputs are finite; a program needn't handle non-finite values.
Results may differ from a plain program's by a relative error of at most 0.00052.
Values may be sent and summed in bfloat16 or wider, within the bound.
No kernel may reach another device: no remote copies, remote signals or barrier semaphores. Data moves between devices by JAX's collectives and lax.ppermute only.
A program may use at most 64 MiB of HBM per device.

v0:
```python
import jax
import jax.numpy as jnp
from jax import lax
from jax.sharding import PartitionSpec as P

ITERS = 2


ridge_share = 0.2


def token_product(left, right):
    return lax.dot_general(
        left, right, (((1,), (1,)), ((), ())), preferred_element_type=jnp.float32
    )


def body(entering, leaving):
    row_count = entering.shape[0]
    order_all = row_count * lax.axis_size("feat")
    token_total = entering.shape[1] * lax.axis_size("tok")
    gram_piece = token_product(entering, lax.all_gather(entering, "feat", axis=0, tiled=True))
    cross_piece = token_product(entering, lax.all_gather(leaving, "feat", axis=0, tiled=True))
    gram_tile, cross_tile = (
        lax.psum_scatter(gram_piece, "tok", scatter_dimension=1, tiled=True),
        lax.psum_scatter(cross_piece, "tok", scatter_dimension=1, tiled=True),
    )
    gram_rows = lax.all_gather(gram_tile, "tok", axis=1, tiled=True)
    row_peak = jnp.max(jnp.sum(jnp.abs(gram_rows), axis=1))
    own_squares = jnp.sum(jnp.square(entering.astype(jnp.float32)))
    energy = lax.psum(own_squares, ("tok", "feat"))
    peak_all = lax.pmax(row_peak, "feat")
    ridge_term = ridge_share * energy / (token_total * order_all)
    upper_bound = peak_all / token_total + ridge_term
    center = (upper_bound + ridge_term) / 2.0
    half_span = (upper_bound - ridge_term) / 2.0
    target = cross_tile / token_total
    transform = target / center
    update = transform
    ratio_now = half_span / center
    for sweep in range(ITERS):
        iterate_half = transform.astype(jnp.bfloat16)
        applied = jnp.dot(
            gram_rows,
            lax.all_gather(iterate_half, "feat", axis=0, tiled=True).astype(jnp.float32),
            precision=lax.Precision.HIGHEST,
        )
        residual_now = target - (
            applied / token_total + ridge_term * iterate_half.astype(jnp.float32)
        )
        ratio_next = 1.0 / (2.0 * center / half_span - ratio_now)
        update = ratio_next * ratio_now * update + 2.0 * ratio_next / half_span * residual_now
        transform = transform + update
        ratio_now = ratio_next
    return transform


def solution(mesh):
    in_specs = (P("feat", "tok"), P("feat", "tok"))
    out_specs = P("feat", "tok")
    return jax.shard_map(body, mesh=mesh, in_specs=in_specs, out_specs=out_specs, check_vma=False)
```

profile of v0, /device:TPU:8, one launch (start us, length us, event | category | flops | bytes accessed | tf_op | source)
XLA Modules:
  0.0 565.1 jit_solution(4109793425515158281)
XLA Ops:
  6.5 0.7 all-gather.6.cloned.1.call-update
  7.3 0.0 reduce-scatter.9.cloned.1.call-start
  7.3 88.5 %all-gather.6.cloned.1.call-done = bf16[2560,1024]{1,0:T(8,128)(2,1)} async-done(((bf16[160,1024]{1,0:T(8,128)(2,1)}), bf16[2560,1024]{1,0:T(8,128)(2,1)}) %all-gather.6.cloned.1.call-update) | async-done | bytes 5242896 | tf_op jit(solution)/shard_map/all_gather | solution.py:22
  95.8 5.6 convolution_bitcast_fusion
  101.4 0.0 reduce-scatter.9.cloned.1.call-update
  101.5 0.0 all-gather.4.cloned.1.call-start
  101.5 0.7 all-gather.4.cloned.1.call-update
  102.2 0.0 all-gather.8.cloned.1.call-start
  102.2 97.2 %reduce-scatter.9.cloned.1.call-done = f32[80,160]{1,0:T(8,128)} async-done(((f32[2560,160]{1,0:T(8,128)}), f32[80,160]{1,0:T(8,128)}) %reduce-scatter.9.cloned.1.call-update) | async-done | bytes 51216
  199.4 0.0 reduce-scatter.7.cloned.1.call-start
  199.5 82.7 %all-gather.4.cloned.1.call-done = bf16[2560,1024]{1,0:T(8,128)(2,1)} async-done(((bf16[160,1024]{1,0:T(8,128)(2,1)}), bf16[2560,1024]{1,0:T(8,128)(2,1)}) %all-gather.4.cloned.1.call-update) | async-done | bytes 5242896 | tf_op jit(solution)/shard_map/all_gather | solution.py:23
  282.2 5.6 convolution_bitcast_fusion.1
  287.8 0.8 multiply_reduce_fusion
  288.6 97.6 %psum.7 = f32[]{:T(128)} all-reduce(f32[]{:T(128)} %multiply_reduce_fusion), channel_id=1, replica_groups=mesh['tok'=32,'feat'=16] {'tok','feat'}, use_global_device_ids=true, to_apply=%region_6.0 | all-reduce | flops 1 | bytes 8 | tf_op jit(solution)/shard_map/psum | solution.py:31
  386.8 0.0 all-gather.8.cloned.1.call-done
  386.8 2.3 abs_reduce_fusion
  389.1 0.6 reduce_max.9
  389.7 57.4 %reduce-scatter.7.cloned.1.call-done = f32[80,160]{1,0:T(8,128)} async-done(((f32[2560,160]{1,0:T(8,128)}), f32[80,160]{1,0:T(8,128)}) %reduce-scatter.7.cloned.1.call-update) | async-done | bytes 51216
  447.2 1.0 copy.5
  448.1 36.0 %pmax.7 = f32[]{:T(128)} all-reduce(f32[]{:T(128)} %reduce_max.9), channel_id=1, replica_groups=mesh['tok'=32,'feat'=16] {'feat'}, use_global_device_ids=true, to_apply=%region_4.0 | all-reduce | flops 1 | bytes 8 | tf_op jit(solution)/shard_map/pmax | solution.py:32
  485.1 34.0 %all_gather.18 = bf16[2560,80]{1,0:T(8,128)(2,1)S(1)} all-gather(bf16[160,80]{1,0:T(8,128)(2,1)S(1)} %fusion.10), channel_id=1, replica_groups=mesh['tok'=32,'feat'=16] {'feat'}, dimensions={0}, use_global_device_ids=true | all-gather | bytes 435200 | tf_op jit(solution)/shard_map/all_gather | solution.py:45
  519.1 2.2 fusion.11
  521.3 34.4 %all_gather.19 = bf16[2560,80]{1,0:T(8,128)(2,1)S(1)} all-gather(bf16[160,80]{1,0:T(8,128)(2,1)S(1)} %get-tuple-element.5), channel_id=1, replica_groups=mesh['tok'=32,'feat'=16] {'feat'}, dimensions={0}, use_global_device_ids=true | all-gather | bytes 435200 | tf_op jit(solution)/shard_map/all_gather | solution.py:45
  555.7 2.9 fusion.4
  (8 shorter events, 0.1 us)
Async XLA Ops:
  6.5 89.2 %all-gather.6.cloned.1.call-start = ((), (), s32[]{:S(2)}) async-start(), calls=%async_computation.3 | async-start | bytes 5570560 | tf_op jit(solution)/shard_map/all_gather | solution.py:22
  7.3 192.1 %reduce-scatter.9.cloned.1.call-start = ((), (), s32[]{:S(2)}) async-start(), calls=%async_computation.6 | async-start | bytes 2703360
  101.4 180.8 %copy-start.1 = (bf16[160,1024]{1,0:T(8,128)(2,1)S(1)}, bf16[160,1024]{1,0:T(8,128)(2,1)}, u32[]{:S(2)}) copy-start(bf16[160,1024]{1,0:T(8,128)(2,1)} %param.2) | copy-start | bytes 983044
  101.5 180.7 %all-gather.4.cloned.1.call-start = ((), (), s32[]{:S(2)}) async-start(), calls=%async_computation.2 | async-start | bytes 5570560 | tf_op jit(solution)/shard_map/all_gather | solution.py:23
  102.2 284.6 %all-gather.8.cloned.1.call-start = ((), (), s32[]{:S(2)}) async-start(), calls=%async_computation.4 | async-start | bytes 2703360 | tf_op jit(solution)/shard_map/all_gather | solution.py:28
  199.4 247.7 %reduce-scatter.7.cloned.1.call-start = ((), (), s32[]{:S(2)}) async-start(), calls=%async_computation.5 | async-start | bytes 2703360
  386.8 132.2 %copy-start = (f32[160,2560]{0,1:T(8,128)S(1)}, f32[160,2560]{0,1:T(8,128)}, u32[]{:S(2)}) copy-start(f32[160,2560]{0,1:T(8,128)} %all-gather.8.cloned.1.call-done) | copy-start | bytes 4915204
Sparse Core Ops, SparseCore 0:
  9.4 86.3 all-gather.5
  101.6 97.7 reduce-scatter.8
  201.7 80.4 all-gather.3
  285.6 57.1 all-gather.7
  347.8 99.3 reduce-scatter.6
where the time goes:
time: 565 us
  waiting for transfers between devices  327 us (58%)
  blocking collectives  202 us (36%)
  matrix products  16.3 us (3%)
  between operations  14.7 us (3%)
    unnamed x7, waiting for transfers between devices  156 us
    psum x1, blocking collectives, body(): energy = lax.psum(own_squares, ('tok', 'feat'))  97.6 us
    all_gather x1, waiting for transfers between devices, body(): lax.all_gather(entering, 'feat', axis=0, tiled=True)  88.5 us
    all_gather x1, waiting for transfers between devices, body(): lax.all_gather(leaving, 'feat', axis=0, tiled=True)  82.7 us
    all_gather x2, blocking collectives, body(): lax.all_gather(iterate_half, 'feat', axis=0, tiled=True).astype(jnp.float32)  68.4 us
    pmax x1, blocking collectives, body(): peak_all = lax.pmax(row_peak, 'feat')  36 us
  transfers between devices with their start and end apart: 5, of which 4 were waited for; matrix products, arithmetic and copies ran while one was open for 2% of the time, Pallas kernels for 0%

commit v1 on v0

v1 whole, which is shorter than its diff:
```python
import jax
import jax.numpy as jnp
import numpy as np
from jax import lax
from jax.sharding import Mesh, PartitionSpec as P

ITERS = 2
ridge_share = 0.2
TOK = ("yh", "x", "c")
FEAT = ("yl", "z")
ALL = TOK + FEAT
SIZES = (4, 4, 2, 2, 8)


def shift(array, axis, size, step):
    return lax.ppermute(array, axis, [(i, (i + step) % size) for i in range(size)])


def spread(array, axes, count):
    return lax.all_to_all(
        jnp.broadcast_to(array[None], (count,) + array.shape), axes, 0, 0
    )


def tile_moves():
    moves = []
    for yh in range(4):
        for x in range(4):
            for c in range(2):
                for yl in range(2):
                    for z in range(8):
                        other_yl, half = yh // 2, yh % 2
                        source = (((yh * 4 + x) * 2 + c) * 2 + yl) * 8 + z
                        to_z = (z + 4 * c + x) % 8
                        to_yh, to_x = other_yl * 2 + z // 4, z % 4
                        target = (((to_yh * 4 + to_x) * 2 + half) * 2 + yl) * 8 + to_z
                        moves.append((source, target))
    return moves


def body(entering, leaving):
    yl = lax.axis_index("yl")
    z = lax.axis_index("z")
    rows = entering.shape[0]
    quarter = rows // 4
    half_cols = rows // 2
    token_total = entering.shape[1] * 32
    order_all = rows * 16
    low = yl == 0

    pair = jnp.concatenate([entering, leaving], 0)
    other = shift(pair, "yl", 2, 1)
    first = jnp.where(low, pair, other)
    second = jnp.where(low, other, pair)
    columns = jnp.concatenate([first[:rows], second[:rows], first[rows:], second[rows:]], 0)

    blocks = {0: entering}
    up = down = entering
    for step in range(1, 5):
        down = shift(down, "z", 8, -1)
        blocks[step] = down
        if step < 4:
            up = shift(up, "z", 8, 1)
            blocks[8 - step] = up

    pieces = [
        lax.dot_general(
            blocks[s], columns, (((1,), (1,)), ((), ())), preferred_element_type=jnp.float32
        )
        for s in range(8)
    ]
    partial = jnp.stack(pieces).reshape(2, 4, rows, 4 * rows)
    partial = jnp.sum(lax.all_to_all(partial, "c", 0, 0), 0)
    partial = jnp.sum(lax.all_to_all(partial, "x", 0, 0), 0)
    packed = jnp.stack(
        [
            jnp.concatenate(
                [partial[quarter * q : quarter * (q + 1), : 2 * rows]]
                + [
                    partial[
                        quarter * r : quarter * (r + 1),
                        2 * rows + half_cols * q : 2 * rows + half_cols * (q + 1),
                    ]
                    for r in range(4)
                ],
                1,
            )
            for q in range(4)
        ]
    )
    own = jnp.sum(lax.all_to_all(packed, "yh", 0, 0), 0)
    gram_own = own[:, : 2 * rows]
    cross_own = lax.ppermute(own[:, 2 * rows :], ALL, tile_moves())
    cross_tile = jnp.concatenate(
        [cross_own[:, half_cols * r : half_cols * (r + 1)] for r in range(4)], 0
    )

    gram_swap = shift(gram_own, "yl", 2, 1)
    gram_swap = jnp.concatenate([gram_swap[:, rows:], gram_swap[:, :rows]], 1)
    slot = lax.broadcasted_iota(jnp.int32, gram_own.shape, 1) // rows
    gram_part = jnp.where(slot == yl, gram_own, gram_swap)
    gram_part = spread(gram_part, "yh", 4).reshape(rows, 2 * rows)
    gram_part = spread(gram_part, "x", 4)
    gram = spread(gram_part, "c", 2).reshape(8, rows, 2 * rows)

    sums = jnp.sum(jnp.abs(gram), (0, 1))
    row_peak = jnp.max(sums[:rows] + sums[rows:])
    at_row = lax.broadcasted_iota(jnp.int32, (rows, 2 * rows), 0)
    at_col = lax.broadcasted_iota(jnp.int32, (rows, 2 * rows), 1)
    trace = jnp.sum(jnp.where(at_col == at_row + rows * yl, gram[0], 0.0))
    lane = lax.broadcasted_iota(jnp.int32, (1, 128), 1)
    scalars = spread(jnp.where(lane == 0, row_peak, trace), FEAT, 16)
    peak_all = jnp.max(scalars[:, 0, 0])
    energy = jnp.sum(scalars[:, 0, 1])

    ridge_term = ridge_share * energy / (token_total * order_all)
    upper_bound = peak_all / token_total + ridge_term
    center = (upper_bound + ridge_term) / 2.0
    half_span = (upper_bound - ridge_term) / 2.0

    gram_flat = gram.reshape(8 * rows, 2 * rows)
    gram_hi = gram_flat.astype(jnp.bfloat16)
    gram_lo = (gram_flat - gram_hi.astype(jnp.float32)).astype(jnp.bfloat16)
    gram_both = jnp.concatenate([gram_hi, gram_lo], 1)

    target = cross_tile / token_total
    transform = target / center
    update = transform
    ratio_now = half_span / center
    for sweep in range(ITERS):
        iterate_half = transform.astype(jnp.bfloat16)
        full = spread(iterate_half, FEAT, 16).reshape(2, 8, rows, half_cols)
        full = jnp.concatenate([full, full], 1)
        full = lax.dynamic_slice_in_dim(full, z, 8, 1).reshape(2, 8 * rows, half_cols)
        products = [
            lax.dot_general(
                gram_both, full[k], (((0,), (0,)), ((), ())), preferred_element_type=jnp.float32
            )
            for k in range(2)
        ]
        applied = (
            products[0][:rows] + products[0][2 * rows : 3 * rows]
        ) + (products[1][rows : 2 * rows] + products[1][3 * rows :])
        residual_now = target - (
            applied / token_total + ridge_term * iterate_half.astype(jnp.float32)
        )
        ratio_next = 1.0 / (2.0 * center / half_span - ratio_now)
        update = ratio_next * ratio_now * update + 2.0 * ratio_next / half_span * residual_now
        transform = transform + update
        ratio_now = ratio_next
    return transform


def solution(mesh):
    fine = Mesh(mesh.devices.reshape(SIZES), ALL)
    spec = P(FEAT, TOK)
    return jax.shard_map(
        body, mesh=fine, in_specs=(spec, spec), out_specs=spec, check_vma=False
    )
```

time: 565 us -> 232 us (0.41)
  the two profiles are of different devices: /device:TPU:8 before, /device:TPU:66 now
where the time goes in v1:
time: 232 us; the launch traced here: 231 us
  waiting for transfers between devices  89.5 us (39%)
  starting transfers between devices  65.2 us (28%)
  blocking collectives  49.3 us (21%)
  other arithmetic  9.68 us (4%)
  local copies, waits for them, and re-layouts  8.25 us (4%)
  matrix products  7.16 us (3%)
    all_to_all x4, waiting for transfers between devices, spread(): lax.all_to_all(jnp.broadcast_to(array[None], (count,) + array.shape), axe...  53.1 us
    ppermute x9, starting transfers between devices, shift(): lax.ppermute(array, axis, [(i, (i + step) % size) for i in range(size)])  35.4 us
    all_to_all x1, blocking collectives, body(): partial = jnp.sum(lax.all_to_all(partial, 'x', 0, 0), 0)  25.1 us
    ppermute x9, waiting for transfers between devices, shift(): lax.ppermute(array, axis, [(i, (i + step) % size) for i in range(size)])  23.4 us
    all_to_all x4, starting transfers between devices, spread(): lax.all_to_all(jnp.broadcast_to(array[None], (count,) + array.shape), axe...  21.7 us
    all_to_all x2, blocking collectives, spread(): lax.all_to_all(jnp.broadcast_to(array[None], (count,) + array.shape), axe...  17.8 us
    all_to_all x1, waiting for transfers between devices, body(): own = jnp.sum(lax.all_to_all(packed, 'yh', 0, 0), 0)  13 us
    all_to_all x1, blocking collectives, body(): partial = jnp.sum(lax.all_to_all(partial, 'c', 0, 0), 0)  6.37 us
  transfers between devices with their start and end apart: 15, of which 12 were waited for; matrix products, arithmetic and copies ran while one was open for 4% of the time, Pallas kernels for 0%

profile of v1, /device:TPU:66, one launch (start us, length us, event | category | flops | bytes accessed | tf_op | source)
XLA Modules:
  0.0 231.1 jit_solution(11445955946772467356)
XLA Ops:
  2.0 3.5 %collective-permute-start = (bf16[320,1024]{1,0:T(8,128)(2,1)S(1)}, bf16[320,1024]{1,0:T(8,128)(2,1)S(1)}, u32[]{:S(2)}, u32[]{:S(2)}) collective-permute-start(bf16[320,1024]{1,0:T(8,128)(2,1)S(1)} %constant_dynamic-update-slice_fusion), channel_id=1, source_target_pairs={{0,8},{8,0},{1,9},{9,1},{2,10},{10,2},{3,11},{11,3},{4,12},{12,4},... | collective-permute-start | bytes 1966088 | tf_op jit(solution)/shard_map/ppermute | solution.py:16
  7.4 4.3 %collective-permute-start.5 = (bf16[160,1024]{1,0:T(8,128)(2,1)}, bf16[160,1024]{1,0:T(8,128)(2,1)S(1)}, u32[]{:S(2)}, u32[]{:S(2)}) collective-permute-start(bf16[160,1024]{1,0:T(8,128)(2,1)} %param.2), channel_id=1, source_target_pairs={{0,1},{1,2},{2,3},{3,4},{4,5},{5,6},{6,7},{7,0},{8,9},{9,10},{10,1... | collective-permute-start | bytes 983048 | tf_op jit(solution)/shard_map/ppermute | solution.py:16
  11.7 5.7 %collective-permute-done.1 = bf16[160,1024]{1,0:T(8,128)(2,1)S(1)} collective-permute-done((bf16[160,1024]{1,0:T(8,128)(2,1)}, bf16[160,1024]{1,0:T(8,128)(2,1)S(1)}, u32[]{:S(2)}, u32[]{:S(2)}) %collective-permute-start.1) | collective-permute-done | bytes 327712 | tf_op jit(solution)/shard_map/ppermute | solution.py:16
  17.4 7.6 %collective-permute-start.2 = (bf16[160,1024]{1,0:T(8,128)(2,1)S(1)}, bf16[160,1024]{1,0:T(8,128)(2,1)S(1)}, u32[]{:S(2)}, u32[]{:S(2)}) collective-permute-start(bf16[160,1024]{1,0:T(8,128)(2,1)S(1)} %collective-permute-done.1), channel_id=1, source_target_pairs={{0,7},{1,0},{2,1},{3,2},{4,3},{5,4},{6,5},{7,6},{8,15},{9,8},{10,9... | collective-permute-start | bytes 983048 | tf_op jit(solution)/shard_map/ppermute | solution.py:16
  27.5 3.2 %collective-permute-done.2 = bf16[160,1024]{1,0:T(8,128)(2,1)S(1)} collective-permute-done((bf16[160,1024]{1,0:T(8,128)(2,1)S(1)}, bf16[160,1024]{1,0:T(8,128)(2,1)S(1)}, u32[]{:S(2)}, u32[]{:S(2)}) %collective-permute-start.2) | collective-permute-done | bytes 327712 | tf_op jit(solution)/shard_map/ppermute | solution.py:16
  30.7 5.5 %collective-permute-start.3 = (bf16[160,1024]{1,0:T(8,128)(2,1)S(1)}, bf16[160,1024]{1,0:T(8,128)(2,1)S(1)}, u32[]{:S(2)}, u32[]{:S(2)}) collective-permute-start(bf16[160,1024]{1,0:T(8,128)(2,1)S(1)} %collective-permute-done.2), channel_id=1, source_target_pairs={{0,7},{1,0},{2,1},{3,2},{4,3},{5,4},{6,5},{7,6},{8,15},{9,8},{10,9... | collective-permute-start | bytes 983048 | tf_op jit(solution)/shard_map/ppermute | solution.py:16
  37.4 3.7 %collective-permute-done.3 = bf16[160,1024]{1,0:T(8,128)(2,1)S(1)} collective-permute-done((bf16[160,1024]{1,0:T(8,128)(2,1)S(1)}, bf16[160,1024]{1,0:T(8,128)(2,1)S(1)}, u32[]{:S(2)}, u32[]{:S(2)}) %collective-permute-start.3) | collective-permute-done | bytes 327712 | tf_op jit(solution)/shard_map/ppermute | solution.py:16
  41.1 5.6 %collective-permute-start.4 = (bf16[160,1024]{1,0:T(8,128)(2,1)S(1)}, bf16[160,1024]{1,0:T(8,128)(2,1)S(1)}, u32[]{:S(2)}, u32[]{:S(2)}) collective-permute-start(bf16[160,1024]{1,0:T(8,128)(2,1)S(1)} %collective-permute-done.3), channel_id=1, source_target_pairs={{0,7},{1,0},{2,1},{3,2},{4,3},{5,4},{6,5},{7,6},{8,15},{9,8},{10,9... | collective-permute-start | bytes 983048 | tf_op jit(solution)/shard_map/ppermute | solution.py:16
  51.8 6.1 %collective-permute-done.7 = bf16[160,1024]{1,0:T(8,128)(2,1)S(1)} collective-permute-done((bf16[160,1024]{1,0:T(8,128)(2,1)S(1)}, bf16[160,1024]{1,0:T(8,128)(2,1)S(1)}, u32[]{:S(2)}, u32[]{:S(2)}) %collective-permute-start.7) | collective-permute-done | bytes 327712 | tf_op jit(solution)/shard_map/ppermute | solution.py:16
  59.6 6.4 %all_to_all.45 = f32[2,4,160,640]{3,2,1,0:T(8,128)S(1)} all-to-all(f32[2,4,160,640]{3,2,1,0:T(8,128)S(1)} %bitcast.88), channel_id=1, replica_groups=mesh['yh'=4,'x'=4,'c'=2,'yl'=2,'z'=8] {'c'}, dimensions={0} | all-to-all | bytes 6553600 | tf_op jit(solution)/shard_map/all_to_all | solution.py:73
  67.6 25.1 %all_to_all.46 = f32[4,160,640]{2,1,0:T(8,128)S(1)} all-to-all(f32[4,160,640]{2,1,0:T(8,128)} %reduce_sum.54), channel_id=1, replica_groups=mesh['yh'=4,'x'=4,'c'=2,'yl'=2,'z'=8] {'x'}, dimensions={0} | all-to-all | bytes 3276800 | tf_op jit(solution)/shard_map/all_to_all | solution.py:74
  94.1 6.2 %all-to-all-start.2 = ((f32[4,40,640]{2,1,0:T(8,128)}), f32[4,40,640]{2,1,0:T(8,128)S(1)}, u32[]{:S(2)}, u32[]{:S(2)}) async-start(f32[4,40,640]{2,1,0:T(8,128)} %pad_maximum_fusion.2), calls=%async_computation.2 | async-start | bytes 819200 | tf_op jit(solution)/shard_map/all_to_all | solution.py:91
  100.3 13.0 %all-to-all-done.2 = f32[4,40,640]{2,1,0:T(8,128)S(1)} async-done(((f32[4,40,640]{2,1,0:T(8,128)}), f32[4,40,640]{2,1,0:T(8,128)S(1)}, u32[]{:S(2)}, u32[]{:S(2)}) %all-to-all-start.2) | async-done | bytes 409632 | tf_op jit(solution)/shard_map/all_to_all | solution.py:91
  113.4 3.3 %collective-permute-start.9 = (f32[40,320]{1,0:T(8,128)S(1)}, f32[40,320]{1,0:T(8,128)S(1)}, u32[]{:S(2)}, u32[]{:S(2)}) collective-permute-start(f32[40,320]{1,0:T(8,128)S(1)} %slice.226), channel_id=1, source_target_pairs={{0,8},{8,0},{1,9},{9,1},{2,10},{10,2},{3,11},{11,3},{4,12},{12,4},... | collective-permute-start | bytes 153608 | tf_op jit(solution)/shard_map/ppermute | solution.py:16
  119.7 12.5 %all_to_all.47 = f32[4,40,320]{2,1,0:T(8,128)S(1)} all-to-all(f32[4,40,320]{2,1,0:T(8,128)S(1)} %broadcast_in_dim.26), channel_id=1, replica_groups=mesh['yh'=4,'x'=4,'c'=2,'yl'=2,'z'=8] {'yh'}, dimensions={0} | all-to-all | bytes 409600 | tf_op jit(solution)/shard_map/all_to_all | solution.py:20
  133.3 4.9 %all-to-all-start.4 = ((f32[4,160,320]{2,1,0:T(8,128)}), f32[4,160,320]{2,1,0:T(8,128)S(1)}, u32[]{:S(2)}, u32[]{:S(2)}) async-start(f32[4,160,320]{2,1,0:T(8,128)} %broadcast_in_dim.28), calls=%async_computation.4 | async-start | bytes 1966080 | tf_op jit(solution)/shard_map/all_to_all | solution.py:20
  140.3 11.1 %all-to-all-done.4 = f32[4,160,320]{2,1,0:T(8,128)S(1)} async-done(((f32[4,160,320]{2,1,0:T(8,128)}), f32[4,160,320]{2,1,0:T(8,128)S(1)}, u32[]{:S(2)}, u32[]{:S(2)}) %all-to-all-start.4) | async-done | bytes 819232 | tf_op jit(solution)/shard_map/all_to_all | solution.py:20
  151.5 5.3 %all_to_all.48 = f32[2,4,160,320]{3,2,1,0:T(8,128)S(1)} all-to-all(f32[2,4,160,320]{3,2,1,0:T(8,128)S(1)} %broadcast_in_dim.52), channel_id=1, replica_groups=mesh['yh'=4,'x'=4,'c'=2,'yl'=2,'z'=8] {'c'}, dimensions={0} | all-to-all | bytes 3276800 | tf_op jit(solution)/shard_map/all_to_all | solution.py:20
  161.3 6.5 %all-to-all-start.6 = ((f32[16,1,128]{2,1,0:T(1,128)}), f32[16,1,128]{2,1,0:T(1,128)S(1)}, u32[]{:S(2)}, u32[]{:S(2)}) async-start(f32[16,1,128]{2,1,0:T(1,128)} %broadcast_in_dim.56), calls=%async_computation.6 | async-start | bytes 16384 | tf_op jit(solution)/shard_map/all_to_all | solution.py:20
  167.9 7.1 %all-to-all-done.6 = f32[16,1,128]{2,1,0:T(1,128)S(1)} async-done(((f32[16,1,128]{2,1,0:T(1,128)}), f32[16,1,128]{2,1,0:T(1,128)S(1)}, u32[]{:S(2)}, u32[]{:S(2)}) %all-to-all-start.6) | async-done | bytes 8224 | tf_op jit(solution)/shard_map/all_to_all | solution.py:20
  178.2 4.8 %all-to-all-start.7 = ((bf16[16,160,80]{2,1,0:T(8,128)(2,1)}), bf16[16,160,80]{2,1,0:T(8,128)(2,1)S(1)}, u32[]{:S(2)}, u32[]{:S(2)}) async-start(bf16[16,160,80]{2,1,0:T(8,128)(2,1)} %broadcast_in_dim.57), calls=%async_computation.7 | async-start | bytes 1310720 | tf_op jit(solution)/shard_map/all_to_all | solution.py:20
  184.3 16.5 %all-to-all-done.7 = bf16[16,160,80]{2,1,0:T(8,128)(2,1)S(1)} async-done(((bf16[16,160,80]{2,1,0:T(8,128)(2,1)}), bf16[16,160,80]{2,1,0:T(8,128)(2,1)S(1)}, u32[]{:S(2)}, u32[]{:S(2)}) %all-to-all-start.7) | async-done | bytes 409632 | tf_op jit(solution)/shard_map/all_to_all | solution.py:20
  204.5 5.4 %all-to-all-start.8 = ((bf16[16,160,80]{2,1,0:T(8,128)(2,1)}), bf16[16,160,80]{2,1,0:T(8,128)(2,1)S(1)}, u32[]{:S(2)}, u32[]{:S(2)}) async-start(bf16[16,160,80]{2,1,0:T(8,128)(2,1)} %broadcast_in_dim.58), calls=%async_computation.8 | async-start | bytes 1310720 | tf_op jit(solution)/shard_map/all_to_all | solution.py:20
  210.1 18.4 %all-to-all-done.8 = bf16[16,160,80]{2,1,0:T(8,128)(2,1)S(1)} async-done(((bf16[16,160,80]{2,1,0:T(8,128)(2,1)}), bf16[16,160,80]{2,1,0:T(8,128)(2,1)S(1)}, u32[]{:S(2)}, u32[]{:S(2)}) %all-to-all-start.8) | async-done | bytes 409632 | tf_op jit(solution)/shard_map/all_to_all | solution.py:20
  (75 shorter events, 37.5 us)
Async XLA Ops:
  2.0 25.3 %collective-permute-start = (bf16[320,1024]{1,0:T(8,128)(2,1)S(1)}, bf16[320,1024]{1,0:T(8,128)(2,1)S(1)}, u32[]{:S(2)}, u32[]{:S(2)}) collective-permute-start(bf16[320,1024]{1,0:T(8,128)(2,1)S(1)} %constant_dynamic-update-slice_fusion), channel_id=1, source_target_pairs={{0,8},{8,0},{1,9},{9,1},{2,10},{10,2},{3,11},{11,3},{4,12},{12,4},... | collective-permute-start | bytes 1966088 | tf_op jit(solution)/shard_map/ppermute | solution.py:16
  5.5 11.9 %collective-permute-start.1 = (bf16[160,1024]{1,0:T(8,128)(2,1)}, bf16[160,1024]{1,0:T(8,128)(2,1)S(1)}, u32[]{:S(2)}, u32[]{:S(2)}) collective-permute-start(bf16[160,1024]{1,0:T(8,128)(2,1)} %param.2), channel_id=1, source_target_pairs={{0,7},{1,0},{2,1},{3,2},{4,3},{5,4},{6,5},{7,6},{8,15},{9,8},{10,9... | collective-permute-start | bytes 983048 | tf_op jit(solution)/shard_map/ppermute | solution.py:16
  7.4 17.9 %collective-permute-start.5 = (bf16[160,1024]{1,0:T(8,128)(2,1)}, bf16[160,1024]{1,0:T(8,128)(2,1)S(1)}, u32[]{:S(2)}, u32[]{:S(2)}) collective-permute-start(bf16[160,1024]{1,0:T(8,128)(2,1)} %param.2), channel_id=1, source_target_pairs={{0,1},{1,2},{2,3},{3,4},{4,5},{5,6},{6,7},{7,0},{8,9},{9,10},{10,1... | collective-permute-start | bytes 983048 | tf_op jit(solution)/shard_map/ppermute | solution.py:16
  11.7 24.5 %copy-start.3 = (bf16[160,1024]{1,0:T(8,128)(2,1)S(1)}, bf16[160,1024]{1,0:T(8,128)(2,1)}, u32[]{:S(2)}) copy-start(bf16[160,1024]{1,0:T(8,128)(2,1)} %param.2) | copy-start | bytes 983044
  17.4 13.3 %collective-permute-start.2 = (bf16[160,1024]{1,0:T(8,128)(2,1)S(1)}, bf16[160,1024]{1,0:T(8,128)(2,1)S(1)}, u32[]{:S(2)}, u32[]{:S(2)}) collective-permute-start(bf16[160,1024]{1,0:T(8,128)(2,1)S(1)} %collective-permute-done.1), channel_id=1, source_target_pairs={{0,7},{1,0},{2,1},{3,2},{4,3},{5,4},{6,5},{7,6},{8,15},{9,8},{10,9... | collective-permute-start | bytes 983048 | tf_op jit(solution)/shard_map/ppermute | solution.py:16
  25.4 21.9 %collective-permute-start.6 = (bf16[160,1024]{1,0:T(8,128)(2,1)S(1)}, bf16[160,1024]{1,0:T(8,128)(2,1)S(1)}, u32[]{:S(2)}, u32[]{:S(2)}) collective-permute-start(bf16[160,1024]{1,0:T(8,128)(2,1)S(1)} %collective-permute-done.5), channel_id=1, source_target_pairs={{0,1},{1,2},{2,3},{3,4},{4,5},{5,6},{6,7},{7,0},{8,9},{9,10},{10,1... | collective-permute-start | bytes 983048 | tf_op jit(solution)/shard_map/ppermute | solution.py:16
  30.7 10.3 %collective-permute-start.3 = (bf16[160,1024]{1,0:T(8,128)(2,1)S(1)}, bf16[160,1024]{1,0:T(8,128)(2,1)S(1)}, u32[]{:S(2)}, u32[]{:S(2)}) collective-permute-start(bf16[160,1024]{1,0:T(8,128)(2,1)S(1)} %collective-permute-done.2), channel_id=1, source_target_pairs={{0,7},{1,0},{2,1},{3,2},{4,3},{5,4},{6,5},{7,6},{8,15},{9,8},{10,9... | collective-permute-start | bytes 983048 | tf_op jit(solution)/shard_map/ppermute | solution.py:16
  41.1 10.2 %collective-permute-start.4 = (bf16[160,1024]{1,0:T(8,128)(2,1)S(1)}, bf16[160,1024]{1,0:T(8,128)(2,1)S(1)}, u32[]{:S(2)}, u32[]{:S(2)}) collective-permute-start(bf16[160,1024]{1,0:T(8,128)(2,1)S(1)} %collective-permute-done.3), channel_id=1, source_target_pairs={{0,7},{1,0},{2,1},{3,2},{4,3},{5,4},{6,5},{7,6},{8,15},{9,8},{10,9... | collective-permute-start | bytes 983048 | tf_op jit(solution)/shard_map/ppermute | solution.py:16
  47.3 10.6 %collective-permute-start.7 = (bf16[160,1024]{1,0:T(8,128)(2,1)S(1)}, bf16[160,1024]{1,0:T(8,128)(2,1)S(1)}, u32[]{:S(2)}, u32[]{:S(2)}) collective-permute-start(bf16[160,1024]{1,0:T(8,128)(2,1)S(1)} %collective-permute-done.6), channel_id=1, source_target_pairs={{0,1},{1,2},{2,3},{3,4},{4,5},{5,6},{6,7},{7,0},{8,9},{9,10},{10,1... | collective-permute-start | bytes 983048 | tf_op jit(solution)/shard_map/ppermute | solution.py:16
  94.1 19.2 %all-to-all-start.2 = ((f32[4,40,640]{2,1,0:T(8,128)}), f32[4,40,640]{2,1,0:T(8,128)S(1)}, u32[]{:S(2)}, u32[]{:S(2)}) async-start(f32[4,40,640]{2,1,0:T(8,128)} %pad_maximum_fusion.2), calls=%async_computation.2 | async-start | bytes 819200 | tf_op jit(solution)/shard_map/all_to_all | solution.py:91
  113.4 6.1 %collective-permute-start.9 = (f32[40,320]{1,0:T(8,128)S(1)}, f32[40,320]{1,0:T(8,128)S(1)}, u32[]{:S(2)}, u32[]{:S(2)}) collective-permute-start(f32[40,320]{1,0:T(8,128)S(1)} %slice.226), channel_id=1, source_target_pairs={{0,8},{8,0},{1,9},{9,1},{2,10},{10,2},{3,11},{11,3},{4,12},{12,4},... | collective-permute-start | bytes 153608 | tf_op jit(solution)/shard_map/ppermute | solution.py:16
  133.3 18.1 %all-to-all-start.4 = ((f32[4,160,320]{2,1,0:T(8,128)}), f32[4,160,320]{2,1,0:T(8,128)S(1)}, u32[]{:S(2)}, u32[]{:S(2)}) async-start(f32[4,160,320]{2,1,0:T(8,128)} %broadcast_in_dim.28), calls=%async_computation.4 | async-start | bytes 1966080 | tf_op jit(solution)/shard_map/all_to_all | solution.py:20
  138.3 29.5 %collective-permute-start.8 = (f32[40,320]{0,1:T(8,128)S(1)}, f32[40,320]{0,1:T(8,128)S(1)}, u32[]{:S(2)}, u32[]{:S(2)}) collective-permute-start(f32[40,320]{0,1:T(8,128)S(1)} %copy.26), channel_id=1, source_target_pairs={{0,0},{1,33},{2,66},{3,99},{4,132},{5,165},{6,198},{7,231},{8,8},{... | collective-permute-start | bytes 153608 | tf_op jit(solution)/shard_map/ppermute | solution.py:93
  161.3 13.6 %all-to-all-start.6 = ((f32[16,1,128]{2,1,0:T(1,128)}), f32[16,1,128]{2,1,0:T(1,128)S(1)}, u32[]{:S(2)}, u32[]{:S(2)}) async-start(f32[16,1,128]{2,1,0:T(1,128)} %broadcast_in_dim.56), calls=%async_computation.6 | async-start | bytes 16384 | tf_op jit(solution)/shard_map/all_to_all | solution.py:20
  178.2 22.6 %all-to-all-start.7 = ((bf16[16,160,80]{2,1,0:T(8,128)(2,1)}), bf16[16,160,80]{2,1,0:T(8,128)(2,1)S(1)}, u32[]{:S(2)}, u32[]{:S(2)}) async-start(bf16[16,160,80]{2,1,0:T(8,128)(2,1)} %broadcast_in_dim.57), calls=%async_computation.7 | async-start | bytes 1310720 | tf_op jit(solution)/shard_map/all_to_all | solution.py:20
  184.1 17.1 %copy-start = (bf16[1280,320]{1,0:T(8,128)(2,1)S(1)}, bf16[1280,320]{1,0:T(8,128)(2,1)}, u32[]{:S(2)}) copy-start(bf16[1280,320]{1,0:T(8,128)(2,1)} %get-tuple-element.11) | copy-start | bytes 2457604
  200.8 1.2 copy-start.1
  203.3 25.5 %copy-start.2 = (bf16[1280,320]{1,0:T(8,128)(2,1)S(1)}, bf16[1280,320]{1,0:T(8,128)(2,1)}, u32[]{:S(2)}) copy-start(bf16[1280,320]{1,0:T(8,128)(2,1)} %fusion) | copy-start | bytes 2457604
  204.5 23.9 %all-to-all-start.8 = ((bf16[16,160,80]{2,1,0:T(8,128)(2,1)}), bf16[16,160,80]{2,1,0:T(8,128)(2,1)S(1)}, u32[]{:S(2)}, u32[]{:S(2)}) async-start(bf16[16,160,80]{2,1,0:T(8,128)(2,1)} %broadcast_in_dim.58), calls=%async_computation.8 | async-start | bytes 1310720 | tf_op jit(solution)/shard_map/all_to_all | solution.py:20

commit v2 on v1

v2 whole, which is shorter than its diff:
```python
import jax
import jax.numpy as jnp
import numpy as np
from jax import lax
from jax.sharding import Mesh, PartitionSpec as P

ITERS = 2
ridge_share = 0.2
TOK = ("yh", "x", "c")
FEAT = ("yl", "z")
ALL = TOK + FEAT
SIZES = (4, 4, 2, 2, 8)


def shift(array, axis, size, step):
    return lax.ppermute(array, axis, [(i, (i + step) % size) for i in range(size)])


def spread(array, axes, count):
    return lax.all_to_all(
        jnp.broadcast_to(array[None], (count,) + array.shape), axes, 0, 0
    )


def tile_moves():
    moves = []
    for yh in range(4):
        for x in range(4):
            for c in range(2):
                for yl in range(2):
                    for z in range(8):
                        other_yl, half = yh // 2, yh % 2
                        source = (((yh * 4 + x) * 2 + c) * 2 + yl) * 8 + z
                        to_z = (z + 4 * c + x) % 8
                        to_yh, to_x = other_yl * 2 + z // 4, z % 4
                        target = (((to_yh * 4 + to_x) * 2 + half) * 2 + yl) * 8 + to_z
                        moves.append((source, target))
    return moves


def body(entering, leaving):
    yl = lax.axis_index("yl")
    z = lax.axis_index("z")
    rows = entering.shape[0]
    quarter = rows // 4
    half_cols = rows // 2
    token_total = entering.shape[1] * 32
    order_all = rows * 16
    low = yl == 0

    pair = jnp.concatenate([entering, leaving], 0)
    other = shift(pair, "yl", 2, 1)
    first = jnp.where(low, pair, other)
    second = jnp.where(low, other, pair)
    columns = jnp.concatenate([first[:rows], second[:rows], first[rows:], second[rows:]], 0)

    blocks = {0: entering}
    up = down = entering
    for step in range(1, 5):
        down = shift(down, "z", 8, -1)
        blocks[step] = down
        if step < 4:
            up = shift(up, "z", 8, 1)
            blocks[8 - step] = up

    pieces = [
        lax.dot_general(
            blocks[s], columns, (((1,), (1,)), ((), ())), preferred_element_type=jnp.float32
        )
        for s in range(8)
    ]
    partial = jnp.stack(pieces).reshape(2, 4, rows, 4 * rows)
    partial = jnp.sum(lax.all_to_all(partial, "c", 0, 0), 0)
    partial = jnp.sum(lax.all_to_all(partial, "x", 0, 0), 0)
    packed = []
    for to_yh in range(4):
        for to_yl in range(2):
            top = half_cols * to_yl
            left = 2 * rows + half_cols * to_yh
            packed.append(
                jnp.concatenate(
                    [
                        partial[
                            quarter * to_yh : quarter * (to_yh + 1),
                            rows * to_yl : rows * (to_yl + 1),
                        ],
                        partial[top : top + quarter, left : left + half_cols],
                        partial[top + quarter : top + 2 * quarter, left : left + half_cols],
                    ],
                    1,
                )
            )
    own = lax.all_to_all(jnp.stack(packed), ("yh", "yl"), 0, 0)
    own = jnp.sum(own.reshape(4, 2, quarter, 2 * rows), 0)

    cross_own = jnp.concatenate([own[0, :, rows:], own[1, :, rows:]], 1)
    cross_own = lax.ppermute(cross_own, ALL, tile_moves()) / token_total
    cross_all = spread(cross_own, FEAT, 16).reshape(2, 8 * quarter, 2 * rows)
    target_all = jnp.concatenate(
        [
            cross_all[0, :, :rows],
            cross_all[1, :, :rows],
            cross_all[0, :, rows:],
            cross_all[1, :, rows:],
        ],
        1,
    )

    gram_part = jnp.concatenate([own[0, :, :rows], own[1, :, :rows]], 1)
    gram_part = spread(gram_part, "yh", 4)
    gram_part = jnp.concatenate([gram_part[q] for q in range(4)], 1)
    gram_part = spread(gram_part, "x", 4)
    gram = spread(gram_part, "c", 2).reshape(8 * quarter, 8 * rows)

    sums = jnp.sum(jnp.abs(gram), 0)
    row_peak = jnp.max(jnp.sum(sums.reshape(8, rows), 0))
    at_row = lax.broadcasted_iota(jnp.int32, (quarter, 8 * rows), 0)
    at_col = lax.broadcasted_iota(jnp.int32, (quarter, 8 * rows), 1)
    on_diagonal = at_col % (2 * rows) == rows * yl + quarter * (at_col // (2 * rows)) + at_row
    trace = jnp.sum(jnp.where(on_diagonal, gram[:quarter], 0.0))

    def halves(array):
        high = lax.reduce_precision(array, 8, 7)
        return high.astype(jnp.bfloat16), (array - high).astype(jnp.bfloat16)

    gram_high, gram_low = halves(gram)

    def turn(array):
        twice = jnp.concatenate([array, array], 0)
        return lax.dynamic_slice_in_dim(twice, quarter * z, 8 * quarter, 0)

    def times_gram(sides):
        product = 0.0
        for part in (gram_high, gram_low):
            for side in sides:
                wide = lax.dot_general(
                    part, side, (((0,), (0,)), ((), ())), preferred_element_type=jnp.float32
                )
                for q in range(4):
                    for k in range(2):
                        r0, c0 = (q * 2 + k) * rows, (k * 4 + q) * half_cols
                        product += wide[r0 : r0 + rows, c0 : c0 + half_cols]
        return jnp.concatenate([product[quarter * g : quarter * (g + 1)] for g in range(4)], 1)

    def own_tile(array):
        return lax.dynamic_slice(
            array, (quarter * z, 2 * rows * yl), (quarter, 2 * rows)
        )

    first_own = times_gram([turn(p) for p in halves(target_all)]) / token_total
    lane = lax.broadcasted_iota(jnp.int32, (quarter, 64), 1)
    tail = jnp.where(lane == 0, row_peak, trace)
    gathered = spread(jnp.concatenate([first_own, tail], 1), FEAT, 16)
    peak_all = jnp.max(gathered[:, 0, 2 * rows])
    energy = jnp.sum(gathered[:, 0, 2 * rows + 1])
    gathered = gathered.reshape(2, 8 * quarter, 2 * rows + 64)
    first_all = jnp.concatenate([gathered[0, :, : 2 * rows], gathered[1, :, : 2 * rows]], 1)

    ridge_term = ridge_share * energy / (token_total * order_all)
    upper_bound = peak_all / token_total + ridge_term
    center = (upper_bound + ridge_term) / 2.0
    half_span = (upper_bound - ridge_term) / 2.0

    ratio_now = half_span / center
    ratio_next = 1.0 / (2.0 * center / half_span - ratio_now)
    start = target_all / center
    residual = target_all - (first_all / center + ridge_term * start)
    update = ratio_next * ratio_now * start + 2.0 * ratio_next / half_span * residual
    transform = start + update
    ratio_now = ratio_next

    iterate_half = lax.reduce_precision(transform, 8, 7)
    applied = times_gram([turn(iterate_half.astype(jnp.bfloat16))]) / token_total
    residual = own_tile(target_all) - (applied + ridge_term * own_tile(iterate_half))
    ratio_next = 1.0 / (2.0 * center / half_span - ratio_now)
    final = own_tile(transform) + (
        ratio_next * ratio_now * own_tile(update) + 2.0 * ratio_next / half_span * residual
    )
    return jnp.concatenate(
        [final[:, half_cols * g : half_cols * (g + 1)] for g in range(4)], 0
    )


def solution(mesh):
    fine = Mesh(mesh.devices.reshape(SIZES), ALL)
    spec = P(FEAT, TOK)
    return jax.shard_map(
        body, mesh=fine, in_specs=(spec, spec), out_specs=spec, check_vma=False
    )
```

time: 232 us -> 239 us (1.030)
  the two profiles are of different devices: /device:TPU:66 before, /device:TPU:86 now
where the time goes in v2:
time: 239 us
  waiting for transfers between devices  74.6 us (31%)
  blocking collectives  68.4 us (29%)
  starting transfers between devices  57 us (24%)
  matrix products  16.1 us (7%)
  other arithmetic  12.9 us (5%)
  local copies, waits for them, and re-layouts  7.54 us (3%)
    all_to_all x3, waiting for transfers between devices, spread(): lax.all_to_all(jnp.broadcast_to(array[None], (count,) + array.shape), axe...  49.4 us
    ppermute x8, starting transfers between devices, shift(): lax.ppermute(array, axis, [(i, (i + step) % size) for i in range(size)])  32 us
    all_to_all x1, blocking collectives, body(): partial = jnp.sum(lax.all_to_all(partial, 'x', 0, 0), 0)  24.4 us
    all_to_all x3, starting transfers between devices, spread(): lax.all_to_all(jnp.broadcast_to(array[None], (count,) + array.shape), axe...  20.8 us
    all_to_all x1, blocking collectives, body(): own = lax.all_to_all(jnp.stack(packed), ('yh', 'yl'), 0, 0)  19.6 us
    all_to_all x2, blocking collectives, spread(): lax.all_to_all(jnp.broadcast_to(array[None], (count,) + array.shape), axe...  18 us
    ppermute x8, waiting for transfers between devices, shift(): lax.ppermute(array, axis, [(i, (i + step) % size) for i in range(size)])  17 us
    dot_general x6, matrix products, times_gram(): lax.dot_general(part, side, (((0,), (0,)), ((), ())), preferred_element_t...  11.6 us
  transfers between devices with their start and end apart: 12, of which 8 were waited for; matrix products, arithmetic and copies ran while one was open for 3% of the time, Pallas kernels for 0%

profile of v2, /device:TPU:86, one launch (start us, length us, event | category | flops | bytes accessed | tf_op | source)
XLA Modules:
  0.0 238.5 jit_solution(6111822207917741385)
XLA Ops:
  2.0 3.5 %collective-permute-start = (bf16[320,1024]{1,0:T(8,128)(2,1)S(1)}, bf16[320,1024]{1,0:T(8,128)(2,1)S(1)}, u32[]{:S(2)}, u32[]{:S(2)}) collective-permute-start(bf16[320,1024]{1,0:T(8,128)(2,1)S(1)} %constant_dynamic-update-slice_fusion), channel_id=1, source_target_pairs={{0,8},{8,0},{1,9},{9,1},{2,10},{10,2},{3,11},{11,3},{4,12},{12,4},... | collective-permute-start | bytes 1966088 | tf_op jit(solution)/shard_map/ppermute | solution.py:16
  5.5 4.3 %collective-permute-start.5 = (bf16[160,1024]{1,0:T(8,128)(2,1)}, bf16[160,1024]{1,0:T(8,128)(2,1)S(1)}, u32[]{:S(2)}, u32[]{:S(2)}) collective-permute-start(bf16[160,1024]{1,0:T(8,128)(2,1)} %param.2), channel_id=1, source_target_pairs={{0,1},{1,2},{2,3},{3,4},{4,5},{5,6},{6,7},{7,0},{8,9},{9,10},{10,1... | collective-permute-start | bytes 983048 | tf_op jit(solution)/shard_map/ppermute | solution.py:16
  11.7 5.0 %collective-permute-done.5 = bf16[160,1024]{1,0:T(8,128)(2,1)S(1)} collective-permute-done((bf16[160,1024]{1,0:T(8,128)(2,1)}, bf16[160,1024]{1,0:T(8,128)(2,1)S(1)}, u32[]{:S(2)}, u32[]{:S(2)}) %collective-permute-start.5) | collective-permute-done | bytes 327712 | tf_op jit(solution)/shard_map/ppermute | solution.py:16
  16.8 4.3 %collective-permute-start.6 = (bf16[160,1024]{1,0:T(8,128)(2,1)S(1)}, bf16[160,1024]{1,0:T(8,128)(2,1)S(1)}, u32[]{:S(2)}, u32[]{:S(2)}) collective-permute-start(bf16[160,1024]{1,0:T(8,128)(2,1)S(1)} %collective-permute-done.5), channel_id=1, source_target_pairs={{0,1},{1,2},{2,3},{3,4},{4,5},{5,6},{6,7},{7,0},{8,9},{9,10},{10,1... | collective-permute-start | bytes 983048 | tf_op jit(solution)/shard_map/ppermute | solution.py:16
  21.4 6.1 %collective-permute-start.2 = (bf16[160,1024]{1,0:T(8,128)(2,1)S(1)}, bf16[160,1024]{1,0:T(8,128)(2,1)S(1)}, u32[]{:S(2)}, u32[]{:S(2)}) collective-permute-start(bf16[160,1024]{1,0:T(8,128)(2,1)S(1)} %collective-permute-done.1), channel_id=1, source_target_pairs={{0,7},{1,0},{2,1},{3,2},{4,3},{5,4},{6,5},{7,6},{8,15},{9,8},{10,9... | collective-permute-start | bytes 983048 | tf_op jit(solution)/shard_map/ppermute | solution.py:16
  27.8 5.9 %collective-permute-done.2 = bf16[160,1024]{1,0:T(8,128)(2,1)S(1)} collective-permute-done((bf16[160,1024]{1,0:T(8,128)(2,1)S(1)}, bf16[160,1024]{1,0:T(8,128)(2,1)S(1)}, u32[]{:S(2)}, u32[]{:S(2)}) %collective-permute-start.2) | collective-permute-done | bytes 327712 | tf_op jit(solution)/shard_map/ppermute | solution.py:16
  33.6 4.8 %collective-permute-start.3 = (bf16[160,1024]{1,0:T(8,128)(2,1)S(1)}, bf16[160,1024]{1,0:T(8,128)(2,1)S(1)}, u32[]{:S(2)}, u32[]{:S(2)}) collective-permute-start(bf16[160,1024]{1,0:T(8,128)(2,1)S(1)} %collective-permute-done.2), channel_id=1, source_target_pairs={{0,7},{1,0},{2,1},{3,2},{4,3},{5,4},{6,5},{7,6},{8,15},{9,8},{10,9... | collective-permute-start | bytes 983048 | tf_op jit(solution)/shard_map/ppermute | solution.py:16
  41.6 2.3 collective-permute-done.3
  43.8 5.1 %collective-permute-start.4 = (bf16[160,1024]{1,0:T(8,128)(2,1)S(1)}, bf16[160,1024]{1,0:T(8,128)(2,1)S(1)}, u32[]{:S(2)}, u32[]{:S(2)}) collective-permute-start(bf16[160,1024]{1,0:T(8,128)(2,1)S(1)} %collective-permute-done.3), channel_id=1, source_target_pairs={{0,7},{1,0},{2,1},{3,2},{4,3},{5,4},{6,5},{7,6},{8,15},{9,8},{10,9... | collective-permute-start | bytes 983048 | tf_op jit(solution)/shard_map/ppermute | solution.py:16
  50.1 3.4 %collective-permute-done.4 = bf16[160,1024]{1,0:T(8,128)(2,1)S(1)} collective-permute-done((bf16[160,1024]{1,0:T(8,128)(2,1)S(1)}, bf16[160,1024]{1,0:T(8,128)(2,1)S(1)}, u32[]{:S(2)}, u32[]{:S(2)}) %collective-permute-start.4) | collective-permute-done | bytes 327712 | tf_op jit(solution)/shard_map/ppermute | solution.py:16
  55.8 6.4 %all_to_all.40 = f32[2,4,160,640]{3,2,1,0:T(8,128)S(1)} all-to-all(f32[2,4,160,640]{3,2,1,0:T(8,128)S(1)} %bitcast.131), channel_id=1, replica_groups=mesh['yh'=4,'x'=4,'c'=2,'yl'=2,'z'=8] {'c'}, dimensions={0} | all-to-all | bytes 6553600 | tf_op jit(solution)/shard_map/all_to_all | solution.py:73
  63.8 24.4 %all_to_all.41 = f32[4,160,640]{2,1,0:T(8,128)S(1)} all-to-all(f32[4,160,640]{2,1,0:T(8,128)} %reduce_sum.63), channel_id=1, replica_groups=mesh['yh'=4,'x'=4,'c'=2,'yl'=2,'z'=8] {'x'}, dimensions={0} | all-to-all | bytes 3276800 | tf_op jit(solution)/shard_map/all_to_all | solution.py:74
  89.3 19.6 %all_to_all.42 = f32[8,40,320]{2,1,0:T(8,128)S(1)} all-to-all(f32[8,40,320]{2,1,0:T(8,128)S(1)} %fusion.25), channel_id=1, replica_groups=mesh['yh'=4,'x'=4,'c'=2,'yl'=2,'z'=8] {'yh','yl'}, dimensions={0} | all-to-all | bytes 819200 | tf_op jit(solution)/shard_map/all_to_all | solution.py:93
  109.2 13.0 %all_to_all.43 = f32[4,40,320]{2,1,0:T(8,128)S(1)} all-to-all(f32[4,40,320]{2,1,0:T(8,128)S(1)} %broadcast_in_dim.23), channel_id=1, replica_groups=mesh['yh'=4,'x'=4,'c'=2,'yl'=2,'z'=8] {'yh'}, dimensions={0} | all-to-all | bytes 409600 | tf_op jit(solution)/shard_map/all_to_all | solution.py:20
  123.3 5.5 %all-to-all-start.5 = ((f32[4,40,1280]{2,1,0:T(8,128)}), f32[4,40,1280]{2,1,0:T(8,128)S(1)}, u32[]{:S(2)}, u32[]{:S(2)}) async-start(f32[4,40,1280]{2,1,0:T(8,128)} %broadcast_in_dim.24), calls=%async_computation.5 | async-start | bytes 1638400 | tf_op jit(solution)/shard_map/all_to_all | solution.py:20
  128.9 4.1 %collective-permute-start.8 = (f32[40,320]{1,0:T(8,128)S(1)}, f32[40,320]{1,0:T(8,128)S(1)}, u32[]{:S(2)}, u32[]{:S(2)}) collective-permute-start(f32[40,320]{1,0:T(8,128)S(1)} %pad_maximum_fusion.3), channel_id=1, source_target_pairs={{0,0},{1,33},{2,66},{3,99},{4,132},{5,165},{6,198},{7,231},{8,8},{... | collective-permute-start | bytes 153608 | tf_op jit(solution)/shard_map/ppermute | solution.py:97
  133.0 8.3 %collective-permute-done.8 = f32[40,320]{1,0:T(8,128)S(1)} collective-permute-done((f32[40,320]{1,0:T(8,128)S(1)}, f32[40,320]{1,0:T(8,128)S(1)}, u32[]{:S(2)}, u32[]{:S(2)}) %collective-permute-start.8) | collective-permute-done | bytes 51232 | tf_op jit(solution)/shard_map/ppermute | solution.py:97
  141.5 5.0 %all_to_all.44 = f32[2,4,40,1280]{3,2,1,0:T(8,128)S(1)} all-to-all(f32[2,4,40,1280]{3,2,1,0:T(8,128)S(1)} %broadcast_in_dim.25), channel_id=1, replica_groups=mesh['yh'=4,'x'=4,'c'=2,'yl'=2,'z'=8] {'c'}, dimensions={0} | all-to-all | bytes 3276800 | tf_op jit(solution)/shard_map/all_to_all | solution.py:20
  147.6 10.2 %all-to-all-start.3 = ((f32[16,40,320]{2,1,0:T(8,128)}), f32[16,40,320]{2,1,0:T(8,128)}, u32[]{:S(2)}, u32[]{:S(2)}) async-start(f32[16,40,320]{2,1,0:T(8,128)} %broadcast_in_dim.22), calls=%async_computation.3 | async-start | bytes 1966080 | tf_op jit(solution)/shard_map/all_to_all | solution.py:20
  160.9 23.1 %all-to-all-done.3 = f32[16,40,320]{2,1,0:T(8,128)} async-done(((f32[16,40,320]{2,1,0:T(8,128)}), f32[16,40,320]{2,1,0:T(8,128)}, u32[]{:S(2)}, u32[]{:S(2)}) %all-to-all-start.3) | async-done | bytes 819232 | tf_op jit(solution)/shard_map/all_to_all | solution.py:20
  193.4 5.1 %all-to-all-start.7 = ((f32[16,40,384]{2,1,0:T(8,128)}), f32[16,40,384]{2,1,0:T(8,128)S(1)}, u32[]{:S(2)}, u32[]{:S(2)}) async-start(f32[16,40,384]{2,1,0:T(8,128)} %broadcast_in_dim.49), calls=%async_computation.7 | async-start | bytes 1966080 | tf_op jit(solution)/shard_map/all_to_all | solution.py:20
  198.5 26.2 %all-to-all-done.7 = f32[16,40,384]{2,1,0:T(8,128)S(1)} async-done(((f32[16,40,384]{2,1,0:T(8,128)}), f32[16,40,384]{2,1,0:T(8,128)S(1)}, u32[]{:S(2)}, u32[]{:S(2)}) %all-to-all-start.7) | async-done | bytes 983072 | tf_op jit(solution)/shard_map/all_to_all | solution.py:20
  228.5 3.1 %fusion.45 = f32[1280,640]{1,0:T(8,128)} fusion(bf16[320,1280]{1,0:T(8,128)(2,1)S(1)} %get-tuple-element.12, s32[]{:T(128)S(6)} %select_n.53, bf16[320,640]{1,0:T(8,128)(2,1)S(1)} %reduce-precision_convert_fusion.2), kind=kOutput, calls=%fused_computation.153 | convolution fusion | flops 525107200 | bytes 4505604 | tf_op jit(solution)/shard_map/dot_general | solution.py:136
  231.6 3.0 %fusion.47 = f32[1280,640]{1,0:T(8,128)} fusion(bf16[320,1280]{1,0:T(8,128)(2,1)S(1)} %get-tuple-element.13, s32[]{:T(128)S(6)} %select_n.53, bf16[320,640]{1,0:T(8,128)(2,1)S(1)} %reduce-precision_convert_fusion.2), kind=kOutput, calls=%fused_computation.154 | convolution fusion | flops 525107200 | bytes 4505604 | tf_op jit(solution)/shard_map/dot_general | solution.py:136
  (76 shorter events, 34.7 us)
Async XLA Ops:
  2.0 25.6 %collective-permute-start = (bf16[320,1024]{1,0:T(8,128)(2,1)S(1)}, bf16[320,1024]{1,0:T(8,128)(2,1)S(1)}, u32[]{:S(2)}, u32[]{:S(2)}) collective-permute-start(bf16[320,1024]{1,0:T(8,128)(2,1)S(1)} %constant_dynamic-update-slice_fusion), channel_id=1, source_target_pairs={{0,8},{8,0},{1,9},{9,1},{2,10},{10,2},{3,11},{11,3},{4,12},{12,4},... | collective-permute-start | bytes 1966088 | tf_op jit(solution)/shard_map/ppermute | solution.py:16
  5.5 11.3 %collective-permute-start.5 = (bf16[160,1024]{1,0:T(8,128)(2,1)}, bf16[160,1024]{1,0:T(8,128)(2,1)S(1)}, u32[]{:S(2)}, u32[]{:S(2)}) collective-permute-start(bf16[160,1024]{1,0:T(8,128)(2,1)} %param.2), channel_id=1, source_target_pairs={{0,1},{1,2},{2,3},{3,4},{4,5},{5,6},{6,7},{7,0},{8,9},{9,10},{10,1... | collective-permute-start | bytes 983048 | tf_op jit(solution)/shard_map/ppermute | solution.py:16
  9.8 11.6 %collective-permute-start.1 = (bf16[160,1024]{1,0:T(8,128)(2,1)}, bf16[160,1024]{1,0:T(8,128)(2,1)S(1)}, u32[]{:S(2)}, u32[]{:S(2)}) collective-permute-start(bf16[160,1024]{1,0:T(8,128)(2,1)} %param.2), channel_id=1, source_target_pairs={{0,7},{1,0},{2,1},{3,2},{4,3},{5,4},{6,5},{7,6},{8,15},{9,8},{10,9... | collective-permute-start | bytes 983048 | tf_op jit(solution)/shard_map/ppermute | solution.py:16
  11.7 26.8 %copy-start = (bf16[160,1024]{1,0:T(8,128)(2,1)S(1)}, bf16[160,1024]{1,0:T(8,128)(2,1)}, u32[]{:S(2)}) copy-start(bf16[160,1024]{1,0:T(8,128)(2,1)} %param.2) | copy-start | bytes 983044
  16.8 22.3 %collective-permute-start.6 = (bf16[160,1024]{1,0:T(8,128)(2,1)S(1)}, bf16[160,1024]{1,0:T(8,128)(2,1)S(1)}, u32[]{:S(2)}, u32[]{:S(2)}) collective-permute-start(bf16[160,1024]{1,0:T(8,128)(2,1)S(1)} %collective-permute-done.5), channel_id=1, source_target_pairs={{0,1},{1,2},{2,3},{3,4},{4,5},{5,6},{6,7},{7,0},{8,9},{9,10},{10,1... | collective-permute-start | bytes 983048 | tf_op jit(solution)/shard_map/ppermute | solution.py:16
  21.4 12.2 %collective-permute-start.2 = (bf16[160,1024]{1,0:T(8,128)(2,1)S(1)}, bf16[160,1024]{1,0:T(8,128)(2,1)S(1)}, u32[]{:S(2)}, u32[]{:S(2)}) collective-permute-start(bf16[160,1024]{1,0:T(8,128)(2,1)S(1)} %collective-permute-done.1), channel_id=1, source_target_pairs={{0,7},{1,0},{2,1},{3,2},{4,3},{5,4},{6,5},{7,6},{8,15},{9,8},{10,9... | collective-permute-start | bytes 983048 | tf_op jit(solution)/shard_map/ppermute | solution.py:16
  33.6 10.2 %collective-permute-start.3 = (bf16[160,1024]{1,0:T(8,128)(2,1)S(1)}, bf16[160,1024]{1,0:T(8,128)(2,1)S(1)}, u32[]{:S(2)}, u32[]{:S(2)}) collective-permute-start(bf16[160,1024]{1,0:T(8,128)(2,1)S(1)} %collective-permute-done.2), channel_id=1, source_target_pairs={{0,7},{1,0},{2,1},{3,2},{4,3},{5,4},{6,5},{7,6},{8,15},{9,8},{10,9... | collective-permute-start | bytes 983048 | tf_op jit(solution)/shard_map/ppermute | solution.py:16
  39.1 15.0 %collective-permute-start.7 = (bf16[160,1024]{1,0:T(8,128)(2,1)S(1)}, bf16[160,1024]{1,0:T(8,128)(2,1)S(1)}, u32[]{:S(2)}, u32[]{:S(2)}) collective-permute-start(bf16[160,1024]{1,0:T(8,128)(2,1)S(1)} %collective-permute-done.6), channel_id=1, source_target_pairs={{0,1},{1,2},{2,3},{3,4},{4,5},{5,6},{6,7},{7,0},{8,9},{9,10},{10,1... | collective-permute-start | bytes 983048 | tf_op jit(solution)/shard_map/ppermute | solution.py:16
  43.8 9.7 %collective-permute-start.4 = (bf16[160,1024]{1,0:T(8,128)(2,1)S(1)}, bf16[160,1024]{1,0:T(8,128)(2,1)S(1)}, u32[]{:S(2)}, u32[]{:S(2)}) collective-permute-start(bf16[160,1024]{1,0:T(8,128)(2,1)S(1)} %collective-permute-done.3), channel_id=1, source_target_pairs={{0,7},{1,0},{2,1},{3,2},{4,3},{5,4},{6,5},{7,6},{8,15},{9,8},{10,9... | collective-permute-start | bytes 983048 | tf_op jit(solution)/shard_map/ppermute | solution.py:16
  123.3 18.1 %all-to-all-start.5 = ((f32[4,40,1280]{2,1,0:T(8,128)}), f32[4,40,1280]{2,1,0:T(8,128)S(1)}, u32[]{:S(2)}, u32[]{:S(2)}) async-start(f32[4,40,1280]{2,1,0:T(8,128)} %broadcast_in_dim.24), calls=%async_computation.5 | async-start | bytes 1638400 | tf_op jit(solution)/shard_map/all_to_all | solution.py:20
  128.9 12.5 %collective-permute-start.8 = (f32[40,320]{1,0:T(8,128)S(1)}, f32[40,320]{1,0:T(8,128)S(1)}, u32[]{:S(2)}, u32[]{:S(2)}) collective-permute-start(f32[40,320]{1,0:T(8,128)S(1)} %pad_maximum_fusion.3), channel_id=1, source_target_pairs={{0,0},{1,33},{2,66},{3,99},{4,132},{5,165},{6,198},{7,231},{8,8},{... | collective-permute-start | bytes 153608 | tf_op jit(solution)/shard_map/ppermute | solution.py:97
  147.6 36.5 %all-to-all-start.3 = ((f32[16,40,320]{2,1,0:T(8,128)}), f32[16,40,320]{2,1,0:T(8,128)}, u32[]{:S(2)}, u32[]{:S(2)}) async-start(f32[16,40,320]{2,1,0:T(8,128)} %broadcast_in_dim.22), calls=%async_computation.3 | async-start | bytes 1966080 | tf_op jit(solution)/shard_map/all_to_all | solution.py:20
  193.4 31.3 %all-to-all-start.7 = ((f32[16,40,384]{2,1,0:T(8,128)}), f32[16,40,384]{2,1,0:T(8,128)S(1)}, u32[]{:S(2)}, u32[]{:S(2)}) async-start(f32[16,40,384]{2,1,0:T(8,128)} %broadcast_in_dim.49), calls=%async_computation.7 | async-start | bytes 1966080 | tf_op jit(solution)/shard_map/all_to_all | solution.py:20

commit v3 on v2

--- a/solution.py
+++ b/solution.py
@@ -95,7 +95,9 @@
 
     cross_own = jnp.concatenate([own[0, :, rows:], own[1, :, rows:]], 1)
     cross_own = lax.ppermute(cross_own, ALL, tile_moves()) / token_total
-    cross_all = spread(cross_own, FEAT, 16).reshape(2, 8 * quarter, 2 * rows)
+    gram_part = jnp.concatenate([own[0, :, :rows], own[1, :, :rows]], 1)
+    cross_own, gram_part = lax.optimization_barrier((cross_own, gram_part))
+    cross_all = lax.all_gather(jnp.concatenate([cross_own, gram_part[:, :192]], 1), FEAT, axis=0)[:, :, : 2 * rows].reshape(2, 8 * quarter, 2 * rows)
     target_all = jnp.concatenate(
         [
             cross_all[0, :, :rows],
@@ -106,7 +108,6 @@
         1,
     )
 
-    gram_part = jnp.concatenate([own[0, :, :rows], own[1, :, :rows]], 1)
     gram_part = spread(gram_part, "yh", 4)
     gram_part = jnp.concatenate([gram_part[q] for q in range(4)], 1)
     gram_part = spread(gram_part, "x", 4)

time: 239 us -> 256 us (1.071)
  the two profiles are of different devices: /device:TPU:86 before, /device:TPU:78 now
where the time goes in v3:
time: 256 us; the launch traced here: 255 us
  waiting for transfers between devices  80.5 us (31%)
  blocking collectives  72.1 us (28%)
  starting transfers between devices  50.7 us (20%)
  matrix products  16.1 us (6%)
  between operations  15.4 us (6%)
  other arithmetic  13.7 us (5%)
  local copies, waits for them, and re-layouts  6.46 us (3%)
    all_gather x1, waiting for transfers between devices, body(): lax.all_gather(jnp.concatenate([cross_own, gram_part[:, :192]], 1), FEAT,...  36.3 us
    ppermute x8, starting transfers between devices, shift(): lax.ppermute(array, axis, [(i, (i + step) % size) for i in range(size)])  30.8 us
    all_to_all x2, waiting for transfers between devices, spread(): lax.all_to_all(jnp.broadcast_to(array[None], (count,) + array.shape), axe...  25.4 us
    all_to_all x1, blocking collectives, body(): partial = jnp.sum(lax.all_to_all(partial, 'x', 0, 0), 0)  24.4 us
    all_to_all x1, blocking collectives, body(): own = lax.all_to_all(jnp.stack(packed), ('yh', 'yl'), 0, 0)  22.1 us
    all_to_all x2, blocking collectives, spread(): lax.all_to_all(jnp.broadcast_to(array[None], (count,) + array.shape), axe...  19.2 us
    ppermute x8, waiting for transfers between devices, shift(): lax.ppermute(array, axis, [(i, (i + step) % size) for i in range(size)])  17 us
    all_to_all x2, starting transfers between devices, spread(): lax.all_to_all(jnp.broadcast_to(array[None], (count,) + array.shape), axe...  11.9 us
  transfers between devices with their start and end apart: 12, of which 9 were waited for; matrix products, arithmetic and copies ran while one was open for 3% of the time, Pallas kernels for 0%

profile of v3, /device:TPU:78, one launch (start us, length us, event | category | flops | bytes accessed | tf_op | source)
XLA Modules:
  0.0 255.0 jit_solution(13881605969009917210)
XLA Ops:
  8.5 2.4 collective-permute-start
  10.9 4.3 %collective-permute-start.5 = (bf16[160,1024]{1,0:T(8,128)(2,1)}, bf16[160,1024]{1,0:T(8,128)(2,1)S(1)}, u32[]{:S(2)}, u32[]{:S(2)}) collective-permute-start(bf16[160,1024]{1,0:T(8,128)(2,1)} %param.2), channel_id=1, source_target_pairs={{0,1},{1,2},{2,3},{3,4},{4,5},{5,6},{6,7},{7,0},{8,9},{9,10},{10,1... | collective-permute-start | bytes 983048 | tf_op jit(solution)/shard_map/ppermute | solution.py:16
  17.1 5.0 %collective-permute-done.5 = bf16[160,1024]{1,0:T(8,128)(2,1)S(1)} collective-permute-done((bf16[160,1024]{1,0:T(8,128)(2,1)}, bf16[160,1024]{1,0:T(8,128)(2,1)S(1)}, u32[]{:S(2)}, u32[]{:S(2)}) %collective-permute-start.5) | collective-permute-done | bytes 327712 | tf_op jit(solution)/shard_map/ppermute | solution.py:16
  22.2 4.3 %collective-permute-start.6 = (bf16[160,1024]{1,0:T(8,128)(2,1)S(1)}, bf16[160,1024]{1,0:T(8,128)(2,1)S(1)}, u32[]{:S(2)}, u32[]{:S(2)}) collective-permute-start(bf16[160,1024]{1,0:T(8,128)(2,1)S(1)} %collective-permute-done.5), channel_id=1, source_target_pairs={{0,1},{1,2},{2,3},{3,4},{4,5},{5,6},{6,7},{7,0},{8,9},{9,10},{10,1... | collective-permute-start | bytes 983048 | tf_op jit(solution)/shard_map/ppermute | solution.py:16
  26.8 6.1 %collective-permute-start.2 = (bf16[160,1024]{1,0:T(8,128)(2,1)S(1)}, bf16[160,1024]{1,0:T(8,128)(2,1)S(1)}, u32[]{:S(2)}, u32[]{:S(2)}) collective-permute-start(bf16[160,1024]{1,0:T(8,128)(2,1)S(1)} %collective-permute-done.1), channel_id=1, source_target_pairs={{0,7},{1,0},{2,1},{3,2},{4,3},{5,4},{6,5},{7,6},{8,15},{9,8},{10,9... | collective-permute-start | bytes 983048 | tf_op jit(solution)/shard_map/ppermute | solution.py:16
  33.2 5.9 %collective-permute-done.2 = bf16[160,1024]{1,0:T(8,128)(2,1)S(1)} collective-permute-done((bf16[160,1024]{1,0:T(8,128)(2,1)S(1)}, bf16[160,1024]{1,0:T(8,128)(2,1)S(1)}, u32[]{:S(2)}, u32[]{:S(2)}) %collective-permute-start.2) | collective-permute-done | bytes 327712 | tf_op jit(solution)/shard_map/ppermute | solution.py:16
  39.1 4.8 %collective-permute-start.3 = (bf16[160,1024]{1,0:T(8,128)(2,1)S(1)}, bf16[160,1024]{1,0:T(8,128)(2,1)S(1)}, u32[]{:S(2)}, u32[]{:S(2)}) collective-permute-start(bf16[160,1024]{1,0:T(8,128)(2,1)S(1)} %collective-permute-done.2), channel_id=1, source_target_pairs={{0,7},{1,0},{2,1},{3,2},{4,3},{5,4},{6,5},{7,6},{8,15},{9,8},{10,9... | collective-permute-start | bytes 983048 | tf_op jit(solution)/shard_map/ppermute | solution.py:16
  47.0 2.3 collective-permute-done.3
  49.3 5.1 %collective-permute-start.4 = (bf16[160,1024]{1,0:T(8,128)(2,1)S(1)}, bf16[160,1024]{1,0:T(8,128)(2,1)S(1)}, u32[]{:S(2)}, u32[]{:S(2)}) collective-permute-start(bf16[160,1024]{1,0:T(8,128)(2,1)S(1)} %collective-permute-done.3), channel_id=1, source_target_pairs={{0,7},{1,0},{2,1},{3,2},{4,3},{5,4},{6,5},{7,6},{8,15},{9,8},{10,9... | collective-permute-start | bytes 983048 | tf_op jit(solution)/shard_map/ppermute | solution.py:16
  55.5 3.4 %collective-permute-done.4 = bf16[160,1024]{1,0:T(8,128)(2,1)S(1)} collective-permute-done((bf16[160,1024]{1,0:T(8,128)(2,1)S(1)}, bf16[160,1024]{1,0:T(8,128)(2,1)S(1)}, u32[]{:S(2)}, u32[]{:S(2)}) %collective-permute-start.4) | collective-permute-done | bytes 327712 | tf_op jit(solution)/shard_map/ppermute | solution.py:16
  61.2 6.4 %all_to_all.35 = f32[2,4,160,640]{3,2,1,0:T(8,128)S(1)} all-to-all(f32[2,4,160,640]{3,2,1,0:T(8,128)S(1)} %bitcast.133), channel_id=1, replica_groups=mesh['yh'=4,'x'=4,'c'=2,'yl'=2,'z'=8] {'c'}, dimensions={0} | all-to-all | bytes 6553600 | tf_op jit(solution)/shard_map/all_to_all | solution.py:73
  69.2 24.4 %all_to_all.36 = f32[4,160,640]{2,1,0:T(8,128)S(1)} all-to-all(f32[4,160,640]{2,1,0:T(8,128)} %reduce_sum.63), channel_id=1, replica_groups=mesh['yh'=4,'x'=4,'c'=2,'yl'=2,'z'=8] {'x'}, dimensions={0} | all-to-all | bytes 3276800 | tf_op jit(solution)/shard_map/all_to_all | solution.py:74
  94.8 22.1 %all_to_all.37 = f32[8,40,320]{2,1,0:T(8,128)S(1)} all-to-all(f32[8,40,320]{2,1,0:T(8,128)S(1)} %fusion.25), channel_id=1, replica_groups=mesh['yh'=4,'x'=4,'c'=2,'yl'=2,'z'=8] {'yh','yl'}, dimensions={0} | all-to-all | bytes 819200 | tf_op jit(solution)/shard_map/all_to_all | solution.py:93
  117.0 7.9 %collective-permute-start.8 = (f32[40,320]{1,0:T(8,128)S(1)}, f32[40,320]{1,0:T(8,128)S(1)}, u32[]{:S(2)}, u32[]{:S(2)}) collective-permute-start(f32[40,320]{1,0:T(8,128)S(1)} %pad_maximum_fusion.4), channel_id=1, source_target_pairs={{0,0},{1,33},{2,66},{3,99},{4,132},{5,165},{6,198},{7,231},{8,8},{... | collective-permute-start | bytes 153608 | tf_op jit(solution)/shard_map/ppermute | solution.py:97
  127.6 14.2 %all_to_all.38 = f32[4,40,320]{2,1,0:T(8,128)S(1)} all-to-all(f32[4,40,320]{2,1,0:T(8,128)S(1)} %broadcast_in_dim.20), channel_id=1, replica_groups=mesh['yh'=4,'x'=4,'c'=2,'yl'=2,'z'=8] {'yh'}, dimensions={0} | all-to-all | bytes 409600 | tf_op jit(solution)/shard_map/all_to_all | solution.py:20
  142.9 5.5 %all-to-all-start.4 = ((f32[4,40,1280]{2,1,0:T(8,128)}), f32[4,40,1280]{2,1,0:T(8,128)S(1)}, u32[]{:S(2)}, u32[]{:S(2)}) async-start(f32[4,40,1280]{2,1,0:T(8,128)} %broadcast_in_dim.21), calls=%async_computation.4 | async-start | bytes 1638400 | tf_op jit(solution)/shard_map/all_to_all | solution.py:20
  148.4 8.2 %all-to-all-done.4 = f32[4,40,1280]{2,1,0:T(8,128)S(1)} async-done(((f32[4,40,1280]{2,1,0:T(8,128)}), f32[4,40,1280]{2,1,0:T(8,128)S(1)}, u32[]{:S(2)}, u32[]{:S(2)}) %all-to-all-start.4) | async-done | bytes 819232 | tf_op jit(solution)/shard_map/all_to_all | solution.py:20
  156.8 5.1 %all_to_all.39 = f32[2,4,40,1280]{3,2,1,0:T(8,128)S(1)} all-to-all(f32[2,4,40,1280]{3,2,1,0:T(8,128)S(1)} %broadcast_in_dim.38), channel_id=1, replica_groups=mesh['yh'=4,'x'=4,'c'=2,'yl'=2,'z'=8] {'c'}, dimensions={0} | all-to-all | bytes 3276800 | tf_op jit(solution)/shard_map/all_to_all | solution.py:20
  164.9 36.3 %all-gather.3.cloned.1.call-done = f32[640,512]{1,0:T(8,128)} async-done(((f32[40,512]{1,0:T(8,128)}), f32[640,512]{1,0:T(8,128)}) %all-gather.3.cloned.1.call-update) | async-done | bytes 1310736 | tf_op jit(solution)/shard_map/all_gather | solution.py:100
  210.6 6.4 %all-to-all-start.6 = ((f32[16,40,384]{2,1,0:T(8,128)}), f32[16,40,384]{2,1,0:T(8,128)S(1)}, u32[]{:S(2)}, u32[]{:S(2)}) async-start(f32[16,40,384]{2,1,0:T(8,128)} %broadcast_in_dim.42), calls=%async_computation.6 | async-start | bytes 1966080 | tf_op jit(solution)/shard_map/all_to_all | solution.py:20
  217.0 17.2 %all-to-all-done.6 = f32[16,40,384]{2,1,0:T(8,128)S(1)} async-done(((f32[16,40,384]{2,1,0:T(8,128)}), f32[16,40,384]{2,1,0:T(8,128)S(1)}, u32[]{:S(2)}, u32[]{:S(2)}) %all-to-all-start.6) | async-done | bytes 983072 | tf_op jit(solution)/shard_map/all_to_all | solution.py:20
  238.2 3.1 %fusion.45 = f32[1280,640]{1,0:T(8,128)} fusion(bf16[320,1280]{1,0:T(8,128)(2,1)S(1)} %get-tuple-element.16, s32[]{:T(128)S(6)} %select_n.53, bf16[320,640]{1,0:T(8,128)(2,1)S(1)} %reduce-precision_convert_fusion.2), kind=kOutput, calls=%fused_computation.154 | convolution fusion | flops 525107200 | bytes 4505604 | tf_op jit(solution)/shard_map/dot_general | solution.py:137
  241.3 3.0 %fusion.47 = f32[1280,640]{1,0:T(8,128)} fusion(bf16[320,1280]{1,0:T(8,128)(2,1)S(1)} %get-tuple-element.17, s32[]{:T(128)S(6)} %select_n.53, bf16[320,640]{1,0:T(8,128)(2,1)S(1)} %reduce-precision_convert_fusion.2), kind=kOutput, calls=%fused_computation.155 | convolution fusion | flops 525107200 | bytes 4505604 | tf_op jit(solution)/shard_map/dot_general | solution.py:137
  244.4 2.0 slice_add_fusion
  (79 shorter events, 34.2 us)
Async XLA Ops:
  6.5 194.7 %all-gather.3.cloned.1.call-start = ((), (), s32[]{:S(2)}) async-start(), calls=%async_computation.7 | async-start | bytes 1392640 | tf_op jit(solution)/shard_map/all_gather | solution.py:100
  8.5 24.4 %collective-permute-start = (bf16[320,1024]{1,0:T(8,128)(2,1)S(1)}, bf16[320,1024]{1,0:T(8,128)(2,1)S(1)}, u32[]{:S(2)}, u32[]{:S(2)}) collective-permute-start(bf16[320,1024]{1,0:T(8,128)(2,1)S(1)} %constant_dynamic-update-slice_fusion), channel_id=1, source_target_pairs={{0,8},{8,0},{1,9},{9,1},{2,10},{10,2},{3,11},{11,3},{4,12},{12,4},... | collective-permute-start | bytes 1966088 | tf_op jit(solution)/shard_map/ppermute | solution.py:16
  10.9 11.3 %collective-permute-start.5 = (bf16[160,1024]{1,0:T(8,128)(2,1)}, bf16[160,1024]{1,0:T(8,128)(2,1)S(1)}, u32[]{:S(2)}, u32[]{:S(2)}) collective-permute-start(bf16[160,1024]{1,0:T(8,128)(2,1)} %param.2), channel_id=1, source_target_pairs={{0,1},{1,2},{2,3},{3,4},{4,5},{5,6},{6,7},{7,0},{8,9},{9,10},{10,1... | collective-permute-start | bytes 983048 | tf_op jit(solution)/shard_map/ppermute | solution.py:16
  15.2 11.6 %collective-permute-start.1 = (bf16[160,1024]{1,0:T(8,128)(2,1)}, bf16[160,1024]{1,0:T(8,128)(2,1)S(1)}, u32[]{:S(2)}, u32[]{:S(2)}) collective-permute-start(bf16[160,1024]{1,0:T(8,128)(2,1)} %param.2), channel_id=1, source_target_pairs={{0,7},{1,0},{2,1},{3,2},{4,3},{5,4},{6,5},{7,6},{8,15},{9,8},{10,9... | collective-permute-start | bytes 983048 | tf_op jit(solution)/shard_map/ppermute | solution.py:16
  17.1 26.8 %copy-start = (bf16[160,1024]{1,0:T(8,128)(2,1)S(1)}, bf16[160,1024]{1,0:T(8,128)(2,1)}, u32[]{:S(2)}) copy-start(bf16[160,1024]{1,0:T(8,128)(2,1)} %param.2) | copy-start | bytes 983044
  22.2 22.3 %collective-permute-start.6 = (bf16[160,1024]{1,0:T(8,128)(2,1)S(1)}, bf16[160,1024]{1,0:T(8,128)(2,1)S(1)}, u32[]{:S(2)}, u32[]{:S(2)}) collective-permute-start(bf16[160,1024]{1,0:T(8,128)(2,1)S(1)} %collective-permute-done.5), channel_id=1, source_target_pairs={{0,1},{1,2},{2,3},{3,4},{4,5},{5,6},{6,7},{7,0},{8,9},{9,10},{10,1... | collective-permute-start | bytes 983048 | tf_op jit(solution)/shard_map/ppermute | solution.py:16
  26.8 12.2 %collective-permute-start.2 = (bf16[160,1024]{1,0:T(8,128)(2,1)S(1)}, bf16[160,1024]{1,0:T(8,128)(2,1)S(1)}, u32[]{:S(2)}, u32[]{:S(2)}) collective-permute-start(bf16[160,1024]{1,0:T(8,128)(2,1)S(1)} %collective-permute-done.1), channel_id=1, source_target_pairs={{0,7},{1,0},{2,1},{3,2},{4,3},{5,4},{6,5},{7,6},{8,15},{9,8},{10,9... | collective-permute-start | bytes 983048 | tf_op jit(solution)/shard_map/ppermute | solution.py:16
  39.1 10.2 %collective-permute-start.3 = (bf16[160,1024]{1,0:T(8,128)(2,1)S(1)}, bf16[160,1024]{1,0:T(8,128)(2,1)S(1)}, u32[]{:S(2)}, u32[]{:S(2)}) collective-permute-start(bf16[160,1024]{1,0:T(8,128)(2,1)S(1)} %collective-permute-done.2), channel_id=1, source_target_pairs={{0,7},{1,0},{2,1},{3,2},{4,3},{5,4},{6,5},{7,6},{8,15},{9,8},{10,9... | collective-permute-start | bytes 983048 | tf_op jit(solution)/shard_map/ppermute | solution.py:16
  44.5 15.0 %collective-permute-start.7 = (bf16[160,1024]{1,0:T(8,128)(2,1)S(1)}, bf16[160,1024]{1,0:T(8,128)(2,1)S(1)}, u32[]{:S(2)}, u32[]{:S(2)}) collective-permute-start(bf16[160,1024]{1,0:T(8,128)(2,1)S(1)} %collective-permute-done.6), channel_id=1, source_target_pairs={{0,1},{1,2},{2,3},{3,4},{4,5},{5,6},{6,7},{7,0},{8,9},{9,10},{10,1... | collective-permute-start | bytes 983048 | tf_op jit(solution)/shard_map/ppermute | solution.py:16
  49.3 9.7 %collective-permute-start.4 = (bf16[160,1024]{1,0:T(8,128)(2,1)S(1)}, bf16[160,1024]{1,0:T(8,128)(2,1)S(1)}, u32[]{:S(2)}, u32[]{:S(2)}) collective-permute-start(bf16[160,1024]{1,0:T(8,128)(2,1)S(1)} %collective-permute-done.3), channel_id=1, source_target_pairs={{0,7},{1,0},{2,1},{3,2},{4,3},{5,4},{6,5},{7,6},{8,15},{9,8},{10,9... | collective-permute-start | bytes 983048 | tf_op jit(solution)/shard_map/ppermute | solution.py:16
  117.0 9.8 %collective-permute-start.8 = (f32[40,320]{1,0:T(8,128)S(1)}, f32[40,320]{1,0:T(8,128)S(1)}, u32[]{:S(2)}, u32[]{:S(2)}) collective-permute-start(f32[40,320]{1,0:T(8,128)S(1)} %pad_maximum_fusion.4), channel_id=1, source_target_pairs={{0,0},{1,33},{2,66},{3,99},{4,132},{5,165},{6,198},{7,231},{8,8},{... | collective-permute-start | bytes 153608 | tf_op jit(solution)/shard_map/ppermute | solution.py:97
  142.9 13.8 %all-to-all-start.4 = ((f32[4,40,1280]{2,1,0:T(8,128)}), f32[4,40,1280]{2,1,0:T(8,128)S(1)}, u32[]{:S(2)}, u32[]{:S(2)}) async-start(f32[4,40,1280]{2,1,0:T(8,128)} %broadcast_in_dim.21), calls=%async_computation.4 | async-start | bytes 1638400 | tf_op jit(solution)/shard_map/all_to_all | solution.py:20
  210.6 23.6 %all-to-all-start.6 = ((f32[16,40,384]{2,1,0:T(8,128)}), f32[16,40,384]{2,1,0:T(8,128)S(1)}, u32[]{:S(2)}, u32[]{:S(2)}) async-start(f32[16,40,384]{2,1,0:T(8,128)} %broadcast_in_dim.42), calls=%async_computation.6 | async-start | bytes 1966080 | tf_op jit(solution)/shard_map/all_to_all | solution.py:20
Sparse Core Ops, SparseCore 0:
  127.7 73.5 all-gather.2

commit v4 on v2

v4 whole, which is shorter than its diff:
```python
import functools

import jax
import jax.numpy as jnp
from jax import lax
from jax.experimental import pallas as pl
from jax.experimental.pallas import tpu as pltpu
from jax.sharding import Mesh, PartitionSpec as P

ITERS = 2
ridge_share = 0.2
TOK = ("yh", "x", "c")
FEAT = ("yl", "z")
ALL = TOK + FEAT
SIZES = (4, 4, 2, 2, 8)


def shift(array, axis, size, step):
    return lax.ppermute(array, axis, [(i, (i + step) % size) for i in range(size)])


def spread(array, axes, count):
    return lax.all_to_all(
        jnp.broadcast_to(array[None], (count,) + array.shape), axes, 0, 0
    )


def tile_moves():
    moves = []
    for yh in range(4):
        for x in range(4):
            for c in range(2):
                for yl in range(2):
                    for z in range(8):
                        other_yl, half = yh // 2, yh % 2
                        source = (((yh * 4 + x) * 2 + c) * 2 + yl) * 8 + z
                        to_z = (z + 4 * c + x) % 8
                        to_yh, to_x = other_yl * 2 + z // 4, z % 4
                        target = (((to_yh * 4 + to_x) * 2 + half) * 2 + yl) * 8 + to_z
                        moves.append((source, target))
    return moves


def round_half(array):
    return array.astype(jnp.bfloat16).astype(jnp.float32)


def split_kernel(place, gram, target, high_out, low_out, sent):
    yl = place[0]
    rows, quarter = 160, 40
    sums = jnp.zeros((1, rows), jnp.float32)
    trace = jnp.zeros((1, 1), jnp.float32)
    at_row = lax.broadcasted_iota(jnp.int32, (quarter, rows), 0)
    at_col = lax.broadcasted_iota(jnp.int32, (quarter, rows), 1)
    for q in range(4):
        for k in range(2):
            n = q * 2 + k
            block = gram[:, :, n * rows : (n + 1) * rows].reshape(2 * rows, rows)
            sums += jnp.sum(jnp.abs(block), 0, keepdims=True)
            on_diagonal = (at_col == at_row + quarter * q) & (yl == k)
            trace += jnp.sum(jnp.where(on_diagonal, block[:quarter], 0.0), keepdims=True)
            high = block.astype(jnp.bfloat16)
            high_out[n * 2 * rows : (n + 1) * 2 * rows, :] = high
            low_out[n * 2 * rows : (n + 1) * 2 * rows, :] = (
                block - high.astype(jnp.float32)
            ).astype(jnp.bfloat16)
    peak = jnp.max(sums, keepdims=True)
    lane = lax.broadcasted_iota(jnp.int32, (quarter, 64), 1)
    value = jnp.where(lane < 3, peak, trace)
    first = round_half(value)
    second = round_half(value - first)
    third = value - first - second
    which = lane % 3
    tail = jnp.where(which == 0, first, jnp.where(which == 1, second, third))
    body_half = target[...].astype(jnp.bfloat16)
    tail_half = tail.astype(jnp.bfloat16)
    for d in range(16):
        sent[d, :, : 2 * rows] = body_half
        sent[d, :, 2 * rows :] = tail_half


def times_gram(z, got, high, low, seen):
    rows, quarter, half_cols = 160, 40, 80
    for k in range(2):
        for s in range(8):
            block = got[8 * k + lax.rem(z + s, 8)].astype(jnp.float32)
            for q in range(4):
                top = (q * 2 + k) * 2 * rows + s * quarter
                seen[top : top + quarter, :] = block[:, q * half_cols : (q + 1) * half_cols]
    side = seen[...].astype(jnp.bfloat16)
    product = 0.0
    for part in (high, low):
        product += lax.dot_general(
            part[...], side, (((0,), (0,)), ((), ())), preferred_element_type=jnp.float32
        )
    return jnp.concatenate([product[quarter * g : quarter * (g + 1)] for g in range(4)], 1)


def first_kernel(
    token_total, order_all, place, got, high, low, target_in, transform_out, update_out,
    sent, scalars, seen,
):
    rows = 160
    applied = times_gram(place[1], got, high, low, seen) / token_total
    peak_all = energy = None
    for d in range(16):
        tail = got[d][:, 2 * rows :].astype(jnp.float32)[:1]
        peak = tail[:, 0:1] + tail[:, 1:2] + tail[:, 2:3]
        trace = tail[:, 3:4] + tail[:, 4:5] + tail[:, 5:6]
        peak_all = peak if d == 0 else jnp.maximum(peak_all, peak)
        energy = trace if d == 0 else energy + trace
    ridge_term = ridge_share * energy / (token_total * order_all)
    upper_bound = peak_all / token_total + ridge_term
    center = (upper_bound + ridge_term) / 2.0
    half_span = (upper_bound - ridge_term) / 2.0
    ratio_now = half_span / center
    ratio_next = 1.0 / (2.0 * center / half_span - ratio_now)
    target = target_in[...]
    start = target / center
    residual = target - (applied + ridge_term * round_half(target)) / center
    update = ratio_next * ratio_now * start + 2.0 * ratio_next / half_span * residual
    transform = start + update
    ratio_last = 1.0 / (2.0 * center / half_span - ratio_next)
    transform_out[...] = transform
    update_out[...] = update
    lane = lax.broadcasted_iota(jnp.int32, (8, 128), 1)
    scalars[...] = jnp.where(
        lane == 0,
        ridge_term,
        jnp.where(lane == 1, ratio_last * ratio_next, 2.0 * ratio_last / half_span),
    )
    half = transform.astype(jnp.bfloat16)
    for d in range(16):
        sent[d, :, : 2 * rows] = half
        sent[d, :, 2 * rows :] = jnp.zeros((40, 64), jnp.bfloat16)


def second_kernel(
    token_total, place, got, high, low, target_in, transform_in, update_in, scalars, out, seen
):
    quarter, half_cols = 40, 80
    applied = times_gram(place[1], got, high, low, seen) / token_total
    ridge_term, keep, gain = scalars[0:1, 0:1], scalars[0:1, 1:2], scalars[0:1, 2:3]
    transform = transform_in[...]
    residual = target_in[...] - (applied + ridge_term * round_half(transform))
    final = transform + (keep * update_in[...] + gain * residual)
    for g in range(4):
        out[quarter * g : quarter * (g + 1), :] = final[:, half_cols * g : half_cols * (g + 1)]


def body(entering, leaving):
    yl = lax.axis_index("yl")
    z = lax.axis_index("z")
    rows = entering.shape[0]
    quarter = rows // 4
    half_cols = rows // 2
    token_total = entering.shape[1] * 32
    order_all = rows * 16
    low = yl == 0

    pair = jnp.concatenate([entering, leaving], 0)
    other = shift(pair, "yl", 2, 1)
    first = jnp.where(low, pair, other)
    second = jnp.where(low, other, pair)
    columns = jnp.concatenate([first[:rows], second[:rows], first[rows:], second[rows:]], 0)

    blocks = {0: entering}
    up = down = entering
    for step in range(1, 5):
        down = shift(down, "z", 8, -1)
        blocks[step] = down
        if step < 4:
            up = shift(up, "z", 8, 1)
            blocks[8 - step] = up

    pieces = [
        lax.dot_general(
            blocks[s], columns, (((1,), (1,)), ((), ())), preferred_element_type=jnp.float32
        )
        for s in range(8)
    ]
    partial = jnp.stack(pieces).reshape(2, 4, rows, 4 * rows)
    partial = jnp.sum(lax.all_to_all(partial, "c", 0, 0), 0)
    partial = jnp.sum(lax.all_to_all(partial, "x", 0, 0), 0)
    packed = []
    for to_yh in range(4):
        for to_yl in range(2):
            top = half_cols * to_yl
            left = 2 * rows + half_cols * to_yh
            packed.append(
                jnp.concatenate(
                    [
                        partial[
                            quarter * to_yh : quarter * (to_yh + 1),
                            rows * to_yl : rows * (to_yl + 1),
                        ],
                        partial[top : top + quarter, left : left + half_cols],
                        partial[top + quarter : top + 2 * quarter, left : left + half_cols],
                    ],
                    1,
                )
            )
    own = lax.all_to_all(jnp.stack(packed), ("yh", "yl"), 0, 0)
    own = jnp.sum(own.reshape(4, 2, quarter, 2 * rows), 0)

    cross_own = jnp.concatenate([own[0, :, rows:], own[1, :, rows:]], 1)
    cross_own = lax.ppermute(cross_own, ALL, tile_moves())
    cross_swap = shift(cross_own, "yl", 2, 1)
    target = jnp.where(
        low,
        jnp.concatenate([cross_own[:, :rows], cross_swap[:, :rows]], 1),
        jnp.concatenate([cross_swap[:, rows:], cross_own[:, rows:]], 1),
    ) / token_total

    gram_part = jnp.concatenate([own[0, :, :rows], own[1, :, :rows]], 1)
    gram_part = spread(gram_part, "yh", 4)
    gram_part = jnp.concatenate([gram_part[q] for q in range(4)], 1)
    gram_part = spread(gram_part, "x", 4)
    gram = spread(gram_part, "c", 2).reshape(8, quarter, 8 * rows)

    place = jnp.stack([yl, z]).astype(jnp.int32)
    vmem = pl.BlockSpec(memory_space=pltpu.VMEM)
    smem = pl.BlockSpec(memory_space=pltpu.SMEM)
    params = pltpu.CompilerParams(vmem_limit_bytes=40 * 2**20)
    tile = jax.ShapeDtypeStruct((quarter, 2 * rows), jnp.float32)
    message = jax.ShapeDtypeStruct((16, quarter, 2 * rows + 64), jnp.bfloat16)
    half_gram = jax.ShapeDtypeStruct((16 * rows, rows), jnp.bfloat16)
    columns_seen = pltpu.VMEM((16 * rows, half_cols), jnp.float32)
    gram_high, gram_low, sent = pl.pallas_call(
        split_kernel,
        out_shape=(half_gram, half_gram, message),
        in_specs=[smem, vmem, vmem],
        out_specs=(vmem, vmem, vmem),
        compiler_params=params,
    )(place, gram, target)
    got = lax.all_to_all(sent, FEAT, 0, 0)
    transform, update, sent, scalars = pl.pallas_call(
        functools.partial(first_kernel, token_total, order_all),
        out_shape=(tile, tile, message, jax.ShapeDtypeStruct((8, 128), jnp.float32)),
        in_specs=[smem] + [vmem] * 4,
        out_specs=(vmem,) * 4,
        scratch_shapes=[columns_seen],
        compiler_params=params,
    )(place, got, gram_high, gram_low, target)
    got = lax.all_to_all(sent, FEAT, 0, 0)
    return pl.pallas_call(
        functools.partial(second_kernel, token_total),
        out_shape=jax.ShapeDtypeStruct((rows, half_cols), jnp.float32),
        in_specs=[smem] + [vmem] * 7,
        out_specs=vmem,
        scratch_shapes=[columns_seen],
        compiler_params=params,
    )(place, got, gram_high, gram_low, target, transform, update, scalars)


def solution(mesh):
    fine = Mesh(mesh.devices.reshape(SIZES), ALL)
    spec = P(FEAT, TOK)
    return jax.shard_map(
        body, mesh=fine, in_specs=(spec, spec), out_specs=spec, check_vma=False
    )
```

time: 239 us -> 200 us (0.84)
  the two profiles are of different devices: /device:TPU:86 before, /device:TPU:72 now
where the time goes in v4:
time: 200 us; the launch traced here: 199 us
  blocking collectives  104 us (52%)
  starting transfers between devices  46.1 us (23%)
  waiting for transfers between devices  30.8 us (15%)
  Pallas kernels  6.07 us (3%)
  matrix products  4.52 us (2%)
  local copies, waits for them, and re-layouts  4.5 us (2%)
  other arithmetic  2.85 us (1%)
    all_to_all x2, blocking collectives, body(): got = lax.all_to_all(sent, FEAT, 0, 0)  44.7 us
    ppermute x9, starting transfers between devices, shift(): lax.ppermute(array, axis, [(i, (i + step) % size) for i in range(size)])  36.8 us
    all_to_all x1, blocking collectives, body(): partial = jnp.sum(lax.all_to_all(partial, 'x', 0, 0), 0)  26 us
    all_to_all x1, blocking collectives, body(): own = lax.all_to_all(jnp.stack(packed), ('yh', 'yl'), 0, 0)  22.1 us
    ppermute x9, waiting for transfers between devices, shift(): lax.ppermute(array, axis, [(i, (i + step) % size) for i in range(size)])  20.8 us
    all_to_all x2, waiting for transfers between devices, spread(): lax.all_to_all(jnp.broadcast_to(array[None], (count,) + array.shape), axe...  9.94 us
    all_to_all x2, starting transfers between devices, spread(): lax.all_to_all(jnp.broadcast_to(array[None], (count,) + array.shape), axe...  6.89 us
    all_to_all x1, blocking collectives, body(): partial = jnp.sum(lax.all_to_all(partial, 'c', 0, 0), 0)  6.37 us
  transfers between devices with their start and end apart: 12, of which 9 were waited for; matrix products, arithmetic and copies ran while one was open for 2% of the time, Pallas kernels for 0%

profile of v4, /device:TPU:72, one launch (start us, length us, event | category | flops | bytes accessed | tf_op | source)
XLA Modules:
  0.0 199.4 jit_solution(4479163492744039499)
XLA Ops:
  2.0 2.4 %collective-permute-start = (bf16[320,1024]{1,0:T(8,128)(2,1)S(1)}, bf16[320,1024]{1,0:T(8,128)(2,1)S(1)}, u32[]{:S(2)}, u32[]{:S(2)}) collective-permute-start(bf16[320,1024]{1,0:T(8,128)(2,1)S(1)} %constant_dynamic-update-slice_fusion), channel_id=1, source_target_pairs={{0,8},{8,0},{1,9},{9,1},{2,10},{10,2},{3,11},{11,3},{4,12},{12,4},... | collective-permute-start | bytes 1966088 | tf_op jit(solution)/shard_map/ppermute | solution.py:19
  4.4 6.9 %collective-permute-start.1 = (bf16[160,1024]{1,0:T(8,128)(2,1)}, bf16[160,1024]{1,0:T(8,128)(2,1)S(1)}, u32[]{:S(2)}, u32[]{:S(2)}) collective-permute-start(bf16[160,1024]{1,0:T(8,128)(2,1)} %param.2), channel_id=1, source_target_pairs={{0,7},{1,0},{2,1},{3,2},{4,3},{5,4},{6,5},{7,6},{8,15},{9,8},{10,9... | collective-permute-start | bytes 983048 | tf_op jit(solution)/shard_map/ppermute | solution.py:19
  11.3 1.9 collective-permute-start.5
  13.3 3.0 %collective-permute-done.1 = bf16[160,1024]{1,0:T(8,128)(2,1)S(1)} collective-permute-done((bf16[160,1024]{1,0:T(8,128)(2,1)}, bf16[160,1024]{1,0:T(8,128)(2,1)S(1)}, u32[]{:S(2)}, u32[]{:S(2)}) %collective-permute-start.1) | collective-permute-done | bytes 327712 | tf_op jit(solution)/shard_map/ppermute | solution.py:19
  16.3 7.6 %collective-permute-start.2 = (bf16[160,1024]{1,0:T(8,128)(2,1)S(1)}, bf16[160,1024]{1,0:T(8,128)(2,1)S(1)}, u32[]{:S(2)}, u32[]{:S(2)}) collective-permute-start(bf16[160,1024]{1,0:T(8,128)(2,1)S(1)} %collective-permute-done.1), channel_id=1, source_target_pairs={{0,7},{1,0},{2,1},{3,2},{4,3},{5,4},{6,5},{7,6},{8,15},{9,8},{10,9... | collective-permute-start | bytes 983048 | tf_op jit(solution)/shard_map/ppermute | solution.py:19
  26.4 3.2 %collective-permute-done.2 = bf16[160,1024]{1,0:T(8,128)(2,1)S(1)} collective-permute-done((bf16[160,1024]{1,0:T(8,128)(2,1)S(1)}, bf16[160,1024]{1,0:T(8,128)(2,1)S(1)}, u32[]{:S(2)}, u32[]{:S(2)}) %collective-permute-start.2) | collective-permute-done | bytes 327712 | tf_op jit(solution)/shard_map/ppermute | solution.py:19
  29.6 5.5 %collective-permute-start.3 = (bf16[160,1024]{1,0:T(8,128)(2,1)S(1)}, bf16[160,1024]{1,0:T(8,128)(2,1)S(1)}, u32[]{:S(2)}, u32[]{:S(2)}) collective-permute-start(bf16[160,1024]{1,0:T(8,128)(2,1)S(1)} %collective-permute-done.2), channel_id=1, source_target_pairs={{0,7},{1,0},{2,1},{3,2},{4,3},{5,4},{6,5},{7,6},{8,15},{9,8},{10,9... | collective-permute-start | bytes 983048 | tf_op jit(solution)/shard_map/ppermute | solution.py:19
  36.3 3.7 %collective-permute-done.3 = bf16[160,1024]{1,0:T(8,128)(2,1)S(1)} collective-permute-done((bf16[160,1024]{1,0:T(8,128)(2,1)S(1)}, bf16[160,1024]{1,0:T(8,128)(2,1)S(1)}, u32[]{:S(2)}, u32[]{:S(2)}) %collective-permute-start.3) | collective-permute-done | bytes 327712 | tf_op jit(solution)/shard_map/ppermute | solution.py:19
  39.9 5.6 %collective-permute-start.4 = (bf16[160,1024]{1,0:T(8,128)(2,1)S(1)}, bf16[160,1024]{1,0:T(8,128)(2,1)S(1)}, u32[]{:S(2)}, u32[]{:S(2)}) collective-permute-start(bf16[160,1024]{1,0:T(8,128)(2,1)S(1)} %collective-permute-done.3), channel_id=1, source_target_pairs={{0,7},{1,0},{2,1},{3,2},{4,3},{5,4},{6,5},{7,6},{8,15},{9,8},{10,9... | collective-permute-start | bytes 983048 | tf_op jit(solution)/shard_map/ppermute | solution.py:19
  50.7 6.1 %collective-permute-done.7 = bf16[160,1024]{1,0:T(8,128)(2,1)S(1)} collective-permute-done((bf16[160,1024]{1,0:T(8,128)(2,1)S(1)}, bf16[160,1024]{1,0:T(8,128)(2,1)S(1)}, u32[]{:S(2)}, u32[]{:S(2)}) %collective-permute-start.7) | collective-permute-done | bytes 327712 | tf_op jit(solution)/shard_map/ppermute | solution.py:19
  58.5 6.4 %all_to_all.40 = f32[2,4,160,640]{3,2,1,0:T(8,128)S(1)} all-to-all(f32[2,4,160,640]{3,2,1,0:T(8,128)S(1)} %bitcast.110), channel_id=1, replica_groups=mesh['yh'=4,'x'=4,'c'=2,'yl'=2,'z'=8] {'c'}, dimensions={0} | all-to-all | bytes 6553600 | tf_op jit(solution)/shard_map/all_to_all | solution.py:183
  66.4 26.0 %all_to_all.41 = f32[4,160,640]{2,1,0:T(8,128)S(1)} all-to-all(f32[4,160,640]{2,1,0:T(8,128)} %reduce_sum.27), channel_id=1, replica_groups=mesh['yh'=4,'x'=4,'c'=2,'yl'=2,'z'=8] {'x'}, dimensions={0} | all-to-all | bytes 3276800 | tf_op jit(solution)/shard_map/all_to_all | solution.py:184
  93.6 22.1 %all_to_all.42 = f32[8,40,320]{2,1,0:T(8,128)S(1)} all-to-all(f32[8,40,320]{2,1,0:T(8,128)S(1)} %fusion.15), channel_id=1, replica_groups=mesh['yh'=4,'x'=4,'c'=2,'yl'=2,'z'=8] {'yh','yl'}, dimensions={0} | all-to-all | bytes 819200 | tf_op jit(solution)/shard_map/all_to_all | solution.py:203
  116.6 3.4 %all-to-all-start.3 = ((f32[4,40,320]{2,1,0:T(8,128)}), f32[4,40,320]{2,1,0:T(8,128)S(1)}, u32[]{:S(2)}, u32[]{:S(2)}) async-start(f32[4,40,320]{2,1,0:T(8,128)} %broadcast_in_dim.6), calls=%async_computation.3 | async-start | bytes 491520 | tf_op jit(solution)/shard_map/all_to_all | solution.py:23
  120.1 2.5 %collective-permute-start.8 = (f32[40,320]{1,0:T(8,128)S(1)}, f32[40,320]{1,0:T(8,128)S(1)}, u32[]{:S(2)}, u32[]{:S(2)}) collective-permute-start(f32[40,320]{1,0:T(8,128)S(1)} %pad_maximum_fusion.2), channel_id=1, source_target_pairs={{0,0},{1,33},{2,66},{3,99},{4,132},{5,165},{6,198},{7,231},{8,8},{... | collective-permute-start | bytes 153608 | tf_op jit(solution)/shard_map/ppermute | solution.py:207
  122.5 6.7 %all-to-all-done.3 = f32[4,40,320]{2,1,0:T(8,128)S(1)} async-done(((f32[4,40,320]{2,1,0:T(8,128)}), f32[4,40,320]{2,1,0:T(8,128)S(1)}, u32[]{:S(2)}, u32[]{:S(2)}) %all-to-all-start.3) | async-done | bytes 204832 | tf_op jit(solution)/shard_map/all_to_all | solution.py:23
  130.3 3.5 %all-to-all-start.4 = ((f32[4,40,1280]{2,1,0:T(8,128)}), f32[4,40,1280]{2,1,0:T(8,128)S(1)}, u32[]{:S(2)}, u32[]{:S(2)}) async-start(f32[4,40,1280]{2,1,0:T(8,128)} %broadcast_in_dim.7), calls=%async_computation.4 | async-start | bytes 1638400 | tf_op jit(solution)/shard_map/all_to_all | solution.py:23
  133.9 3.1 %collective-permute-start.9 = (f32[40,320]{1,0:T(8,128)S(1)}, f32[40,320]{1,0:T(8,128)S(1)}, u32[]{:S(2)}, u32[]{:S(2)}) collective-permute-start(f32[40,320]{1,0:T(8,128)S(1)} %collective-permute-done.8), channel_id=1, source_target_pairs={{0,8},{8,0},{1,9},{9,1},{2,10},{10,2},{3,11},{11,3},{4,12},{12,4},... | collective-permute-start | bytes 153608 | tf_op jit(solution)/shard_map/ppermute | solution.py:19
  137.1 2.9 %collective-permute-done.9 = f32[40,320]{1,0:T(8,128)S(1)} collective-permute-done((f32[40,320]{1,0:T(8,128)S(1)}, f32[40,320]{1,0:T(8,128)S(1)}, u32[]{:S(2)}, u32[]{:S(2)}) %collective-permute-start.9) | collective-permute-done | bytes 51232 | tf_op jit(solution)/shard_map/ppermute | solution.py:19
  140.2 3.3 %all-to-all-done.4 = f32[4,40,1280]{2,1,0:T(8,128)S(1)} async-done(((f32[4,40,1280]{2,1,0:T(8,128)}), f32[4,40,1280]{2,1,0:T(8,128)S(1)}, u32[]{:S(2)}, u32[]{:S(2)}) %all-to-all-start.4) | async-done | bytes 819232 | tf_op jit(solution)/shard_map/all_to_all | solution.py:23
  143.6 5.0 %all_to_all.43 = f32[2,4,40,1280]{3,2,1,0:T(8,128)S(1)} all-to-all(f32[2,4,40,1280]{3,2,1,0:T(8,128)S(1)} %broadcast_in_dim.8), channel_id=1, replica_groups=mesh['yh'=4,'x'=4,'c'=2,'yl'=2,'z'=8] {'c'}, dimensions={0} | all-to-all | bytes 3276800 | tf_op jit(solution)/shard_map/all_to_all | solution.py:23
  150.3 25.0 %all_to_all.44.got = bf16[16,40,384]{2,1,0:T(8,128)(2,1)S(1)} all-to-all(bf16[16,40,384]{2,1,0:T(8,128)(2,1)S(1)} %get-tuple-element.12), channel_id=1, replica_groups=mesh['yh'=4,'x'=4,'c'=2,'yl'=2,'z'=8] {'yl','z'}, dimensions={0} | all-to-all | bytes 983040 | tf_op jit(solution)/shard_map/all_to_all | solution.py:236
  177.2 19.8 %all_to_all.45.got = bf16[16,40,384]{2,1,0:T(8,128)(2,1)S(1)} all-to-all(bf16[16,40,384]{2,1,0:T(8,128)(2,1)S(1)} %get-tuple-element.15), channel_id=1, replica_groups=mesh['yh'=4,'x'=4,'c'=2,'yl'=2,'z'=8] {'yl','z'}, dimensions={0} | all-to-all | bytes 983040 | tf_op jit(solution)/shard_map/all_to_all | solution.py:245
  197.0 2.5 %shard_map.30 = f32[160,80]{1,0:T(8,128)} custom-call(s32[2]{0:T(128)S(1)} %pad_add_fusion.place, bf16[16,40,384]{2,1,0:T(8,128)(2,1)S(1)} %all_to_all.45.got, bf16[2560,160]{1,0:T(8,128)(2,1)S(1)} %get-tuple-element.13.high, bf16[2560,160]{1,0:T(8,128)(2,1)S(1)} %get-tuple-element.14.low, f32[40,320]{1,0:T(8,128)S(1)} %fusion.16.target.target_in, ...), custom_call_target="tpu_custom_call" | custom-call | tf_op jit(solution)/shard_map/pallas_call | solution.py:246
  (48 shorter events, 21.2 us)
Async XLA Ops:
  2.0 24.2 %collective-permute-start = (bf16[320,1024]{1,0:T(8,128)(2,1)S(1)}, bf16[320,1024]{1,0:T(8,128)(2,1)S(1)}, u32[]{:S(2)}, u32[]{:S(2)}) collective-permute-start(bf16[320,1024]{1,0:T(8,128)(2,1)S(1)} %constant_dynamic-update-slice_fusion), channel_id=1, source_target_pairs={{0,8},{8,0},{1,9},{9,1},{2,10},{10,2},{3,11},{11,3},{4,12},{12,4},... | collective-permute-start | bytes 1966088 | tf_op jit(solution)/shard_map/ppermute | solution.py:19
  4.4 11.9 %collective-permute-start.1 = (bf16[160,1024]{1,0:T(8,128)(2,1)}, bf16[160,1024]{1,0:T(8,128)(2,1)S(1)}, u32[]{:S(2)}, u32[]{:S(2)}) collective-permute-start(bf16[160,1024]{1,0:T(8,128)(2,1)} %param.2), channel_id=1, source_target_pairs={{0,7},{1,0},{2,1},{3,2},{4,3},{5,4},{6,5},{7,6},{8,15},{9,8},{10,9... | collective-permute-start | bytes 983048 | tf_op jit(solution)/shard_map/ppermute | solution.py:19
  11.3 12.9 %collective-permute-start.5 = (bf16[160,1024]{1,0:T(8,128)(2,1)}, bf16[160,1024]{1,0:T(8,128)(2,1)S(1)}, u32[]{:S(2)}, u32[]{:S(2)}) collective-permute-start(bf16[160,1024]{1,0:T(8,128)(2,1)} %param.2), channel_id=1, source_target_pairs={{0,1},{1,2},{2,3},{3,4},{4,5},{5,6},{6,7},{7,0},{8,9},{9,10},{10,1... | collective-permute-start | bytes 983048 | tf_op jit(solution)/shard_map/ppermute | solution.py:19
  13.2 21.9 %copy-start = (bf16[160,1024]{1,0:T(8,128)(2,1)S(1)}, bf16[160,1024]{1,0:T(8,128)(2,1)}, u32[]{:S(2)}) copy-start(bf16[160,1024]{1,0:T(8,128)(2,1)} %param.2) | copy-start | bytes 983044
  16.3 13.3 %collective-permute-start.2 = (bf16[160,1024]{1,0:T(8,128)(2,1)S(1)}, bf16[160,1024]{1,0:T(8,128)(2,1)S(1)}, u32[]{:S(2)}, u32[]{:S(2)}) collective-permute-start(bf16[160,1024]{1,0:T(8,128)(2,1)S(1)} %collective-permute-done.1), channel_id=1, source_target_pairs={{0,7},{1,0},{2,1},{3,2},{4,3},{5,4},{6,5},{7,6},{8,15},{9,8},{10,9... | collective-permute-start | bytes 983048 | tf_op jit(solution)/shard_map/ppermute | solution.py:19
  24.2 21.9 %collective-permute-start.6 = (bf16[160,1024]{1,0:T(8,128)(2,1)S(1)}, bf16[160,1024]{1,0:T(8,128)(2,1)S(1)}, u32[]{:S(2)}, u32[]{:S(2)}) collective-permute-start(bf16[160,1024]{1,0:T(8,128)(2,1)S(1)} %collective-permute-done.5), channel_id=1, source_target_pairs={{0,1},{1,2},{2,3},{3,4},{4,5},{5,6},{6,7},{7,0},{8,9},{9,10},{10,1... | collective-permute-start | bytes 983048 | tf_op jit(solution)/shard_map/ppermute | solution.py:19
  29.6 10.3 %collective-permute-start.3 = (bf16[160,1024]{1,0:T(8,128)(2,1)S(1)}, bf16[160,1024]{1,0:T(8,128)(2,1)S(1)}, u32[]{:S(2)}, u32[]{:S(2)}) collective-permute-start(bf16[160,1024]{1,0:T(8,128)(2,1)S(1)} %collective-permute-done.2), channel_id=1, source_target_pairs={{0,7},{1,0},{2,1},{3,2},{4,3},{5,4},{6,5},{7,6},{8,15},{9,8},{10,9... | collective-permute-start | bytes 983048 | tf_op jit(solution)/shard_map/ppermute | solution.py:19
  39.9 10.2 %collective-permute-start.4 = (bf16[160,1024]{1,0:T(8,128)(2,1)S(1)}, bf16[160,1024]{1,0:T(8,128)(2,1)S(1)}, u32[]{:S(2)}, u32[]{:S(2)}) collective-permute-start(bf16[160,1024]{1,0:T(8,128)(2,1)S(1)} %collective-permute-done.3), channel_id=1, source_target_pairs={{0,7},{1,0},{2,1},{3,2},{4,3},{5,4},{6,5},{7,6},{8,15},{9,8},{10,9... | collective-permute-start | bytes 983048 | tf_op jit(solution)/shard_map/ppermute | solution.py:19
  46.1 10.6 %collective-permute-start.7 = (bf16[160,1024]{1,0:T(8,128)(2,1)S(1)}, bf16[160,1024]{1,0:T(8,128)(2,1)S(1)}, u32[]{:S(2)}, u32[]{:S(2)}) collective-permute-start(bf16[160,1024]{1,0:T(8,128)(2,1)S(1)} %collective-permute-done.6), channel_id=1, source_target_pairs={{0,1},{1,2},{2,3},{3,4},{4,5},{5,6},{6,7},{7,0},{8,9},{9,10},{10,1... | collective-permute-start | bytes 983048 | tf_op jit(solution)/shard_map/ppermute | solution.py:19
  116.6 12.6 %all-to-all-start.3 = ((f32[4,40,320]{2,1,0:T(8,128)}), f32[4,40,320]{2,1,0:T(8,128)S(1)}, u32[]{:S(2)}, u32[]{:S(2)}) async-start(f32[4,40,320]{2,1,0:T(8,128)} %broadcast_in_dim.6), calls=%async_computation.3 | async-start | bytes 491520 | tf_op jit(solution)/shard_map/all_to_all | solution.py:23
  120.1 13.8 %collective-permute-start.8 = (f32[40,320]{1,0:T(8,128)S(1)}, f32[40,320]{1,0:T(8,128)S(1)}, u32[]{:S(2)}, u32[]{:S(2)}) collective-permute-start(f32[40,320]{1,0:T(8,128)S(1)} %pad_maximum_fusion.2), channel_id=1, source_target_pairs={{0,0},{1,33},{2,66},{3,99},{4,132},{5,165},{6,198},{7,231},{8,8},{... | collective-permute-start | bytes 153608 | tf_op jit(solution)/shard_map/ppermute | solution.py:207
  130.3 13.1 %all-to-all-start.4 = ((f32[4,40,1280]{2,1,0:T(8,128)}), f32[4,40,1280]{2,1,0:T(8,128)S(1)}, u32[]{:S(2)}, u32[]{:S(2)}) async-start(f32[4,40,1280]{2,1,0:T(8,128)} %broadcast_in_dim.7), calls=%async_computation.4 | async-start | bytes 1638400 | tf_op jit(solution)/shard_map/all_to_all | solution.py:23
  133.9 6.1 %collective-permute-start.9 = (f32[40,320]{1,0:T(8,128)S(1)}, f32[40,320]{1,0:T(8,128)S(1)}, u32[]{:S(2)}, u32[]{:S(2)}) collective-permute-start(f32[40,320]{1,0:T(8,128)S(1)} %collective-permute-done.8), channel_id=1, source_target_pairs={{0,8},{8,0},{1,9},{9,1},{2,10},{10,2},{3,11},{11,3},{4,12},{12,4},... | collective-permute-start | bytes 153608 | tf_op jit(solution)/shard_map/ppermute | solution.py:19

commit v5 on v4

--- a/solution.py
+++ b/solution.py
@@ -34,7 +34,7 @@
                     for z in range(8):
                         other_yl, half = yh // 2, yh % 2
                         source = (((yh * 4 + x) * 2 + c) * 2 + yl) * 8 + z
-                        to_z = (z + 4 * c + x) % 8
+                        to_z = 4 * c + x
                         to_yh, to_x = other_yl * 2 + z // 4, z % 4
                         target = (((to_yh * 4 + to_x) * 2 + half) * 2 + yl) * 8 + to_z
                         moves.append((source, target))
@@ -45,9 +45,38 @@
     return array.astype(jnp.bfloat16).astype(jnp.float32)
 
 
+def outer_kernel(place, block, pair, other, gram_out, cross_out, columns):
+    rows, quarter, half_cols = 160, 40, 80
+
+    @pl.when(pl.program_id(0) == 0)
+    def _():
+        low = place[0] == 0
+        for part in range(2):
+            here = slice(part * rows, (part + 1) * rows)
+            mine, theirs = pair[here, :], other[here, :]
+            top = part * 2 * rows
+            columns[top : top + rows, :] = jnp.where(low, mine, theirs)
+            columns[top + rows : top + 2 * rows, :] = jnp.where(low, theirs, mine)
+
+    product = lax.dot_general(
+        block[...], columns[...], (((1,), (1,)), ((), ())), preferred_element_type=jnp.float32
+    )
+    for n in range(2):
+        one = product[n * rows : (n + 1) * rows]
+        gram_out[n, :, : 2 * rows] = one[:half_cols, : 2 * rows]
+        gram_out[n, :, 2 * rows :] = one[half_cols:, : 2 * rows]
+        for q in range(4):
+            left = 2 * rows + q * half_cols
+            for g in range(4):
+                cross_out[q, n, 0, :, g * half_cols : (g + 1) * half_cols] = one[
+                    g * quarter : (g + 1) * quarter, left : left + half_cols
+                ]
+
+
 def split_kernel(place, gram, target, high_out, low_out, sent):
-    yl = place[0]
+    yl, z = place[0], place[1]
     rows, quarter = 160, 40
+    here = gram[z]
     sums = jnp.zeros((1, rows), jnp.float32)
     trace = jnp.zeros((1, 1), jnp.float32)
     at_row = lax.broadcasted_iota(jnp.int32, (quarter, rows), 0)
@@ -58,7 +87,8 @@
             block = gram[:, :, n * rows : (n + 1) * rows].reshape(2 * rows, rows)
             sums += jnp.sum(jnp.abs(block), 0, keepdims=True)
             on_diagonal = (at_col == at_row + quarter * q) & (yl == k)
-            trace += jnp.sum(jnp.where(on_diagonal, block[:quarter], 0.0), keepdims=True)
+            own = here[:, n * rows : (n + 1) * rows]
+            trace += jnp.sum(jnp.where(on_diagonal, own, 0.0), keepdims=True)
             high = block.astype(jnp.bfloat16)
             high_out[n * 2 * rows : (n + 1) * 2 * rows, :] = high
             low_out[n * 2 * rows : (n + 1) * 2 * rows, :] = (
@@ -79,11 +109,11 @@
         sent[d, :, 2 * rows :] = tail_half
 
 
-def times_gram(z, got, high, low, seen):
+def times_gram(got, high, low, seen):
     rows, quarter, half_cols = 160, 40, 80
     for k in range(2):
         for s in range(8):
-            block = got[8 * k + lax.rem(z + s, 8)].astype(jnp.float32)
+            block = got[8 * k + s].astype(jnp.float32)
             for q in range(4):
                 top = (q * 2 + k) * 2 * rows + s * quarter
                 seen[top : top + quarter, :] = block[:, q * half_cols : (q + 1) * half_cols]
@@ -97,11 +127,11 @@
 
 
 def first_kernel(
-    token_total, order_all, place, got, high, low, target_in, transform_out, update_out,
+    token_total, order_all, got, high, low, target_in, transform_out, update_out,
     sent, scalars, seen,
 ):
     rows = 160
-    applied = times_gram(place[1], got, high, low, seen) / token_total
+    applied = times_gram(got, high, low, seen) / token_total
     peak_all = energy = None
     for d in range(16):
         tail = got[d][:, 2 * rows :].astype(jnp.float32)[:1]
@@ -136,10 +166,10 @@
 
 
 def second_kernel(
-    token_total, place, got, high, low, target_in, transform_in, update_in, scalars, out, seen
+    token_total, got, high, low, target_in, transform_in, update_in, scalars, out, seen
 ):
     quarter, half_cols = 40, 80
-    applied = times_gram(place[1], got, high, low, seen) / token_total
+    applied = times_gram(got, high, low, seen) / token_total
     ridge_term, keep, gain = scalars[0:1, 0:1], scalars[0:1, 1:2], scalars[0:1, 2:3]
     transform = transform_in[...]
     residual = target_in[...] - (applied + ridge_term * round_half(transform))
@@ -156,72 +186,60 @@
     half_cols = rows // 2
     token_total = entering.shape[1] * 32
     order_all = rows * 16
-    low = yl == 0
-
-    pair = jnp.concatenate([entering, leaving], 0)
-    other = shift(pair, "yl", 2, 1)
-    first = jnp.where(low, pair, other)
-    second = jnp.where(low, other, pair)
-    columns = jnp.concatenate([first[:rows], second[:rows], first[rows:], second[rows:]], 0)
-
-    blocks = {0: entering}
-    up = down = entering
-    for step in range(1, 5):
-        down = shift(down, "z", 8, -1)
-        blocks[step] = down
-        if step < 4:
-            up = shift(up, "z", 8, 1)
-            blocks[8 - step] = up
-
-    pieces = [
-        lax.dot_general(
-            blocks[s], columns, (((1,), (1,)), ((), ())), preferred_element_type=jnp.float32
-        )
-        for s in range(8)
-    ]
-    partial = jnp.stack(pieces).reshape(2, 4, rows, 4 * rows)
-    partial = jnp.sum(lax.all_to_all(partial, "c", 0, 0), 0)
-    partial = jnp.sum(lax.all_to_all(partial, "x", 0, 0), 0)
-    packed = []
-    for to_yh in range(4):
-        for to_yl in range(2):
-            top = half_cols * to_yl
-            left = 2 * rows + half_cols * to_yh
-            packed.append(
-                jnp.concatenate(
-                    [
-                        partial[
-                            quarter * to_yh : quarter * (to_yh + 1),
-                            rows * to_yl : rows * (to_yl + 1),
-                        ],
-                        partial[top : top + quarter, left : left + half_cols],
-                        partial[top + quarter : top + 2 * quarter, left : left + half_cols],
-                    ],
-                    1,
-                )
-            )
-    own = lax.all_to_all(jnp.stack(packed), ("yh", "yl"), 0, 0)
-    own = jnp.sum(own.reshape(4, 2, quarter, 2 * rows), 0)
-
-    cross_own = jnp.concatenate([own[0, :, rows:], own[1, :, rows:]], 1)
-    cross_own = lax.ppermute(cross_own, ALL, tile_moves())
-    cross_swap = shift(cross_own, "yl", 2, 1)
-    target = jnp.where(
-        low,
-        jnp.concatenate([cross_own[:, :rows], cross_swap[:, :rows]], 1),
-        jnp.concatenate([cross_swap[:, rows:], cross_own[:, rows:]], 1),
-    ) / token_total
-
-    gram_part = jnp.concatenate([own[0, :, :rows], own[1, :, :rows]], 1)
-    gram_part = spread(gram_part, "yh", 4)
-    gram_part = jnp.concatenate([gram_part[q] for q in range(4)], 1)
-    gram_part = spread(gram_part, "x", 4)
-    gram = spread(gram_part, "c", 2).reshape(8, quarter, 8 * rows)
 
     place = jnp.stack([yl, z]).astype(jnp.int32)
     vmem = pl.BlockSpec(memory_space=pltpu.VMEM)
     smem = pl.BlockSpec(memory_space=pltpu.SMEM)
     params = pltpu.CompilerParams(vmem_limit_bytes=40 * 2**20)
+
+    all_rows = lax.all_gather(entering, "z", axis=0, tiled=True)
+    pair = jnp.concatenate([entering, leaving], 0)
+    other = shift(pair, "yl", 2, 1)
+    length = entering.shape[1]
+    gram, cross = pl.pallas_call(
+        outer_kernel,
+        grid=(4,),
+        out_shape=(
+            jax.ShapeDtypeStruct((8, half_cols, 4 * rows), jnp.float32),
+            jax.ShapeDtypeStruct((4, 4, 2, quarter, 2 * rows), jnp.float32),
+        ),
+        in_specs=[
+            smem,
+            pl.BlockSpec((2 * rows, length), lambda n: (n, 0)),
+            pl.BlockSpec((2 * rows, length), lambda n: (0, 0)),
+            pl.BlockSpec((2 * rows, length), lambda n: (0, 0)),
+        ],
+        out_specs=(
+            pl.BlockSpec((2, half_cols, 4 * rows), lambda n: (n, 0, 0)),
+            pl.BlockSpec((4, 2, 1, quarter, 2 * rows), lambda n: (0, n % 2, n // 2, 0, 0)),
+        ),
+        scratch_shapes=[pltpu.VMEM((4 * rows, length), jnp.bfloat16)],
+        compiler_params=params,
+    )(place, all_rows, pair, other)
+
+    target = lax.psum_scatter(
+        cross.reshape(32 * quarter, 2 * rows), TOK, scatter_dimension=0, tiled=True
+    )
+
+    gram = jnp.sum(lax.all_to_all(gram.reshape(2, 4, half_cols, 4 * rows), "c", 0, 0), 0)
+    gram = jnp.sum(lax.all_to_all(gram, "x", 0, 0), 0)
+    packed = []
+    for to_yh in range(4):
+        top, left = quarter * (to_yh % 2), 2 * rows * (to_yh // 2)
+        for to_yl in range(2):
+            at = left + rows * to_yl
+            packed.append(gram[top : top + quarter, at : at + rows])
+    own = lax.all_to_all(jnp.stack(packed), ("yh", "yl"), 0, 0)
+    own = jnp.sum(own.reshape(4, 2, quarter, rows), 0)
+
+    gram_part = jnp.concatenate([own[0], own[1]], 1)
+    gram_part = spread(gram_part, "yh", 4)
+    gram_part = jnp.concatenate([gram_part[q] for q in range(4)], 1)
+    gram_part = lax.all_gather(gram_part, "x", axis=0)
+    target, gram_part = lax.optimization_barrier((target, gram_part))
+    target = lax.ppermute(target, ALL, tile_moves()) / token_total
+    gram = spread(gram_part, "c", 2).reshape(8, quarter, 8 * rows)
+
     tile = jax.ShapeDtypeStruct((quarter, 2 * rows), jnp.float32)
     message = jax.ShapeDtypeStruct((16, quarter, 2 * rows + 64), jnp.bfloat16)
     half_gram = jax.ShapeDtypeStruct((16 * rows, rows), jnp.bfloat16)
@@ -237,20 +255,20 @@
     transform, update, sent, scalars = pl.pallas_call(
         functools.partial(first_kernel, token_total, order_all),
         out_shape=(tile, tile, message, jax.ShapeDtypeStruct((8, 128), jnp.float32)),
-        in_specs=[smem] + [vmem] * 4,
+        in_specs=[vmem] * 4,
         out_specs=(vmem,) * 4,
         scratch_shapes=[columns_seen],
         compiler_params=params,
-    )(place, got, gram_high, gram_low, target)
+    )(got, gram_high, gram_low, target)
     got = lax.all_to_all(sent, FEAT, 0, 0)
     return pl.pallas_call(
         functools.partial(second_kernel, token_total),
         out_shape=jax.ShapeDtypeStruct((rows, half_cols), jnp.float32),
-        in_specs=[smem] + [vmem] * 7,
+        in_specs=[vmem] * 7,
         out_specs=vmem,
         scratch_shapes=[columns_seen],
         compiler_params=params,
-    )(place, got, gram_high, gram_low, target, transform, update, scalars)
+    )(got, gram_high, gram_low, target, transform, update, scalars)
 
 
 def solution(mesh):

time: 200 us -> 247 us (1.24)
  waiting for transfers between devices: 30.8 us -> 109 us
  starting transfers between devices: 46.1 us -> 14.8 us
  between operations: 0.36 us -> 13.5 us
  blocking collectives: 104 us -> 91.5 us
  matrix products: 4.52 us -> 0 us
  Pallas kernels: 6.07 us -> 10.5 us
    optimization_barrier x0 -> x1, waiting for transfers between devices: none -> 43.9 us  [body(): target, gram_part = lax.optimization_barrier((target, gram_part))]
    ppermute x9 -> x1, starting transfers between devices: 36.8 us -> 2.36 us  [shift(): lax.ppermute(array, axis, [(i, (i + step) % size) for i in range(size)])]
    all_gather x0 -> x1, waiting for transfers between devices: none -> 30.9 us  [body(): all_rows = lax.all_gather(entering, 'z', axis=0, tiled=True)]
    all_to_all x2 -> x1, blocking collectives: 32.4 us -> 5.04 us  [body(): lax.all_to_all(gram.reshape(2, 4, half_cols, 4 * rows), 'c', 0, 0)]
    all_gather x0 -> x1, blocking collectives: none -> 13.7 us  [body(): gram_part = lax.all_gather(gram_part, 'x', axis=0)]
    all_to_all x0 -> x1, waiting for transfers between devices: none -> 12.2 us  [body(): gram = jnp.sum(lax.all_to_all(gram, 'x', 0, 0), 0)]
    all_to_all x1, blocking collectives: 5.05 us -> 12.4 us  [spread(): lax.all_to_all(jnp.broadcast_to(array[None], (count,) + array.shape), axe...]
    all_to_all x2 -> x1, waiting for transfers between devices: 9.94 us -> 4.43 us  [spread(): lax.all_to_all(jnp.broadcast_to(array[None], (count,) + array.shape), axe...]
  transfers between devices with their start and end apart: 12 -> 6, of which waited for: 9 -> 5; matrix products, arithmetic and copies ran while one was open for 2% -> 2% of each run, Pallas kernels for 0% -> 0%
where the time goes in v5:
time: 247 us; the launch traced here: 246 us
  waiting for transfers between devices  109 us (44%)
  blocking collectives  91.5 us (37%)
  starting transfers between devices  14.8 us (6%)
  between operations  13.5 us (5%)
  Pallas kernels  10.5 us (4%)
  local copies, waits for them, and re-layouts  5.65 us (2%)
    optimization_barrier x1, waiting for transfers between devices, body(): target, gram_part = lax.optimization_barrier((target, gram_part))  43.9 us
    all_to_all x2, blocking collectives, body(): got = lax.all_to_all(sent, FEAT, 0, 0)  42.4 us
    all_gather x1, waiting for transfers between devices, body(): all_rows = lax.all_gather(entering, 'z', axis=0, tiled=True)  30.9 us
    all_to_all x1, blocking collectives, body(): own = lax.all_to_all(jnp.stack(packed), ('yh', 'yl'), 0, 0)  18.1 us
    ppermute x1, waiting for transfers between devices, shift(): lax.ppermute(array, axis, [(i, (i + step) % size) for i in range(size)])  15.9 us
    all_gather x1, blocking collectives, body(): gram_part = lax.all_gather(gram_part, 'x', axis=0)  13.7 us
    all_to_all x1, blocking collectives, spread(): lax.all_to_all(jnp.broadcast_to(array[None], (count,) + array.shape), axe...  12.4 us
    all_to_all x1, waiting for transfers between devices, body(): gram = jnp.sum(lax.all_to_all(gram, 'x', 0, 0), 0)  12.2 us
  transfers between devices with their start and end apart: 6, of which 5 were waited for; matrix products, arithmetic and copies ran while one was open for 2% of the time, Pallas kernels for 0%

profile of v5, /device:TPU:72, one launch (start us, length us, event | category | flops | bytes accessed | tf_op | source)
XLA Modules:
  0.0 246.1 jit_solution(18283665990549981391)
XLA Ops:
  7.3 1.0 constant_dynamic-update-slice_fusion.1
  8.3 1.0 constant_dynamic-update-slice_fusion.pair
  9.3 2.4 collective-permute-start
  11.7 15.9 %collective-permute-done.other = bf16[320,1024]{1,0:T(8,128)(2,1)S(1)} collective-permute-done((bf16[320,1024]{1,0:T(8,128)(2,1)S(1)}, bf16[320,1024]{1,0:T(8,128)(2,1)S(1)}, u32[]{:S(2)}, u32[]{:S(2)}) %collective-permute-start) | collective-permute-done | bytes 655392 | tf_op jit(solution)/shard_map/ppermute | solution.py:19
  27.6 30.9 %all-gather.3.cloned.1.call-done.block = bf16[1280,1024]{1,0:T(8,128)(2,1)} async-done(((bf16[160,1024]{1,0:T(8,128)(2,1)}), bf16[1280,1024]{1,0:T(8,128)(2,1)}) %all-gather.3.cloned.1.call-update) | async-done | bytes 2621456 | tf_op jit(solution)/shard_map/all_gather | solution.py:195
  58.5 1.7 copy-done
  60.3 5.5 %shard_map.28 = (f32[8,80,640]{2,1,0:T(8,128)S(1)}, f32[4,4,2,40,320]{4,3,2,1,0:T(8,128)}) custom-call(s32[2]{0:T(128)S(1)} %pad_add_fusion.place, bf16[1280,1024]{1,0:T(8,128)(2,1)S(1)} %copy-done, bf16[320,1024]{1,0:T(8,128)(2,1)S(1)} %constant_dynamic-update-slice_fusion.pair, bf16[320,1024]{1,0:T(8,128)(2,1)S(1)} %collective-permute-done.other), custom_call_target="tpu_custom_call" | custom-call | tf_op jit(solution)/shard_map/pallas_call | solution.py:199
  65.8 5.0 %all_to_all.35 = f32[2,4,80,640]{3,2,1,0:T(8,128)S(1)} all-to-all(f32[2,4,80,640]{3,2,1,0:T(8,128)S(1)} %bitcast.53), channel_id=1, replica_groups=mesh['yh'=4,'x'=4,'c'=2,'yl'=2,'z'=8] {'c'}, dimensions={0} | all-to-all | bytes 3276800 | tf_op jit(solution)/shard_map/all_to_all | solution.py:224
  70.8 1.1 reduce_sum.27
  71.9 4.2 %all-to-all-start.1 = ((f32[4,80,640]{2,1,0:T(8,128)}), f32[4,80,640]{2,1,0:T(8,128)S(1)}, u32[]{:S(2)}, u32[]{:S(2)}) async-start(f32[4,80,640]{2,1,0:T(8,128)} %reduce_sum.27), calls=%async_computation.1 | async-start | bytes 1638400 | tf_op jit(solution)/shard_map/all_to_all | solution.py:225
  76.9 12.2 %all-to-all-done.1 = f32[4,80,640]{2,1,0:T(8,128)S(1)} async-done(((f32[4,80,640]{2,1,0:T(8,128)}), f32[4,80,640]{2,1,0:T(8,128)S(1)}, u32[]{:S(2)}, u32[]{:S(2)}) %all-to-all-start.1) | async-done | bytes 819232 | tf_op jit(solution)/shard_map/all_to_all | solution.py:225
  89.6 18.1 %all_to_all.36 = f32[8,40,160]{2,1,0:T(8,128)S(1)} all-to-all(f32[8,40,160]{2,1,0:T(8,128)S(1)} %fusion), channel_id=1, replica_groups=mesh['yh'=4,'x'=4,'c'=2,'yl'=2,'z'=8] {'yh','yl'}, dimensions={0} | all-to-all | bytes 409600 | tf_op jit(solution)/shard_map/all_to_all | solution.py:232
  107.8 12.4 %all_to_all.37 = f32[4,40,320]{2,1,0:T(8,128)S(1)} all-to-all(f32[4,40,320]{2,1,0:T(8,128)S(1)} %broadcast_in_dim.4), channel_id=1, replica_groups=mesh['yh'=4,'x'=4,'c'=2,'yl'=2,'z'=8] {'yh'}, dimensions={0} | all-to-all | bytes 409600 | tf_op jit(solution)/shard_map/all_to_all | solution.py:23
  120.3 13.7 %all-gather = f32[160,1280]{1,0:T(8,128)S(1)} all-gather(f32[40,1280]{1,0:T(8,128)S(1)} %concatenate.11), channel_id=2, replica_groups=mesh['yh'=4,'x'=4,'c'=2,'yl'=2,'z'=8] {'x'}, dimensions={0}, use_global_device_ids=true | all-gather | bytes 1024000 | tf_op jit(solution)/shard_map/all_gather | solution.py:238
  134.0 43.9 %reduce-scatter.4.cloned.1.call-done = f32[40,320]{1,0:T(8,128)} async-done(((f32[1280,320]{1,0:T(8,128)}), f32[40,320]{1,0:T(8,128)}) %reduce-scatter.4.cloned.1.call-update) | async-done | bytes 51216 | tf_op jit(solution)/shard_map/optimization_barrier | solution.py:239
  177.9 2.2 collective-permute-start.1
  180.1 1.3 broadcast_in_dim.5
  181.4 6.0 %all-to-all-start.4 = ((f32[2,4,40,1280]{3,2,1,0:T(8,128)}), f32[2,4,40,1280]{3,2,1,0:T(8,128)S(1)}, u32[]{:S(2)}, u32[]{:S(2)}) async-start(f32[2,4,40,1280]{3,2,1,0:T(8,128)} %broadcast_in_dim.5), calls=%async_computation.4 | async-start | bytes 3276800 | tf_op jit(solution)/shard_map/all_to_all | solution.py:23
  187.4 4.4 %all-to-all-done.4 = f32[2,4,40,1280]{3,2,1,0:T(8,128)S(1)} async-done(((f32[2,4,40,1280]{3,2,1,0:T(8,128)}), f32[2,4,40,1280]{3,2,1,0:T(8,128)S(1)}, u32[]{:S(2)}, u32[]{:S(2)}) %all-to-all-start.4) | async-done | bytes 1638432 | tf_op jit(solution)/shard_map/all_to_all | solution.py:23
  191.9 1.8 shard_map.29
  193.6 22.6 %all_to_all.38.got = bf16[16,40,384]{2,1,0:T(8,128)(2,1)S(1)} all-to-all(bf16[16,40,384]{2,1,0:T(8,128)(2,1)S(1)} %get-tuple-element.20), channel_id=1, replica_groups=mesh['yh'=4,'x'=4,'c'=2,'yl'=2,'z'=8] {'yl','z'}, dimensions={0} | all-to-all | bytes 983040 | tf_op jit(solution)/shard_map/all_to_all | solution.py:254
  216.2 1.3 shard_map.30
  217.6 19.8 %all_to_all.39.got = bf16[16,40,384]{2,1,0:T(8,128)(2,1)S(1)} all-to-all(bf16[16,40,384]{2,1,0:T(8,128)(2,1)S(1)} %get-tuple-element.23), channel_id=1, replica_groups=mesh['yh'=4,'x'=4,'c'=2,'yl'=2,'z'=8] {'yl','z'}, dimensions={0} | all-to-all | bytes 983040 | tf_op jit(solution)/shard_map/all_to_all | solution.py:263
  237.3 1.9 shard_map.31
  (23 shorter events, 2.3 us)
Async XLA Ops:
  6.5 52.0 %all-gather.3.cloned.1.call-start = ((), (), s32[]{:S(2)}) async-start(), calls=%async_computation.8 | async-start | bytes 2949120 | tf_op jit(solution)/shard_map/all_gather | solution.py:195
  9.3 18.4 %collective-permute-start = (bf16[320,1024]{1,0:T(8,128)(2,1)S(1)}, bf16[320,1024]{1,0:T(8,128)(2,1)S(1)}, u32[]{:S(2)}, u32[]{:S(2)}) collective-permute-start(bf16[320,1024]{1,0:T(8,128)(2,1)S(1)} %constant_dynamic-update-slice_fusion.pair), channel_id=1, source_target_pairs={{0,8},{8,0},{1,9},{9,1},{2,10},{10,2},{3,11},{11,3},{4,12},{12,4},... | collective-permute-start | bytes 1966088 | tf_op jit(solution)/shard_map/ppermute | solution.py:19
  58.5 1.7 copy-start
  71.9 17.2 %all-to-all-start.1 = ((f32[4,80,640]{2,1,0:T(8,128)}), f32[4,80,640]{2,1,0:T(8,128)S(1)}, u32[]{:S(2)}, u32[]{:S(2)}) async-start(f32[4,80,640]{2,1,0:T(8,128)} %reduce_sum.27), calls=%async_computation.1 | async-start | bytes 1638400 | tf_op jit(solution)/shard_map/all_to_all | solution.py:225
  76.2 101.7 %reduce-scatter.4.cloned.1.call-start = ((), (), s32[]{:S(2)}) async-start(), calls=%async_computation.9 | async-start | bytes 2027520
  177.9 9.5 %collective-permute-start.1 = (f32[40,320]{1,0:T(8,128)}, f32[40,320]{1,0:T(8,128)S(1)}, u32[]{:S(2)}, u32[]{:S(2)}) collective-permute-start(f32[40,320]{1,0:T(8,128)} %reduce-scatter.4.cloned.1.call-done), channel_id=1, source_target_pairs={{0,0},{1,32},{2,64},{3,96},{4,128},{5,160},{6,192},{7,224},{8,8},{... | collective-permute-start | bytes 153608 | tf_op jit(solution)/shard_map/ppermute | solution.py:240
  181.4 10.5 %all-to-all-start.4 = ((f32[2,4,40,1280]{3,2,1,0:T(8,128)}), f32[2,4,40,1280]{3,2,1,0:T(8,128)S(1)}, u32[]{:S(2)}, u32[]{:S(2)}) async-start(f32[2,4,40,1280]{3,2,1,0:T(8,128)} %broadcast_in_dim.5), calls=%async_computation.4 | async-start | bytes 3276800 | tf_op jit(solution)/shard_map/all_to_all | solution.py:23
Sparse Core Ops, SparseCore 0:
  9.4 49.0 all-gather.2
  81.4 96.4 reduce-scatter.3

commit v6 on v4

--- a/solution.py
+++ b/solution.py
@@ -158,20 +158,30 @@
     order_all = rows * 16
     low = yl == 0
 
-    pair = jnp.concatenate([entering, leaving], 0)
-    other = shift(pair, "yl", 2, 1)
-    first = jnp.where(low, pair, other)
-    second = jnp.where(low, other, pair)
-    columns = jnp.concatenate([first[:rows], second[:rows], first[rows:], second[rows:]], 0)
-
     blocks = {0: entering}
-    up = down = entering
-    for step in range(1, 5):
-        down = shift(down, "z", 8, -1)
-        blocks[step] = down
-        if step < 4:
-            up = shift(up, "z", 8, 1)
-            blocks[8 - step] = up
+    down = shift(entering, "z", 8, -1)
+    up = shift(entering, "z", 8, 1)
+    other_entering = shift(entering, "yl", 2, 1)
+    down, up, other_entering, leaving = lax.optimization_barrier(
+        (down, up, other_entering, leaving)
+    )
+    blocks[1], blocks[7] = down, up
+    down, up = shift(down, "z", 8, -1), shift(up, "z", 8, 1)
+    other_leaving = shift(leaving, "yl", 2, 1)
+    down, up, other_leaving = lax.optimization_barrier((down, up, other_leaving))
+    blocks[2], blocks[6] = down, up
+    down, up = lax.optimization_barrier((shift(down, "z", 8, -1), shift(up, "z", 8, 1)))
+    blocks[3], blocks[5] = down, up
+    blocks[4] = shift(down, "z", 8, -1)
+    columns = jnp.concatenate(
+        [
+            jnp.where(low, entering, other_entering),
+            jnp.where(low, other_entering, entering),
+            jnp.where(low, leaving, other_leaving),
+            jnp.where(low, other_leaving, leaving),
+        ],
+        0,
+    )
 
     pieces = [
         lax.dot_general(

time: 200 us -> 206 us (1.030)
  waiting for transfers between devices: 30.8 us -> 38.6 us
  local copies, waits for them, and re-layouts: 4.5 us -> 2.39 us
    ppermute x9 -> x10, waiting for transfers between devices: 20.8 us -> 28.7 us  [shift(): lax.ppermute(array, axis, [(i, (i + step) % size) for i in range(size)])]
    ppermute x9 -> x10, starting transfers between devices: 36.8 us -> 35.9 us  [shift(): lax.ppermute(array, axis, [(i, (i + step) % size) for i in range(size)])]
  transfers between devices with their start and end apart: 12 -> 13, of which waited for: 9 -> 11; matrix products, arithmetic and copies ran while one was open for 2% -> 2% of each run, Pallas kernels for 0% -> 0%
where the time goes in v6:
time: 206 us; the launch traced here: 205 us
  blocking collectives  103 us (50%)
  starting transfers between devices  45.3 us (22%)
  waiting for transfers between devices  38.6 us (19%)
  Pallas kernels  6.07 us (3%)
  other arithmetic  4.79 us (2%)
  matrix products  4.57 us (2%)
  local copies, waits for them, and re-layouts  2.39 us (1%)
    all_to_all x2, blocking collectives, body(): got = lax.all_to_all(sent, FEAT, 0, 0)  44 us
    ppermute x10, starting transfers between devices, shift(): lax.ppermute(array, axis, [(i, (i + step) % size) for i in range(size)])  35.9 us
    ppermute x10, waiting for transfers between devices, shift(): lax.ppermute(array, axis, [(i, (i + step) % size) for i in range(size)])  28.7 us
    all_to_all x1, blocking collectives, body(): partial = jnp.sum(lax.all_to_all(partial, 'x', 0, 0), 0)  26 us
    all_to_all x1, blocking collectives, body(): own = lax.all_to_all(jnp.stack(packed), ('yh', 'yl'), 0, 0)  21.8 us
    all_to_all x2, waiting for transfers between devices, spread(): lax.all_to_all(jnp.broadcast_to(array[None], (count,) + array.shape), axe...  9.92 us
    all_to_all x2, starting transfers between devices, spread(): lax.all_to_all(jnp.broadcast_to(array[None], (count,) + array.shape), axe...  6.89 us
    all_to_all x1, blocking collectives, body(): partial = jnp.sum(lax.all_to_all(partial, 'c', 0, 0), 0)  6.37 us
  transfers between devices with their start and end apart: 13, of which 11 were waited for; matrix products, arithmetic and copies ran while one was open for 2% of the time, Pallas kernels for 0%

profile of v6, /device:TPU:72, one launch (start us, length us, event | category | flops | bytes accessed | tf_op | source)
XLA Modules:
  0.0 205.3 jit_solution(5336655593012626003)
XLA Ops:
  2.0 4.3 %collective-permute-start.1 = (bf16[160,1024]{1,0:T(8,128)(2,1)}, bf16[160,1024]{1,0:T(8,128)(2,1)S(1)}, u32[]{:S(2)}, u32[]{:S(2)}) collective-permute-start(bf16[160,1024]{1,0:T(8,128)(2,1)} %param.2), channel_id=1, source_target_pairs={{0,1},{1,2},{2,3},{3,4},{4,5},{5,6},{6,7},{7,0},{8,9},{9,10},{10,1... | collective-permute-start | bytes 983048 | tf_op jit(solution)/shard_map/ppermute | solution.py:19
  6.3 5.0 %collective-permute-start.2 = (bf16[160,1024]{1,0:T(8,128)(2,1)}, bf16[160,1024]{1,0:T(8,128)(2,1)S(1)}, u32[]{:S(2)}, u32[]{:S(2)}) collective-permute-start(bf16[160,1024]{1,0:T(8,128)(2,1)} %param.2), channel_id=1, source_target_pairs={{0,8},{8,0},{1,9},{9,1},{2,10},{10,2},{3,11},{11,3},{4,12},{12,4},... | collective-permute-start | bytes 983048 | tf_op jit(solution)/shard_map/ppermute | solution.py:19
  12.3 8.0 %collective-permute-done.1 = bf16[160,1024]{1,0:T(8,128)(2,1)S(1)} collective-permute-done((bf16[160,1024]{1,0:T(8,128)(2,1)}, bf16[160,1024]{1,0:T(8,128)(2,1)S(1)}, u32[]{:S(2)}, u32[]{:S(2)}) %collective-permute-start.1) | collective-permute-done | bytes 327712 | tf_op jit(solution)/shard_map/ppermute | solution.py:19
  20.3 5.6 %collective-permute-start.3 = (bf16[160,1024]{1,0:T(8,128)(2,1)S(1)}, bf16[160,1024]{1,0:T(8,128)(2,1)S(1)}, u32[]{:S(2)}, u32[]{:S(2)}) collective-permute-start(bf16[160,1024]{1,0:T(8,128)(2,1)S(1)} %collective-permute-done), channel_id=1, source_target_pairs={{0,7},{1,0},{2,1},{3,2},{4,3},{5,4},{6,5},{7,6},{8,15},{9,8},{10,9... | collective-permute-start | bytes 983048 | tf_op jit(solution)/shard_map/ppermute | solution.py:19
  27.8 2.4 %collective-permute-start.5 = (bf16[160,1024]{1,0:T(8,128)(2,1)}, bf16[160,1024]{1,0:T(8,128)(2,1)S(1)}, u32[]{:S(2)}, u32[]{:S(2)}) collective-permute-start(bf16[160,1024]{1,0:T(8,128)(2,1)} %param.3), channel_id=1, source_target_pairs={{0,8},{8,0},{1,9},{9,1},{2,10},{10,2},{3,11},{11,3},{4,12},{12,4},... | collective-permute-start | bytes 983048 | tf_op jit(solution)/shard_map/ppermute | solution.py:19
  31.6 5.0 %collective-permute-done.4 = bf16[160,1024]{1,0:T(8,128)(2,1)S(1)} collective-permute-done((bf16[160,1024]{1,0:T(8,128)(2,1)S(1)}, bf16[160,1024]{1,0:T(8,128)(2,1)S(1)}, u32[]{:S(2)}, u32[]{:S(2)}) %collective-permute-start.4) | collective-permute-done | bytes 327712 | tf_op jit(solution)/shard_map/ppermute | solution.py:19
  38.9 4.6 %collective-permute-start.6 = (bf16[160,1024]{1,0:T(8,128)(2,1)S(1)}, bf16[160,1024]{1,0:T(8,128)(2,1)S(1)}, u32[]{:S(2)}, u32[]{:S(2)}) collective-permute-start(bf16[160,1024]{1,0:T(8,128)(2,1)S(1)} %collective-permute-done.3), channel_id=1, source_target_pairs={{0,7},{1,0},{2,1},{3,2},{4,3},{5,4},{6,5},{7,6},{8,15},{9,8},{10,9... | collective-permute-start | bytes 983048 | tf_op jit(solution)/shard_map/ppermute | solution.py:19
  48.0 5.3 %collective-permute-done.7 = bf16[160,1024]{1,0:T(8,128)(2,1)S(1)} collective-permute-done((bf16[160,1024]{1,0:T(8,128)(2,1)S(1)}, bf16[160,1024]{1,0:T(8,128)(2,1)S(1)}, u32[]{:S(2)}, u32[]{:S(2)}) %collective-permute-start.7) | collective-permute-done | bytes 327712 | tf_op jit(solution)/shard_map/ppermute | solution.py:19
  53.3 5.1 %collective-permute-start.8 = (bf16[160,1024]{1,0:T(8,128)(2,1)S(1)}, bf16[160,1024]{1,0:T(8,128)(2,1)S(1)}, u32[]{:S(2)}, u32[]{:S(2)}) collective-permute-start(bf16[160,1024]{1,0:T(8,128)(2,1)S(1)} %collective-permute-done.6), channel_id=1, source_target_pairs={{0,7},{1,0},{2,1},{3,2},{4,3},{5,4},{6,5},{7,6},{8,15},{9,8},{10,9... | collective-permute-start | bytes 983048 | tf_op jit(solution)/shard_map/ppermute | solution.py:19
  59.6 3.4 %collective-permute-done.8 = bf16[160,1024]{1,0:T(8,128)(2,1)S(1)} collective-permute-done((bf16[160,1024]{1,0:T(8,128)(2,1)S(1)}, bf16[160,1024]{1,0:T(8,128)(2,1)S(1)}, u32[]{:S(2)}, u32[]{:S(2)}) %collective-permute-start.8) | collective-permute-done | bytes 327712 | tf_op jit(solution)/shard_map/ppermute | solution.py:19
  65.4 6.4 %all_to_all.40 = f32[2,4,160,640]{3,2,1,0:T(8,128)S(1)} all-to-all(f32[2,4,160,640]{3,2,1,0:T(8,128)S(1)} %bitcast.96), channel_id=1, replica_groups=mesh['yh'=4,'x'=4,'c'=2,'yl'=2,'z'=8] {'c'}, dimensions={0} | all-to-all | bytes 6553600 | tf_op jit(solution)/shard_map/all_to_all | solution.py:193
  73.3 26.0 %all_to_all.41 = f32[4,160,640]{2,1,0:T(8,128)S(1)} all-to-all(f32[4,160,640]{2,1,0:T(8,128)} %reduce_sum.27), channel_id=1, replica_groups=mesh['yh'=4,'x'=4,'c'=2,'yl'=2,'z'=8] {'x'}, dimensions={0} | all-to-all | bytes 3276800 | tf_op jit(solution)/shard_map/all_to_all | solution.py:194
  100.5 21.8 %all_to_all.42 = f32[8,40,320]{2,1,0:T(8,128)S(1)} all-to-all(f32[8,40,320]{2,1,0:T(8,128)S(1)} %fusion.15), channel_id=1, replica_groups=mesh['yh'=4,'x'=4,'c'=2,'yl'=2,'z'=8] {'yh','yl'}, dimensions={0} | all-to-all | bytes 819200 | tf_op jit(solution)/shard_map/all_to_all | solution.py:213
  123.2 3.4 %all-to-all-start.3 = ((f32[4,40,320]{2,1,0:T(8,128)}), f32[4,40,320]{2,1,0:T(8,128)S(1)}, u32[]{:S(2)}, u32[]{:S(2)}) async-start(f32[4,40,320]{2,1,0:T(8,128)} %broadcast_in_dim.6), calls=%async_computation.3 | async-start | bytes 491520 | tf_op jit(solution)/shard_map/all_to_all | solution.py:23
  126.7 2.5 %collective-permute-start.9 = (f32[40,320]{1,0:T(8,128)S(1)}, f32[40,320]{1,0:T(8,128)S(1)}, u32[]{:S(2)}, u32[]{:S(2)}) collective-permute-start(f32[40,320]{1,0:T(8,128)S(1)} %pad_maximum_fusion.2), channel_id=1, source_target_pairs={{0,0},{1,33},{2,66},{3,99},{4,132},{5,165},{6,198},{7,231},{8,8},{... | collective-permute-start | bytes 153608 | tf_op jit(solution)/shard_map/ppermute | solution.py:217
  129.2 6.6 %all-to-all-done.3 = f32[4,40,320]{2,1,0:T(8,128)S(1)} async-done(((f32[4,40,320]{2,1,0:T(8,128)}), f32[4,40,320]{2,1,0:T(8,128)S(1)}, u32[]{:S(2)}, u32[]{:S(2)}) %all-to-all-start.3) | async-done | bytes 204832 | tf_op jit(solution)/shard_map/all_to_all | solution.py:23
  136.9 3.5 %all-to-all-start.4 = ((f32[4,40,1280]{2,1,0:T(8,128)}), f32[4,40,1280]{2,1,0:T(8,128)S(1)}, u32[]{:S(2)}, u32[]{:S(2)}) async-start(f32[4,40,1280]{2,1,0:T(8,128)} %broadcast_in_dim.7), calls=%async_computation.4 | async-start | bytes 1638400 | tf_op jit(solution)/shard_map/all_to_all | solution.py:23
  140.4 3.2 %collective-permute-start.10 = (f32[40,320]{1,0:T(8,128)S(1)}, f32[40,320]{1,0:T(8,128)S(1)}, u32[]{:S(2)}, u32[]{:S(2)}) collective-permute-start(f32[40,320]{1,0:T(8,128)S(1)} %collective-permute-done.9), channel_id=1, source_target_pairs={{0,8},{8,0},{1,9},{9,1},{2,10},{10,2},{3,11},{11,3},{4,12},{12,4},... | collective-permute-start | bytes 153608 | tf_op jit(solution)/shard_map/ppermute | solution.py:19
  143.7 2.9 %collective-permute-done.10 = f32[40,320]{1,0:T(8,128)S(1)} collective-permute-done((f32[40,320]{1,0:T(8,128)S(1)}, f32[40,320]{1,0:T(8,128)S(1)}, u32[]{:S(2)}, u32[]{:S(2)}) %collective-permute-start.10) | collective-permute-done | bytes 51232 | tf_op jit(solution)/shard_map/ppermute | solution.py:19
  146.7 3.3 %all-to-all-done.4 = f32[4,40,1280]{2,1,0:T(8,128)S(1)} async-done(((f32[4,40,1280]{2,1,0:T(8,128)}), f32[4,40,1280]{2,1,0:T(8,128)S(1)}, u32[]{:S(2)}, u32[]{:S(2)}) %all-to-all-start.4) | async-done | bytes 819232 | tf_op jit(solution)/shard_map/all_to_all | solution.py:23
  150.2 5.0 %all_to_all.43 = f32[2,4,40,1280]{3,2,1,0:T(8,128)S(1)} all-to-all(f32[2,4,40,1280]{3,2,1,0:T(8,128)S(1)} %broadcast_in_dim.8), channel_id=1, replica_groups=mesh['yh'=4,'x'=4,'c'=2,'yl'=2,'z'=8] {'c'}, dimensions={0} | all-to-all | bytes 3276800 | tf_op jit(solution)/shard_map/all_to_all | solution.py:23
  156.9 24.3 %all_to_all.44.got = bf16[16,40,384]{2,1,0:T(8,128)(2,1)S(1)} all-to-all(bf16[16,40,384]{2,1,0:T(8,128)(2,1)S(1)} %get-tuple-element.30), channel_id=1, replica_groups=mesh['yh'=4,'x'=4,'c'=2,'yl'=2,'z'=8] {'yl','z'}, dimensions={0} | all-to-all | bytes 983040 | tf_op jit(solution)/shard_map/all_to_all | solution.py:246
  183.1 19.8 %all_to_all.45.got = bf16[16,40,384]{2,1,0:T(8,128)(2,1)S(1)} all-to-all(bf16[16,40,384]{2,1,0:T(8,128)(2,1)S(1)} %get-tuple-element.33), channel_id=1, replica_groups=mesh['yh'=4,'x'=4,'c'=2,'yl'=2,'z'=8] {'yl','z'}, dimensions={0} | all-to-all | bytes 983040 | tf_op jit(solution)/shard_map/all_to_all | solution.py:255
  202.8 2.5 %shard_map.30 = f32[160,80]{1,0:T(8,128)} custom-call(s32[2]{0:T(128)S(1)} %pad_add_fusion.place, bf16[16,40,384]{2,1,0:T(8,128)(2,1)S(1)} %all_to_all.45.got, bf16[2560,160]{1,0:T(8,128)(2,1)S(1)} %get-tuple-element.31.high, bf16[2560,160]{1,0:T(8,128)(2,1)S(1)} %get-tuple-element.32.low, f32[40,320]{1,0:T(8,128)S(1)} %fusion.16.target.target_in, ...), custom_call_target="tpu_custom_call" | custom-call | tf_op jit(solution)/shard_map/pallas_call | solution.py:256
  (48 shorter events, 25.3 us)
Async XLA Ops:
  0.0 45.4 %copy-start = (bf16[160,1024]{1,0:T(8,128)(2,1)S(1)}, bf16[160,1024]{1,0:T(8,128)(2,1)}, u32[]{:S(2)}) copy-start(bf16[160,1024]{1,0:T(8,128)(2,1)} %param.2) | copy-start | bytes 983044
  0.0 12.3 %collective-permute-start = (bf16[160,1024]{1,0:T(8,128)(2,1)}, bf16[160,1024]{1,0:T(8,128)(2,1)S(1)}, u32[]{:S(2)}, u32[]{:S(2)}) collective-permute-start(bf16[160,1024]{1,0:T(8,128)(2,1)} %param.2), channel_id=1, source_target_pairs={{0,7},{1,0},{2,1},{3,2},{4,3},{5,4},{6,5},{7,6},{8,15},{9,8},{10,9... | collective-permute-start | bytes 983048 | tf_op jit(solution)/shard_map/ppermute | solution.py:19
  2.0 18.2 %collective-permute-start.1 = (bf16[160,1024]{1,0:T(8,128)(2,1)}, bf16[160,1024]{1,0:T(8,128)(2,1)S(1)}, u32[]{:S(2)}, u32[]{:S(2)}) collective-permute-start(bf16[160,1024]{1,0:T(8,128)(2,1)} %param.2), channel_id=1, source_target_pairs={{0,1},{1,2},{2,3},{3,4},{4,5},{5,6},{6,7},{7,0},{8,9},{9,10},{10,1... | collective-permute-start | bytes 983048 | tf_op jit(solution)/shard_map/ppermute | solution.py:19
  6.3 13.9 %collective-permute-start.2 = (bf16[160,1024]{1,0:T(8,128)(2,1)}, bf16[160,1024]{1,0:T(8,128)(2,1)S(1)}, u32[]{:S(2)}, u32[]{:S(2)}) collective-permute-start(bf16[160,1024]{1,0:T(8,128)(2,1)} %param.2), channel_id=1, source_target_pairs={{0,8},{8,0},{1,9},{9,1},{2,10},{10,2},{3,11},{11,3},{4,12},{12,4},... | collective-permute-start | bytes 983048 | tf_op jit(solution)/shard_map/ppermute | solution.py:19
  20.3 11.3 %collective-permute-start.3 = (bf16[160,1024]{1,0:T(8,128)(2,1)S(1)}, bf16[160,1024]{1,0:T(8,128)(2,1)S(1)}, u32[]{:S(2)}, u32[]{:S(2)}) collective-permute-start(bf16[160,1024]{1,0:T(8,128)(2,1)S(1)} %collective-permute-done), channel_id=1, source_target_pairs={{0,7},{1,0},{2,1},{3,2},{4,3},{5,4},{6,5},{7,6},{8,15},{9,8},{10,9... | collective-permute-start | bytes 983048 | tf_op jit(solution)/shard_map/ppermute | solution.py:19
  25.8 10.8 %collective-permute-start.4 = (bf16[160,1024]{1,0:T(8,128)(2,1)S(1)}, bf16[160,1024]{1,0:T(8,128)(2,1)S(1)}, u32[]{:S(2)}, u32[]{:S(2)}) collective-permute-start(bf16[160,1024]{1,0:T(8,128)(2,1)S(1)} %collective-permute-done.1), channel_id=1, source_target_pairs={{0,1},{1,2},{2,3},{3,4},{4,5},{5,6},{6,7},{7,0},{8,9},{9,10},{10,1... | collective-permute-start | bytes 983048 | tf_op jit(solution)/shard_map/ppermute | solution.py:19
  27.8 10.1 %collective-permute-start.5 = (bf16[160,1024]{1,0:T(8,128)(2,1)}, bf16[160,1024]{1,0:T(8,128)(2,1)S(1)}, u32[]{:S(2)}, u32[]{:S(2)}) collective-permute-start(bf16[160,1024]{1,0:T(8,128)(2,1)} %param.3), channel_id=1, source_target_pairs={{0,8},{8,0},{1,9},{9,1},{2,10},{10,2},{3,11},{11,3},{4,12},{12,4},... | collective-permute-start | bytes 983048 | tf_op jit(solution)/shard_map/ppermute | solution.py:19
  38.9 9.1 %collective-permute-start.6 = (bf16[160,1024]{1,0:T(8,128)(2,1)S(1)}, bf16[160,1024]{1,0:T(8,128)(2,1)S(1)}, u32[]{:S(2)}, u32[]{:S(2)}) collective-permute-start(bf16[160,1024]{1,0:T(8,128)(2,1)S(1)} %collective-permute-done.3), channel_id=1, source_target_pairs={{0,7},{1,0},{2,1},{3,2},{4,3},{5,4},{6,5},{7,6},{8,15},{9,8},{10,9... | collective-permute-start | bytes 983048 | tf_op jit(solution)/shard_map/ppermute | solution.py:19
  43.4 9.9 %collective-permute-start.7 = (bf16[160,1024]{1,0:T(8,128)(2,1)S(1)}, bf16[160,1024]{1,0:T(8,128)(2,1)S(1)}, u32[]{:S(2)}, u32[]{:S(2)}) collective-permute-start(bf16[160,1024]{1,0:T(8,128)(2,1)S(1)} %collective-permute-done.4), channel_id=1, source_target_pairs={{0,1},{1,2},{2,3},{3,4},{4,5},{5,6},{6,7},{7,0},{8,9},{9,10},{10,1... | collective-permute-start | bytes 983048 | tf_op jit(solution)/shard_map/ppermute | solution.py:19
  53.3 9.7 %collective-permute-start.8 = (bf16[160,1024]{1,0:T(8,128)(2,1)S(1)}, bf16[160,1024]{1,0:T(8,128)(2,1)S(1)}, u32[]{:S(2)}, u32[]{:S(2)}) collective-permute-start(bf16[160,1024]{1,0:T(8,128)(2,1)S(1)} %collective-permute-done.6), channel_id=1, source_target_pairs={{0,7},{1,0},{2,1},{3,2},{4,3},{5,4},{6,5},{7,6},{8,15},{9,8},{10,9... | collective-permute-start | bytes 983048 | tf_op jit(solution)/shard_map/ppermute | solution.py:19
  123.2 12.6 %all-to-all-start.3 = ((f32[4,40,320]{2,1,0:T(8,128)}), f32[4,40,320]{2,1,0:T(8,128)S(1)}, u32[]{:S(2)}, u32[]{:S(2)}) async-start(f32[4,40,320]{2,1,0:T(8,128)} %broadcast_in_dim.6), calls=%async_computation.3 | async-start | bytes 491520 | tf_op jit(solution)/shard_map/all_to_all | solution.py:23
  126.7 13.8 %collective-permute-start.9 = (f32[40,320]{1,0:T(8,128)S(1)}, f32[40,320]{1,0:T(8,128)S(1)}, u32[]{:S(2)}, u32[]{:S(2)}) collective-permute-start(f32[40,320]{1,0:T(8,128)S(1)} %pad_maximum_fusion.2), channel_id=1, source_target_pairs={{0,0},{1,33},{2,66},{3,99},{4,132},{5,165},{6,198},{7,231},{8,8},{... | collective-permute-start | bytes 153608 | tf_op jit(solution)/shard_map/ppermute | solution.py:217
  136.9 13.2 %all-to-all-start.4 = ((f32[4,40,1280]{2,1,0:T(8,128)}), f32[4,40,1280]{2,1,0:T(8,128)S(1)}, u32[]{:S(2)}, u32[]{:S(2)}) async-start(f32[4,40,1280]{2,1,0:T(8,128)} %broadcast_in_dim.7), calls=%async_computation.4 | async-start | bytes 1638400 | tf_op jit(solution)/shard_map/all_to_all | solution.py:23
  140.4 6.1 %collective-permute-start.10 = (f32[40,320]{1,0:T(8,128)S(1)}, f32[40,320]{1,0:T(8,128)S(1)}, u32[]{:S(2)}, u32[]{:S(2)}) collective-permute-start(f32[40,320]{1,0:T(8,128)S(1)} %collective-permute-done.9), channel_id=1, source_target_pairs={{0,8},{8,0},{1,9},{9,1},{2,10},{10,2},{3,11},{11,3},{4,12},{12,4},... | collective-permute-start | bytes 153608 | tf_op jit(solution)/shard_map/ppermute | solution.py:19

commit v7 on v4

--- a/solution.py
+++ b/solution.py
@@ -25,7 +25,7 @@
     )
 
 
-def tile_moves():
+def tile_moves(flip):
     moves = []
     for yh in range(4):
         for x in range(4):
@@ -34,9 +34,10 @@
                     for z in range(8):
                         other_yl, half = yh // 2, yh % 2
                         source = (((yh * 4 + x) * 2 + c) * 2 + yl) * 8 + z
-                        to_z = (z + 4 * c + x) % 8
+                        to_yl = (x % 2) ^ flip
+                        to_z = (z + 7 + 4 * yl + 2 * c + x // 2) % 8
                         to_yh, to_x = other_yl * 2 + z // 4, z % 4
-                        target = (((to_yh * 4 + to_x) * 2 + half) * 2 + yl) * 8 + to_z
+                        target = (((to_yh * 4 + to_x) * 2 + half) * 2 + to_yl) * 8 + to_z
                         moves.append((source, target))
     return moves
 
@@ -57,8 +58,11 @@
             n = q * 2 + k
             block = gram[:, :, n * rows : (n + 1) * rows].reshape(2 * rows, rows)
             sums += jnp.sum(jnp.abs(block), 0, keepdims=True)
-            on_diagonal = (at_col == at_row + quarter * q) & (yl == k)
-            trace += jnp.sum(jnp.where(on_diagonal, block[:quarter], 0.0), keepdims=True)
+            if q < 2:
+                for m in range(2):
+                    own = block[(2 + m) * quarter : (3 + m) * quarter]
+                    on_diagonal = (at_col == at_row + 80 * m + quarter * q) & (yl == k)
+                    trace += jnp.sum(jnp.where(on_diagonal, own, 0.0), keepdims=True)
             high = block.astype(jnp.bfloat16)
             high_out[n * 2 * rows : (n + 1) * 2 * rows, :] = high
             low_out[n * 2 * rows : (n + 1) * 2 * rows, :] = (
@@ -83,10 +87,13 @@
     rows, quarter, half_cols = 160, 40, 80
     for k in range(2):
         for s in range(8):
-            block = got[8 * k + lax.rem(z + s, 8)].astype(jnp.float32)
-            for q in range(4):
-                top = (q * 2 + k) * 2 * rows + s * quarter
-                seen[top : top + quarter, :] = block[:, q * half_cols : (q + 1) * half_cols]
+            p, c, l = s // 4, s // 2 % 2, s % 2
+            block = got[8 * k + lax.rem(z + 7 + s, 8)].astype(jnp.float32)
+            for m in range(2):
+                for a in range(2):
+                    g = 2 * m + a
+                    top = ((2 * p + a) * 2 + k) * 2 * rows + (4 * c + 2 * l + m) * quarter
+                    seen[top : top + quarter, :] = block[:, g * half_cols : (g + 1) * half_cols]
     side = seen[...].astype(jnp.bfloat16)
     product = 0.0
     for part in (high, low):
@@ -164,38 +171,42 @@
     second = jnp.where(low, other, pair)
     columns = jnp.concatenate([first[:rows], second[:rows], first[rows:], second[rows:]], 0)
 
-    blocks = {0: entering}
-    up = down = entering
-    for step in range(1, 5):
-        down = shift(down, "z", 8, -1)
-        blocks[step] = down
-        if step < 4:
-            up = shift(up, "z", 8, 1)
-            blocks[8 - step] = up
-
-    pieces = [
-        lax.dot_general(
-            blocks[s], columns, (((1,), (1,)), ((), ())), preferred_element_type=jnp.float32
+    def products(blocks):
+        return jnp.stack(
+            [
+                lax.dot_general(
+                    block, columns, (((1,), (1,)), ((), ())), preferred_element_type=jnp.float32
+                )
+                for block in blocks
+            ]
         )
-        for s in range(8)
-    ]
-    partial = jnp.stack(pieces).reshape(2, 4, rows, 4 * rows)
-    partial = jnp.sum(lax.all_to_all(partial, "c", 0, 0), 0)
-    partial = jnp.sum(lax.all_to_all(partial, "x", 0, 0), 0)
+
+    def core_sum(array):
+        array = lax.all_to_all(array.reshape(2, 2, rows, 4 * rows), "c", 0, 0)
+        return jnp.sum(array, 0).reshape(4, half_cols, 4 * rows)
+
+    down_1, up_1 = shift(entering, "z", 8, -1), shift(entering, "z", 8, 1)
+    down_2, up_2 = shift(down_1, "z", 8, -1), shift(up_1, "z", 8, 1)
+    down_3 = shift(down_2, "z", 8, -1)
+    early = core_sum(products([up_1, entering, down_1, down_2]))
+    early, down_3, up_2 = lax.optimization_barrier((early, down_3, up_2))
+    early = lax.all_to_all(early, "x", 0, 0)
+    down_4, up_3 = shift(down_3, "z", 8, -1), shift(up_2, "z", 8, 1)
+    early, down_4, up_3 = lax.optimization_barrier((early, down_4, up_3))
+    late = core_sum(products([down_3, down_4, up_3, up_2]))
+    late = lax.all_to_all(late, "x", 0, 0)
+    sums = (jnp.sum(early, 0), jnp.sum(late, 0))
     packed = []
     for to_yh in range(4):
+        gram_from, top = sums[to_yh // 2], quarter * (to_yh % 2)
+        left = 2 * rows + half_cols * to_yh
         for to_yl in range(2):
-            top = half_cols * to_yl
-            left = 2 * rows + half_cols * to_yh
             packed.append(
                 jnp.concatenate(
                     [
-                        partial[
-                            quarter * to_yh : quarter * (to_yh + 1),
-                            rows * to_yl : rows * (to_yl + 1),
-                        ],
-                        partial[top : top + quarter, left : left + half_cols],
-                        partial[top + quarter : top + 2 * quarter, left : left + half_cols],
+                        gram_from[top : top + quarter, rows * to_yl : rows * (to_yl + 1)],
+                        sums[to_yl][:quarter, left : left + half_cols],
+                        sums[to_yl][quarter:, left : left + half_cols],
                     ],
                     1,
                 )
@@ -203,14 +214,14 @@
     own = lax.all_to_all(jnp.stack(packed), ("yh", "yl"), 0, 0)
     own = jnp.sum(own.reshape(4, 2, quarter, 2 * rows), 0)
 
-    cross_own = jnp.concatenate([own[0, :, rows:], own[1, :, rows:]], 1)
-    cross_own = lax.ppermute(cross_own, ALL, tile_moves())
-    cross_swap = shift(cross_own, "yl", 2, 1)
-    target = jnp.where(
-        low,
-        jnp.concatenate([cross_own[:, :rows], cross_swap[:, :rows]], 1),
-        jnp.concatenate([cross_swap[:, rows:], cross_own[:, rows:]], 1),
-    ) / token_total
+    even = (lax.axis_index("x") & 1) == 0
+    near = jnp.where(even, own[0, :, rows:], own[1, :, rows:])
+    far = jnp.where(even, own[1, :, rows:], own[0, :, rows:])
+    near = lax.ppermute(near, ALL, tile_moves(0))
+    far = lax.ppermute(far, ALL, tile_moves(1))
+    target = (
+        jnp.concatenate([jnp.where(low, near, far), jnp.where(low, far, near)], 1) / token_total
+    )
 
     gram_part = jnp.concatenate([own[0, :, :rows], own[1, :, :rows]], 1)
     gram_part = spread(gram_part, "yh", 4)

time: 200 us -> 212 us (1.060)
  blocking collectives: 104 us -> 74.5 us
  starting transfers between devices: 46.1 us -> 61.7 us
  waiting for transfers between devices: 30.8 us -> 44.6 us
  other arithmetic: 2.85 us -> 8.66 us
  matrix products: 4.52 us -> 9.39 us
    all_to_all x3 -> x2, blocking collectives: 54.4 us -> 10.1 us  [core_sum(): array = lax.all_to_all(array.reshape(2, 2, rows, 4 * rows), 'c', 0, 0)]
    all_to_all x0 -> x3, waiting for transfers between devices: none -> 26.5 us  [the longest x1 14.5 us: body(): own = lax.all_to_all(jnp.stack(packed), ('yh', 'yl'), 0, 0)]
    all_to_all x0 -> x3, starting transfers between devices: none -> 16.6 us  [the longest x1 7.77 us: body(): own = lax.all_to_all(jnp.stack(packed), ('yh', 'yl'), 0, 0)]
    all_to_all x1 -> x2, blocking collectives: 5.05 us -> 17.8 us  [spread(): lax.all_to_all(jnp.broadcast_to(array[None], (count,) + array.shape), axe...]
    all_to_all x2 -> x1, waiting for transfers between devices: 9.94 us -> 0.01 us  [spread(): lax.all_to_all(jnp.broadcast_to(array[None], (count,) + array.shape), axe...]
    ppermute x9 -> x8, waiting for transfers between devices: 20.8 us -> 13.9 us  [shift(): lax.ppermute(array, axis, [(i, (i + step) % size) for i in range(size)])]
    ppermute x1 -> x2, starting transfers between devices: 2.47 us -> 8.35 us  [the longest x1 6.43 us: body(): near = lax.ppermute(near, ALL, tile_moves(0))]
    dot_general x8, matrix products: 4.52 us -> 9.39 us  [products(): lax.dot_general(block, columns, (((1,), (1,)), ((), ())), preferred_eleme...]
  transfers between devices with their start and end apart: 12 -> 14, of which waited for: 9 -> 8; matrix products, arithmetic and copies ran while one was open for 2% -> 4% of each run, Pallas kernels for 0% -> 0%
where the time goes in v7:
time: 212 us; the launch traced here: 210 us
  blocking collectives  74.5 us (35%)
  starting transfers between devices  61.7 us (29%)
  waiting for transfers between devices  44.6 us (21%)
  matrix products  9.39 us (4%)
  other arithmetic  8.66 us (4%)
  Pallas kernels  6.01 us (3%)
  local copies, waits for them, and re-layouts  5.27 us (2%)
    all_to_all x2, blocking collectives, body(): got = lax.all_to_all(sent, FEAT, 0, 0)  46.6 us
    ppermute x8, starting transfers between devices, shift(): lax.ppermute(array, axis, [(i, (i + step) % size) for i in range(size)])  33.3 us
    all_to_all x2, blocking collectives, spread(): lax.all_to_all(jnp.broadcast_to(array[None], (count,) + array.shape), axe...  17.8 us
    all_to_all x1, waiting for transfers between devices, body(): own = lax.all_to_all(jnp.stack(packed), ('yh', 'yl'), 0, 0)  14.5 us
    ppermute x8, waiting for transfers between devices, shift(): lax.ppermute(array, axis, [(i, (i + step) % size) for i in range(size)])  13.9 us
    all_to_all x1, waiting for transfers between devices, body(): late = lax.all_to_all(late, 'x', 0, 0)  12 us
    all_to_all x2, blocking collectives, core_sum(): array = lax.all_to_all(array.reshape(2, 2, rows, 4 * rows), 'c', 0, 0)  10.1 us
    dot_general x8, matrix products, products(): lax.dot_general(block, columns, (((1,), (1,)), ((), ())), preferred_eleme...  9.39 us
  transfers between devices with their start and end apart: 14, of which 8 were waited for; matrix products, arithmetic and copies ran while one was open for 4% of the time, Pallas kernels for 0%

profile of v7, /device:TPU:72, one launch (start us, length us, event | category | flops | bytes accessed | tf_op | source)
XLA Modules:
  0.0 210.5 jit_solution(11117021301900331721)
XLA Ops:
  4.4 4.3 %collective-permute-start.1 = (bf16[160,1024]{1,0:T(8,128)(2,1)}, bf16[160,1024]{1,0:T(8,128)(2,1)}, u32[]{:S(2)}, u32[]{:S(2)}) collective-permute-start(bf16[160,1024]{1,0:T(8,128)(2,1)} %param.2), channel_id=1, source_target_pairs={{0,1},{1,2},{2,3},{3,4},{4,5},{5,6},{6,7},{7,0},{8,9},{9,10},{10,1... | collective-permute-start | bytes 983048 | tf_op jit(solution)/shard_map/ppermute | solution.py:19
  8.7 4.6 %collective-permute-start.2 = (bf16[160,1024]{1,0:T(8,128)(2,1)}, bf16[160,1024]{1,0:T(8,128)(2,1)S(1)}, u32[]{:S(2)}, u32[]{:S(2)}) collective-permute-start(bf16[160,1024]{1,0:T(8,128)(2,1)} %param.2), channel_id=1, source_target_pairs={{0,7},{1,0},{2,1},{3,2},{4,3},{5,4},{6,5},{7,6},{8,15},{9,8},{10,9... | collective-permute-start | bytes 983048 | tf_op jit(solution)/shard_map/ppermute | solution.py:19
  13.2 3.4 %collective-permute-done.1 = bf16[160,1024]{1,0:T(8,128)(2,1)} collective-permute-done((bf16[160,1024]{1,0:T(8,128)(2,1)}, bf16[160,1024]{1,0:T(8,128)(2,1)}, u32[]{:S(2)}, u32[]{:S(2)}) %collective-permute-start.1) | collective-permute-done | bytes 327712 | tf_op jit(solution)/shard_map/ppermute | solution.py:19
  16.7 3.4 %collective-permute-start.5 = (bf16[160,1024]{1,0:T(8,128)(2,1)}, bf16[160,1024]{1,0:T(8,128)(2,1)S(1)}, u32[]{:S(2)}, u32[]{:S(2)}) collective-permute-start(bf16[160,1024]{1,0:T(8,128)(2,1)} %collective-permute-done.1), channel_id=1, source_target_pairs={{0,1},{1,2},{2,3},{3,4},{4,5},{5,6},{6,7},{7,0},{8,9},{9,10},{10,1... | collective-permute-start | bytes 983048 | tf_op jit(solution)/shard_map/ppermute | solution.py:19
  20.3 6.3 %collective-permute-start.3 = (bf16[160,1024]{1,0:T(8,128)(2,1)S(1)}, bf16[160,1024]{1,0:T(8,128)(2,1)}, u32[]{:S(2)}, u32[]{:S(2)}) collective-permute-start(bf16[160,1024]{1,0:T(8,128)(2,1)S(1)} %collective-permute-done.2), channel_id=1, source_target_pairs={{0,7},{1,0},{2,1},{3,2},{4,3},{5,4},{6,5},{7,6},{8,15},{9,8},{10,9... | collective-permute-start | bytes 983048 | tf_op jit(solution)/shard_map/ppermute | solution.py:19
  28.8 3.8 %collective-permute-done.3 = bf16[160,1024]{1,0:T(8,128)(2,1)} collective-permute-done((bf16[160,1024]{1,0:T(8,128)(2,1)S(1)}, bf16[160,1024]{1,0:T(8,128)(2,1)}, u32[]{:S(2)}, u32[]{:S(2)}) %collective-permute-start.3) | collective-permute-done | bytes 327712 | tf_op jit(solution)/shard_map/ppermute | solution.py:19
  32.6 4.8 %collective-permute-start.4 = (bf16[160,1024]{1,0:T(8,128)(2,1)}, bf16[160,1024]{1,0:T(8,128)(2,1)}, u32[]{:S(2)}, u32[]{:S(2)}) collective-permute-start(bf16[160,1024]{1,0:T(8,128)(2,1)} %collective-permute-done.3), channel_id=1, source_target_pairs={{0,7},{1,0},{2,1},{3,2},{4,3},{5,4},{6,5},{7,6},{8,15},{9,8},{10,9... | collective-permute-start | bytes 983048 | tf_op jit(solution)/shard_map/ppermute | solution.py:19
  40.7 5.0 %all_to_all.50 = f32[2,2,160,640]{3,2,1,0:T(8,128)S(1)} all-to-all(f32[2,2,160,640]{3,2,1,0:T(8,128)S(1)} %bitcast.89), channel_id=1, replica_groups=mesh['yh'=4,'x'=4,'c'=2,'yl'=2,'z'=8] {'c'}, dimensions={0} | all-to-all | bytes 3276800 | tf_op jit(solution)/shard_map/all_to_all | solution.py:185
  46.8 4.3 %all-to-all-start.1 = ((f32[4,80,640]{2,1,0:T(8,128)}), f32[4,80,640]{2,1,0:T(8,128)S(1)}, u32[]{:S(2)}, u32[]{:S(2)}) async-start(f32[4,80,640]{2,1,0:T(8,128)} %bitcast.11), calls=%async_computation.1 | async-start | bytes 1638400 | tf_op jit(solution)/shard_map/all_to_all | solution.py:193
  51.1 5.7 %collective-permute-start.6 = (bf16[160,1024]{1,0:T(8,128)(2,1)}, bf16[160,1024]{1,0:T(8,128)(2,1)S(1)}, u32[]{:S(2)}, u32[]{:S(2)}) collective-permute-start(bf16[160,1024]{1,0:T(8,128)(2,1)} %collective-permute-done.4), channel_id=1, source_target_pairs={{0,7},{1,0},{2,1},{3,2},{4,3},{5,4},{6,5},{7,6},{8,15},{9,8},{10,9... | collective-permute-start | bytes 983048 | tf_op jit(solution)/shard_map/ppermute | solution.py:19
  60.9 3.2 %collective-permute-done.6 = bf16[160,1024]{1,0:T(8,128)(2,1)S(1)} collective-permute-done((bf16[160,1024]{1,0:T(8,128)(2,1)}, bf16[160,1024]{1,0:T(8,128)(2,1)S(1)}, u32[]{:S(2)}, u32[]{:S(2)}) %collective-permute-start.6) | collective-permute-done | bytes 327712 | tf_op jit(solution)/shard_map/ppermute | solution.py:19
  64.8 3.2 %collective-permute-done.7 = bf16[160,1024]{1,0:T(8,128)(2,1)} collective-permute-done((bf16[160,1024]{1,0:T(8,128)(2,1)S(1)}, bf16[160,1024]{1,0:T(8,128)(2,1)}, u32[]{:S(2)}, u32[]{:S(2)}) %collective-permute-start.7) | collective-permute-done | bytes 327712 | tf_op jit(solution)/shard_map/ppermute | solution.py:19
  71.2 5.0 %all_to_all.51 = f32[2,2,160,640]{3,2,1,0:T(8,128)S(1)} all-to-all(f32[2,2,160,640]{3,2,1,0:T(8,128)S(1)} %bitcast.90), channel_id=1, replica_groups=mesh['yh'=4,'x'=4,'c'=2,'yl'=2,'z'=8] {'c'}, dimensions={0} | all-to-all | bytes 3276800 | tf_op jit(solution)/shard_map/all_to_all | solution.py:185
  77.4 4.5 %all-to-all-start.3 = ((f32[4,80,640]{2,1,0:T(8,128)}), f32[4,80,640]{2,1,0:T(8,128)S(1)}, u32[]{:S(2)}, u32[]{:S(2)}) async-start(f32[4,80,640]{2,1,0:T(8,128)} %bitcast.18), calls=%async_computation.3 | async-start | bytes 1638400 | tf_op jit(solution)/shard_map/all_to_all | solution.py:197
  82.8 12.0 %all-to-all-done.3 = f32[4,80,640]{2,1,0:T(8,128)S(1)} async-done(((f32[4,80,640]{2,1,0:T(8,128)}), f32[4,80,640]{2,1,0:T(8,128)S(1)}, u32[]{:S(2)}, u32[]{:S(2)}) %all-to-all-start.3) | async-done | bytes 819232 | tf_op jit(solution)/shard_map/all_to_all | solution.py:197
  100.1 7.8 %all-to-all-start.4 = ((f32[8,40,320]{2,1,0:T(8,128)}), f32[8,40,320]{2,1,0:T(8,128)S(1)}, u32[]{:S(2)}, u32[]{:S(2)}) async-start(f32[8,40,320]{2,1,0:T(8,128)} %fusion.7), calls=%async_computation.4 | async-start | bytes 983040 | tf_op jit(solution)/shard_map/all_to_all | solution.py:214
  107.9 14.5 %all-to-all-done.4 = f32[8,40,320]{2,1,0:T(8,128)S(1)} async-done(((f32[8,40,320]{2,1,0:T(8,128)}), f32[8,40,320]{2,1,0:T(8,128)S(1)}, u32[]{:S(2)}, u32[]{:S(2)}) %all-to-all-start.4) | async-done | bytes 409632 | tf_op jit(solution)/shard_map/all_to_all | solution.py:214
  122.6 12.7 %all_to_all.52 = f32[4,40,320]{2,1,0:T(8,128)S(1)} all-to-all(f32[4,40,320]{2,1,0:T(8,128)S(1)} %broadcast_in_dim.6), channel_id=1, replica_groups=mesh['yh'=4,'x'=4,'c'=2,'yl'=2,'z'=8] {'yh'}, dimensions={0} | all-to-all | bytes 409600 | tf_op jit(solution)/shard_map/all_to_all | solution.py:23
  136.4 3.5 %all-to-all-start.6 = ((f32[4,40,1280]{2,1,0:T(8,128)}), f32[4,40,1280]{2,1,0:T(8,128)S(1)}, u32[]{:S(2)}, u32[]{:S(2)}) async-start(f32[4,40,1280]{2,1,0:T(8,128)} %broadcast_in_dim.7), calls=%async_computation.6 | async-start | bytes 1638400 | tf_op jit(solution)/shard_map/all_to_all | solution.py:23
  139.9 6.4 %collective-permute-start.8 = (f32[40,160]{1,0:T(8,128)S(1)}, f32[40,160]{1,0:T(8,128)S(1)}, u32[]{:S(2)}, u32[]{:S(2)}) collective-permute-start(f32[40,160]{1,0:T(8,128)S(1)} %get-tuple-element.65), channel_id=1, source_target_pairs={{0,7},{1,32},{2,65},{3,98},{4,131},{5,164},{6,197},{7,230},{8,3},{... | collective-permute-start | bytes 76808 | tf_op jit(solution)/shard_map/ppermute | solution.py:220
  148.3 4.2 %collective-permute-done.9 = f32[40,160]{1,0:T(8,128)S(1)} collective-permute-done((f32[40,160]{1,0:T(8,128)S(1)}, f32[40,160]{1,0:T(8,128)S(1)}, u32[]{:S(2)}, u32[]{:S(2)}) %collective-permute-start.9) | collective-permute-done | bytes 25632 | tf_op jit(solution)/shard_map/ppermute | solution.py:221
  152.8 5.0 %all_to_all.53 = f32[2,4,40,1280]{3,2,1,0:T(8,128)S(1)} all-to-all(f32[2,4,40,1280]{3,2,1,0:T(8,128)S(1)} %broadcast_in_dim.8), channel_id=1, replica_groups=mesh['yh'=4,'x'=4,'c'=2,'yl'=2,'z'=8] {'c'}, dimensions={0} | all-to-all | bytes 3276800 | tf_op jit(solution)/shard_map/all_to_all | solution.py:23
  159.5 26.9 %all_to_all.54.got = bf16[16,40,384]{2,1,0:T(8,128)(2,1)S(1)} all-to-all(bf16[16,40,384]{2,1,0:T(8,128)(2,1)S(1)} %get-tuple-element.24), channel_id=1, replica_groups=mesh['yh'=4,'x'=4,'c'=2,'yl'=2,'z'=8] {'yl','z'}, dimensions={0} | all-to-all | bytes 983040 | tf_op jit(solution)/shard_map/all_to_all | solution.py:247
  188.2 19.8 %all_to_all.55.got = bf16[16,40,384]{2,1,0:T(8,128)(2,1)S(1)} all-to-all(bf16[16,40,384]{2,1,0:T(8,128)(2,1)S(1)} %get-tuple-element.27), channel_id=1, replica_groups=mesh['yh'=4,'x'=4,'c'=2,'yl'=2,'z'=8] {'yl','z'}, dimensions={0} | all-to-all | bytes 983040 | tf_op jit(solution)/shard_map/all_to_all | solution.py:256
  (58 shorter events, 35.8 us)
Async XLA Ops:
  2.0 24.6 %collective-permute-start = (bf16[320,1024]{1,0:T(8,128)(2,1)S(1)}, bf16[320,1024]{1,0:T(8,128)(2,1)S(1)}, u32[]{:S(2)}, u32[]{:S(2)}) collective-permute-start(bf16[320,1024]{1,0:T(8,128)(2,1)S(1)} %constant_dynamic-update-slice_fusion), channel_id=1, source_target_pairs={{0,8},{8,0},{1,9},{9,1},{2,10},{10,2},{3,11},{11,3},{4,12},{12,4},... | collective-permute-start | bytes 1966088 | tf_op jit(solution)/shard_map/ppermute | solution.py:19
  4.4 12.3 %collective-permute-start.1 = (bf16[160,1024]{1,0:T(8,128)(2,1)}, bf16[160,1024]{1,0:T(8,128)(2,1)}, u32[]{:S(2)}, u32[]{:S(2)}) collective-permute-start(bf16[160,1024]{1,0:T(8,128)(2,1)} %param.2), channel_id=1, source_target_pairs={{0,1},{1,2},{2,3},{3,4},{4,5},{5,6},{6,7},{7,0},{8,9},{9,10},{10,1... | collective-permute-start | bytes 983048 | tf_op jit(solution)/shard_map/ppermute | solution.py:19
  8.7 11.6 %collective-permute-start.2 = (bf16[160,1024]{1,0:T(8,128)(2,1)}, bf16[160,1024]{1,0:T(8,128)(2,1)S(1)}, u32[]{:S(2)}, u32[]{:S(2)}) collective-permute-start(bf16[160,1024]{1,0:T(8,128)(2,1)} %param.2), channel_id=1, source_target_pairs={{0,7},{1,0},{2,1},{3,2},{4,3},{5,4},{6,5},{7,6},{8,15},{9,8},{10,9... | collective-permute-start | bytes 983048 | tf_op jit(solution)/shard_map/ppermute | solution.py:19
  16.7 30.2 %collective-permute-start.5 = (bf16[160,1024]{1,0:T(8,128)(2,1)}, bf16[160,1024]{1,0:T(8,128)(2,1)S(1)}, u32[]{:S(2)}, u32[]{:S(2)}) collective-permute-start(bf16[160,1024]{1,0:T(8,128)(2,1)} %collective-permute-done.1), channel_id=1, source_target_pairs={{0,1},{1,2},{2,3},{3,4},{4,5},{5,6},{6,7},{7,0},{8,9},{9,10},{10,1... | collective-permute-start | bytes 983048 | tf_op jit(solution)/shard_map/ppermute | solution.py:19
  20.3 12.3 %collective-permute-start.3 = (bf16[160,1024]{1,0:T(8,128)(2,1)S(1)}, bf16[160,1024]{1,0:T(8,128)(2,1)}, u32[]{:S(2)}, u32[]{:S(2)}) collective-permute-start(bf16[160,1024]{1,0:T(8,128)(2,1)S(1)} %collective-permute-done.2), channel_id=1, source_target_pairs={{0,7},{1,0},{2,1},{3,2},{4,3},{5,4},{6,5},{7,6},{8,15},{9,8},{10,9... | collective-permute-start | bytes 983048 | tf_op jit(solution)/shard_map/ppermute | solution.py:19
  26.7 1.0 copy-start
  32.6 14.2 %collective-permute-start.4 = (bf16[160,1024]{1,0:T(8,128)(2,1)}, bf16[160,1024]{1,0:T(8,128)(2,1)}, u32[]{:S(2)}, u32[]{:S(2)}) collective-permute-start(bf16[160,1024]{1,0:T(8,128)(2,1)} %collective-permute-done.3), channel_id=1, source_target_pairs={{0,7},{1,0},{2,1},{3,2},{4,3},{5,4},{6,5},{7,6},{8,15},{9,8},{10,9... | collective-permute-start | bytes 983048 | tf_op jit(solution)/shard_map/ppermute | solution.py:19
  46.8 21.2 %all-to-all-start.1 = ((f32[4,80,640]{2,1,0:T(8,128)}), f32[4,80,640]{2,1,0:T(8,128)S(1)}, u32[]{:S(2)}, u32[]{:S(2)}) async-start(f32[4,80,640]{2,1,0:T(8,128)} %bitcast.11), calls=%async_computation.1 | async-start | bytes 1638400 | tf_op jit(solution)/shard_map/all_to_all | solution.py:193
  51.1 13.0 %collective-permute-start.6 = (bf16[160,1024]{1,0:T(8,128)(2,1)}, bf16[160,1024]{1,0:T(8,128)(2,1)S(1)}, u32[]{:S(2)}, u32[]{:S(2)}) collective-permute-start(bf16[160,1024]{1,0:T(8,128)(2,1)} %collective-permute-done.4), channel_id=1, source_target_pairs={{0,7},{1,0},{2,1},{3,2},{4,3},{5,4},{6,5},{7,6},{8,15},{9,8},{10,9... | collective-permute-start | bytes 983048 | tf_op jit(solution)/shard_map/ppermute | solution.py:19
  56.8 11.2 %collective-permute-start.7 = (bf16[160,1024]{1,0:T(8,128)(2,1)S(1)}, bf16[160,1024]{1,0:T(8,128)(2,1)}, u32[]{:S(2)}, u32[]{:S(2)}) collective-permute-start(bf16[160,1024]{1,0:T(8,128)(2,1)S(1)} %collective-permute-done.5), channel_id=1, source_target_pairs={{0,1},{1,2},{2,3},{3,4},{4,5},{5,6},{6,7},{7,0},{8,9},{9,10},{10,1... | collective-permute-start | bytes 983048 | tf_op jit(solution)/shard_map/ppermute | solution.py:19
  64.1 0.7 copy-start.1
  77.4 17.5 %all-to-all-start.3 = ((f32[4,80,640]{2,1,0:T(8,128)}), f32[4,80,640]{2,1,0:T(8,128)S(1)}, u32[]{:S(2)}, u32[]{:S(2)}) async-start(f32[4,80,640]{2,1,0:T(8,128)} %bitcast.18), calls=%async_computation.3 | async-start | bytes 1638400 | tf_op jit(solution)/shard_map/all_to_all | solution.py:197
  100.1 22.3 %all-to-all-start.4 = ((f32[8,40,320]{2,1,0:T(8,128)}), f32[8,40,320]{2,1,0:T(8,128)S(1)}, u32[]{:S(2)}, u32[]{:S(2)}) async-start(f32[8,40,320]{2,1,0:T(8,128)} %fusion.7), calls=%async_computation.4 | async-start | bytes 983040 | tf_op jit(solution)/shard_map/all_to_all | solution.py:214
  136.4 16.3 %all-to-all-start.6 = ((f32[4,40,1280]{2,1,0:T(8,128)}), f32[4,40,1280]{2,1,0:T(8,128)S(1)}, u32[]{:S(2)}, u32[]{:S(2)}) async-start(f32[4,40,1280]{2,1,0:T(8,128)} %broadcast_in_dim.7), calls=%async_computation.6 | async-start | bytes 1638400 | tf_op jit(solution)/shard_map/all_to_all | solution.py:23
  139.9 8.4 %collective-permute-start.8 = (f32[40,160]{1,0:T(8,128)S(1)}, f32[40,160]{1,0:T(8,128)S(1)}, u32[]{:S(2)}, u32[]{:S(2)}) collective-permute-start(f32[40,160]{1,0:T(8,128)S(1)} %get-tuple-element.65), channel_id=1, source_target_pairs={{0,7},{1,32},{2,65},{3,98},{4,131},{5,164},{6,197},{7,230},{8,3},{... | collective-permute-start | bytes 76808 | tf_op jit(solution)/shard_map/ppermute | solution.py:220
  146.3 6.2 %collective-permute-start.9 = (f32[40,160]{1,0:T(8,128)S(1)}, f32[40,160]{1,0:T(8,128)S(1)}, u32[]{:S(2)}, u32[]{:S(2)}) collective-permute-start(f32[40,160]{1,0:T(8,128)S(1)} %get-tuple-element.66), channel_id=1, source_target_pairs={{0,15},{1,40},{2,73},{3,106},{4,139},{5,172},{6,205},{7,238},{8,11... | collective-permute-start | bytes 76808 | tf_op jit(solution)/shard_map/ppermute | solution.py:221

commit v8 on v7

--- a/solution.py
+++ b/solution.py
@@ -44,6 +44,24 @@
 
 def round_half(array):
     return array.astype(jnp.bfloat16).astype(jnp.float32)
+
+
+def pack_kernel(early, late, packed):
+    rows, quarter, half_cols = 160, 40, 80
+    sums = [(part[0] + part[1]) + (part[2] + part[3]) for part in (early, late)]
+    for to_yh in range(4):
+        gram_from, top = sums[to_yh // 2], quarter * (to_yh % 2)
+        left = 2 * rows + half_cols * to_yh
+        for to_yl in range(2):
+            to = 2 * to_yh + to_yl
+            packed[to, :, :rows] = gram_from[
+                top : top + quarter, rows * to_yl : rows * (to_yl + 1)
+            ]
+            for n in range(2):
+                at = rows + half_cols * n
+                packed[to, :, at : at + half_cols] = sums[to_yl][
+                    quarter * n : quarter * (n + 1), left : left + half_cols
+                ]
 
 
 def split_kernel(place, gram, target, high_out, low_out, sent):
@@ -171,15 +189,14 @@
     second = jnp.where(low, other, pair)
     columns = jnp.concatenate([first[:rows], second[:rows], first[rows:], second[rows:]], 0)
 
-    def products(blocks):
-        return jnp.stack(
-            [
-                lax.dot_general(
-                    block, columns, (((1,), (1,)), ((), ())), preferred_element_type=jnp.float32
-                )
-                for block in blocks
-            ]
-        )
+    def products(blocks, order):
+        whole = jnp.zeros((len(blocks), rows, 4 * rows), jnp.float32)
+        for n in order:
+            product = lax.dot_general(
+                blocks[n], columns, (((1,), (1,)), ((), ())), preferred_element_type=jnp.float32
+            )
+            whole = lax.dynamic_update_index_in_dim(whole, product, n, 0)
+        return whole
 
     def core_sum(array):
         array = lax.all_to_all(array.reshape(2, 2, rows, 4 * rows), "c", 0, 0)
@@ -188,30 +205,21 @@
     down_1, up_1 = shift(entering, "z", 8, -1), shift(entering, "z", 8, 1)
     down_2, up_2 = shift(down_1, "z", 8, -1), shift(up_1, "z", 8, 1)
     down_3 = shift(down_2, "z", 8, -1)
-    early = core_sum(products([up_1, entering, down_1, down_2]))
+    early = core_sum(products([up_1, entering, down_1, down_2], (1, 0, 2, 3)))
     early, down_3, up_2 = lax.optimization_barrier((early, down_3, up_2))
     early = lax.all_to_all(early, "x", 0, 0)
     down_4, up_3 = shift(down_3, "z", 8, -1), shift(up_2, "z", 8, 1)
     early, down_4, up_3 = lax.optimization_barrier((early, down_4, up_3))
-    late = core_sum(products([down_3, down_4, up_3, up_2]))
+    late = core_sum(products([down_3, down_4, up_3, up_2], (0, 3, 1, 2)))
     late = lax.all_to_all(late, "x", 0, 0)
-    sums = (jnp.sum(early, 0), jnp.sum(late, 0))
-    packed = []
-    for to_yh in range(4):
-        gram_from, top = sums[to_yh // 2], quarter * (to_yh % 2)
-        left = 2 * rows + half_cols * to_yh
-        for to_yl in range(2):
-            packed.append(
-                jnp.concatenate(
-                    [
-                        gram_from[top : top + quarter, rows * to_yl : rows * (to_yl + 1)],
-                        sums[to_yl][:quarter, left : left + half_cols],
-                        sums[to_yl][quarter:, left : left + half_cols],
-                    ],
-                    1,
-                )
-            )
-    own = lax.all_to_all(jnp.stack(packed), ("yh", "yl"), 0, 0)
+    packed = pl.pallas_call(
+        pack_kernel,
+        out_shape=jax.ShapeDtypeStruct((8, quarter, 2 * rows), jnp.float32),
+        in_specs=[pl.BlockSpec(memory_space=pltpu.VMEM)] * 2,
+        out_specs=pl.BlockSpec(memory_space=pltpu.VMEM),
+        compiler_params=pltpu.CompilerParams(vmem_limit_bytes=40 * 2**20),
+    )(early, late)
+    own = lax.all_to_all(packed, ("yh", "yl"), 0, 0)
     own = jnp.sum(own.reshape(4, 2, quarter, 2 * rows), 0)
 
     even = (lax.axis_index("x") & 1) == 0

time: 212 us -> 204 us (0.962)
  blocking collectives: 74.5 us -> 93.7 us
  waiting for transfers between devices: 44.6 us -> 27.6 us
  other arithmetic: 8.66 us -> 3.13 us
  starting transfers between devices: 61.7 us -> 56.7 us
    all_to_all x0 -> x1, blocking collectives: none -> 17.3 us  [body(): late = lax.all_to_all(late, 'x', 0, 0)]
    all_to_all x2 -> x1, waiting for transfers between devices: 26.5 us -> 14.5 us  [body(): own = lax.all_to_all(packed, ('yh', 'yl'), 0, 0)]
    unnamed x7 -> x0, other arithmetic: 5.03 us -> none
    all_to_all x2 -> x1, starting transfers between devices: 12.3 us -> 7.77 us  [body(): own = lax.all_to_all(packed, ('yh', 'yl'), 0, 0)]
    ppermute x8, waiting for transfers between devices: 13.9 us -> 9.93 us  [shift(): lax.ppermute(array, axis, [(i, (i + step) % size) for i in range(size)])]
  transfers between devices with their start and end apart: 14 -> 13, of which waited for: 8 -> 7; matrix products, arithmetic and copies ran while one was open for 4% -> 4% of each run, Pallas kernels for 0% -> 0%
where the time goes in v8:
time: 204 us; the launch traced here: 203 us
  blocking collectives  93.7 us (46%)
  starting transfers between devices  56.7 us (28%)
  waiting for transfers between devices  27.6 us (14%)
  matrix products  9.52 us (5%)
  Pallas kernels  7.03 us (3%)
  local copies, waits for them, and re-layouts  5.22 us (3%)
  other arithmetic  3.13 us (2%)
    all_to_all x2, blocking collectives, body(): got = lax.all_to_all(sent, FEAT, 0, 0)  46.7 us
    ppermute x8, starting transfers between devices, shift(): lax.ppermute(array, axis, [(i, (i + step) % size) for i in range(size)])  33.8 us
    all_to_all x2, blocking collectives, spread(): lax.all_to_all(jnp.broadcast_to(array[None], (count,) + array.shape), axe...  18.8 us
    all_to_all x1, blocking collectives, body(): late = lax.all_to_all(late, 'x', 0, 0)  17.3 us
    all_to_all x1, waiting for transfers between devices, body(): own = lax.all_to_all(packed, ('yh', 'yl'), 0, 0)  14.5 us
    all_to_all x2, blocking collectives, core_sum(): array = lax.all_to_all(array.reshape(2, 2, rows, 4 * rows), 'c', 0, 0)  10.9 us
    ppermute x8, waiting for transfers between devices, shift(): lax.ppermute(array, axis, [(i, (i + step) % size) for i in range(size)])  9.93 us
    dot_general x8, matrix products, products(): lax.dot_general(blocks[n], columns, (((1,), (1,)), ((), ())), preferred_e...  9.52 us
  transfers between devices with their start and end apart: 13, of which 7 were waited for; matrix products, arithmetic and copies ran while one was open for 4% of the time, Pallas kernels for 0%

profile of v8, /device:TPU:72, one launch (start us, length us, event | category | flops | bytes accessed | tf_op | source)
XLA Modules:
  0.0 203.3 jit_solution(1551132035109535295)
XLA Ops:
  2.0 2.4 %collective-permute-start = (bf16[320,1024]{1,0:T(8,128)(2,1)S(1)}, bf16[320,1024]{1,0:T(8,128)(2,1)S(1)}, u32[]{:S(2)}, u32[]{:S(2)}) collective-permute-start(bf16[320,1024]{1,0:T(8,128)(2,1)S(1)} %constant_dynamic-update-slice_fusion), channel_id=1, source_target_pairs={{0,8},{8,0},{1,9},{9,1},{2,10},{10,2},{3,11},{11,3},{4,12},{12,4},... | collective-permute-start | bytes 1966088 | tf_op jit(solution)/shard_map/ppermute | solution.py:19
  4.4 6.9 %collective-permute-start.2 = (bf16[160,1024]{1,0:T(8,128)(2,1)}, bf16[160,1024]{1,0:T(8,128)(2,1)S(1)}, u32[]{:S(2)}, u32[]{:S(2)}) collective-permute-start(bf16[160,1024]{1,0:T(8,128)(2,1)} %param.2), channel_id=1, source_target_pairs={{0,7},{1,0},{2,1},{3,2},{4,3},{5,4},{6,5},{7,6},{8,15},{9,8},{10,9... | collective-permute-start | bytes 983048 | tf_op jit(solution)/shard_map/ppermute | solution.py:19
  11.3 1.9 collective-permute-start.1
  13.2 3.0 %collective-permute-done.2 = bf16[160,1024]{1,0:T(8,128)(2,1)S(1)} collective-permute-done((bf16[160,1024]{1,0:T(8,128)(2,1)}, bf16[160,1024]{1,0:T(8,128)(2,1)S(1)}, u32[]{:S(2)}, u32[]{:S(2)}) %collective-permute-start.2) | collective-permute-done | bytes 327712 | tf_op jit(solution)/shard_map/ppermute | solution.py:19
  16.3 7.6 %collective-permute-start.3 = (bf16[160,1024]{1,0:T(8,128)(2,1)S(1)}, bf16[160,1024]{1,0:T(8,128)(2,1)}, u32[]{:S(2)}, u32[]{:S(2)}) collective-permute-start(bf16[160,1024]{1,0:T(8,128)(2,1)S(1)} %collective-permute-done.2), channel_id=1, source_target_pairs={{0,7},{1,0},{2,1},{3,2},{4,3},{5,4},{6,5},{7,6},{8,15},{9,8},{10,9... | collective-permute-start | bytes 983048 | tf_op jit(solution)/shard_map/ppermute | solution.py:19
  29.6 5.5 %collective-permute-start.4 = (bf16[160,1024]{1,0:T(8,128)(2,1)}, bf16[160,1024]{1,0:T(8,128)(2,1)}, u32[]{:S(2)}, u32[]{:S(2)}) collective-permute-start(bf16[160,1024]{1,0:T(8,128)(2,1)} %collective-permute-done.3), channel_id=1, source_target_pairs={{0,7},{1,0},{2,1},{3,2},{4,3},{5,4},{6,5},{7,6},{8,15},{9,8},{10,9... | collective-permute-start | bytes 983048 | tf_op jit(solution)/shard_map/ppermute | solution.py:19
  37.2 5.0 %all_to_all.50 = f32[2,2,160,640]{3,2,1,0:T(8,128)S(1)} all-to-all(f32[2,2,160,640]{3,2,1,0:T(8,128)S(1)} %bitcast.69), channel_id=1, replica_groups=mesh['yh'=4,'x'=4,'c'=2,'yl'=2,'z'=8] {'c'}, dimensions={0} | all-to-all | bytes 3276800 | tf_op jit(solution)/shard_map/all_to_all | solution.py:202
  43.3 4.3 %all-to-all-start.1 = ((f32[4,80,640]{2,1,0:T(8,128)}), f32[4,80,640]{2,1,0:T(8,128)S(1)}, u32[]{:S(2)}, u32[]{:S(2)}) async-start(f32[4,80,640]{2,1,0:T(8,128)} %bitcast.11), calls=%async_computation.1 | async-start | bytes 1638400 | tf_op jit(solution)/shard_map/all_to_all | solution.py:210
  47.6 5.7 %collective-permute-start.6 = (bf16[160,1024]{1,0:T(8,128)(2,1)}, bf16[160,1024]{1,0:T(8,128)(2,1)}, u32[]{:S(2)}, u32[]{:S(2)}) collective-permute-start(bf16[160,1024]{1,0:T(8,128)(2,1)} %collective-permute-done.4), channel_id=1, source_target_pairs={{0,7},{1,0},{2,1},{3,2},{4,3},{5,4},{6,5},{7,6},{8,15},{9,8},{10,9... | collective-permute-start | bytes 983048 | tf_op jit(solution)/shard_map/ppermute | solution.py:19
  53.3 1.9 collective-permute-start.7
  60.6 4.1 %collective-permute-done.7 = bf16[160,1024]{1,0:T(8,128)(2,1)} collective-permute-done((bf16[160,1024]{1,0:T(8,128)(2,1)}, bf16[160,1024]{1,0:T(8,128)(2,1)}, u32[]{:S(2)}, u32[]{:S(2)}) %collective-permute-start.7) | collective-permute-done | bytes 327712 | tf_op jit(solution)/shard_map/ppermute | solution.py:19
  68.0 5.9 %all_to_all.51 = f32[2,2,160,640]{3,2,1,0:T(8,128)} all-to-all(f32[2,2,160,640]{3,2,1,0:T(8,128)S(1)} %bitcast.70), channel_id=1, replica_groups=mesh['yh'=4,'x'=4,'c'=2,'yl'=2,'z'=8] {'c'}, dimensions={0} | all-to-all | bytes 3276800 | tf_op jit(solution)/shard_map/all_to_all | solution.py:202
  75.5 17.3 %all_to_all.52.late = f32[4,80,640]{2,1,0:T(8,128)S(1)} all-to-all(f32[4,80,640]{2,1,0:T(8,128)S(1)} %bitcast.71), channel_id=1, replica_groups=mesh['yh'=4,'x'=4,'c'=2,'yl'=2,'z'=8] {'x'}, dimensions={0} | all-to-all | bytes 1638400 | tf_op jit(solution)/shard_map/all_to_all | solution.py:214
  93.8 7.8 %all-to-all-start.4 = ((f32[8,40,320]{2,1,0:T(8,128)}), f32[8,40,320]{2,1,0:T(8,128)S(1)}, u32[]{:S(2)}, u32[]{:S(2)}) async-start(f32[8,40,320]{2,1,0:T(8,128)} %shard_map.28), calls=%async_computation.4 | async-start | bytes 983040 | tf_op jit(solution)/shard_map/all_to_all | solution.py:222
  101.6 14.5 %all-to-all-done.4 = f32[8,40,320]{2,1,0:T(8,128)S(1)} async-done(((f32[8,40,320]{2,1,0:T(8,128)}), f32[8,40,320]{2,1,0:T(8,128)S(1)}, u32[]{:S(2)}, u32[]{:S(2)}) %all-to-all-start.4) | async-done | bytes 409632 | tf_op jit(solution)/shard_map/all_to_all | solution.py:222
  116.3 12.7 %all_to_all.53 = f32[4,40,320]{2,1,0:T(8,128)S(1)} all-to-all(f32[4,40,320]{2,1,0:T(8,128)S(1)} %broadcast_in_dim.51), channel_id=1, replica_groups=mesh['yh'=4,'x'=4,'c'=2,'yl'=2,'z'=8] {'yh'}, dimensions={0} | all-to-all | bytes 409600 | tf_op jit(solution)/shard_map/all_to_all | solution.py:23
  130.1 3.5 %all-to-all-start.6 = ((f32[4,40,1280]{2,1,0:T(8,128)}), f32[4,40,1280]{2,1,0:T(8,128)S(1)}, u32[]{:S(2)}, u32[]{:S(2)}) async-start(f32[4,40,1280]{2,1,0:T(8,128)} %broadcast_in_dim.52), calls=%async_computation.6 | async-start | bytes 1638400 | tf_op jit(solution)/shard_map/all_to_all | solution.py:23
  133.6 4.4 %collective-permute-start.8 = (f32[40,160]{1,0:T(8,128)S(1)}, f32[40,160]{1,0:T(8,128)S(1)}, u32[]{:S(2)}, u32[]{:S(2)}) collective-permute-start(f32[40,160]{1,0:T(8,128)S(1)} %get-tuple-element.41), channel_id=1, source_target_pairs={{0,7},{1,32},{2,65},{3,98},{4,131},{5,164},{6,197},{7,230},{8,3},{... | collective-permute-start | bytes 76808 | tf_op jit(solution)/shard_map/ppermute | solution.py:228
  138.0 3.0 %collective-permute-start.9 = (f32[40,160]{1,0:T(8,128)S(1)}, f32[40,160]{1,0:T(8,128)S(1)}, u32[]{:S(2)}, u32[]{:S(2)}) collective-permute-start(f32[40,160]{1,0:T(8,128)S(1)} %get-tuple-element.42), channel_id=1, source_target_pairs={{0,15},{1,40},{2,73},{3,106},{4,139},{5,172},{6,205},{7,238},{8,11... | collective-permute-start | bytes 76808 | tf_op jit(solution)/shard_map/ppermute | solution.py:229
  141.0 3.2 %collective-permute-done.9 = f32[40,160]{1,0:T(8,128)S(1)} collective-permute-done((f32[40,160]{1,0:T(8,128)S(1)}, f32[40,160]{1,0:T(8,128)S(1)}, u32[]{:S(2)}, u32[]{:S(2)}) %collective-permute-start.9) | collective-permute-done | bytes 25632 | tf_op jit(solution)/shard_map/ppermute | solution.py:229
  144.4 6.1 %all_to_all.54 = f32[2,4,40,1280]{3,2,1,0:T(8,128)S(1)} all-to-all(f32[2,4,40,1280]{3,2,1,0:T(8,128)S(1)} %broadcast_in_dim.53), channel_id=1, replica_groups=mesh['yh'=4,'x'=4,'c'=2,'yl'=2,'z'=8] {'c'}, dimensions={0} | all-to-all | bytes 3276800 | tf_op jit(solution)/shard_map/all_to_all | solution.py:23
  152.3 26.9 %all_to_all.55.got = bf16[16,40,384]{2,1,0:T(8,128)(2,1)S(1)} all-to-all(bf16[16,40,384]{2,1,0:T(8,128)(2,1)S(1)} %get-tuple-element.24), channel_id=1, replica_groups=mesh['yh'=4,'x'=4,'c'=2,'yl'=2,'z'=8] {'yl','z'}, dimensions={0} | all-to-all | bytes 983040 | tf_op jit(solution)/shard_map/all_to_all | solution.py:255
  181.0 19.8 %all_to_all.56.got = bf16[16,40,384]{2,1,0:T(8,128)(2,1)S(1)} all-to-all(bf16[16,40,384]{2,1,0:T(8,128)(2,1)S(1)} %get-tuple-element.27), channel_id=1, replica_groups=mesh['yh'=4,'x'=4,'c'=2,'yl'=2,'z'=8] {'yl','z'}, dimensions={0} | all-to-all | bytes 983040 | tf_op jit(solution)/shard_map/all_to_all | solution.py:264
  200.8 2.5 %shard_map.31 = f32[160,80]{1,0:T(8,128)} custom-call(s32[2]{0:T(128)S(1)} %pad_add_fusion.place, bf16[16,40,384]{2,1,0:T(8,128)(2,1)S(1)} %all_to_all.56.got, bf16[2560,160]{1,0:T(8,128)(2,1)S(1)} %get-tuple-element.25.high, bf16[2560,160]{1,0:T(8,128)(2,1)S(1)} %get-tuple-element.26.low, f32[40,320]{1,0:T(8,128)S(1)} %maximum_multiply_fusion.target.target_in, ...), custom_call_target="tpu_custom_call" | custom-call | tf_op jit(solution)/shard_map/pallas_call | solution.py:265
  (48 shorter events, 27.1 us)
Async XLA Ops:
  2.0 24.2 %collective-permute-start = (bf16[320,1024]{1,0:T(8,128)(2,1)S(1)}, bf16[320,1024]{1,0:T(8,128)(2,1)S(1)}, u32[]{:S(2)}, u32[]{:S(2)}) collective-permute-start(bf16[320,1024]{1,0:T(8,128)(2,1)S(1)} %constant_dynamic-update-slice_fusion), channel_id=1, source_target_pairs={{0,8},{8,0},{1,9},{9,1},{2,10},{10,2},{3,11},{11,3},{4,12},{12,4},... | collective-permute-start | bytes 1966088 | tf_op jit(solution)/shard_map/ppermute | solution.py:19
  4.4 11.9 %collective-permute-start.2 = (bf16[160,1024]{1,0:T(8,128)(2,1)}, bf16[160,1024]{1,0:T(8,128)(2,1)S(1)}, u32[]{:S(2)}, u32[]{:S(2)}) collective-permute-start(bf16[160,1024]{1,0:T(8,128)(2,1)} %param.2), channel_id=1, source_target_pairs={{0,7},{1,0},{2,1},{3,2},{4,3},{5,4},{6,5},{7,6},{8,15},{9,8},{10,9... | collective-permute-start | bytes 983048 | tf_op jit(solution)/shard_map/ppermute | solution.py:19
  11.3 12.9 %collective-permute-start.1 = (bf16[160,1024]{1,0:T(8,128)(2,1)}, bf16[160,1024]{1,0:T(8,128)(2,1)S(1)}, u32[]{:S(2)}, u32[]{:S(2)}) collective-permute-start(bf16[160,1024]{1,0:T(8,128)(2,1)} %param.2), channel_id=1, source_target_pairs={{0,1},{1,2},{2,3},{3,4},{4,5},{5,6},{6,7},{7,0},{8,9},{9,10},{10,1... | collective-permute-start | bytes 983048 | tf_op jit(solution)/shard_map/ppermute | solution.py:19
  16.3 13.3 %collective-permute-start.3 = (bf16[160,1024]{1,0:T(8,128)(2,1)S(1)}, bf16[160,1024]{1,0:T(8,128)(2,1)}, u32[]{:S(2)}, u32[]{:S(2)}) collective-permute-start(bf16[160,1024]{1,0:T(8,128)(2,1)S(1)} %collective-permute-done.2), channel_id=1, source_target_pairs={{0,7},{1,0},{2,1},{3,2},{4,3},{5,4},{6,5},{7,6},{8,15},{9,8},{10,9... | collective-permute-start | bytes 983048 | tf_op jit(solution)/shard_map/ppermute | solution.py:19
  24.2 19.1 %collective-permute-start.5 = (bf16[160,1024]{1,0:T(8,128)(2,1)S(1)}, bf16[160,1024]{1,0:T(8,128)(2,1)}, u32[]{:S(2)}, u32[]{:S(2)}) collective-permute-start(bf16[160,1024]{1,0:T(8,128)(2,1)S(1)} %collective-permute-done.1), channel_id=1, source_target_pairs={{0,1},{1,2},{2,3},{3,4},{4,5},{5,6},{6,7},{7,0},{8,9},{9,10},{10,1... | collective-permute-start | bytes 983048 | tf_op jit(solution)/shard_map/ppermute | solution.py:19
  26.3 1.0 copy-start.3
  26.4 28.9 %copy-start = (bf16[160,1024]{1,0:T(8,128)(2,1)}, bf16[160,1024]{1,0:T(8,128)(2,1)S(1)}, u32[]{:S(2)}) copy-start(bf16[160,1024]{1,0:T(8,128)(2,1)S(1)} %get-tuple-element.48) | copy-start | bytes 983044
  29.6 13.7 %collective-permute-start.4 = (bf16[160,1024]{1,0:T(8,128)(2,1)}, bf16[160,1024]{1,0:T(8,128)(2,1)}, u32[]{:S(2)}, u32[]{:S(2)}) collective-permute-start(bf16[160,1024]{1,0:T(8,128)(2,1)} %collective-permute-done.3), channel_id=1, source_target_pairs={{0,7},{1,0},{2,1},{3,2},{4,3},{5,4},{6,5},{7,6},{8,15},{9,8},{10,9... | collective-permute-start | bytes 983048 | tf_op jit(solution)/shard_map/ppermute | solution.py:19
  43.3 21.4 %all-to-all-start.1 = ((f32[4,80,640]{2,1,0:T(8,128)}), f32[4,80,640]{2,1,0:T(8,128)S(1)}, u32[]{:S(2)}, u32[]{:S(2)}) async-start(f32[4,80,640]{2,1,0:T(8,128)} %bitcast.11), calls=%async_computation.1 | async-start | bytes 1638400 | tf_op jit(solution)/shard_map/all_to_all | solution.py:210
  47.6 13.0 %collective-permute-start.6 = (bf16[160,1024]{1,0:T(8,128)(2,1)}, bf16[160,1024]{1,0:T(8,128)(2,1)}, u32[]{:S(2)}, u32[]{:S(2)}) collective-permute-start(bf16[160,1024]{1,0:T(8,128)(2,1)} %collective-permute-done.4), channel_id=1, source_target_pairs={{0,7},{1,0},{2,1},{3,2},{4,3},{5,4},{6,5},{7,6},{8,15},{9,8},{10,9... | collective-permute-start | bytes 983048 | tf_op jit(solution)/shard_map/ppermute | solution.py:19
  53.3 11.4 %collective-permute-start.7 = (bf16[160,1024]{1,0:T(8,128)(2,1)}, bf16[160,1024]{1,0:T(8,128)(2,1)}, u32[]{:S(2)}, u32[]{:S(2)}) collective-permute-start(bf16[160,1024]{1,0:T(8,128)(2,1)} %collective-permute-done.5), channel_id=1, source_target_pairs={{0,1},{1,2},{2,3},{3,4},{4,5},{5,6},{6,7},{7,0},{8,9},{9,10},{10,1... | collective-permute-start | bytes 983048 | tf_op jit(solution)/shard_map/ppermute | solution.py:19
  56.8 1.0 copy-start.1
  64.8 1.7 copy-start.2
  93.8 22.3 %all-to-all-start.4 = ((f32[8,40,320]{2,1,0:T(8,128)}), f32[8,40,320]{2,1,0:T(8,128)S(1)}, u32[]{:S(2)}, u32[]{:S(2)}) async-start(f32[8,40,320]{2,1,0:T(8,128)} %shard_map.28), calls=%async_computation.4 | async-start | bytes 983040 | tf_op jit(solution)/shard_map/all_to_all | solution.py:222
  130.1 14.2 %all-to-all-start.6 = ((f32[4,40,1280]{2,1,0:T(8,128)}), f32[4,40,1280]{2,1,0:T(8,128)S(1)}, u32[]{:S(2)}, u32[]{:S(2)}) async-start(f32[4,40,1280]{2,1,0:T(8,128)} %broadcast_in_dim.52), calls=%async_computation.6 | async-start | bytes 1638400 | tf_op jit(solution)/shard_map/all_to_all | solution.py:23
  133.6 7.5 %collective-permute-start.8 = (f32[40,160]{1,0:T(8,128)S(1)}, f32[40,160]{1,0:T(8,128)S(1)}, u32[]{:S(2)}, u32[]{:S(2)}) collective-permute-start(f32[40,160]{1,0:T(8,128)S(1)} %get-tuple-element.41), channel_id=1, source_target_pairs={{0,7},{1,32},{2,65},{3,98},{4,131},{5,164},{6,197},{7,230},{8,3},{... | collective-permute-start | bytes 76808 | tf_op jit(solution)/shard_map/ppermute | solution.py:228
  138.0 6.2 %collective-permute-start.9 = (f32[40,160]{1,0:T(8,128)S(1)}, f32[40,160]{1,0:T(8,128)S(1)}, u32[]{:S(2)}, u32[]{:S(2)}) collective-permute-start(f32[40,160]{1,0:T(8,128)S(1)} %get-tuple-element.42), channel_id=1, source_target_pairs={{0,15},{1,40},{2,73},{3,106},{4,139},{5,172},{6,205},{7,238},{8,11... | collective-permute-start | bytes 76808 | tf_op jit(solution)/shard_map/ppermute | solution.py:229

commit v9 on v8

--- a/solution.py
+++ b/solution.py
@@ -205,13 +205,13 @@
     down_1, up_1 = shift(entering, "z", 8, -1), shift(entering, "z", 8, 1)
     down_2, up_2 = shift(down_1, "z", 8, -1), shift(up_1, "z", 8, 1)
     down_3 = shift(down_2, "z", 8, -1)
-    early = core_sum(products([up_1, entering, down_1, down_2], (1, 0, 2, 3)))
+    early = products([up_1, entering, down_1, down_2], (1, 0, 2, 3))
     early, down_3, up_2 = lax.optimization_barrier((early, down_3, up_2))
-    early = lax.all_to_all(early, "x", 0, 0)
     down_4, up_3 = shift(down_3, "z", 8, -1), shift(up_2, "z", 8, 1)
-    early, down_4, up_3 = lax.optimization_barrier((early, down_4, up_3))
-    late = core_sum(products([down_3, down_4, up_3, up_2], (0, 3, 1, 2)))
-    late = lax.all_to_all(late, "x", 0, 0)
+    early = lax.all_to_all(core_sum(early), "x", 0, 0)
+    late = products([down_3, down_4, up_3, up_2], (0, 3, 1, 2))
+    early, late = lax.optimization_barrier((early, late))
+    late = lax.all_to_all(core_sum(late), "x", 0, 0)
     packed = pl.pallas_call(
         pack_kernel,
         out_shape=jax.ShapeDtypeStruct((8, quarter, 2 * rows), jnp.float32),
@@ -227,12 +227,12 @@
     far = jnp.where(even, own[1, :, rows:], own[0, :, rows:])
     near = lax.ppermute(near, ALL, tile_moves(0))
     far = lax.ppermute(far, ALL, tile_moves(1))
+    gram_part = jnp.concatenate([own[0, :, :rows], own[1, :, :rows]], 1)
+    gram_part = spread(gram_part, "yh", 4)
+    gram_part, near, far = lax.optimization_barrier((gram_part, near, far))
     target = (
         jnp.concatenate([jnp.where(low, near, far), jnp.where(low, far, near)], 1) / token_total
     )
-
-    gram_part = jnp.concatenate([own[0, :, :rows], own[1, :, :rows]], 1)
-    gram_part = spread(gram_part, "yh", 4)
     gram_part = jnp.concatenate([gram_part[q] for q in range(4)], 1)
     gram_part = spread(gram_part, "x", 4)
     gram = spread(gram_part, "c", 2).reshape(8, quarter, 8 * rows)

time: 204 us -> 216 us (1.059)
  waiting for transfers between devices: 27.6 us -> 44.6 us
  blocking collectives: 93.7 us -> 81 us
  starting transfers between devices: 56.7 us -> 66 us
  matrix products: 9.52 us -> 6.52 us
    all_to_all x2 -> x1, blocking collectives: 18.8 us -> 5.05 us  [spread(): lax.all_to_all(jnp.broadcast_to(array[None], (count,) + array.shape), axe...]
    all_to_all x1 -> x2, waiting for transfers between devices: 0.01 us -> 11 us  [spread(): lax.all_to_all(jnp.broadcast_to(array[None], (count,) + array.shape), axe...]
    ppermute x8, waiting for transfers between devices: 9.93 us -> 17.5 us  [shift(): lax.ppermute(array, axis, [(i, (i + step) % size) for i in range(size)])]
    all_to_all x1 -> x2, starting transfers between devices: 3.5 us -> 8.96 us  [spread(): lax.all_to_all(jnp.broadcast_to(array[None], (count,) + array.shape), axe...]
    ppermute x1, starting transfers between devices: 2.96 us -> 6.13 us  [body(): far = lax.ppermute(far, ALL, tile_moves(1))]
    dot_general x8, matrix products: 9.52 us -> 6.52 us  [products(): lax.dot_general(blocks[n], columns, (((1,), (1,)), ((), ())), preferred_e...]
  transfers between devices with their start and end apart: 13 -> 14, of which waited for: 7 -> 8; matrix products, arithmetic and copies ran while one was open for 4% -> 4% of each run, Pallas kernels for 0% -> 0%
where the time goes in v9:
time: 216 us; the launch traced here: 215 us
  blocking collectives  81 us (38%)
  starting transfers between devices  66 us (31%)
  waiting for transfers between devices  44.6 us (21%)
  Pallas kernels  7.03 us (3%)
  matrix products  6.52 us (3%)
  local copies, waits for them, and re-layouts  5.91 us (3%)
  other arithmetic  3.12 us (1%)
    all_to_all x2, blocking collectives, body(): got = lax.all_to_all(sent, FEAT, 0, 0)  47.8 us
    ppermute x8, starting transfers between devices, shift(): lax.ppermute(array, axis, [(i, (i + step) % size) for i in range(size)])  33.7 us
    ppermute x8, waiting for transfers between devices, shift(): lax.ppermute(array, axis, [(i, (i + step) % size) for i in range(size)])  17.5 us
    all_to_all x1, blocking collectives, body(): late = lax.all_to_all(core_sum(late), 'x', 0, 0)  17.3 us
    all_to_all x1, waiting for transfers between devices, body(): own = lax.all_to_all(packed, ('yh', 'yl'), 0, 0)  14.5 us
    all_to_all x2, waiting for transfers between devices, spread(): lax.all_to_all(jnp.broadcast_to(array[None], (count,) + array.shape), axe...  11 us
    all_to_all x2, blocking collectives, core_sum(): array = lax.all_to_all(array.reshape(2, 2, rows, 4 * rows), 'c', 0, 0)  10.9 us
    all_to_all x2, starting transfers between devices, spread(): lax.all_to_all(jnp.broadcast_to(array[None], (count,) + array.shape), axe...  8.96 us
  transfers between devices with their start and end apart: 14, of which 8 were waited for; matrix products, arithmetic and copies ran while one was open for 4% of the time, Pallas kernels for 0%

profile of v9, /device:TPU:72, one launch (start us, length us, event | category | flops | bytes accessed | tf_op | source)
XLA Modules:
  0.0 214.6 jit_solution(12369254149405731836)
XLA Ops:
  2.0 2.4 %collective-permute-start = (bf16[320,1024]{1,0:T(8,128)(2,1)S(1)}, bf16[320,1024]{1,0:T(8,128)(2,1)S(1)}, u32[]{:S(2)}, u32[]{:S(2)}) collective-permute-start(bf16[320,1024]{1,0:T(8,128)(2,1)S(1)} %constant_dynamic-update-slice_fusion), channel_id=1, source_target_pairs={{0,8},{8,0},{1,9},{9,1},{2,10},{10,2},{3,11},{11,3},{4,12},{12,4},... | collective-permute-start | bytes 1966088 | tf_op jit(solution)/shard_map/ppermute | solution.py:19
  4.4 6.9 %collective-permute-start.2 = (bf16[160,1024]{1,0:T(8,128)(2,1)}, bf16[160,1024]{1,0:T(8,128)(2,1)S(1)}, u32[]{:S(2)}, u32[]{:S(2)}) collective-permute-start(bf16[160,1024]{1,0:T(8,128)(2,1)} %param.2), channel_id=1, source_target_pairs={{0,7},{1,0},{2,1},{3,2},{4,3},{5,4},{6,5},{7,6},{8,15},{9,8},{10,9... | collective-permute-start | bytes 983048 | tf_op jit(solution)/shard_map/ppermute | solution.py:19
  11.3 1.9 collective-permute-start.1
  13.2 3.0 %collective-permute-done.2 = bf16[160,1024]{1,0:T(8,128)(2,1)S(1)} collective-permute-done((bf16[160,1024]{1,0:T(8,128)(2,1)}, bf16[160,1024]{1,0:T(8,128)(2,1)S(1)}, u32[]{:S(2)}, u32[]{:S(2)}) %collective-permute-start.2) | collective-permute-done | bytes 327712 | tf_op jit(solution)/shard_map/ppermute | solution.py:19
  16.3 7.6 %collective-permute-start.3 = (bf16[160,1024]{1,0:T(8,128)(2,1)S(1)}, bf16[160,1024]{1,0:T(8,128)(2,1)S(1)}, u32[]{:S(2)}, u32[]{:S(2)}) collective-permute-start(bf16[160,1024]{1,0:T(8,128)(2,1)S(1)} %collective-permute-done.2), channel_id=1, source_target_pairs={{0,7},{1,0},{2,1},{3,2},{4,3},{5,4},{6,5},{7,6},{8,15},{9,8},{10,9... | collective-permute-start | bytes 983048 | tf_op jit(solution)/shard_map/ppermute | solution.py:19
  29.6 5.5 %collective-permute-start.4 = (bf16[160,1024]{1,0:T(8,128)(2,1)S(1)}, bf16[160,1024]{1,0:T(8,128)(2,1)}, u32[]{:S(2)}, u32[]{:S(2)}) collective-permute-start(bf16[160,1024]{1,0:T(8,128)(2,1)S(1)} %collective-permute-done.3), channel_id=1, source_target_pairs={{0,7},{1,0},{2,1},{3,2},{4,3},{5,4},{6,5},{7,6},{8,15},{9,8},{10,9... | collective-permute-start | bytes 983048 | tf_op jit(solution)/shard_map/ppermute | solution.py:19
  36.3 3.7 %collective-permute-done.4 = bf16[160,1024]{1,0:T(8,128)(2,1)} collective-permute-done((bf16[160,1024]{1,0:T(8,128)(2,1)S(1)}, bf16[160,1024]{1,0:T(8,128)(2,1)}, u32[]{:S(2)}, u32[]{:S(2)}) %collective-permute-start.4) | collective-permute-done | bytes 327712 | tf_op jit(solution)/shard_map/ppermute | solution.py:19
  39.9 5.6 %collective-permute-start.6 = (bf16[160,1024]{1,0:T(8,128)(2,1)}, bf16[160,1024]{1,0:T(8,128)(2,1)}, u32[]{:S(2)}, u32[]{:S(2)}) collective-permute-start(bf16[160,1024]{1,0:T(8,128)(2,1)} %collective-permute-done.4), channel_id=1, source_target_pairs={{0,7},{1,0},{2,1},{3,2},{4,3},{5,4},{6,5},{7,6},{8,15},{9,8},{10,9... | collective-permute-start | bytes 983048 | tf_op jit(solution)/shard_map/ppermute | solution.py:19
  47.1 5.0 %all_to_all.50 = f32[2,2,160,640]{3,2,1,0:T(8,128)S(1)} all-to-all(f32[2,2,160,640]{3,2,1,0:T(8,128)S(1)} %bitcast.70), channel_id=1, replica_groups=mesh['yh'=4,'x'=4,'c'=2,'yl'=2,'z'=8] {'c'}, dimensions={0} | all-to-all | bytes 3276800 | tf_op jit(solution)/shard_map/all_to_all | solution.py:202
  53.3 4.3 %all-to-all-start.1 = ((f32[4,80,640]{2,1,0:T(8,128)}), f32[4,80,640]{2,1,0:T(8,128)S(1)}, u32[]{:S(2)}, u32[]{:S(2)}) async-start(f32[4,80,640]{2,1,0:T(8,128)} %bitcast.11), calls=%async_computation.1 | async-start | bytes 1638400 | tf_op jit(solution)/shard_map/all_to_all | solution.py:211
  62.6 9.3 %collective-permute-done.7 = bf16[160,1024]{1,0:T(8,128)(2,1)S(1)} collective-permute-done((bf16[160,1024]{1,0:T(8,128)(2,1)S(1)}, bf16[160,1024]{1,0:T(8,128)(2,1)S(1)}, u32[]{:S(2)}, u32[]{:S(2)}) %collective-permute-start.7) | collective-permute-done | bytes 327712 | tf_op jit(solution)/shard_map/ppermute | solution.py:19
  72.5 5.9 %all_to_all.51 = f32[2,2,160,640]{3,2,1,0:T(8,128)} all-to-all(f32[2,2,160,640]{3,2,1,0:T(8,128)S(1)} %bitcast.69), channel_id=1, replica_groups=mesh['yh'=4,'x'=4,'c'=2,'yl'=2,'z'=8] {'c'}, dimensions={0} | all-to-all | bytes 3276800 | tf_op jit(solution)/shard_map/all_to_all | solution.py:202
  80.0 17.3 %all_to_all.52.late = f32[4,80,640]{2,1,0:T(8,128)S(1)} all-to-all(f32[4,80,640]{2,1,0:T(8,128)S(1)} %bitcast.71), channel_id=1, replica_groups=mesh['yh'=4,'x'=4,'c'=2,'yl'=2,'z'=8] {'x'}, dimensions={0} | all-to-all | bytes 1638400 | tf_op jit(solution)/shard_map/all_to_all | solution.py:214
  98.3 7.8 %all-to-all-start.4 = ((f32[8,40,320]{2,1,0:T(8,128)}), f32[8,40,320]{2,1,0:T(8,128)S(1)}, u32[]{:S(2)}, u32[]{:S(2)}) async-start(f32[8,40,320]{2,1,0:T(8,128)} %shard_map.28), calls=%async_computation.4 | async-start | bytes 983040 | tf_op jit(solution)/shard_map/all_to_all | solution.py:222
  106.1 14.5 %all-to-all-done.4 = f32[8,40,320]{2,1,0:T(8,128)S(1)} async-done(((f32[8,40,320]{2,1,0:T(8,128)}), f32[8,40,320]{2,1,0:T(8,128)S(1)}, u32[]{:S(2)}, u32[]{:S(2)}) %all-to-all-start.4) | async-done | bytes 409632 | tf_op jit(solution)/shard_map/all_to_all | solution.py:222
  121.5 3.4 %all-to-all-start.5 = ((f32[4,40,320]{2,1,0:T(8,128)}), f32[4,40,320]{2,1,0:T(8,128)S(1)}, u32[]{:S(2)}, u32[]{:S(2)}) async-start(f32[4,40,320]{2,1,0:T(8,128)} %broadcast_in_dim.51), calls=%async_computation.5 | async-start | bytes 491520 | tf_op jit(solution)/shard_map/all_to_all | solution.py:23
  124.9 5.2 %collective-permute-start.8 = (f32[40,160]{1,0:T(8,128)S(1)}, f32[40,160]{1,0:T(8,128)S(1)}, u32[]{:S(2)}, u32[]{:S(2)}) collective-permute-start(f32[40,160]{1,0:T(8,128)S(1)} %get-tuple-element.46), channel_id=1, source_target_pairs={{0,7},{1,32},{2,65},{3,98},{4,131},{5,164},{6,197},{7,230},{8,3},{... | collective-permute-start | bytes 76808 | tf_op jit(solution)/shard_map/ppermute | solution.py:228
  130.1 6.1 %collective-permute-start.9 = (f32[40,160]{1,0:T(8,128)S(1)}, f32[40,160]{1,0:T(8,128)S(1)}, u32[]{:S(2)}, u32[]{:S(2)}) collective-permute-start(f32[40,160]{1,0:T(8,128)S(1)} %get-tuple-element.45), channel_id=1, source_target_pairs={{0,15},{1,40},{2,73},{3,106},{4,139},{5,172},{6,205},{7,238},{8,11... | collective-permute-start | bytes 76808 | tf_op jit(solution)/shard_map/ppermute | solution.py:229
  139.0 5.6 %all-to-all-start.6 = ((f32[4,40,1280]{2,1,0:T(8,128)}), f32[4,40,1280]{2,1,0:T(8,128)S(1)}, u32[]{:S(2)}, u32[]{:S(2)}) async-start(f32[4,40,1280]{2,1,0:T(8,128)} %broadcast_in_dim.52), calls=%async_computation.6 | async-start | bytes 1638400 | tf_op jit(solution)/shard_map/all_to_all | solution.py:23
  144.7 11.0 %all-to-all-done.6 = f32[4,40,1280]{2,1,0:T(8,128)S(1)} async-done(((f32[4,40,1280]{2,1,0:T(8,128)}), f32[4,40,1280]{2,1,0:T(8,128)S(1)}, u32[]{:S(2)}, u32[]{:S(2)}) %all-to-all-start.6) | async-done | bytes 819232 | tf_op jit(solution)/shard_map/all_to_all | solution.py:23
  155.8 5.0 %all_to_all.53 = f32[2,4,40,1280]{3,2,1,0:T(8,128)S(1)} all-to-all(f32[2,4,40,1280]{3,2,1,0:T(8,128)S(1)} %broadcast_in_dim.53), channel_id=1, replica_groups=mesh['yh'=4,'x'=4,'c'=2,'yl'=2,'z'=8] {'c'}, dimensions={0} | all-to-all | bytes 3276800 | tf_op jit(solution)/shard_map/all_to_all | solution.py:23
  162.5 28.0 %all_to_all.54.got = bf16[16,40,384]{2,1,0:T(8,128)(2,1)S(1)} all-to-all(bf16[16,40,384]{2,1,0:T(8,128)(2,1)S(1)} %get-tuple-element.28), channel_id=1, replica_groups=mesh['yh'=4,'x'=4,'c'=2,'yl'=2,'z'=8] {'yl','z'}, dimensions={0} | all-to-all | bytes 983040 | tf_op jit(solution)/shard_map/all_to_all | solution.py:255
  192.4 19.8 %all_to_all.55.got = bf16[16,40,384]{2,1,0:T(8,128)(2,1)S(1)} all-to-all(bf16[16,40,384]{2,1,0:T(8,128)(2,1)S(1)} %get-tuple-element.31), channel_id=1, replica_groups=mesh['yh'=4,'x'=4,'c'=2,'yl'=2,'z'=8] {'yl','z'}, dimensions={0} | all-to-all | bytes 983040 | tf_op jit(solution)/shard_map/all_to_all | solution.py:264
  212.1 2.5 %shard_map.31 = f32[160,80]{1,0:T(8,128)} custom-call(s32[2]{0:T(128)S(1)} %pad_add_fusion.place, bf16[16,40,384]{2,1,0:T(8,128)(2,1)S(1)} %all_to_all.55.got, bf16[2560,160]{1,0:T(8,128)(2,1)S(1)} %get-tuple-element.29.high, bf16[2560,160]{1,0:T(8,128)(2,1)S(1)} %get-tuple-element.30.low, f32[40,320]{1,0:T(8,128)S(1)} %maximum_multiply_fusion.target.target_in, ...), custom_call_target="tpu_custom_call" | custom-call | tf_op jit(solution)/shard_map/pallas_call | solution.py:265
  (55 shorter events, 27.1 us)
Async XLA Ops:
  2.0 24.2 %collective-permute-start = (bf16[320,1024]{1,0:T(8,128)(2,1)S(1)}, bf16[320,1024]{1,0:T(8,128)(2,1)S(1)}, u32[]{:S(2)}, u32[]{:S(2)}) collective-permute-start(bf16[320,1024]{1,0:T(8,128)(2,1)S(1)} %constant_dynamic-update-slice_fusion), channel_id=1, source_target_pairs={{0,8},{8,0},{1,9},{9,1},{2,10},{10,2},{3,11},{11,3},{4,12},{12,4},... | collective-permute-start | bytes 1966088 | tf_op jit(solution)/shard_map/ppermute | solution.py:19
  4.4 11.9 %collective-permute-start.2 = (bf16[160,1024]{1,0:T(8,128)(2,1)}, bf16[160,1024]{1,0:T(8,128)(2,1)S(1)}, u32[]{:S(2)}, u32[]{:S(2)}) collective-permute-start(bf16[160,1024]{1,0:T(8,128)(2,1)} %param.2), channel_id=1, source_target_pairs={{0,7},{1,0},{2,1},{3,2},{4,3},{5,4},{6,5},{7,6},{8,15},{9,8},{10,9... | collective-permute-start | bytes 983048 | tf_op jit(solution)/shard_map/ppermute | solution.py:19
  11.3 12.9 %collective-permute-start.1 = (bf16[160,1024]{1,0:T(8,128)(2,1)}, bf16[160,1024]{1,0:T(8,128)(2,1)S(1)}, u32[]{:S(2)}, u32[]{:S(2)}) collective-permute-start(bf16[160,1024]{1,0:T(8,128)(2,1)} %param.2), channel_id=1, source_target_pairs={{0,1},{1,2},{2,3},{3,4},{4,5},{5,6},{6,7},{7,0},{8,9},{9,10},{10,1... | collective-permute-start | bytes 983048 | tf_op jit(solution)/shard_map/ppermute | solution.py:19
  16.3 13.3 %collective-permute-start.3 = (bf16[160,1024]{1,0:T(8,128)(2,1)S(1)}, bf16[160,1024]{1,0:T(8,128)(2,1)S(1)}, u32[]{:S(2)}, u32[]{:S(2)}) collective-permute-start(bf16[160,1024]{1,0:T(8,128)(2,1)S(1)} %collective-permute-done.2), channel_id=1, source_target_pairs={{0,7},{1,0},{2,1},{3,2},{4,3},{5,4},{6,5},{7,6},{8,15},{9,8},{10,9... | collective-permute-start | bytes 983048 | tf_op jit(solution)/shard_map/ppermute | solution.py:19
  24.2 12.0 %collective-permute-start.5 = (bf16[160,1024]{1,0:T(8,128)(2,1)S(1)}, bf16[160,1024]{1,0:T(8,128)(2,1)S(1)}, u32[]{:S(2)}, u32[]{:S(2)}) collective-permute-start(bf16[160,1024]{1,0:T(8,128)(2,1)S(1)} %collective-permute-done.1), channel_id=1, source_target_pairs={{0,1},{1,2},{2,3},{3,4},{4,5},{5,6},{6,7},{7,0},{8,9},{9,10},{10,1... | collective-permute-start | bytes 983048 | tf_op jit(solution)/shard_map/ppermute | solution.py:19
  26.3 1.0 copy-start.4
  26.4 19.1 %copy-start = (bf16[160,1024]{1,0:T(8,128)(2,1)}, bf16[160,1024]{1,0:T(8,128)(2,1)S(1)}, u32[]{:S(2)}) copy-start(bf16[160,1024]{1,0:T(8,128)(2,1)S(1)} %get-tuple-element.51) | copy-start | bytes 983044
  26.4 19.1 %copy-start.2 = (bf16[160,1024]{1,0:T(8,128)(2,1)}, bf16[160,1024]{1,0:T(8,128)(2,1)S(1)}, u32[]{:S(2)}) copy-start(bf16[160,1024]{1,0:T(8,128)(2,1)S(1)} %get-tuple-element.52) | copy-start | bytes 983044
  29.6 10.3 %collective-permute-start.4 = (bf16[160,1024]{1,0:T(8,128)(2,1)S(1)}, bf16[160,1024]{1,0:T(8,128)(2,1)}, u32[]{:S(2)}, u32[]{:S(2)}) collective-permute-start(bf16[160,1024]{1,0:T(8,128)(2,1)S(1)} %collective-permute-done.3), channel_id=1, source_target_pairs={{0,7},{1,0},{2,1},{3,2},{4,3},{5,4},{6,5},{7,6},{8,15},{9,8},{10,9... | collective-permute-start | bytes 983048 | tf_op jit(solution)/shard_map/ppermute | solution.py:19
  36.3 10.9 %copy-start.5 = (bf16[160,1024]{1,0:T(8,128)(2,1)}, bf16[160,1024]{1,0:T(8,128)(2,1)S(1)}, u32[]{:S(2)}) copy-start(bf16[160,1024]{1,0:T(8,128)(2,1)S(1)} %collective-permute-done.5) | copy-start | bytes 983044
  39.9 21.1 %collective-permute-start.6 = (bf16[160,1024]{1,0:T(8,128)(2,1)}, bf16[160,1024]{1,0:T(8,128)(2,1)}, u32[]{:S(2)}, u32[]{:S(2)}) collective-permute-start(bf16[160,1024]{1,0:T(8,128)(2,1)} %collective-permute-done.4), channel_id=1, source_target_pairs={{0,7},{1,0},{2,1},{3,2},{4,3},{5,4},{6,5},{7,6},{8,15},{9,8},{10,9... | collective-permute-start | bytes 983048 | tf_op jit(solution)/shard_map/ppermute | solution.py:19
  53.3 19.3 %all-to-all-start.1 = ((f32[4,80,640]{2,1,0:T(8,128)}), f32[4,80,640]{2,1,0:T(8,128)S(1)}, u32[]{:S(2)}, u32[]{:S(2)}) async-start(f32[4,80,640]{2,1,0:T(8,128)} %bitcast.11), calls=%async_computation.1 | async-start | bytes 1638400 | tf_op jit(solution)/shard_map/all_to_all | solution.py:211
  57.5 1.0 copy-start.6
  57.6 2.9 %copy-start.1 = (bf16[160,1024]{1,0:T(8,128)(2,1)S(1)}, bf16[160,1024]{1,0:T(8,128)(2,1)}, u32[]{:S(2)}) copy-start(bf16[160,1024]{1,0:T(8,128)(2,1)} %copy-done) | copy-start | bytes 983044
  57.6 2.9 %copy-start.3 = (bf16[160,1024]{1,0:T(8,128)(2,1)S(1)}, bf16[160,1024]{1,0:T(8,128)(2,1)}, u32[]{:S(2)}) copy-start(bf16[160,1024]{1,0:T(8,128)(2,1)} %copy-done.2) | copy-start | bytes 983044
  58.5 13.4 %collective-permute-start.7 = (bf16[160,1024]{1,0:T(8,128)(2,1)S(1)}, bf16[160,1024]{1,0:T(8,128)(2,1)S(1)}, u32[]{:S(2)}, u32[]{:S(2)}) collective-permute-start(bf16[160,1024]{1,0:T(8,128)(2,1)S(1)} %copy-done.6), channel_id=1, source_target_pairs={{0,1},{1,2},{2,3},{3,4},{4,5},{5,6},{6,7},{7,0},{8,9},{9,10},{10,1... | collective-permute-start | bytes 983048 | tf_op jit(solution)/shard_map/ppermute | solution.py:19
  98.3 22.3 %all-to-all-start.4 = ((f32[8,40,320]{2,1,0:T(8,128)}), f32[8,40,320]{2,1,0:T(8,128)S(1)}, u32[]{:S(2)}, u32[]{:S(2)}) async-start(f32[8,40,320]{2,1,0:T(8,128)} %shard_map.28), calls=%async_computation.4 | async-start | bytes 983040 | tf_op jit(solution)/shard_map/all_to_all | solution.py:222
  121.5 16.4 %all-to-all-start.5 = ((f32[4,40,320]{2,1,0:T(8,128)}), f32[4,40,320]{2,1,0:T(8,128)S(1)}, u32[]{:S(2)}, u32[]{:S(2)}) async-start(f32[4,40,320]{2,1,0:T(8,128)} %broadcast_in_dim.51), calls=%async_computation.5 | async-start | bytes 491520 | tf_op jit(solution)/shard_map/all_to_all | solution.py:23
  124.9 11.3 %collective-permute-start.8 = (f32[40,160]{1,0:T(8,128)S(1)}, f32[40,160]{1,0:T(8,128)S(1)}, u32[]{:S(2)}, u32[]{:S(2)}) collective-permute-start(f32[40,160]{1,0:T(8,128)S(1)} %get-tuple-element.46), channel_id=1, source_target_pairs={{0,7},{1,32},{2,65},{3,98},{4,131},{5,164},{6,197},{7,230},{8,3},{... | collective-permute-start | bytes 76808 | tf_op jit(solution)/shard_map/ppermute | solution.py:228
  130.1 7.8 %collective-permute-start.9 = (f32[40,160]{1,0:T(8,128)S(1)}, f32[40,160]{1,0:T(8,128)S(1)}, u32[]{:S(2)}, u32[]{:S(2)}) collective-permute-start(f32[40,160]{1,0:T(8,128)S(1)} %get-tuple-element.45), channel_id=1, source_target_pairs={{0,15},{1,40},{2,73},{3,106},{4,139},{5,172},{6,205},{7,238},{8,11... | collective-permute-start | bytes 76808 | tf_op jit(solution)/shard_map/ppermute | solution.py:229
  139.0 16.7 %all-to-all-start.6 = ((f32[4,40,1280]{2,1,0:T(8,128)}), f32[4,40,1280]{2,1,0:T(8,128)S(1)}, u32[]{:S(2)}, u32[]{:S(2)}) async-start(f32[4,40,1280]{2,1,0:T(8,128)} %broadcast_in_dim.52), calls=%async_computation.6 | async-start | bytes 1638400 | tf_op jit(solution)/shard_map/all_to_all | solution.py:23

commit v10 on v4

--- a/solution.py
+++ b/solution.py
@@ -13,6 +13,7 @@
 FEAT = ("yl", "z")
 ALL = TOK + FEAT
 SIZES = (4, 4, 2, 2, 8)
+OFFSETS = (7, 6, 5, 4, 0, 1, 2, 3)
 
 
 def shift(array, axis, size, step):
@@ -34,7 +35,7 @@
                     for z in range(8):
                         other_yl, half = yh // 2, yh % 2
                         source = (((yh * 4 + x) * 2 + c) * 2 + yl) * 8 + z
-                        to_z = (z + 4 * c + x) % 8
+                        to_z = (z + OFFSETS[4 * c + x]) % 8
                         to_yh, to_x = other_yl * 2 + z // 4, z % 4
                         target = (((to_yh * 4 + to_x) * 2 + half) * 2 + yl) * 8 + to_z
                         moves.append((source, target))
@@ -58,7 +59,8 @@
             block = gram[:, :, n * rows : (n + 1) * rows].reshape(2 * rows, rows)
             sums += jnp.sum(jnp.abs(block), 0, keepdims=True)
             on_diagonal = (at_col == at_row + quarter * q) & (yl == k)
-            trace += jnp.sum(jnp.where(on_diagonal, block[:quarter], 0.0), keepdims=True)
+            own = block[4 * quarter : 5 * quarter]
+            trace += jnp.sum(jnp.where(on_diagonal, own, 0.0), keepdims=True)
             high = block.astype(jnp.bfloat16)
             high_out[n * 2 * rows : (n + 1) * 2 * rows, :] = high
             low_out[n * 2 * rows : (n + 1) * 2 * rows, :] = (
@@ -83,7 +85,7 @@
     rows, quarter, half_cols = 160, 40, 80
     for k in range(2):
         for s in range(8):
-            block = got[8 * k + lax.rem(z + s, 8)].astype(jnp.float32)
+            block = got[8 * k + lax.rem(z + OFFSETS[s], 8)].astype(jnp.float32)
             for q in range(4):
                 top = (q * 2 + k) * 2 * rows + s * quarter
                 seen[top : top + quarter, :] = block[:, q * half_cols : (q + 1) * half_cols]
@@ -164,23 +166,22 @@
     second = jnp.where(low, other, pair)
     columns = jnp.concatenate([first[:rows], second[:rows], first[rows:], second[rows:]], 0)
 
-    blocks = {0: entering}
-    up = down = entering
-    for step in range(1, 5):
-        down = shift(down, "z", 8, -1)
-        blocks[step] = down
-        if step < 4:
-            up = shift(up, "z", 8, 1)
-            blocks[8 - step] = up
-
-    pieces = [
-        lax.dot_general(
-            blocks[s], columns, (((1,), (1,)), ((), ())), preferred_element_type=jnp.float32
+    columns_there = shift(columns, "c", 2, 1)
+    first = [(z, (z + 1) % 8) for z in range(8)] + [(8 + z, 8 + z) for z in range(8)]
+    later = [(z, (z + 1) % 8) for z in range(8)] + [(8 + z, 8 + (z + 7) % 8) for z in range(8)]
+    here, there = entering, shift(entering, "c", 2, 1)
+    partial = jnp.zeros((4, rows, 4 * rows), jnp.float32)
+    for step in range(4):
+        if step == 3:
+            here, columns_there = lax.optimization_barrier((here, columns_there))
+        here = lax.ppermute(here, ("c", "z"), later if step else first)
+        there = lax.ppermute(there, ("c", "z"), later if step else first)
+        product = lax.dot_general(
+            here, columns, (((1,), (1,)), ((), ())), preferred_element_type=jnp.float32
+        ) + lax.dot_general(
+            there, columns_there, (((1,), (1,)), ((), ())), preferred_element_type=jnp.float32
         )
-        for s in range(8)
-    ]
-    partial = jnp.stack(pieces).reshape(2, 4, rows, 4 * rows)
-    partial = jnp.sum(lax.all_to_all(partial, "c", 0, 0), 0)
+        partial = lax.dynamic_update_index_in_dim(partial, product, step, 0)
     partial = jnp.sum(lax.all_to_all(partial, "x", 0, 0), 0)
     packed = []
     for to_yh in range(4):

time: 200 us -> 195 us (0.975)
  blocking collectives: 104 us -> 84.3 us
  waiting for transfers between devices: 30.8 us -> 40.2 us
  starting transfers between devices: 46.1 us -> 52.2 us
    ppermute x0 -> x8, starting transfers between devices: none -> 30.9 us  [the longest x4 17.4 us: body(): here = lax.ppermute(here, ('c', 'z'), later if step else first)]
    ppermute x9 -> x4, starting transfers between devices: 36.8 us -> 8.88 us  [shift(): lax.ppermute(array, axis, [(i, (i + step) % size) for i in range(size)])]
    ppermute x0 -> x8, waiting for transfers between devices: none -> 16.1 us  [the longest x4 9.84 us: body(): there = lax.ppermute(there, ('c', 'z'), later if step else first)]
    all_to_all x1, blocking collectives: 26 us -> 18.2 us  [body(): partial = jnp.sum(lax.all_to_all(partial, 'x', 0, 0), 0)]
    ppermute x9 -> x4, waiting for transfers between devices: 20.8 us -> 13.1 us  [shift(): lax.ppermute(array, axis, [(i, (i + step) % size) for i in range(size)])]
    all_to_all x1 -> x0, blocking collectives: 6.37 us -> none  [body(): partial = jnp.sum(lax.all_to_all(partial, 'c', 0, 0), 0)]
    all_to_all x1, blocking collectives: 22.1 us -> 18.8 us  [body(): own = lax.all_to_all(jnp.stack(packed), ('yh', 'yl'), 0, 0)]
    ppermute x1, starting transfers between devices: 2.47 us -> 5.52 us  [body(): cross_own = lax.ppermute(cross_own, ALL, tile_moves())]
  transfers between devices with their start and end apart: 12 -> 15, of which waited for: 9 -> 9; matrix products, arithmetic and copies ran while one was open for 2% -> 3% of each run, Pallas kernels for 0% -> 0%
where the time goes in v10:
time: 195 us; the launch traced here: 194 us
  blocking collectives  84.3 us (43%)
  starting transfers between devices  52.2 us (27%)
  waiting for transfers between devices  40.2 us (21%)
  Pallas kernels  6.09 us (3%)
  local copies, waits for them, and re-layouts  4.69 us (2%)
  matrix products  4.64 us (2%)
    all_to_all x2, blocking collectives, body(): got = lax.all_to_all(sent, FEAT, 0, 0)  42.3 us
    all_to_all x1, blocking collectives, body(): own = lax.all_to_all(jnp.stack(packed), ('yh', 'yl'), 0, 0)  18.8 us
    all_to_all x1, blocking collectives, body(): partial = jnp.sum(lax.all_to_all(partial, 'x', 0, 0), 0)  18.2 us
    ppermute x4, starting transfers between devices, body(): here = lax.ppermute(here, ('c', 'z'), later if step else first)  17.4 us
    ppermute x4, starting transfers between devices, body(): there = lax.ppermute(there, ('c', 'z'), later if step else first)  13.5 us
    ppermute x4, waiting for transfers between devices, shift(): lax.ppermute(array, axis, [(i, (i + step) % size) for i in range(size)])  13.1 us
    all_to_all x2, waiting for transfers between devices, spread(): lax.all_to_all(jnp.broadcast_to(array[None], (count,) + array.shape), axe...  11 us
    ppermute x4, waiting for transfers between devices, body(): there = lax.ppermute(there, ('c', 'z'), later if step else first)  9.84 us
  transfers between devices with their start and end apart: 15, of which 9 were waited for; matrix products, arithmetic and copies ran while one was open for 3% of the time, Pallas kernels for 0%

profile of v10, /device:TPU:72, one launch (start us, length us, event | category | flops | bytes accessed | tf_op | source)
XLA Modules:
  0.0 193.9 jit_solution(10780728306198816359)
XLA Ops:
  2.1 2.4 %collective-permute-start = (bf16[320,1024]{1,0:T(8,128)(2,1)S(1)}, bf16[320,1024]{1,0:T(8,128)(2,1)S(1)}, u32[]{:S(2)}, u32[]{:S(2)}) collective-permute-start(bf16[320,1024]{1,0:T(8,128)(2,1)S(1)} %constant_dynamic-update-slice_fusion), channel_id=1, source_target_pairs={{0,8},{8,0},{1,9},{9,1},{2,10},{10,2},{3,11},{11,3},{4,12},{12,4},... | collective-permute-start | bytes 1966088 | tf_op jit(solution)/shard_map/ppermute | solution.py:20
  6.4 4.3 %collective-permute-start.1 = (bf16[160,1024]{1,0:T(8,128)(2,1)S(1)}, bf16[160,1024]{1,0:T(8,128)(2,1)S(1)}, u32[]{:S(2)}, u32[]{:S(2)}) collective-permute-start(bf16[160,1024]{1,0:T(8,128)(2,1)S(1)} %copy-done), channel_id=1, source_target_pairs={{0,1},{1,2},{2,3},{3,4},{4,5},{5,6},{6,7},{7,0},{16,16},{17,17},{1... | collective-permute-start | bytes 983048 | tf_op jit(solution)/shard_map/ppermute | solution.py:177
  10.7 9.8 %collective-permute-done = bf16[320,1024]{1,0:T(8,128)(2,1)S(1)} collective-permute-done((bf16[320,1024]{1,0:T(8,128)(2,1)S(1)}, bf16[320,1024]{1,0:T(8,128)(2,1)S(1)}, u32[]{:S(2)}, u32[]{:S(2)}) %collective-permute-start) | collective-permute-done | bytes 655392 | tf_op jit(solution)/shard_map/ppermute | solution.py:20
  22.7 4.3 %collective-permute-start.4 = (bf16[160,1024]{1,0:T(8,128)(2,1)S(1)}, bf16[160,1024]{1,0:T(8,128)(2,1)S(1)}, u32[]{:S(2)}, u32[]{:S(2)}) collective-permute-start(bf16[160,1024]{1,0:T(8,128)(2,1)S(1)} %collective-permute-done.3), channel_id=1, source_target_pairs={{0,1},{1,2},{2,3},{3,4},{4,5},{5,6},{6,7},{7,0},{16,16},{17,17},{1... | collective-permute-start | bytes 983048 | tf_op jit(solution)/shard_map/ppermute | solution.py:178
  27.0 4.3 %collective-permute-start.5 = (bf16[160,1024]{1,0:T(8,128)(2,1)S(1)}, bf16[160,1024]{1,0:T(8,128)(2,1)S(1)}, u32[]{:S(2)}, u32[]{:S(2)}) collective-permute-start(bf16[160,1024]{1,0:T(8,128)(2,1)S(1)} %collective-permute-done.1), channel_id=1, source_target_pairs={{0,1},{1,2},{2,3},{3,4},{4,5},{5,6},{6,7},{7,0},{16,23},{17,16},{1... | collective-permute-start | bytes 983048 | tf_op jit(solution)/shard_map/ppermute | solution.py:177
  31.7 5.1 %collective-permute-start.6 = (bf16[160,1024]{1,0:T(8,128)(2,1)S(1)}, bf16[160,1024]{1,0:T(8,128)(2,1)S(1)}, u32[]{:S(2)}, u32[]{:S(2)}) collective-permute-start(bf16[160,1024]{1,0:T(8,128)(2,1)S(1)} %collective-permute-done.4), channel_id=1, source_target_pairs={{0,1},{1,2},{2,3},{3,4},{4,5},{5,6},{6,7},{7,0},{16,23},{17,16},{1... | collective-permute-start | bytes 983048 | tf_op jit(solution)/shard_map/ppermute | solution.py:178
  36.8 4.5 %collective-permute-start.7 = (bf16[160,1024]{1,0:T(8,128)(2,1)S(1)}, bf16[160,1024]{1,0:T(8,128)(2,1)S(1)}, u32[]{:S(2)}, u32[]{:S(2)}) collective-permute-start(bf16[160,1024]{1,0:T(8,128)(2,1)S(1)} %collective-permute-done.5), channel_id=1, source_target_pairs={{0,1},{1,2},{2,3},{3,4},{4,5},{5,6},{6,7},{7,0},{16,23},{17,16},{1... | collective-permute-start | bytes 983048 | tf_op jit(solution)/shard_map/ppermute | solution.py:177
  41.9 3.4 %collective-permute-done.6 = bf16[160,1024]{1,0:T(8,128)(2,1)S(1)} collective-permute-done((bf16[160,1024]{1,0:T(8,128)(2,1)S(1)}, bf16[160,1024]{1,0:T(8,128)(2,1)S(1)}, u32[]{:S(2)}, u32[]{:S(2)}) %collective-permute-start.6) | collective-permute-done | bytes 327712 | tf_op jit(solution)/shard_map/ppermute | solution.py:178
  49.4 6.1 %collective-permute-done.8 = bf16[160,1024]{1,0:T(8,128)(2,1)S(1)} collective-permute-done((bf16[160,1024]{1,0:T(8,128)(2,1)S(1)}, bf16[160,1024]{1,0:T(8,128)(2,1)S(1)}, u32[]{:S(2)}, u32[]{:S(2)}) %collective-permute-start.8) | collective-permute-done | bytes 327712 | tf_op jit(solution)/shard_map/ppermute | solution.py:178
  57.4 4.3 %collective-permute-start.9 = (bf16[160,1024]{1,0:T(8,128)(2,1)S(1)}, bf16[160,1024]{1,0:T(8,128)(2,1)S(1)}, u32[]{:S(2)}, u32[]{:S(2)}) collective-permute-start(bf16[160,1024]{1,0:T(8,128)(2,1)S(1)} %collective-permute-done.7), channel_id=1, source_target_pairs={{0,1},{1,2},{2,3},{3,4},{4,5},{5,6},{6,7},{7,0},{16,23},{17,16},{1... | collective-permute-start | bytes 983048 | tf_op jit(solution)/shard_map/ppermute | solution.py:177
  63.6 5.5 %collective-permute-done.9 = bf16[160,1024]{1,0:T(8,128)(2,1)S(1)} collective-permute-done((bf16[160,1024]{1,0:T(8,128)(2,1)S(1)}, bf16[160,1024]{1,0:T(8,128)(2,1)S(1)}, u32[]{:S(2)}, u32[]{:S(2)}) %collective-permute-start.9) | collective-permute-done | bytes 327712 | tf_op jit(solution)/shard_map/ppermute | solution.py:177
  70.3 18.2 %all_to_all.35 = f32[4,160,640]{2,1,0:T(8,128)S(1)} all-to-all(f32[4,160,640]{2,1,0:T(8,128)S(1)} %fusion.2), channel_id=1, replica_groups=mesh['yh'=4,'x'=4,'c'=2,'yl'=2,'z'=8] {'x'}, dimensions={0} | all-to-all | bytes 3276800 | tf_op jit(solution)/shard_map/all_to_all | solution.py:185
  89.6 18.8 %all_to_all.36 = f32[8,40,320]{2,1,0:T(8,128)S(1)} all-to-all(f32[8,40,320]{2,1,0:T(8,128)S(1)} %fusion.15), channel_id=1, replica_groups=mesh['yh'=4,'x'=4,'c'=2,'yl'=2,'z'=8] {'yh','yl'}, dimensions={0} | all-to-all | bytes 819200 | tf_op jit(solution)/shard_map/all_to_all | solution.py:204
  109.4 3.4 %all-to-all-start.2 = ((f32[4,40,320]{2,1,0:T(8,128)}), f32[4,40,320]{2,1,0:T(8,128)S(1)}, u32[]{:S(2)}, u32[]{:S(2)}) async-start(f32[4,40,320]{2,1,0:T(8,128)} %broadcast_in_dim.36), calls=%async_computation.2 | async-start | bytes 491520 | tf_op jit(solution)/shard_map/all_to_all | solution.py:24
  112.9 5.5 %collective-permute-start.11 = (f32[40,320]{1,0:T(8,128)S(1)}, f32[40,320]{1,0:T(8,128)S(1)}, u32[]{:S(2)}, u32[]{:S(2)}) collective-permute-start(f32[40,320]{1,0:T(8,128)S(1)} %pad_maximum_fusion.2), channel_id=1, source_target_pairs={{0,7},{1,32},{2,65},{3,98},{4,131},{5,164},{6,197},{7,230},{8,15},... | collective-permute-start | bytes 153608 | tf_op jit(solution)/shard_map/ppermute | solution.py:208
  118.4 4.0 %all-to-all-done.2 = f32[4,40,320]{2,1,0:T(8,128)S(1)} async-done(((f32[4,40,320]{2,1,0:T(8,128)}), f32[4,40,320]{2,1,0:T(8,128)S(1)}, u32[]{:S(2)}, u32[]{:S(2)}) %all-to-all-start.2) | async-done | bytes 204832 | tf_op jit(solution)/shard_map/all_to_all | solution.py:24
  123.5 3.5 %all-to-all-start.3 = ((f32[4,40,1280]{2,1,0:T(8,128)}), f32[4,40,1280]{2,1,0:T(8,128)S(1)}, u32[]{:S(2)}, u32[]{:S(2)}) async-start(f32[4,40,1280]{2,1,0:T(8,128)} %broadcast_in_dim.37), calls=%async_computation.3 | async-start | bytes 1638400 | tf_op jit(solution)/shard_map/all_to_all | solution.py:24
  127.1 2.7 %collective-permute-start.12 = (f32[40,320]{1,0:T(8,128)S(1)}, f32[40,320]{1,0:T(8,128)S(1)}, u32[]{:S(2)}, u32[]{:S(2)}) collective-permute-start(f32[40,320]{1,0:T(8,128)S(1)} %collective-permute-done.11), channel_id=1, source_target_pairs={{0,8},{8,0},{1,9},{9,1},{2,10},{10,2},{3,11},{11,3},{4,12},{12,4},... | collective-permute-start | bytes 153608 | tf_op jit(solution)/shard_map/ppermute | solution.py:20
  129.8 3.3 %collective-permute-done.12 = f32[40,320]{1,0:T(8,128)S(1)} collective-permute-done((f32[40,320]{1,0:T(8,128)S(1)}, f32[40,320]{1,0:T(8,128)S(1)}, u32[]{:S(2)}, u32[]{:S(2)}) %collective-permute-start.12) | collective-permute-done | bytes 51232 | tf_op jit(solution)/shard_map/ppermute | solution.py:20
  133.3 7.0 %all-to-all-done.3 = f32[4,40,1280]{2,1,0:T(8,128)S(1)} async-done(((f32[4,40,1280]{2,1,0:T(8,128)}), f32[4,40,1280]{2,1,0:T(8,128)S(1)}, u32[]{:S(2)}, u32[]{:S(2)}) %all-to-all-start.3) | async-done | bytes 819232 | tf_op jit(solution)/shard_map/all_to_all | solution.py:24
  140.4 5.0 %all_to_all.37 = f32[2,4,40,1280]{3,2,1,0:T(8,128)S(1)} all-to-all(f32[2,4,40,1280]{3,2,1,0:T(8,128)S(1)} %broadcast_in_dim.38), channel_id=1, replica_groups=mesh['yh'=4,'x'=4,'c'=2,'yl'=2,'z'=8] {'c'}, dimensions={0} | all-to-all | bytes 3276800 | tf_op jit(solution)/shard_map/all_to_all | solution.py:24
  147.2 22.6 %all_to_all.38.got = bf16[16,40,384]{2,1,0:T(8,128)(2,1)S(1)} all-to-all(bf16[16,40,384]{2,1,0:T(8,128)(2,1)S(1)} %get-tuple-element.16), channel_id=1, replica_groups=mesh['yh'=4,'x'=4,'c'=2,'yl'=2,'z'=8] {'yl','z'}, dimensions={0} | all-to-all | bytes 983040 | tf_op jit(solution)/shard_map/all_to_all | solution.py:237
  171.7 19.8 %all_to_all.39.got = bf16[16,40,384]{2,1,0:T(8,128)(2,1)S(1)} all-to-all(bf16[16,40,384]{2,1,0:T(8,128)(2,1)S(1)} %get-tuple-element.19), channel_id=1, replica_groups=mesh['yh'=4,'x'=4,'c'=2,'yl'=2,'z'=8] {'yl','z'}, dimensions={0} | all-to-all | bytes 983040 | tf_op jit(solution)/shard_map/all_to_all | solution.py:246
  191.4 2.5 %shard_map.30 = f32[160,80]{1,0:T(8,128)} custom-call(s32[2]{0:T(128)S(1)} %pad_add_fusion.place, bf16[16,40,384]{2,1,0:T(8,128)(2,1)S(1)} %all_to_all.39.got, bf16[2560,160]{1,0:T(8,128)(2,1)S(1)} %get-tuple-element.17.high, bf16[2560,160]{1,0:T(8,128)(2,1)S(1)} %get-tuple-element.18.low, f32[40,320]{1,0:T(8,128)S(1)} %fusion.16.target.target_in, ...), custom_call_target="tpu_custom_call" | custom-call | tf_op jit(solution)/shard_map/pallas_call | solution.py:247
  (54 shorter events, 23.4 us)
Async XLA Ops:
  0.0 4.4 %copy-start = (bf16[160,1024]{1,0:T(8,128)(2,1)S(1)}, bf16[160,1024]{1,0:T(8,128)(2,1)}, u32[]{:S(2)}) copy-start(bf16[160,1024]{1,0:T(8,128)(2,1)} %param.2) | copy-start | bytes 983044
  2.1 18.4 %collective-permute-start = (bf16[320,1024]{1,0:T(8,128)(2,1)S(1)}, bf16[320,1024]{1,0:T(8,128)(2,1)S(1)}, u32[]{:S(2)}, u32[]{:S(2)}) collective-permute-start(bf16[320,1024]{1,0:T(8,128)(2,1)S(1)} %constant_dynamic-update-slice_fusion), channel_id=1, source_target_pairs={{0,8},{8,0},{1,9},{9,1},{2,10},{10,2},{3,11},{11,3},{4,12},{12,4},... | collective-permute-start | bytes 1966088 | tf_op jit(solution)/shard_map/ppermute | solution.py:20
  4.4 18.3 %collective-permute-start.3 = (bf16[160,1024]{1,0:T(8,128)(2,1)S(1)}, bf16[160,1024]{1,0:T(8,128)(2,1)S(1)}, u32[]{:S(2)}, u32[]{:S(2)}) collective-permute-start(bf16[160,1024]{1,0:T(8,128)(2,1)S(1)} %copy-done), channel_id=1, source_target_pairs={{0,16},{16,0},{1,17},{17,1},{2,18},{18,2},{3,19},{19,3},{4,20},{20... | collective-permute-start | bytes 983048 | tf_op jit(solution)/shard_map/ppermute | solution.py:20
  6.4 20.6 %collective-permute-start.1 = (bf16[160,1024]{1,0:T(8,128)(2,1)S(1)}, bf16[160,1024]{1,0:T(8,128)(2,1)S(1)}, u32[]{:S(2)}, u32[]{:S(2)}) collective-permute-start(bf16[160,1024]{1,0:T(8,128)(2,1)S(1)} %copy-done), channel_id=1, source_target_pairs={{0,1},{1,2},{2,3},{3,4},{4,5},{5,6},{6,7},{7,0},{16,16},{17,17},{1... | collective-permute-start | bytes 983048 | tf_op jit(solution)/shard_map/ppermute | solution.py:177
  20.8 36.6 %collective-permute-start.2 = (bf16[640,1024]{1,0:T(8,128)(2,1)S(1)}, bf16[640,1024]{1,0:T(8,128)(2,1)S(1)}, u32[]{:S(2)}, u32[]{:S(2)}) collective-permute-start(bf16[640,1024]{1,0:T(8,128)(2,1)S(1)} %pad_maximum_fusion), channel_id=1, source_target_pairs={{0,16},{16,0},{1,17},{17,1},{2,18},{18,2},{3,19},{19,3},{4,20},{20... | collective-permute-start | bytes 3932168 | tf_op jit(solution)/shard_map/ppermute | solution.py:20
  22.7 9.0 %collective-permute-start.4 = (bf16[160,1024]{1,0:T(8,128)(2,1)S(1)}, bf16[160,1024]{1,0:T(8,128)(2,1)S(1)}, u32[]{:S(2)}, u32[]{:S(2)}) collective-permute-start(bf16[160,1024]{1,0:T(8,128)(2,1)S(1)} %collective-permute-done.3), channel_id=1, source_target_pairs={{0,1},{1,2},{2,3},{3,4},{4,5},{5,6},{6,7},{7,0},{16,16},{17,17},{1... | collective-permute-start | bytes 983048 | tf_op jit(solution)/shard_map/ppermute | solution.py:178
  27.0 9.8 %collective-permute-start.5 = (bf16[160,1024]{1,0:T(8,128)(2,1)S(1)}, bf16[160,1024]{1,0:T(8,128)(2,1)S(1)}, u32[]{:S(2)}, u32[]{:S(2)}) collective-permute-start(bf16[160,1024]{1,0:T(8,128)(2,1)S(1)} %collective-permute-done.1), channel_id=1, source_target_pairs={{0,1},{1,2},{2,3},{3,4},{4,5},{5,6},{6,7},{7,0},{16,23},{17,16},{1... | collective-permute-start | bytes 983048 | tf_op jit(solution)/shard_map/ppermute | solution.py:177
  31.7 13.6 %collective-permute-start.6 = (bf16[160,1024]{1,0:T(8,128)(2,1)S(1)}, bf16[160,1024]{1,0:T(8,128)(2,1)S(1)}, u32[]{:S(2)}, u32[]{:S(2)}) collective-permute-start(bf16[160,1024]{1,0:T(8,128)(2,1)S(1)} %collective-permute-done.4), channel_id=1, source_target_pairs={{0,1},{1,2},{2,3},{3,4},{4,5},{5,6},{6,7},{7,0},{16,23},{17,16},{1... | collective-permute-start | bytes 983048 | tf_op jit(solution)/shard_map/ppermute | solution.py:178
  36.8 12.0 %collective-permute-start.7 = (bf16[160,1024]{1,0:T(8,128)(2,1)S(1)}, bf16[160,1024]{1,0:T(8,128)(2,1)S(1)}, u32[]{:S(2)}, u32[]{:S(2)}) collective-permute-start(bf16[160,1024]{1,0:T(8,128)(2,1)S(1)} %collective-permute-done.5), channel_id=1, source_target_pairs={{0,1},{1,2},{2,3},{3,4},{4,5},{5,6},{6,7},{7,0},{16,23},{17,16},{1... | collective-permute-start | bytes 983048 | tf_op jit(solution)/shard_map/ppermute | solution.py:177
  45.3 10.2 %collective-permute-start.8 = (bf16[160,1024]{1,0:T(8,128)(2,1)S(1)}, bf16[160,1024]{1,0:T(8,128)(2,1)S(1)}, u32[]{:S(2)}, u32[]{:S(2)}) collective-permute-start(bf16[160,1024]{1,0:T(8,128)(2,1)S(1)} %collective-permute-done.6), channel_id=1, source_target_pairs={{0,1},{1,2},{2,3},{3,4},{4,5},{5,6},{6,7},{7,0},{16,23},{17,16},{1... | collective-permute-start | bytes 983048 | tf_op jit(solution)/shard_map/ppermute | solution.py:178
  55.5 14.3 %collective-permute-start.10 = (bf16[160,1024]{1,0:T(8,128)(2,1)S(1)}, bf16[160,1024]{1,0:T(8,128)(2,1)S(1)}, u32[]{:S(2)}, u32[]{:S(2)}) collective-permute-start(bf16[160,1024]{1,0:T(8,128)(2,1)S(1)} %collective-permute-done.8), channel_id=1, source_target_pairs={{0,1},{1,2},{2,3},{3,4},{4,5},{5,6},{6,7},{7,0},{16,23},{17,16},{1... | collective-permute-start | bytes 983048 | tf_op jit(solution)/shard_map/ppermute | solution.py:178
  57.4 11.8 %collective-permute-start.9 = (bf16[160,1024]{1,0:T(8,128)(2,1)S(1)}, bf16[160,1024]{1,0:T(8,128)(2,1)S(1)}, u32[]{:S(2)}, u32[]{:S(2)}) collective-permute-start(bf16[160,1024]{1,0:T(8,128)(2,1)S(1)} %collective-permute-done.7), channel_id=1, source_target_pairs={{0,1},{1,2},{2,3},{3,4},{4,5},{5,6},{6,7},{7,0},{16,23},{17,16},{1... | collective-permute-start | bytes 983048 | tf_op jit(solution)/shard_map/ppermute | solution.py:177
  109.4 13.0 %all-to-all-start.2 = ((f32[4,40,320]{2,1,0:T(8,128)}), f32[4,40,320]{2,1,0:T(8,128)S(1)}, u32[]{:S(2)}, u32[]{:S(2)}) async-start(f32[4,40,320]{2,1,0:T(8,128)} %broadcast_in_dim.36), calls=%async_computation.2 | async-start | bytes 491520 | tf_op jit(solution)/shard_map/all_to_all | solution.py:24
  112.9 14.2 %collective-permute-start.11 = (f32[40,320]{1,0:T(8,128)S(1)}, f32[40,320]{1,0:T(8,128)S(1)}, u32[]{:S(2)}, u32[]{:S(2)}) collective-permute-start(f32[40,320]{1,0:T(8,128)S(1)} %pad_maximum_fusion.2), channel_id=1, source_target_pairs={{0,7},{1,32},{2,65},{3,98},{4,131},{5,164},{6,197},{7,230},{8,15},... | collective-permute-start | bytes 153608 | tf_op jit(solution)/shard_map/ppermute | solution.py:208
  123.5 16.8 %all-to-all-start.3 = ((f32[4,40,1280]{2,1,0:T(8,128)}), f32[4,40,1280]{2,1,0:T(8,128)S(1)}, u32[]{:S(2)}, u32[]{:S(2)}) async-start(f32[4,40,1280]{2,1,0:T(8,128)} %broadcast_in_dim.37), calls=%async_computation.3 | async-start | bytes 1638400 | tf_op jit(solution)/shard_map/all_to_all | solution.py:24
  127.1 6.1 %collective-permute-start.12 = (f32[40,320]{1,0:T(8,128)S(1)}, f32[40,320]{1,0:T(8,128)S(1)}, u32[]{:S(2)}, u32[]{:S(2)}) collective-permute-start(f32[40,320]{1,0:T(8,128)S(1)} %collective-permute-done.11), channel_id=1, source_target_pairs={{0,8},{8,0},{1,9},{9,1},{2,10},{10,2},{3,11},{11,3},{4,12},{12,4},... | collective-permute-start | bytes 153608 | tf_op jit(solution)/shard_map/ppermute | solution.py:20

commit v11 on v10

--- a/solution.py
+++ b/solution.py
@@ -160,26 +160,42 @@
     order_all = rows * 16
     low = yl == 0
 
+    first = [(z, (z + 1) % 8) for z in range(8)] + [(8 + z, 8 + z) for z in range(8)]
+    later = [(z, (z + 1) % 8) for z in range(8)] + [(8 + z, 8 + (z + 7) % 8) for z in range(8)]
+    here, there = [lax.ppermute(entering, ("c", "z"), first)], []
+    swapped, entering, leaving = lax.optimization_barrier(
+        (shift(entering, "c", 2, 1), entering, leaving)
+    )
+    there.append(lax.ppermute(swapped, ("c", "z"), first))
     pair = jnp.concatenate([entering, leaving], 0)
     other = shift(pair, "yl", 2, 1)
-    first = jnp.where(low, pair, other)
-    second = jnp.where(low, other, pair)
-    columns = jnp.concatenate([first[:rows], second[:rows], first[rows:], second[rows:]], 0)
-
+    here[0], there[0] = lax.optimization_barrier((here[0], there[0]))
+    here.append(lax.ppermute(here[0], ("c", "z"), later))
+    there.append(lax.ppermute(there[0], ("c", "z"), later))
+    here[1], there[1], other = lax.optimization_barrier((here[1], there[1], other))
+    columns = jnp.concatenate(
+        [
+            jnp.where(low, pair[:rows], other[:rows]),
+            jnp.where(low, other[:rows], pair[:rows]),
+            jnp.where(low, pair[rows:], other[rows:]),
+            jnp.where(low, other[rows:], pair[rows:]),
+        ],
+        0,
+    )
     columns_there = shift(columns, "c", 2, 1)
-    first = [(z, (z + 1) % 8) for z in range(8)] + [(8 + z, 8 + z) for z in range(8)]
-    later = [(z, (z + 1) % 8) for z in range(8)] + [(8 + z, 8 + (z + 7) % 8) for z in range(8)]
-    here, there = entering, shift(entering, "c", 2, 1)
+    here.append(lax.ppermute(here[1], ("c", "z"), later))
+    there.append(lax.ppermute(there[1], ("c", "z"), later))
+    here[2], there[2], columns_there = lax.optimization_barrier(
+        (here[2], there[2], columns_there)
+    )
+    here.append(lax.ppermute(here[2], ("c", "z"), later))
+    there.append(lax.ppermute(there[2], ("c", "z"), later))
     partial = jnp.zeros((4, rows, 4 * rows), jnp.float32)
     for step in range(4):
-        if step == 3:
-            here, columns_there = lax.optimization_barrier((here, columns_there))
-        here = lax.ppermute(here, ("c", "z"), later if step else first)
-        there = lax.ppermute(there, ("c", "z"), later if step else first)
         product = lax.dot_general(
-            here, columns, (((1,), (1,)), ((), ())), preferred_element_type=jnp.float32
+            here[step], columns, (((1,), (1,)), ((), ())), preferred_element_type=jnp.float32
         ) + lax.dot_general(
-            there, columns_there, (((1,), (1,)), ((), ())), preferred_element_type=jnp.float32
+            there[step], columns_there, (((1,), (1,)), ((), ())), preferred_element_type=jnp.float32
         )
         partial = lax.dynamic_update_index_in_dim(partial, product, step, 0)
     partial = jnp.sum(lax.all_to_all(partial, "x", 0, 0), 0)

time: 195 us -> 192 us (0.985)
  waiting for transfers between devices: 40.2 us -> 31.2 us
  blocking collectives: 84.3 us -> 91.9 us
  local copies, waits for them, and re-layouts: 4.69 us -> 2.5 us
  other arithmetic: 1.37 us -> 3.56 us
    ppermute x4, waiting for transfers between devices: 13.1 us -> 2.91 us  [shift(): lax.ppermute(array, axis, [(i, (i + step) % size) for i in range(size)])]
    all_to_all x1, blocking collectives: 18.2 us -> 25 us  [body(): partial = jnp.sum(lax.all_to_all(partial, 'x', 0, 0), 0)]
    ppermute x1, starting transfers between devices: 5.52 us -> 1.91 us  [body(): cross_own = lax.ppermute(cross_own, ALL, tile_moves())]
    all_to_all x1, blocking collectives: 18.8 us -> 20.9 us  [body(): own = lax.all_to_all(jnp.stack(packed), ('yh', 'yl'), 0, 0)]
  transfers between devices with their start and end apart: 15 -> 15, of which waited for: 9 -> 9; matrix products, arithmetic and copies ran while one was open for 3% -> 4% of each run, Pallas kernels for 0% -> 0%
where the time goes in v11:
time: 192 us; the launch traced here: 191 us
  blocking collectives  91.9 us (48%)
  starting transfers between devices  50.6 us (26%)
  waiting for transfers between devices  31.2 us (16%)
  Pallas kernels  6.09 us (3%)
  matrix products  4.64 us (2%)
  other arithmetic  3.56 us (2%)
  local copies, waits for them, and re-layouts  2.5 us (1%)
    all_to_all x2, blocking collectives, body(): got = lax.all_to_all(sent, FEAT, 0, 0)  40.9 us
    all_to_all x1, blocking collectives, body(): partial = jnp.sum(lax.all_to_all(partial, 'x', 0, 0), 0)  25 us
    all_to_all x1, blocking collectives, body(): own = lax.all_to_all(jnp.stack(packed), ('yh', 'yl'), 0, 0)  20.9 us
    all_to_all x2, waiting for transfers between devices, spread(): lax.all_to_all(jnp.broadcast_to(array[None], (count,) + array.shape), axe...  10.7 us
    ppermute x4, starting transfers between devices, shift(): lax.ppermute(array, axis, [(i, (i + step) % size) for i in range(size)])  9.31 us
    all_to_all x2, starting transfers between devices, spread(): lax.all_to_all(jnp.broadcast_to(array[None], (count,) + array.shape), axe...  6.89 us
    ppermute x1, starting transfers between devices, body(): here.append(lax.ppermute(here[0], ('c', 'z'), later))  5.37 us
    all_to_all x1, blocking collectives, spread(): lax.all_to_all(jnp.broadcast_to(array[None], (count,) + array.shape), axe...  5.05 us
  transfers between devices with their start and end apart: 15, of which 9 were waited for; matrix products, arithmetic and copies ran while one was open for 4% of the time, Pallas kernels for 0%

profile of v11, /device:TPU:72, one launch (start us, length us, event | category | flops | bytes accessed | tf_op | source)
XLA Modules:
  0.0 190.9 jit_solution(5967072591556401799)
XLA Ops:
  1.9 4.3 %collective-permute-start = (bf16[160,1024]{1,0:T(8,128)(2,1)}, bf16[160,1024]{1,0:T(8,128)(2,1)S(1)}, u32[]{:S(2)}, u32[]{:S(2)}) collective-permute-start(bf16[160,1024]{1,0:T(8,128)(2,1)} %param.2), channel_id=1, source_target_pairs={{0,1},{1,2},{2,3},{3,4},{4,5},{5,6},{6,7},{7,0},{16,16},{17,17},{1... | collective-permute-start | bytes 983048 | tf_op jit(solution)/shard_map/ppermute | solution.py:165
  6.2 4.3 %collective-permute-start.2 = (bf16[160,1024]{1,0:T(8,128)(2,1)S(1)}, bf16[160,1024]{1,0:T(8,128)(2,1)S(1)}, u32[]{:S(2)}, u32[]{:S(2)}) collective-permute-start(bf16[160,1024]{1,0:T(8,128)(2,1)S(1)} %collective-permute-done.1), channel_id=1, source_target_pairs={{0,1},{1,2},{2,3},{3,4},{4,5},{5,6},{6,7},{7,0},{16,16},{17,17},{1... | collective-permute-start | bytes 983048 | tf_op jit(solution)/shard_map/ppermute | solution.py:169
  15.2 5.4 %collective-permute-start.3 = (bf16[160,1024]{1,0:T(8,128)(2,1)S(1)}, bf16[160,1024]{1,0:T(8,128)(2,1)S(1)}, u32[]{:S(2)}, u32[]{:S(2)}) collective-permute-start(bf16[160,1024]{1,0:T(8,128)(2,1)S(1)} %collective-permute-done), channel_id=1, source_target_pairs={{0,1},{1,2},{2,3},{3,4},{4,5},{5,6},{6,7},{7,0},{16,23},{17,16},{1... | collective-permute-start | bytes 983048 | tf_op jit(solution)/shard_map/ppermute | solution.py:173
  20.6 4.4 %collective-permute-start.4 = (bf16[160,1024]{1,0:T(8,128)(2,1)S(1)}, bf16[160,1024]{1,0:T(8,128)(2,1)S(1)}, u32[]{:S(2)}, u32[]{:S(2)}) collective-permute-start(bf16[160,1024]{1,0:T(8,128)(2,1)S(1)} %collective-permute-done.2), channel_id=1, source_target_pairs={{0,1},{1,2},{2,3},{3,4},{4,5},{5,6},{6,7},{7,0},{16,23},{17,16},{1... | collective-permute-start | bytes 983048 | tf_op jit(solution)/shard_map/ppermute | solution.py:174
  25.0 3.3 %collective-permute-done.3 = bf16[160,1024]{1,0:T(8,128)(2,1)S(1)} collective-permute-done((bf16[160,1024]{1,0:T(8,128)(2,1)S(1)}, bf16[160,1024]{1,0:T(8,128)(2,1)S(1)}, u32[]{:S(2)}, u32[]{:S(2)}) %collective-permute-start.3) | collective-permute-done | bytes 327712 | tf_op jit(solution)/shard_map/ppermute | solution.py:173
  28.2 3.5 %collective-permute-done.4 = bf16[160,1024]{1,0:T(8,128)(2,1)S(1)} collective-permute-done((bf16[160,1024]{1,0:T(8,128)(2,1)S(1)}, bf16[160,1024]{1,0:T(8,128)(2,1)S(1)}, u32[]{:S(2)}, u32[]{:S(2)}) %collective-permute-start.4) | collective-permute-done | bytes 327712 | tf_op jit(solution)/shard_map/ppermute | solution.py:174
  34.9 2.7 %collective-permute-start.6 = (bf16[160,1024]{1,0:T(8,128)(2,1)S(1)}, bf16[160,1024]{1,0:T(8,128)(2,1)S(1)}, u32[]{:S(2)}, u32[]{:S(2)}) collective-permute-start(bf16[160,1024]{1,0:T(8,128)(2,1)S(1)} %collective-permute-done.3), channel_id=1, source_target_pairs={{0,1},{1,2},{2,3},{3,4},{4,5},{5,6},{6,7},{7,0},{16,23},{17,16},{1... | collective-permute-start | bytes 983048 | tf_op jit(solution)/shard_map/ppermute | solution.py:186
  37.7 4.4 %collective-permute-start.7 = (bf16[160,1024]{1,0:T(8,128)(2,1)S(1)}, bf16[160,1024]{1,0:T(8,128)(2,1)S(1)}, u32[]{:S(2)}, u32[]{:S(2)}) collective-permute-start(bf16[160,1024]{1,0:T(8,128)(2,1)S(1)} %collective-permute-done.4), channel_id=1, source_target_pairs={{0,1},{1,2},{2,3},{3,4},{4,5},{5,6},{6,7},{7,0},{16,23},{17,16},{1... | collective-permute-start | bytes 983048 | tf_op jit(solution)/shard_map/ppermute | solution.py:187
  42.1 3.1 %collective-permute-done.6 = bf16[160,1024]{1,0:T(8,128)(2,1)S(1)} collective-permute-done((bf16[160,1024]{1,0:T(8,128)(2,1)S(1)}, bf16[160,1024]{1,0:T(8,128)(2,1)S(1)}, u32[]{:S(2)}, u32[]{:S(2)}) %collective-permute-start.6) | collective-permute-done | bytes 327712 | tf_op jit(solution)/shard_map/ppermute | solution.py:186
  45.1 3.5 %collective-permute-done.7 = bf16[160,1024]{1,0:T(8,128)(2,1)S(1)} collective-permute-done((bf16[160,1024]{1,0:T(8,128)(2,1)S(1)}, bf16[160,1024]{1,0:T(8,128)(2,1)S(1)}, u32[]{:S(2)}, u32[]{:S(2)}) %collective-permute-start.7) | collective-permute-done | bytes 327712 | tf_op jit(solution)/shard_map/ppermute | solution.py:187
  48.6 2.7 %collective-permute-start.10 = (bf16[160,1024]{1,0:T(8,128)(2,1)S(1)}, bf16[160,1024]{1,0:T(8,128)(2,1)S(1)}, u32[]{:S(2)}, u32[]{:S(2)}) collective-permute-start(bf16[160,1024]{1,0:T(8,128)(2,1)S(1)} %collective-permute-done.7), channel_id=1, source_target_pairs={{0,1},{1,2},{2,3},{3,4},{4,5},{5,6},{6,7},{7,0},{16,23},{17,16},{1... | collective-permute-start | bytes 983048 | tf_op jit(solution)/shard_map/ppermute | solution.py:192
  53.7 4.4 %collective-permute-start.9 = (bf16[160,1024]{1,0:T(8,128)(2,1)S(1)}, bf16[160,1024]{1,0:T(8,128)(2,1)S(1)}, u32[]{:S(2)}, u32[]{:S(2)}) collective-permute-start(bf16[160,1024]{1,0:T(8,128)(2,1)S(1)} %collective-permute-done.6), channel_id=1, source_target_pairs={{0,1},{1,2},{2,3},{3,4},{4,5},{5,6},{6,7},{7,0},{16,23},{17,16},{1... | collective-permute-start | bytes 983048 | tf_op jit(solution)/shard_map/ppermute | solution.py:191
  60.0 3.1 %collective-permute-done.9 = bf16[160,1024]{1,0:T(8,128)(2,1)S(1)} collective-permute-done((bf16[160,1024]{1,0:T(8,128)(2,1)S(1)}, bf16[160,1024]{1,0:T(8,128)(2,1)S(1)}, u32[]{:S(2)}, u32[]{:S(2)}) %collective-permute-start.9) | collective-permute-done | bytes 327712 | tf_op jit(solution)/shard_map/ppermute | solution.py:191
  63.7 25.0 %all_to_all.35 = f32[4,160,640]{2,1,0:T(8,128)S(1)} all-to-all(f32[4,160,640]{2,1,0:T(8,128)S(1)} %fusion.1), channel_id=1, replica_groups=mesh['yh'=4,'x'=4,'c'=2,'yl'=2,'z'=8] {'x'}, dimensions={0} | all-to-all | bytes 3276800 | tf_op jit(solution)/shard_map/all_to_all | solution.py:201
  89.8 20.9 %all_to_all.36 = f32[8,40,320]{2,1,0:T(8,128)S(1)} all-to-all(f32[8,40,320]{2,1,0:T(8,128)S(1)} %fusion.14), channel_id=1, replica_groups=mesh['yh'=4,'x'=4,'c'=2,'yl'=2,'z'=8] {'yh','yl'}, dimensions={0} | all-to-all | bytes 819200 | tf_op jit(solution)/shard_map/all_to_all | solution.py:220
  111.6 3.4 %all-to-all-start.2 = ((f32[4,40,320]{2,1,0:T(8,128)}), f32[4,40,320]{2,1,0:T(8,128)S(1)}, u32[]{:S(2)}, u32[]{:S(2)}) async-start(f32[4,40,320]{2,1,0:T(8,128)} %broadcast_in_dim.36), calls=%async_computation.2 | async-start | bytes 491520 | tf_op jit(solution)/shard_map/all_to_all | solution.py:24
  117.0 7.4 %all-to-all-done.2 = f32[4,40,320]{2,1,0:T(8,128)S(1)} async-done(((f32[4,40,320]{2,1,0:T(8,128)}), f32[4,40,320]{2,1,0:T(8,128)S(1)}, u32[]{:S(2)}, u32[]{:S(2)}) %all-to-all-start.2) | async-done | bytes 204832 | tf_op jit(solution)/shard_map/all_to_all | solution.py:24
  125.5 3.5 %all-to-all-start.3 = ((f32[4,40,1280]{2,1,0:T(8,128)}), f32[4,40,1280]{2,1,0:T(8,128)S(1)}, u32[]{:S(2)}, u32[]{:S(2)}) async-start(f32[4,40,1280]{2,1,0:T(8,128)} %broadcast_in_dim.37), calls=%async_computation.3 | async-start | bytes 1638400 | tf_op jit(solution)/shard_map/all_to_all | solution.py:24
  129.1 3.1 %collective-permute-start.12 = (f32[40,320]{1,0:T(8,128)S(1)}, f32[40,320]{1,0:T(8,128)S(1)}, u32[]{:S(2)}, u32[]{:S(2)}) collective-permute-start(f32[40,320]{1,0:T(8,128)S(1)} %collective-permute-done.11), channel_id=1, source_target_pairs={{0,8},{8,0},{1,9},{9,1},{2,10},{10,2},{3,11},{11,3},{4,12},{12,4},... | collective-permute-start | bytes 153608 | tf_op jit(solution)/shard_map/ppermute | solution.py:20
  132.3 2.9 %collective-permute-done.12 = f32[40,320]{1,0:T(8,128)S(1)} collective-permute-done((f32[40,320]{1,0:T(8,128)S(1)}, f32[40,320]{1,0:T(8,128)S(1)}, u32[]{:S(2)}, u32[]{:S(2)}) %collective-permute-start.12) | collective-permute-done | bytes 51232 | tf_op jit(solution)/shard_map/ppermute | solution.py:20
  135.4 3.3 %all-to-all-done.3 = f32[4,40,1280]{2,1,0:T(8,128)S(1)} async-done(((f32[4,40,1280]{2,1,0:T(8,128)}), f32[4,40,1280]{2,1,0:T(8,128)S(1)}, u32[]{:S(2)}, u32[]{:S(2)}) %all-to-all-start.3) | async-done | bytes 819232 | tf_op jit(solution)/shard_map/all_to_all | solution.py:24
  138.8 5.0 %all_to_all.37 = f32[2,4,40,1280]{3,2,1,0:T(8,128)S(1)} all-to-all(f32[2,4,40,1280]{3,2,1,0:T(8,128)S(1)} %broadcast_in_dim.38), channel_id=1, replica_groups=mesh['yh'=4,'x'=4,'c'=2,'yl'=2,'z'=8] {'c'}, dimensions={0} | all-to-all | bytes 3276800 | tf_op jit(solution)/shard_map/all_to_all | solution.py:24
  145.6 21.2 %all_to_all.38.got = bf16[16,40,384]{2,1,0:T(8,128)(2,1)S(1)} all-to-all(bf16[16,40,384]{2,1,0:T(8,128)(2,1)S(1)} %get-tuple-element.34), channel_id=1, replica_groups=mesh['yh'=4,'x'=4,'c'=2,'yl'=2,'z'=8] {'yl','z'}, dimensions={0} | all-to-all | bytes 983040 | tf_op jit(solution)/shard_map/all_to_all | solution.py:253
  168.6 19.8 %all_to_all.39.got = bf16[16,40,384]{2,1,0:T(8,128)(2,1)S(1)} all-to-all(bf16[16,40,384]{2,1,0:T(8,128)(2,1)S(1)} %get-tuple-element.37), channel_id=1, replica_groups=mesh['yh'=4,'x'=4,'c'=2,'yl'=2,'z'=8] {'yl','z'}, dimensions={0} | all-to-all | bytes 983040 | tf_op jit(solution)/shard_map/all_to_all | solution.py:262
  (50 shorter events, 26.1 us)
Async XLA Ops:
  0.0 6.2 %collective-permute-start.1 = (bf16[160,1024]{1,0:T(8,128)(2,1)}, bf16[160,1024]{1,0:T(8,128)(2,1)S(1)}, u32[]{:S(2)}, u32[]{:S(2)}) collective-permute-start(bf16[160,1024]{1,0:T(8,128)(2,1)} %param.2), channel_id=1, source_target_pairs={{0,16},{16,0},{1,17},{17,1},{2,18},{18,2},{3,19},{19,3},{4,20},{20... | collective-permute-start | bytes 983048 | tf_op jit(solution)/shard_map/ppermute | solution.py:20
  1.9 12.1 %collective-permute-start = (bf16[160,1024]{1,0:T(8,128)(2,1)}, bf16[160,1024]{1,0:T(8,128)(2,1)S(1)}, u32[]{:S(2)}, u32[]{:S(2)}) collective-permute-start(bf16[160,1024]{1,0:T(8,128)(2,1)} %param.2), channel_id=1, source_target_pairs={{0,1},{1,2},{2,3},{3,4},{4,5},{5,6},{6,7},{7,0},{16,16},{17,17},{1... | collective-permute-start | bytes 983048 | tf_op jit(solution)/shard_map/ppermute | solution.py:165
  6.2 9.0 %collective-permute-start.2 = (bf16[160,1024]{1,0:T(8,128)(2,1)S(1)}, bf16[160,1024]{1,0:T(8,128)(2,1)S(1)}, u32[]{:S(2)}, u32[]{:S(2)}) collective-permute-start(bf16[160,1024]{1,0:T(8,128)(2,1)S(1)} %collective-permute-done.1), channel_id=1, source_target_pairs={{0,1},{1,2},{2,3},{3,4},{4,5},{5,6},{6,7},{7,0},{16,16},{17,17},{1... | collective-permute-start | bytes 983048 | tf_op jit(solution)/shard_map/ppermute | solution.py:169
  11.6 13.3 %collective-permute-start.5 = (bf16[320,1024]{1,0:T(8,128)(2,1)S(1)}, bf16[320,1024]{1,0:T(8,128)(2,1)S(1)}, u32[]{:S(2)}, u32[]{:S(2)}) collective-permute-start(bf16[320,1024]{1,0:T(8,128)(2,1)S(1)} %pad_maximum_fusion.1), channel_id=1, source_target_pairs={{0,8},{8,0},{1,9},{9,1},{2,10},{10,2},{3,11},{11,3},{4,12},{12,4},... | collective-permute-start | bytes 1966088 | tf_op jit(solution)/shard_map/ppermute | solution.py:20
  15.2 13.0 %collective-permute-start.3 = (bf16[160,1024]{1,0:T(8,128)(2,1)S(1)}, bf16[160,1024]{1,0:T(8,128)(2,1)S(1)}, u32[]{:S(2)}, u32[]{:S(2)}) collective-permute-start(bf16[160,1024]{1,0:T(8,128)(2,1)S(1)} %collective-permute-done), channel_id=1, source_target_pairs={{0,1},{1,2},{2,3},{3,4},{4,5},{5,6},{6,7},{7,0},{16,23},{17,16},{1... | collective-permute-start | bytes 983048 | tf_op jit(solution)/shard_map/ppermute | solution.py:173
  20.6 11.2 %collective-permute-start.4 = (bf16[160,1024]{1,0:T(8,128)(2,1)S(1)}, bf16[160,1024]{1,0:T(8,128)(2,1)S(1)}, u32[]{:S(2)}, u32[]{:S(2)}) collective-permute-start(bf16[160,1024]{1,0:T(8,128)(2,1)S(1)} %collective-permute-done.2), channel_id=1, source_target_pairs={{0,1},{1,2},{2,3},{3,4},{4,5},{5,6},{6,7},{7,0},{16,23},{17,16},{1... | collective-permute-start | bytes 983048 | tf_op jit(solution)/shard_map/ppermute | solution.py:174
  33.0 15.6 %collective-permute-start.8 = (bf16[640,1024]{1,0:T(8,128)(2,1)S(1)}, bf16[640,1024]{1,0:T(8,128)(2,1)S(1)}, u32[]{:S(2)}, u32[]{:S(2)}) collective-permute-start(bf16[640,1024]{1,0:T(8,128)(2,1)S(1)} %pad_maximum_fusion), channel_id=1, source_target_pairs={{0,16},{16,0},{1,17},{17,1},{2,18},{18,2},{3,19},{19,3},{4,20},{20... | collective-permute-start | bytes 3932168 | tf_op jit(solution)/shard_map/ppermute | solution.py:20
  34.9 10.2 %collective-permute-start.6 = (bf16[160,1024]{1,0:T(8,128)(2,1)S(1)}, bf16[160,1024]{1,0:T(8,128)(2,1)S(1)}, u32[]{:S(2)}, u32[]{:S(2)}) collective-permute-start(bf16[160,1024]{1,0:T(8,128)(2,1)S(1)} %collective-permute-done.3), channel_id=1, source_target_pairs={{0,1},{1,2},{2,3},{3,4},{4,5},{5,6},{6,7},{7,0},{16,23},{17,16},{1... | collective-permute-start | bytes 983048 | tf_op jit(solution)/shard_map/ppermute | solution.py:186
  37.7 11.0 %collective-permute-start.7 = (bf16[160,1024]{1,0:T(8,128)(2,1)S(1)}, bf16[160,1024]{1,0:T(8,128)(2,1)S(1)}, u32[]{:S(2)}, u32[]{:S(2)}) collective-permute-start(bf16[160,1024]{1,0:T(8,128)(2,1)S(1)} %collective-permute-done.4), channel_id=1, source_target_pairs={{0,1},{1,2},{2,3},{3,4},{4,5},{5,6},{6,7},{7,0},{16,23},{17,16},{1... | collective-permute-start | bytes 983048 | tf_op jit(solution)/shard_map/ppermute | solution.py:187
  48.6 10.7 %collective-permute-start.10 = (bf16[160,1024]{1,0:T(8,128)(2,1)S(1)}, bf16[160,1024]{1,0:T(8,128)(2,1)S(1)}, u32[]{:S(2)}, u32[]{:S(2)}) collective-permute-start(bf16[160,1024]{1,0:T(8,128)(2,1)S(1)} %collective-permute-done.7), channel_id=1, source_target_pairs={{0,1},{1,2},{2,3},{3,4},{4,5},{5,6},{6,7},{7,0},{16,23},{17,16},{1... | collective-permute-start | bytes 983048 | tf_op jit(solution)/shard_map/ppermute | solution.py:192
  53.7 9.4 %collective-permute-start.9 = (bf16[160,1024]{1,0:T(8,128)(2,1)S(1)}, bf16[160,1024]{1,0:T(8,128)(2,1)S(1)}, u32[]{:S(2)}, u32[]{:S(2)}) collective-permute-start(bf16[160,1024]{1,0:T(8,128)(2,1)S(1)} %collective-permute-done.6), channel_id=1, source_target_pairs={{0,1},{1,2},{2,3},{3,4},{4,5},{5,6},{6,7},{7,0},{16,23},{17,16},{1... | collective-permute-start | bytes 983048 | tf_op jit(solution)/shard_map/ppermute | solution.py:191
  111.6 12.8 %all-to-all-start.2 = ((f32[4,40,320]{2,1,0:T(8,128)}), f32[4,40,320]{2,1,0:T(8,128)S(1)}, u32[]{:S(2)}, u32[]{:S(2)}) async-start(f32[4,40,320]{2,1,0:T(8,128)} %broadcast_in_dim.36), calls=%async_computation.2 | async-start | bytes 491520 | tf_op jit(solution)/shard_map/all_to_all | solution.py:24
  115.1 14.0 %collective-permute-start.11 = (f32[40,320]{1,0:T(8,128)S(1)}, f32[40,320]{1,0:T(8,128)S(1)}, u32[]{:S(2)}, u32[]{:S(2)}) collective-permute-start(f32[40,320]{1,0:T(8,128)S(1)} %pad_maximum_fusion.3), channel_id=1, source_target_pairs={{0,7},{1,32},{2,65},{3,98},{4,131},{5,164},{6,197},{7,230},{8,15},... | collective-permute-start | bytes 153608 | tf_op jit(solution)/shard_map/ppermute | solution.py:224
  125.5 13.1 %all-to-all-start.3 = ((f32[4,40,1280]{2,1,0:T(8,128)}), f32[4,40,1280]{2,1,0:T(8,128)S(1)}, u32[]{:S(2)}, u32[]{:S(2)}) async-start(f32[4,40,1280]{2,1,0:T(8,128)} %broadcast_in_dim.37), calls=%async_computation.3 | async-start | bytes 1638400 | tf_op jit(solution)/shard_map/all_to_all | solution.py:24
  129.1 6.1 %collective-permute-start.12 = (f32[40,320]{1,0:T(8,128)S(1)}, f32[40,320]{1,0:T(8,128)S(1)}, u32[]{:S(2)}, u32[]{:S(2)}) collective-permute-start(f32[40,320]{1,0:T(8,128)S(1)} %collective-permute-done.11), channel_id=1, source_target_pairs={{0,8},{8,0},{1,9},{9,1},{2,10},{10,2},{3,11},{11,3},{4,12},{12,4},... | collective-permute-start | bytes 153608 | tf_op jit(solution)/shard_map/ppermute | solution.py:20

commit v12 on v11

--- a/solution.py
+++ b/solution.py
@@ -162,17 +162,14 @@
 
     first = [(z, (z + 1) % 8) for z in range(8)] + [(8 + z, 8 + z) for z in range(8)]
     later = [(z, (z + 1) % 8) for z in range(8)] + [(8 + z, 8 + (z + 7) % 8) for z in range(8)]
-    here, there = [lax.ppermute(entering, ("c", "z"), first)], []
     swapped, entering, leaving = lax.optimization_barrier(
         (shift(entering, "c", 2, 1), entering, leaving)
     )
-    there.append(lax.ppermute(swapped, ("c", "z"), first))
+    chain = [lax.ppermute(jnp.stack([entering, swapped]), ("c", "z"), first)]
     pair = jnp.concatenate([entering, leaving], 0)
     other = shift(pair, "yl", 2, 1)
-    here[0], there[0] = lax.optimization_barrier((here[0], there[0]))
-    here.append(lax.ppermute(here[0], ("c", "z"), later))
-    there.append(lax.ppermute(there[0], ("c", "z"), later))
-    here[1], there[1], other = lax.optimization_barrier((here[1], there[1], other))
+    chain.append(lax.ppermute(chain[0], ("c", "z"), later))
+    chain[1], other = lax.optimization_barrier((chain[1], other))
     columns = jnp.concatenate(
         [
             jnp.where(low, pair[:rows], other[:rows]),
@@ -183,19 +180,16 @@
         0,
     )
     columns_there = shift(columns, "c", 2, 1)
-    here.append(lax.ppermute(here[1], ("c", "z"), later))
-    there.append(lax.ppermute(there[1], ("c", "z"), later))
-    here[2], there[2], columns_there = lax.optimization_barrier(
-        (here[2], there[2], columns_there)
-    )
-    here.append(lax.ppermute(here[2], ("c", "z"), later))
-    there.append(lax.ppermute(there[2], ("c", "z"), later))
+    chain.append(lax.ppermute(chain[1], ("c", "z"), later))
+    chain[2], columns_there = lax.optimization_barrier((chain[2], columns_there))
+    chain.append(lax.ppermute(chain[2], ("c", "z"), later))
     partial = jnp.zeros((4, rows, 4 * rows), jnp.float32)
     for step in range(4):
+        here, there = chain[step][0], chain[step][1]
         product = lax.dot_general(
-            here[step], columns, (((1,), (1,)), ((), ())), preferred_element_type=jnp.float32
+            here, columns, (((1,), (1,)), ((), ())), preferred_element_type=jnp.float32
         ) + lax.dot_general(
-            there[step], columns_there, (((1,), (1,)), ((), ())), preferred_element_type=jnp.float32
+            there, columns_there, (((1,), (1,)), ((), ())), preferred_element_type=jnp.float32
         )
         partial = lax.dynamic_update_index_in_dim(partial, product, step, 0)
     partial = jnp.sum(lax.all_to_all(partial, "x", 0, 0), 0)

time: 192 us -> 195 us (1.016)
  waiting for transfers between devices: 31.2 us -> 53.3 us
  starting transfers between devices: 50.6 us -> 33.1 us
    ppermute x8 -> x4, starting transfers between devices: 32.5 us -> 12.4 us  [the longest x1 4.28 us: body(): chain = [lax.ppermute(jnp.stack([entering, swapped]), ('c', 'z'), first)]]
    ppermute x8 -> x4, waiting for transfers between devices: 17.6 us -> 36.4 us  [the longest x1 11.2 us: body(): chain.append(lax.ppermute(chain[1], ('c', 'z'), later))]
    ppermute x4, waiting for transfers between devices: 2.91 us -> 7.51 us  [shift(): lax.ppermute(array, axis, [(i, (i + step) % size) for i in range(size)])]
    all_to_all x2, blocking collectives: 40.9 us -> 45.3 us  [body(): got = lax.all_to_all(sent, FEAT, 0, 0)]
    ppermute x1, starting transfers between devices: 1.91 us -> 4.46 us  [body(): cross_own = lax.ppermute(cross_own, ALL, tile_moves())]
    all_to_all x1, blocking collectives: 20.9 us -> 18.5 us  [body(): own = lax.all_to_all(jnp.stack(packed), ('yh', 'yl'), 0, 0)]
    all_to_all x1, blocking collectives: 25 us -> 22.8 us  [body(): partial = jnp.sum(lax.all_to_all(partial, 'x', 0, 0), 0)]
  transfers between devices with their start and end apart: 15 -> 11, of which waited for: 9 -> 9; matrix products, arithmetic and copies ran while one was open for 4% -> 2% of each run, Pallas kernels for 0% -> 0%
where the time goes in v12:
time: 195 us; the launch traced here: 194 us
  blocking collectives  91.6 us (47%)
  waiting for transfers between devices  53.3 us (27%)
  starting transfers between devices  33.1 us (17%)
  Pallas kernels  6.09 us (3%)
  matrix products  4.63 us (2%)
  local copies, waits for them, and re-layouts  2.5 us (1%)
  other arithmetic  2.45 us (1%)
    all_to_all x2, blocking collectives, body(): got = lax.all_to_all(sent, FEAT, 0, 0)  45.3 us
    all_to_all x1, blocking collectives, body(): partial = jnp.sum(lax.all_to_all(partial, 'x', 0, 0), 0)  22.8 us
    all_to_all x1, blocking collectives, body(): own = lax.all_to_all(jnp.stack(packed), ('yh', 'yl'), 0, 0)  18.5 us
    ppermute x1, waiting for transfers between devices, body(): chain.append(lax.ppermute(chain[1], ('c', 'z'), later))  11.2 us
    ppermute x1, waiting for transfers between devices, body(): chain.append(lax.ppermute(chain[0], ('c', 'z'), later))  10.2 us
    all_to_all x2, waiting for transfers between devices, spread(): lax.all_to_all(jnp.broadcast_to(array[None], (count,) + array.shape), axe...  9.39 us
    ppermute x4, starting transfers between devices, shift(): lax.ppermute(array, axis, [(i, (i + step) % size) for i in range(size)])  9.33 us
    ppermute x1, waiting for transfers between devices, body(): chain.append(lax.ppermute(chain[2], ('c', 'z'), later))  9.28 us
  transfers between devices with their start and end apart: 11, of which 9 were waited for; matrix products, arithmetic and copies ran while one was open for 2% of the time, Pallas kernels for 0%

profile of v12, /device:TPU:72, one launch (start us, length us, event | category | flops | bytes accessed | tf_op | source)
XLA Modules:
  0.0 194.0 jit_solution(8016726952771282193)
XLA Ops:
  0.0 2.0 %collective-permute-start = (bf16[160,1024]{1,0:T(8,128)(2,1)}, bf16[160,1024]{1,0:T(8,128)(2,1)S(1)}, u32[]{:S(2)}, u32[]{:S(2)}) collective-permute-start(bf16[160,1024]{1,0:T(8,128)(2,1)} %param.2), channel_id=1, source_target_pairs={{0,16},{16,0},{1,17},{17,1},{2,18},{18,2},{3,19},{19,3},{4,20},{20... | collective-permute-start | bytes 983048 | tf_op jit(solution)/shard_map/ppermute | solution.py:20
  4.9 4.3 %collective-permute-start.1 = (bf16[2,160,1024]{2,1,0:T(8,128)(2,1)S(1)}, bf16[2,160,1024]{2,1,0:T(8,128)(2,1)S(1)}, u32[]{:S(2)}, u32[]{:S(2)}) collective-permute-start(bf16[2,160,1024]{2,1,0:T(8,128)(2,1)S(1)} %pad_maximum_fusion.1), channel_id=1, source_target_pairs={{0,1},{1,2},{2,3},{3,4},{4,5},{5,6},{6,7},{7,0},{16,16},{17,17},{1... | collective-permute-start | bytes 1966088 | tf_op jit(solution)/shard_map/ppermute | solution.py:168
  9.3 2.4 %collective-permute-start.3 = (bf16[320,1024]{1,0:T(8,128)(2,1)S(1)}, bf16[320,1024]{1,0:T(8,128)(2,1)S(1)}, u32[]{:S(2)}, u32[]{:S(2)}) collective-permute-start(bf16[320,1024]{1,0:T(8,128)(2,1)S(1)} %pad_maximum_fusion.2), channel_id=1, source_target_pairs={{0,8},{8,0},{1,9},{9,1},{2,10},{10,2},{3,11},{11,3},{4,12},{12,4},... | collective-permute-start | bytes 1966088 | tf_op jit(solution)/shard_map/ppermute | solution.py:20
  11.6 5.8 %collective-permute-done.1 = bf16[2,160,1024]{2,1,0:T(8,128)(2,1)S(1)} collective-permute-done((bf16[2,160,1024]{2,1,0:T(8,128)(2,1)S(1)}, bf16[2,160,1024]{2,1,0:T(8,128)(2,1)S(1)}, u32[]{:S(2)}, u32[]{:S(2)}) %collective-permute-start.1) | collective-permute-done | bytes 655392 | tf_op jit(solution)/shard_map/ppermute | solution.py:168
  17.4 4.3 %collective-permute-start.2 = (bf16[2,160,1024]{2,1,0:T(8,128)(2,1)S(1)}, bf16[2,160,1024]{2,1,0:T(8,128)(2,1)S(1)}, u32[]{:S(2)}, u32[]{:S(2)}) collective-permute-start(bf16[2,160,1024]{2,1,0:T(8,128)(2,1)S(1)} %collective-permute-done.1), channel_id=1, source_target_pairs={{0,1},{1,2},{2,3},{3,4},{4,5},{5,6},{6,7},{7,0},{16,23},{17,16},{1... | collective-permute-start | bytes 1966088 | tf_op jit(solution)/shard_map/ppermute | solution.py:171
  21.7 2.7 %collective-permute-done.3 = bf16[320,1024]{1,0:T(8,128)(2,1)S(1)} collective-permute-done((bf16[320,1024]{1,0:T(8,128)(2,1)S(1)}, bf16[320,1024]{1,0:T(8,128)(2,1)S(1)}, u32[]{:S(2)}, u32[]{:S(2)}) %collective-permute-start.3) | collective-permute-done | bytes 655392 | tf_op jit(solution)/shard_map/ppermute | solution.py:20
  24.3 10.2 %collective-permute-done.2 = bf16[2,160,1024]{2,1,0:T(8,128)(2,1)S(1)} collective-permute-done((bf16[2,160,1024]{2,1,0:T(8,128)(2,1)S(1)}, bf16[2,160,1024]{2,1,0:T(8,128)(2,1)S(1)}, u32[]{:S(2)}, u32[]{:S(2)}) %collective-permute-start.2) | collective-permute-done | bytes 655392 | tf_op jit(solution)/shard_map/ppermute | solution.py:171
  34.7 1.9 collective-permute-start.5
  36.6 1.9 collective-permute-start.4
  39.1 11.2 %collective-permute-done.4 = bf16[2,160,1024]{2,1,0:T(8,128)(2,1)S(1)} collective-permute-done((bf16[2,160,1024]{2,1,0:T(8,128)(2,1)S(1)}, bf16[2,160,1024]{2,1,0:T(8,128)(2,1)S(1)}, u32[]{:S(2)}, u32[]{:S(2)}) %collective-permute-start.4) | collective-permute-done | bytes 655392 | tf_op jit(solution)/shard_map/ppermute | solution.py:183
  55.3 9.3 %collective-permute-done.6 = bf16[2,160,1024]{2,1,0:T(8,128)(2,1)S(1)} collective-permute-done((bf16[2,160,1024]{2,1,0:T(8,128)(2,1)S(1)}, bf16[2,160,1024]{2,1,0:T(8,128)(2,1)S(1)}, u32[]{:S(2)}, u32[]{:S(2)}) %collective-permute-start.6) | collective-permute-done | bytes 655392 | tf_op jit(solution)/shard_map/ppermute | solution.py:185
  65.8 22.8 %all_to_all.35 = f32[4,160,640]{2,1,0:T(8,128)S(1)} all-to-all(f32[4,160,640]{2,1,0:T(8,128)S(1)} %fusion.1), channel_id=1, replica_groups=mesh['yh'=4,'x'=4,'c'=2,'yl'=2,'z'=8] {'x'}, dimensions={0} | all-to-all | bytes 3276800 | tf_op jit(solution)/shard_map/all_to_all | solution.py:195
  89.7 18.5 %all_to_all.36 = f32[8,40,320]{2,1,0:T(8,128)S(1)} all-to-all(f32[8,40,320]{2,1,0:T(8,128)S(1)} %fusion.26), channel_id=1, replica_groups=mesh['yh'=4,'x'=4,'c'=2,'yl'=2,'z'=8] {'yh','yl'}, dimensions={0} | all-to-all | bytes 819200 | tf_op jit(solution)/shard_map/all_to_all | solution.py:214
  109.1 3.4 %all-to-all-start.2 = ((f32[4,40,320]{2,1,0:T(8,128)}), f32[4,40,320]{2,1,0:T(8,128)S(1)}, u32[]{:S(2)}, u32[]{:S(2)}) async-start(f32[4,40,320]{2,1,0:T(8,128)} %broadcast_in_dim.36), calls=%async_computation.2 | async-start | bytes 491520 | tf_op jit(solution)/shard_map/all_to_all | solution.py:24
  112.6 4.5 %collective-permute-start.7 = (f32[40,320]{1,0:T(8,128)S(1)}, f32[40,320]{1,0:T(8,128)S(1)}, u32[]{:S(2)}, u32[]{:S(2)}) collective-permute-start(f32[40,320]{1,0:T(8,128)S(1)} %pad_maximum_fusion.4), channel_id=1, source_target_pairs={{0,7},{1,32},{2,65},{3,98},{4,131},{5,164},{6,197},{7,230},{8,15},... | collective-permute-start | bytes 153608 | tf_op jit(solution)/shard_map/ppermute | solution.py:218
  117.1 5.1 %all-to-all-done.2 = f32[4,40,320]{2,1,0:T(8,128)S(1)} async-done(((f32[4,40,320]{2,1,0:T(8,128)}), f32[4,40,320]{2,1,0:T(8,128)S(1)}, u32[]{:S(2)}, u32[]{:S(2)}) %all-to-all-start.2) | async-done | bytes 204832 | tf_op jit(solution)/shard_map/all_to_all | solution.py:24
  123.2 3.5 %all-to-all-start.3 = ((f32[4,40,1280]{2,1,0:T(8,128)}), f32[4,40,1280]{2,1,0:T(8,128)S(1)}, u32[]{:S(2)}, u32[]{:S(2)}) async-start(f32[4,40,1280]{2,1,0:T(8,128)} %broadcast_in_dim.37), calls=%async_computation.3 | async-start | bytes 1638400 | tf_op jit(solution)/shard_map/all_to_all | solution.py:24
  126.8 3.0 %collective-permute-start.8 = (f32[40,320]{1,0:T(8,128)S(1)}, f32[40,320]{1,0:T(8,128)S(1)}, u32[]{:S(2)}, u32[]{:S(2)}) collective-permute-start(f32[40,320]{1,0:T(8,128)S(1)} %collective-permute-done.7), channel_id=1, source_target_pairs={{0,8},{8,0},{1,9},{9,1},{2,10},{10,2},{3,11},{11,3},{4,12},{12,4},... | collective-permute-start | bytes 153608 | tf_op jit(solution)/shard_map/ppermute | solution.py:20
  129.9 3.0 %collective-permute-done.8 = f32[40,320]{1,0:T(8,128)S(1)} collective-permute-done((f32[40,320]{1,0:T(8,128)S(1)}, f32[40,320]{1,0:T(8,128)S(1)}, u32[]{:S(2)}, u32[]{:S(2)}) %collective-permute-start.8) | collective-permute-done | bytes 51232 | tf_op jit(solution)/shard_map/ppermute | solution.py:20
  133.1 4.3 %all-to-all-done.3 = f32[4,40,1280]{2,1,0:T(8,128)S(1)} async-done(((f32[4,40,1280]{2,1,0:T(8,128)}), f32[4,40,1280]{2,1,0:T(8,128)S(1)}, u32[]{:S(2)}, u32[]{:S(2)}) %all-to-all-start.3) | async-done | bytes 819232 | tf_op jit(solution)/shard_map/all_to_all | solution.py:24
  137.6 5.0 %all_to_all.37 = f32[2,4,40,1280]{3,2,1,0:T(8,128)S(1)} all-to-all(f32[2,4,40,1280]{3,2,1,0:T(8,128)S(1)} %broadcast_in_dim.38), channel_id=1, replica_groups=mesh['yh'=4,'x'=4,'c'=2,'yl'=2,'z'=8] {'c'}, dimensions={0} | all-to-all | bytes 3276800 | tf_op jit(solution)/shard_map/all_to_all | solution.py:24
  144.4 25.5 %all_to_all.38.got = bf16[16,40,384]{2,1,0:T(8,128)(2,1)S(1)} all-to-all(bf16[16,40,384]{2,1,0:T(8,128)(2,1)S(1)} %get-tuple-element.26), channel_id=1, replica_groups=mesh['yh'=4,'x'=4,'c'=2,'yl'=2,'z'=8] {'yl','z'}, dimensions={0} | all-to-all | bytes 983040 | tf_op jit(solution)/shard_map/all_to_all | solution.py:247
  171.8 19.8 %all_to_all.39.got = bf16[16,40,384]{2,1,0:T(8,128)(2,1)S(1)} all-to-all(bf16[16,40,384]{2,1,0:T(8,128)(2,1)S(1)} %get-tuple-element.29), channel_id=1, replica_groups=mesh['yh'=4,'x'=4,'c'=2,'yl'=2,'z'=8] {'yl','z'}, dimensions={0} | all-to-all | bytes 983040 | tf_op jit(solution)/shard_map/all_to_all | solution.py:256
  191.5 2.5 %shard_map.30 = f32[160,80]{1,0:T(8,128)} custom-call(s32[2]{0:T(128)S(1)} %pad_add_fusion.place, bf16[16,40,384]{2,1,0:T(8,128)(2,1)S(1)} %all_to_all.39.got, bf16[2560,160]{1,0:T(8,128)(2,1)S(1)} %get-tuple-element.27.high, bf16[2560,160]{1,0:T(8,128)(2,1)S(1)} %get-tuple-element.28.low, f32[40,320]{1,0:T(8,128)S(1)} %fusion.27.target.target_in, ...), custom_call_target="tpu_custom_call" | custom-call | tf_op jit(solution)/shard_map/pallas_call | solution.py:257
  (47 shorter events, 16.9 us)
Async XLA Ops:
  0.0 9.2 %copy-start = (bf16[160,1024]{1,0:T(8,128)(2,1)S(1)}, bf16[160,1024]{1,0:T(8,128)(2,1)}, u32[]{:S(2)}) copy-start(bf16[160,1024]{1,0:T(8,128)(2,1)} %param.2) | copy-start | bytes 983044
  0.0 9.2 %copy-start.1 = (bf16[160,1024]{1,0:T(8,128)(2,1)S(1)}, bf16[160,1024]{1,0:T(8,128)(2,1)}, u32[]{:S(2)}) copy-start(bf16[160,1024]{1,0:T(8,128)(2,1)} %param.3) | copy-start | bytes 983044
  0.0 3.9 %collective-permute-start = (bf16[160,1024]{1,0:T(8,128)(2,1)}, bf16[160,1024]{1,0:T(8,128)(2,1)S(1)}, u32[]{:S(2)}, u32[]{:S(2)}) collective-permute-start(bf16[160,1024]{1,0:T(8,128)(2,1)} %param.2), channel_id=1, source_target_pairs={{0,16},{16,0},{1,17},{17,1},{2,18},{18,2},{3,19},{19,3},{4,20},{20... | collective-permute-start | bytes 983048 | tf_op jit(solution)/shard_map/ppermute | solution.py:20
  4.9 12.5 %collective-permute-start.1 = (bf16[2,160,1024]{2,1,0:T(8,128)(2,1)S(1)}, bf16[2,160,1024]{2,1,0:T(8,128)(2,1)S(1)}, u32[]{:S(2)}, u32[]{:S(2)}) collective-permute-start(bf16[2,160,1024]{2,1,0:T(8,128)(2,1)S(1)} %pad_maximum_fusion.1), channel_id=1, source_target_pairs={{0,1},{1,2},{2,3},{3,4},{4,5},{5,6},{6,7},{7,0},{16,16},{17,17},{1... | collective-permute-start | bytes 1966088 | tf_op jit(solution)/shard_map/ppermute | solution.py:168
  9.3 15.1 %collective-permute-start.3 = (bf16[320,1024]{1,0:T(8,128)(2,1)S(1)}, bf16[320,1024]{1,0:T(8,128)(2,1)S(1)}, u32[]{:S(2)}, u32[]{:S(2)}) collective-permute-start(bf16[320,1024]{1,0:T(8,128)(2,1)S(1)} %pad_maximum_fusion.2), channel_id=1, source_target_pairs={{0,8},{8,0},{1,9},{9,1},{2,10},{10,2},{3,11},{11,3},{4,12},{12,4},... | collective-permute-start | bytes 1966088 | tf_op jit(solution)/shard_map/ppermute | solution.py:20
  17.4 17.1 %collective-permute-start.2 = (bf16[2,160,1024]{2,1,0:T(8,128)(2,1)S(1)}, bf16[2,160,1024]{2,1,0:T(8,128)(2,1)S(1)}, u32[]{:S(2)}, u32[]{:S(2)}) collective-permute-start(bf16[2,160,1024]{2,1,0:T(8,128)(2,1)S(1)} %collective-permute-done.1), channel_id=1, source_target_pairs={{0,1},{1,2},{2,3},{3,4},{4,5},{5,6},{6,7},{7,0},{16,23},{17,16},{1... | collective-permute-start | bytes 1966088 | tf_op jit(solution)/shard_map/ppermute | solution.py:171
  34.7 15.6 %collective-permute-start.5 = (bf16[640,1024]{1,0:T(8,128)(2,1)S(1)}, bf16[640,1024]{1,0:T(8,128)(2,1)S(1)}, u32[]{:S(2)}, u32[]{:S(2)}) collective-permute-start(bf16[640,1024]{1,0:T(8,128)(2,1)S(1)} %pad_maximum_fusion), channel_id=1, source_target_pairs={{0,16},{16,0},{1,17},{17,1},{2,18},{18,2},{3,19},{19,3},{4,20},{20... | collective-permute-start | bytes 3932168 | tf_op jit(solution)/shard_map/ppermute | solution.py:20
  36.6 13.7 %collective-permute-start.4 = (bf16[2,160,1024]{2,1,0:T(8,128)(2,1)S(1)}, bf16[2,160,1024]{2,1,0:T(8,128)(2,1)S(1)}, u32[]{:S(2)}, u32[]{:S(2)}) collective-permute-start(bf16[2,160,1024]{2,1,0:T(8,128)(2,1)S(1)} %collective-permute-done.2), channel_id=1, source_target_pairs={{0,1},{1,2},{2,3},{3,4},{4,5},{5,6},{6,7},{7,0},{16,23},{17,16},{1... | collective-permute-start | bytes 1966088 | tf_op jit(solution)/shard_map/ppermute | solution.py:183
  50.9 13.7 %collective-permute-start.6 = (bf16[2,160,1024]{2,1,0:T(8,128)(2,1)S(1)}, bf16[2,160,1024]{2,1,0:T(8,128)(2,1)S(1)}, u32[]{:S(2)}, u32[]{:S(2)}) collective-permute-start(bf16[2,160,1024]{2,1,0:T(8,128)(2,1)S(1)} %collective-permute-done.4), channel_id=1, source_target_pairs={{0,1},{1,2},{2,3},{3,4},{4,5},{5,6},{6,7},{7,0},{16,23},{17,16},{1... | collective-permute-start | bytes 1966088 | tf_op jit(solution)/shard_map/ppermute | solution.py:185
  109.1 13.0 %all-to-all-start.2 = ((f32[4,40,320]{2,1,0:T(8,128)}), f32[4,40,320]{2,1,0:T(8,128)S(1)}, u32[]{:S(2)}, u32[]{:S(2)}) async-start(f32[4,40,320]{2,1,0:T(8,128)} %broadcast_in_dim.36), calls=%async_computation.2 | async-start | bytes 491520 | tf_op jit(solution)/shard_map/all_to_all | solution.py:24
  112.6 14.2 %collective-permute-start.7 = (f32[40,320]{1,0:T(8,128)S(1)}, f32[40,320]{1,0:T(8,128)S(1)}, u32[]{:S(2)}, u32[]{:S(2)}) collective-permute-start(f32[40,320]{1,0:T(8,128)S(1)} %pad_maximum_fusion.4), channel_id=1, source_target_pairs={{0,7},{1,32},{2,65},{3,98},{4,131},{5,164},{6,197},{7,230},{8,15},... | collective-permute-start | bytes 153608 | tf_op jit(solution)/shard_map/ppermute | solution.py:218
  123.2 14.2 %all-to-all-start.3 = ((f32[4,40,1280]{2,1,0:T(8,128)}), f32[4,40,1280]{2,1,0:T(8,128)S(1)}, u32[]{:S(2)}, u32[]{:S(2)}) async-start(f32[4,40,1280]{2,1,0:T(8,128)} %broadcast_in_dim.37), calls=%async_computation.3 | async-start | bytes 1638400 | tf_op jit(solution)/shard_map/all_to_all | solution.py:24
  126.8 6.1 %collective-permute-start.8 = (f32[40,320]{1,0:T(8,128)S(1)}, f32[40,320]{1,0:T(8,128)S(1)}, u32[]{:S(2)}, u32[]{:S(2)}) collective-permute-start(f32[40,320]{1,0:T(8,128)S(1)} %collective-permute-done.7), channel_id=1, source_target_pairs={{0,8},{8,0},{1,9},{9,1},{2,10},{10,2},{3,11},{11,3},{4,12},{12,4},... | collective-permute-start | bytes 153608 | tf_op jit(solution)/shard_map/ppermute | solution.py:20

commit v13 on v11

--- a/solution.py
+++ b/solution.py
@@ -185,9 +185,7 @@
     columns_there = shift(columns, "c", 2, 1)
     here.append(lax.ppermute(here[1], ("c", "z"), later))
     there.append(lax.ppermute(there[1], ("c", "z"), later))
-    here[2], there[2], columns_there = lax.optimization_barrier(
-        (here[2], there[2], columns_there)
-    )
+    here[2], columns_there = lax.optimization_barrier((here[2], columns_there))
     here.append(lax.ppermute(here[2], ("c", "z"), later))
     there.append(lax.ppermute(there[2], ("c", "z"), later))
     partial = jnp.zeros((4, rows, 4 * rows), jnp.float32)

time: 192 us -> 189 us (0.984)
    all_to_all x2, blocking collectives: 40.9 us -> 44.6 us  [body(): got = lax.all_to_all(sent, FEAT, 0, 0)]
    ppermute x1, waiting for transfers between devices: 3.1 us -> 5.58 us  [body(): here.append(lax.ppermute(here[2], ('c', 'z'), later))]
    all_to_all x1, blocking collectives: 20.9 us -> 18.8 us  [body(): own = lax.all_to_all(jnp.stack(packed), ('yh', 'yl'), 0, 0)]
where the time goes in v13:
time: 189 us; the launch traced here: 188 us
  blocking collectives  91.8 us (49%)
  starting transfers between devices  49.6 us (26%)
  waiting for transfers between devices  30.7 us (16%)
  Pallas kernels  6.09 us (3%)
  matrix products  4.62 us (2%)
  local copies, waits for them, and re-layouts  2.51 us (1%)
  other arithmetic  2.49 us (1%)
    all_to_all x2, blocking collectives, body(): got = lax.all_to_all(sent, FEAT, 0, 0)  44.6 us
    all_to_all x1, blocking collectives, body(): partial = jnp.sum(lax.all_to_all(partial, 'x', 0, 0), 0)  23.4 us
    all_to_all x1, blocking collectives, body(): own = lax.all_to_all(jnp.stack(packed), ('yh', 'yl'), 0, 0)  18.8 us
    all_to_all x2, waiting for transfers between devices, spread(): lax.all_to_all(jnp.broadcast_to(array[None], (count,) + array.shape), axe...  9.49 us
    ppermute x4, starting transfers between devices, shift(): lax.ppermute(array, axis, [(i, (i + step) % size) for i in range(size)])  9.33 us
    all_to_all x2, starting transfers between devices, spread(): lax.all_to_all(jnp.broadcast_to(array[None], (count,) + array.shape), axe...  6.89 us
    ppermute x1, waiting for transfers between devices, body(): here.append(lax.ppermute(here[2], ('c', 'z'), later))  5.58 us
    ppermute x1, starting transfers between devices, body(): here.append(lax.ppermute(here[0], ('c', 'z'), later))  5.37 us
  transfers between devices with their start and end apart: 15, of which 9 were waited for; matrix products, arithmetic and copies ran while one was open for 4% of the time, Pallas kernels for 0%

profile of v13, /device:TPU:72, one launch (start us, length us, event | category | flops | bytes accessed | tf_op | source)
XLA Modules:
  0.0 188.2 jit_solution(9051185239814344464)
XLA Ops:
  2.1 4.3 %collective-permute-start = (bf16[160,1024]{1,0:T(8,128)(2,1)}, bf16[160,1024]{1,0:T(8,128)(2,1)S(1)}, u32[]{:S(2)}, u32[]{:S(2)}) collective-permute-start(bf16[160,1024]{1,0:T(8,128)(2,1)} %param.2), channel_id=1, source_target_pairs={{0,1},{1,2},{2,3},{3,4},{4,5},{5,6},{6,7},{7,0},{16,16},{17,17},{1... | collective-permute-start | bytes 983048 | tf_op jit(solution)/shard_map/ppermute | solution.py:165
  6.4 4.3 %collective-permute-start.2 = (bf16[160,1024]{1,0:T(8,128)(2,1)S(1)}, bf16[160,1024]{1,0:T(8,128)(2,1)S(1)}, u32[]{:S(2)}, u32[]{:S(2)}) collective-permute-start(bf16[160,1024]{1,0:T(8,128)(2,1)S(1)} %collective-permute-done.1), channel_id=1, source_target_pairs={{0,1},{1,2},{2,3},{3,4},{4,5},{5,6},{6,7},{7,0},{16,16},{17,17},{1... | collective-permute-start | bytes 983048 | tf_op jit(solution)/shard_map/ppermute | solution.py:169
  15.3 5.4 %collective-permute-start.3 = (bf16[160,1024]{1,0:T(8,128)(2,1)S(1)}, bf16[160,1024]{1,0:T(8,128)(2,1)S(1)}, u32[]{:S(2)}, u32[]{:S(2)}) collective-permute-start(bf16[160,1024]{1,0:T(8,128)(2,1)S(1)} %collective-permute-done), channel_id=1, source_target_pairs={{0,1},{1,2},{2,3},{3,4},{4,5},{5,6},{6,7},{7,0},{16,23},{17,16},{1... | collective-permute-start | bytes 983048 | tf_op jit(solution)/shard_map/ppermute | solution.py:173
  20.7 4.4 %collective-permute-start.4 = (bf16[160,1024]{1,0:T(8,128)(2,1)S(1)}, bf16[160,1024]{1,0:T(8,128)(2,1)S(1)}, u32[]{:S(2)}, u32[]{:S(2)}) collective-permute-start(bf16[160,1024]{1,0:T(8,128)(2,1)S(1)} %collective-permute-done.2), channel_id=1, source_target_pairs={{0,1},{1,2},{2,3},{3,4},{4,5},{5,6},{6,7},{7,0},{16,23},{17,16},{1... | collective-permute-start | bytes 983048 | tf_op jit(solution)/shard_map/ppermute | solution.py:174
  25.1 3.3 %collective-permute-done.3 = bf16[160,1024]{1,0:T(8,128)(2,1)S(1)} collective-permute-done((bf16[160,1024]{1,0:T(8,128)(2,1)S(1)}, bf16[160,1024]{1,0:T(8,128)(2,1)S(1)}, u32[]{:S(2)}, u32[]{:S(2)}) %collective-permute-start.3) | collective-permute-done | bytes 327712 | tf_op jit(solution)/shard_map/ppermute | solution.py:173
  28.4 3.5 %collective-permute-done.4 = bf16[160,1024]{1,0:T(8,128)(2,1)S(1)} collective-permute-done((bf16[160,1024]{1,0:T(8,128)(2,1)S(1)}, bf16[160,1024]{1,0:T(8,128)(2,1)S(1)}, u32[]{:S(2)}, u32[]{:S(2)}) %collective-permute-start.4) | collective-permute-done | bytes 327712 | tf_op jit(solution)/shard_map/ppermute | solution.py:174
  34.0 2.7 %collective-permute-start.8 = (bf16[160,1024]{1,0:T(8,128)(2,1)S(1)}, bf16[160,1024]{1,0:T(8,128)(2,1)S(1)}, u32[]{:S(2)}, u32[]{:S(2)}) collective-permute-start(bf16[160,1024]{1,0:T(8,128)(2,1)S(1)} %collective-permute-done.4), channel_id=1, source_target_pairs={{0,1},{1,2},{2,3},{3,4},{4,5},{5,6},{6,7},{7,0},{16,23},{17,16},{1... | collective-permute-start | bytes 983048 | tf_op jit(solution)/shard_map/ppermute | solution.py:187
  36.7 4.4 %collective-permute-start.6 = (bf16[160,1024]{1,0:T(8,128)(2,1)S(1)}, bf16[160,1024]{1,0:T(8,128)(2,1)S(1)}, u32[]{:S(2)}, u32[]{:S(2)}) collective-permute-start(bf16[160,1024]{1,0:T(8,128)(2,1)S(1)} %collective-permute-done.3), channel_id=1, source_target_pairs={{0,1},{1,2},{2,3},{3,4},{4,5},{5,6},{6,7},{7,0},{16,23},{17,16},{1... | collective-permute-start | bytes 983048 | tf_op jit(solution)/shard_map/ppermute | solution.py:186
  41.1 3.1 %collective-permute-done.8 = bf16[160,1024]{1,0:T(8,128)(2,1)S(1)} collective-permute-done((bf16[160,1024]{1,0:T(8,128)(2,1)S(1)}, bf16[160,1024]{1,0:T(8,128)(2,1)S(1)}, u32[]{:S(2)}, u32[]{:S(2)}) %collective-permute-start.8) | collective-permute-done | bytes 327712 | tf_op jit(solution)/shard_map/ppermute | solution.py:187
  49.5 2.7 %collective-permute-start.9 = (bf16[160,1024]{1,0:T(8,128)(2,1)S(1)}, bf16[160,1024]{1,0:T(8,128)(2,1)S(1)}, u32[]{:S(2)}, u32[]{:S(2)}) collective-permute-start(bf16[160,1024]{1,0:T(8,128)(2,1)S(1)} %collective-permute-done.6), channel_id=1, source_target_pairs={{0,1},{1,2},{2,3},{3,4},{4,5},{5,6},{6,7},{7,0},{16,23},{17,16},{1... | collective-permute-start | bytes 983048 | tf_op jit(solution)/shard_map/ppermute | solution.py:189
  54.1 5.6 %collective-permute-done.9 = bf16[160,1024]{1,0:T(8,128)(2,1)S(1)} collective-permute-done((bf16[160,1024]{1,0:T(8,128)(2,1)S(1)}, bf16[160,1024]{1,0:T(8,128)(2,1)S(1)}, u32[]{:S(2)}, u32[]{:S(2)}) %collective-permute-start.9) | collective-permute-done | bytes 327712 | tf_op jit(solution)/shard_map/ppermute | solution.py:189
  60.8 23.4 %all_to_all.35 = f32[4,160,640]{2,1,0:T(8,128)S(1)} all-to-all(f32[4,160,640]{2,1,0:T(8,128)S(1)} %fusion.1), channel_id=1, replica_groups=mesh['yh'=4,'x'=4,'c'=2,'yl'=2,'z'=8] {'x'}, dimensions={0} | all-to-all | bytes 3276800 | tf_op jit(solution)/shard_map/all_to_all | solution.py:199
  85.4 18.8 %all_to_all.36 = f32[8,40,320]{2,1,0:T(8,128)S(1)} all-to-all(f32[8,40,320]{2,1,0:T(8,128)S(1)} %fusion.14), channel_id=1, replica_groups=mesh['yh'=4,'x'=4,'c'=2,'yl'=2,'z'=8] {'yh','yl'}, dimensions={0} | all-to-all | bytes 819200 | tf_op jit(solution)/shard_map/all_to_all | solution.py:218
  105.1 3.4 %all-to-all-start.2 = ((f32[4,40,320]{2,1,0:T(8,128)}), f32[4,40,320]{2,1,0:T(8,128)S(1)}, u32[]{:S(2)}, u32[]{:S(2)}) async-start(f32[4,40,320]{2,1,0:T(8,128)} %broadcast_in_dim.36), calls=%async_computation.2 | async-start | bytes 491520 | tf_op jit(solution)/shard_map/all_to_all | solution.py:24
  108.5 3.3 %collective-permute-start.11 = (f32[40,320]{1,0:T(8,128)S(1)}, f32[40,320]{1,0:T(8,128)S(1)}, u32[]{:S(2)}, u32[]{:S(2)}) collective-permute-start(f32[40,320]{1,0:T(8,128)S(1)} %pad_maximum_fusion.3), channel_id=1, source_target_pairs={{0,7},{1,32},{2,65},{3,98},{4,131},{5,164},{6,197},{7,230},{8,15},... | collective-permute-start | bytes 153608 | tf_op jit(solution)/shard_map/ppermute | solution.py:222
  111.8 6.2 %all-to-all-done.2 = f32[4,40,320]{2,1,0:T(8,128)S(1)} async-done(((f32[4,40,320]{2,1,0:T(8,128)}), f32[4,40,320]{2,1,0:T(8,128)S(1)}, u32[]{:S(2)}, u32[]{:S(2)}) %all-to-all-start.2) | async-done | bytes 204832 | tf_op jit(solution)/shard_map/all_to_all | solution.py:24
  119.2 3.5 %all-to-all-start.3 = ((f32[4,40,1280]{2,1,0:T(8,128)}), f32[4,40,1280]{2,1,0:T(8,128)S(1)}, u32[]{:S(2)}, u32[]{:S(2)}) async-start(f32[4,40,1280]{2,1,0:T(8,128)} %broadcast_in_dim.37), calls=%async_computation.3 | async-start | bytes 1638400 | tf_op jit(solution)/shard_map/all_to_all | solution.py:24
  122.7 3.0 %collective-permute-start.12 = (f32[40,320]{1,0:T(8,128)S(1)}, f32[40,320]{1,0:T(8,128)S(1)}, u32[]{:S(2)}, u32[]{:S(2)}) collective-permute-start(f32[40,320]{1,0:T(8,128)S(1)} %collective-permute-done.11), channel_id=1, source_target_pairs={{0,8},{8,0},{1,9},{9,1},{2,10},{10,2},{3,11},{11,3},{4,12},{12,4},... | collective-permute-start | bytes 153608 | tf_op jit(solution)/shard_map/ppermute | solution.py:20
  125.8 3.0 %collective-permute-done.12 = f32[40,320]{1,0:T(8,128)S(1)} collective-permute-done((f32[40,320]{1,0:T(8,128)S(1)}, f32[40,320]{1,0:T(8,128)S(1)}, u32[]{:S(2)}, u32[]{:S(2)}) %collective-permute-start.12) | collective-permute-done | bytes 51232 | tf_op jit(solution)/shard_map/ppermute | solution.py:20
  129.0 3.3 %all-to-all-done.3 = f32[4,40,1280]{2,1,0:T(8,128)S(1)} async-done(((f32[4,40,1280]{2,1,0:T(8,128)}), f32[4,40,1280]{2,1,0:T(8,128)S(1)}, u32[]{:S(2)}, u32[]{:S(2)}) %all-to-all-start.3) | async-done | bytes 819232 | tf_op jit(solution)/shard_map/all_to_all | solution.py:24
  132.4 5.0 %all_to_all.37 = f32[2,4,40,1280]{3,2,1,0:T(8,128)S(1)} all-to-all(f32[2,4,40,1280]{3,2,1,0:T(8,128)S(1)} %broadcast_in_dim.38), channel_id=1, replica_groups=mesh['yh'=4,'x'=4,'c'=2,'yl'=2,'z'=8] {'c'}, dimensions={0} | all-to-all | bytes 3276800 | tf_op jit(solution)/shard_map/all_to_all | solution.py:24
  139.2 24.8 %all_to_all.38.got = bf16[16,40,384]{2,1,0:T(8,128)(2,1)S(1)} all-to-all(bf16[16,40,384]{2,1,0:T(8,128)(2,1)S(1)} %get-tuple-element.32), channel_id=1, replica_groups=mesh['yh'=4,'x'=4,'c'=2,'yl'=2,'z'=8] {'yl','z'}, dimensions={0} | all-to-all | bytes 983040 | tf_op jit(solution)/shard_map/all_to_all | solution.py:251
  165.9 19.8 %all_to_all.39.got = bf16[16,40,384]{2,1,0:T(8,128)(2,1)S(1)} all-to-all(bf16[16,40,384]{2,1,0:T(8,128)(2,1)S(1)} %get-tuple-element.35), channel_id=1, replica_groups=mesh['yh'=4,'x'=4,'c'=2,'yl'=2,'z'=8] {'yl','z'}, dimensions={0} | all-to-all | bytes 983040 | tf_op jit(solution)/shard_map/all_to_all | solution.py:260
  185.7 2.5 %shard_map.30 = f32[160,80]{1,0:T(8,128)} custom-call(s32[2]{0:T(128)S(1)} %pad_add_fusion.place, bf16[16,40,384]{2,1,0:T(8,128)(2,1)S(1)} %all_to_all.39.got, bf16[2560,160]{1,0:T(8,128)(2,1)S(1)} %get-tuple-element.33.high, bf16[2560,160]{1,0:T(8,128)(2,1)S(1)} %get-tuple-element.34.low, f32[40,320]{1,0:T(8,128)S(1)} %fusion.15.target.target_in, ...), custom_call_target="tpu_custom_call" | custom-call | tf_op jit(solution)/shard_map/pallas_call | solution.py:261
  (54 shorter events, 24.2 us)
Async XLA Ops:
  0.0 31.9 %copy-start = (bf16[160,1024]{1,0:T(8,128)(2,1)S(1)}, bf16[160,1024]{1,0:T(8,128)(2,1)}, u32[]{:S(2)}) copy-start(bf16[160,1024]{1,0:T(8,128)(2,1)} %param.2) | copy-start | bytes 983044
  0.0 31.9 %copy-start.1 = (bf16[160,1024]{1,0:T(8,128)(2,1)S(1)}, bf16[160,1024]{1,0:T(8,128)(2,1)}, u32[]{:S(2)}) copy-start(bf16[160,1024]{1,0:T(8,128)(2,1)} %param.3) | copy-start | bytes 983044
  0.0 6.3 %collective-permute-start.1 = (bf16[160,1024]{1,0:T(8,128)(2,1)}, bf16[160,1024]{1,0:T(8,128)(2,1)S(1)}, u32[]{:S(2)}, u32[]{:S(2)}) collective-permute-start(bf16[160,1024]{1,0:T(8,128)(2,1)} %param.2), channel_id=1, source_target_pairs={{0,16},{16,0},{1,17},{17,1},{2,18},{18,2},{3,19},{19,3},{4,20},{20... | collective-permute-start | bytes 983048 | tf_op jit(solution)/shard_map/ppermute | solution.py:20
  2.1 12.1 %collective-permute-start = (bf16[160,1024]{1,0:T(8,128)(2,1)}, bf16[160,1024]{1,0:T(8,128)(2,1)S(1)}, u32[]{:S(2)}, u32[]{:S(2)}) collective-permute-start(bf16[160,1024]{1,0:T(8,128)(2,1)} %param.2), channel_id=1, source_target_pairs={{0,1},{1,2},{2,3},{3,4},{4,5},{5,6},{6,7},{7,0},{16,16},{17,17},{1... | collective-permute-start | bytes 983048 | tf_op jit(solution)/shard_map/ppermute | solution.py:165
  6.4 9.0 %collective-permute-start.2 = (bf16[160,1024]{1,0:T(8,128)(2,1)S(1)}, bf16[160,1024]{1,0:T(8,128)(2,1)S(1)}, u32[]{:S(2)}, u32[]{:S(2)}) collective-permute-start(bf16[160,1024]{1,0:T(8,128)(2,1)S(1)} %collective-permute-done.1), channel_id=1, source_target_pairs={{0,1},{1,2},{2,3},{3,4},{4,5},{5,6},{6,7},{7,0},{16,16},{17,17},{1... | collective-permute-start | bytes 983048 | tf_op jit(solution)/shard_map/ppermute | solution.py:169
  11.8 20.1 %collective-permute-start.5 = (bf16[320,1024]{1,0:T(8,128)(2,1)S(1)}, bf16[320,1024]{1,0:T(8,128)(2,1)S(1)}, u32[]{:S(2)}, u32[]{:S(2)}) collective-permute-start(bf16[320,1024]{1,0:T(8,128)(2,1)S(1)} %pad_maximum_fusion.1), channel_id=1, source_target_pairs={{0,8},{8,0},{1,9},{9,1},{2,10},{10,2},{3,11},{11,3},{4,12},{12,4},... | collective-permute-start | bytes 1966088 | tf_op jit(solution)/shard_map/ppermute | solution.py:20
  15.3 13.0 %collective-permute-start.3 = (bf16[160,1024]{1,0:T(8,128)(2,1)S(1)}, bf16[160,1024]{1,0:T(8,128)(2,1)S(1)}, u32[]{:S(2)}, u32[]{:S(2)}) collective-permute-start(bf16[160,1024]{1,0:T(8,128)(2,1)S(1)} %collective-permute-done), channel_id=1, source_target_pairs={{0,1},{1,2},{2,3},{3,4},{4,5},{5,6},{6,7},{7,0},{16,23},{17,16},{1... | collective-permute-start | bytes 983048 | tf_op jit(solution)/shard_map/ppermute | solution.py:173
  20.7 11.2 %collective-permute-start.4 = (bf16[160,1024]{1,0:T(8,128)(2,1)S(1)}, bf16[160,1024]{1,0:T(8,128)(2,1)S(1)}, u32[]{:S(2)}, u32[]{:S(2)}) collective-permute-start(bf16[160,1024]{1,0:T(8,128)(2,1)S(1)} %collective-permute-done.2), channel_id=1, source_target_pairs={{0,1},{1,2},{2,3},{3,4},{4,5},{5,6},{6,7},{7,0},{16,23},{17,16},{1... | collective-permute-start | bytes 983048 | tf_op jit(solution)/shard_map/ppermute | solution.py:174
  32.1 15.6 %collective-permute-start.7 = (bf16[640,1024]{1,0:T(8,128)(2,1)S(1)}, bf16[640,1024]{1,0:T(8,128)(2,1)S(1)}, u32[]{:S(2)}, u32[]{:S(2)}) collective-permute-start(bf16[640,1024]{1,0:T(8,128)(2,1)S(1)} %pad_maximum_fusion), channel_id=1, source_target_pairs={{0,16},{16,0},{1,17},{17,1},{2,18},{18,2},{3,19},{19,3},{4,20},{20... | collective-permute-start | bytes 3932168 | tf_op jit(solution)/shard_map/ppermute | solution.py:20
  34.0 10.2 %collective-permute-start.8 = (bf16[160,1024]{1,0:T(8,128)(2,1)S(1)}, bf16[160,1024]{1,0:T(8,128)(2,1)S(1)}, u32[]{:S(2)}, u32[]{:S(2)}) collective-permute-start(bf16[160,1024]{1,0:T(8,128)(2,1)S(1)} %collective-permute-done.4), channel_id=1, source_target_pairs={{0,1},{1,2},{2,3},{3,4},{4,5},{5,6},{6,7},{7,0},{16,23},{17,16},{1... | collective-permute-start | bytes 983048 | tf_op jit(solution)/shard_map/ppermute | solution.py:187
  36.7 11.0 %collective-permute-start.6 = (bf16[160,1024]{1,0:T(8,128)(2,1)S(1)}, bf16[160,1024]{1,0:T(8,128)(2,1)S(1)}, u32[]{:S(2)}, u32[]{:S(2)}) collective-permute-start(bf16[160,1024]{1,0:T(8,128)(2,1)S(1)} %collective-permute-done.3), channel_id=1, source_target_pairs={{0,1},{1,2},{2,3},{3,4},{4,5},{5,6},{6,7},{7,0},{16,23},{17,16},{1... | collective-permute-start | bytes 983048 | tf_op jit(solution)/shard_map/ppermute | solution.py:186
  44.2 16.0 %collective-permute-start.10 = (bf16[160,1024]{1,0:T(8,128)(2,1)S(1)}, bf16[160,1024]{1,0:T(8,128)(2,1)S(1)}, u32[]{:S(2)}, u32[]{:S(2)}) collective-permute-start(bf16[160,1024]{1,0:T(8,128)(2,1)S(1)} %collective-permute-done.8), channel_id=1, source_target_pairs={{0,1},{1,2},{2,3},{3,4},{4,5},{5,6},{6,7},{7,0},{16,23},{17,16},{1... | collective-permute-start | bytes 983048 | tf_op jit(solution)/shard_map/ppermute | solution.py:190
  49.5 10.2 %collective-permute-start.9 = (bf16[160,1024]{1,0:T(8,128)(2,1)S(1)}, bf16[160,1024]{1,0:T(8,128)(2,1)S(1)}, u32[]{:S(2)}, u32[]{:S(2)}) collective-permute-start(bf16[160,1024]{1,0:T(8,128)(2,1)S(1)} %collective-permute-done.6), channel_id=1, source_target_pairs={{0,1},{1,2},{2,3},{3,4},{4,5},{5,6},{6,7},{7,0},{16,23},{17,16},{1... | collective-permute-start | bytes 983048 | tf_op jit(solution)/shard_map/ppermute | solution.py:189
  105.1 13.0 %all-to-all-start.2 = ((f32[4,40,320]{2,1,0:T(8,128)}), f32[4,40,320]{2,1,0:T(8,128)S(1)}, u32[]{:S(2)}, u32[]{:S(2)}) async-start(f32[4,40,320]{2,1,0:T(8,128)} %broadcast_in_dim.36), calls=%async_computation.2 | async-start | bytes 491520 | tf_op jit(solution)/shard_map/all_to_all | solution.py:24
  108.5 14.2 %collective-permute-start.11 = (f32[40,320]{1,0:T(8,128)S(1)}, f32[40,320]{1,0:T(8,128)S(1)}, u32[]{:S(2)}, u32[]{:S(2)}) collective-permute-start(f32[40,320]{1,0:T(8,128)S(1)} %pad_maximum_fusion.3), channel_id=1, source_target_pairs={{0,7},{1,32},{2,65},{3,98},{4,131},{5,164},{6,197},{7,230},{8,15},... | collective-permute-start | bytes 153608 | tf_op jit(solution)/shard_map/ppermute | solution.py:222
  119.2 13.1 %all-to-all-start.3 = ((f32[4,40,1280]{2,1,0:T(8,128)}), f32[4,40,1280]{2,1,0:T(8,128)S(1)}, u32[]{:S(2)}, u32[]{:S(2)}) async-start(f32[4,40,1280]{2,1,0:T(8,128)} %broadcast_in_dim.37), calls=%async_computation.3 | async-start | bytes 1638400 | tf_op jit(solution)/shard_map/all_to_all | solution.py:24
  122.7 6.1 %collective-permute-start.12 = (f32[40,320]{1,0:T(8,128)S(1)}, f32[40,320]{1,0:T(8,128)S(1)}, u32[]{:S(2)}, u32[]{:S(2)}) collective-permute-start(f32[40,320]{1,0:T(8,128)S(1)} %collective-permute-done.11), channel_id=1, source_target_pairs={{0,8},{8,0},{1,9},{9,1},{2,10},{10,2},{3,11},{11,3},{4,12},{12,4},... | collective-permute-start | bytes 153608 | tf_op jit(solution)/shard_map/ppermute | solution.py:20

commit v14 on v13

--- a/solution.py
+++ b/solution.py
@@ -169,7 +169,6 @@
     there.append(lax.ppermute(swapped, ("c", "z"), first))
     pair = jnp.concatenate([entering, leaving], 0)
     other = shift(pair, "yl", 2, 1)
-    here[0], there[0] = lax.optimization_barrier((here[0], there[0]))
     here.append(lax.ppermute(here[0], ("c", "z"), later))
     there.append(lax.ppermute(there[0], ("c", "z"), later))
     here[1], there[1], other = lax.optimization_barrier((here[1], there[1], other))

time: 189 us -> 186 us (0.984)
  waiting for transfers between devices: 30.7 us -> 25.7 us
  transfers between devices with their start and end apart: 15 -> 15, of which waited for: 9 -> 8; matrix products, arithmetic and copies ran while one was open for 4% -> 4% of each run, Pallas kernels for 0% -> 0%
where the time goes in v14:
time: 186 us; the launch traced here: 185 us
  blocking collectives  93.2 us (50%)
  starting transfers between devices  49.8 us (27%)
  waiting for transfers between devices  25.7 us (14%)
  Pallas kernels  6.09 us (3%)
  matrix products  4.63 us (2%)
  local copies, waits for them, and re-layouts  2.51 us (1%)
  other arithmetic  2.49 us (1%)
    all_to_all x2, blocking collectives, body(): got = lax.all_to_all(sent, FEAT, 0, 0)  45.9 us
    all_to_all x1, blocking collectives, body(): partial = jnp.sum(lax.all_to_all(partial, 'x', 0, 0), 0)  23.4 us
    all_to_all x1, blocking collectives, body(): own = lax.all_to_all(jnp.stack(packed), ('yh', 'yl'), 0, 0)  18.8 us
    ppermute x4, starting transfers between devices, shift(): lax.ppermute(array, axis, [(i, (i + step) % size) for i in range(size)])  9.33 us
    all_to_all x2, waiting for transfers between devices, spread(): lax.all_to_all(jnp.broadcast_to(array[None], (count,) + array.shape), axe...  8.7 us
    all_to_all x2, starting transfers between devices, spread(): lax.all_to_all(jnp.broadcast_to(array[None], (count,) + array.shape), axe...  6.89 us
    ppermute x1, starting transfers between devices, body(): here.append(lax.ppermute(here[0], ('c', 'z'), later))  5.49 us
    all_to_all x1, blocking collectives, spread(): lax.all_to_all(jnp.broadcast_to(array[None], (count,) + array.shape), axe...  5.05 us
  transfers between devices with their start and end apart: 15, of which 8 were waited for; matrix products, arithmetic and copies ran while one was open for 4% of the time, Pallas kernels for 0%

profile of v14, /device:TPU:72, one launch (start us, length us, event | category | flops | bytes accessed | tf_op | source)
XLA Modules:
  0.0 184.8 jit_solution(15716909904952176099)
XLA Ops:
  2.1 4.3 %collective-permute-start.1 = (bf16[160,1024]{1,0:T(8,128)(2,1)}, bf16[160,1024]{1,0:T(8,128)(2,1)S(1)}, u32[]{:S(2)}, u32[]{:S(2)}) collective-permute-start(bf16[160,1024]{1,0:T(8,128)(2,1)} %param.2), channel_id=1, source_target_pairs={{0,1},{1,2},{2,3},{3,4},{4,5},{5,6},{6,7},{7,0},{16,16},{17,17},{1... | collective-permute-start | bytes 983048 | tf_op jit(solution)/shard_map/ppermute | solution.py:165
  6.4 4.3 %collective-permute-start.3 = (bf16[160,1024]{1,0:T(8,128)(2,1)S(1)}, bf16[160,1024]{1,0:T(8,128)(2,1)S(1)}, u32[]{:S(2)}, u32[]{:S(2)}) collective-permute-start(bf16[160,1024]{1,0:T(8,128)(2,1)S(1)} %collective-permute-done), channel_id=1, source_target_pairs={{0,1},{1,2},{2,3},{3,4},{4,5},{5,6},{6,7},{7,0},{16,16},{17,17},{1... | collective-permute-start | bytes 983048 | tf_op jit(solution)/shard_map/ppermute | solution.py:169
  14.1 5.5 %collective-permute-start.2 = (bf16[160,1024]{1,0:T(8,128)(2,1)S(1)}, bf16[160,1024]{1,0:T(8,128)(2,1)S(1)}, u32[]{:S(2)}, u32[]{:S(2)}) collective-permute-start(bf16[160,1024]{1,0:T(8,128)(2,1)S(1)} %collective-permute-done.1), channel_id=1, source_target_pairs={{0,1},{1,2},{2,3},{3,4},{4,5},{5,6},{6,7},{7,0},{16,23},{17,16},{1... | collective-permute-start | bytes 983048 | tf_op jit(solution)/shard_map/ppermute | solution.py:172
  19.6 3.4 %collective-permute-start.4 = (bf16[160,1024]{1,0:T(8,128)(2,1)S(1)}, bf16[160,1024]{1,0:T(8,128)(2,1)S(1)}, u32[]{:S(2)}, u32[]{:S(2)}) collective-permute-start(bf16[160,1024]{1,0:T(8,128)(2,1)S(1)} %collective-permute-done.3), channel_id=1, source_target_pairs={{0,1},{1,2},{2,3},{3,4},{4,5},{5,6},{6,7},{7,0},{16,23},{17,16},{1... | collective-permute-start | bytes 983048 | tf_op jit(solution)/shard_map/ppermute | solution.py:173
  24.9 3.8 %collective-permute-done.4 = bf16[160,1024]{1,0:T(8,128)(2,1)S(1)} collective-permute-done((bf16[160,1024]{1,0:T(8,128)(2,1)S(1)}, bf16[160,1024]{1,0:T(8,128)(2,1)S(1)}, u32[]{:S(2)}, u32[]{:S(2)}) %collective-permute-start.4) | collective-permute-done | bytes 327712 | tf_op jit(solution)/shard_map/ppermute | solution.py:173
  30.8 3.5 %collective-permute-start.8 = (bf16[160,1024]{1,0:T(8,128)(2,1)S(1)}, bf16[160,1024]{1,0:T(8,128)(2,1)S(1)}, u32[]{:S(2)}, u32[]{:S(2)}) collective-permute-start(bf16[160,1024]{1,0:T(8,128)(2,1)S(1)} %collective-permute-done.4), channel_id=1, source_target_pairs={{0,1},{1,2},{2,3},{3,4},{4,5},{5,6},{6,7},{7,0},{16,23},{17,16},{1... | collective-permute-start | bytes 983048 | tf_op jit(solution)/shard_map/ppermute | solution.py:186
  34.3 3.4 %collective-permute-start.6 = (bf16[160,1024]{1,0:T(8,128)(2,1)S(1)}, bf16[160,1024]{1,0:T(8,128)(2,1)S(1)}, u32[]{:S(2)}, u32[]{:S(2)}) collective-permute-start(bf16[160,1024]{1,0:T(8,128)(2,1)S(1)} %collective-permute-done.2), channel_id=1, source_target_pairs={{0,1},{1,2},{2,3},{3,4},{4,5},{5,6},{6,7},{7,0},{16,23},{17,16},{1... | collective-permute-start | bytes 983048 | tf_op jit(solution)/shard_map/ppermute | solution.py:185
  37.6 3.0 %collective-permute-done.8 = bf16[160,1024]{1,0:T(8,128)(2,1)S(1)} collective-permute-done((bf16[160,1024]{1,0:T(8,128)(2,1)S(1)}, bf16[160,1024]{1,0:T(8,128)(2,1)S(1)}, u32[]{:S(2)}, u32[]{:S(2)}) %collective-permute-start.8) | collective-permute-done | bytes 327712 | tf_op jit(solution)/shard_map/ppermute | solution.py:186
  40.7 2.5 %collective-permute-start.10 = (bf16[160,1024]{1,0:T(8,128)(2,1)S(1)}, bf16[160,1024]{1,0:T(8,128)(2,1)S(1)}, u32[]{:S(2)}, u32[]{:S(2)}) collective-permute-start(bf16[160,1024]{1,0:T(8,128)(2,1)S(1)} %collective-permute-done.8), channel_id=1, source_target_pairs={{0,1},{1,2},{2,3},{3,4},{4,5},{5,6},{6,7},{7,0},{16,23},{17,16},{1... | collective-permute-start | bytes 983048 | tf_op jit(solution)/shard_map/ppermute | solution.py:189
  44.8 2.7 %collective-permute-start.9 = (bf16[160,1024]{1,0:T(8,128)(2,1)S(1)}, bf16[160,1024]{1,0:T(8,128)(2,1)S(1)}, u32[]{:S(2)}, u32[]{:S(2)}) collective-permute-start(bf16[160,1024]{1,0:T(8,128)(2,1)S(1)} %collective-permute-done.6), channel_id=1, source_target_pairs={{0,1},{1,2},{2,3},{3,4},{4,5},{5,6},{6,7},{7,0},{16,23},{17,16},{1... | collective-permute-start | bytes 983048 | tf_op jit(solution)/shard_map/ppermute | solution.py:188
  50.5 4.4 %collective-permute-done.9 = bf16[160,1024]{1,0:T(8,128)(2,1)S(1)} collective-permute-done((bf16[160,1024]{1,0:T(8,128)(2,1)S(1)}, bf16[160,1024]{1,0:T(8,128)(2,1)S(1)}, u32[]{:S(2)}, u32[]{:S(2)}) %collective-permute-start.9) | collective-permute-done | bytes 327712 | tf_op jit(solution)/shard_map/ppermute | solution.py:188
  56.1 23.4 %all_to_all.35 = f32[4,160,640]{2,1,0:T(8,128)S(1)} all-to-all(f32[4,160,640]{2,1,0:T(8,128)S(1)} %fusion.3), channel_id=1, replica_groups=mesh['yh'=4,'x'=4,'c'=2,'yl'=2,'z'=8] {'x'}, dimensions={0} | all-to-all | bytes 3276800 | tf_op jit(solution)/shard_map/all_to_all | solution.py:198
  80.7 18.8 %all_to_all.36 = f32[8,40,320]{2,1,0:T(8,128)S(1)} all-to-all(f32[8,40,320]{2,1,0:T(8,128)S(1)} %fusion.15), channel_id=1, replica_groups=mesh['yh'=4,'x'=4,'c'=2,'yl'=2,'z'=8] {'yh','yl'}, dimensions={0} | all-to-all | bytes 819200 | tf_op jit(solution)/shard_map/all_to_all | solution.py:217
  100.5 3.4 %all-to-all-start.2 = ((f32[4,40,320]{2,1,0:T(8,128)}), f32[4,40,320]{2,1,0:T(8,128)S(1)}, u32[]{:S(2)}, u32[]{:S(2)}) async-start(f32[4,40,320]{2,1,0:T(8,128)} %broadcast_in_dim.36), calls=%async_computation.2 | async-start | bytes 491520 | tf_op jit(solution)/shard_map/all_to_all | solution.py:24
  103.9 4.1 %collective-permute-start.11 = (f32[40,320]{1,0:T(8,128)S(1)}, f32[40,320]{1,0:T(8,128)S(1)}, u32[]{:S(2)}, u32[]{:S(2)}) collective-permute-start(f32[40,320]{1,0:T(8,128)S(1)} %pad_maximum_fusion.3), channel_id=1, source_target_pairs={{0,7},{1,32},{2,65},{3,98},{4,131},{5,164},{6,197},{7,230},{8,15},... | collective-permute-start | bytes 153608 | tf_op jit(solution)/shard_map/ppermute | solution.py:221
  108.0 5.4 %all-to-all-done.2 = f32[4,40,320]{2,1,0:T(8,128)S(1)} async-done(((f32[4,40,320]{2,1,0:T(8,128)}), f32[4,40,320]{2,1,0:T(8,128)S(1)}, u32[]{:S(2)}, u32[]{:S(2)}) %all-to-all-start.2) | async-done | bytes 204832 | tf_op jit(solution)/shard_map/all_to_all | solution.py:24
  114.6 3.5 %all-to-all-start.3 = ((f32[4,40,1280]{2,1,0:T(8,128)}), f32[4,40,1280]{2,1,0:T(8,128)S(1)}, u32[]{:S(2)}, u32[]{:S(2)}) async-start(f32[4,40,1280]{2,1,0:T(8,128)} %broadcast_in_dim.37), calls=%async_computation.3 | async-start | bytes 1638400 | tf_op jit(solution)/shard_map/all_to_all | solution.py:24
  118.1 3.0 %collective-permute-start.12 = (f32[40,320]{1,0:T(8,128)S(1)}, f32[40,320]{1,0:T(8,128)S(1)}, u32[]{:S(2)}, u32[]{:S(2)}) collective-permute-start(f32[40,320]{1,0:T(8,128)S(1)} %collective-permute-done.11), channel_id=1, source_target_pairs={{0,8},{8,0},{1,9},{9,1},{2,10},{10,2},{3,11},{11,3},{4,12},{12,4},... | collective-permute-start | bytes 153608 | tf_op jit(solution)/shard_map/ppermute | solution.py:20
  121.2 3.0 %collective-permute-done.12 = f32[40,320]{1,0:T(8,128)S(1)} collective-permute-done((f32[40,320]{1,0:T(8,128)S(1)}, f32[40,320]{1,0:T(8,128)S(1)}, u32[]{:S(2)}, u32[]{:S(2)}) %collective-permute-start.12) | collective-permute-done | bytes 51232 | tf_op jit(solution)/shard_map/ppermute | solution.py:20
  124.4 3.3 %all-to-all-done.3 = f32[4,40,1280]{2,1,0:T(8,128)S(1)} async-done(((f32[4,40,1280]{2,1,0:T(8,128)}), f32[4,40,1280]{2,1,0:T(8,128)S(1)}, u32[]{:S(2)}, u32[]{:S(2)}) %all-to-all-start.3) | async-done | bytes 819232 | tf_op jit(solution)/shard_map/all_to_all | solution.py:24
  127.8 5.0 %all_to_all.37 = f32[2,4,40,1280]{3,2,1,0:T(8,128)S(1)} all-to-all(f32[2,4,40,1280]{3,2,1,0:T(8,128)S(1)} %broadcast_in_dim.38), channel_id=1, replica_groups=mesh['yh'=4,'x'=4,'c'=2,'yl'=2,'z'=8] {'c'}, dimensions={0} | all-to-all | bytes 3276800 | tf_op jit(solution)/shard_map/all_to_all | solution.py:24
  134.6 26.1 %all_to_all.38.got = bf16[16,40,384]{2,1,0:T(8,128)(2,1)S(1)} all-to-all(bf16[16,40,384]{2,1,0:T(8,128)(2,1)S(1)} %get-tuple-element.28), channel_id=1, replica_groups=mesh['yh'=4,'x'=4,'c'=2,'yl'=2,'z'=8] {'yl','z'}, dimensions={0} | all-to-all | bytes 983040 | tf_op jit(solution)/shard_map/all_to_all | solution.py:250
  162.6 19.8 %all_to_all.39.got = bf16[16,40,384]{2,1,0:T(8,128)(2,1)S(1)} all-to-all(bf16[16,40,384]{2,1,0:T(8,128)(2,1)S(1)} %get-tuple-element.31), channel_id=1, replica_groups=mesh['yh'=4,'x'=4,'c'=2,'yl'=2,'z'=8] {'yl','z'}, dimensions={0} | all-to-all | bytes 983040 | tf_op jit(solution)/shard_map/all_to_all | solution.py:259
  182.4 2.5 %shard_map.30 = f32[160,80]{1,0:T(8,128)} custom-call(s32[2]{0:T(128)S(1)} %pad_add_fusion.place, bf16[16,40,384]{2,1,0:T(8,128)(2,1)S(1)} %all_to_all.39.got, bf16[2560,160]{1,0:T(8,128)(2,1)S(1)} %get-tuple-element.29.high, bf16[2560,160]{1,0:T(8,128)(2,1)S(1)} %get-tuple-element.30.low, f32[40,320]{1,0:T(8,128)S(1)} %fusion.16.target.target_in, ...), custom_call_target="tpu_custom_call" | custom-call | tf_op jit(solution)/shard_map/pallas_call | solution.py:260
  (54 shorter events, 22.4 us)
Async XLA Ops:
  0.0 28.6 %copy-start = (bf16[160,1024]{1,0:T(8,128)(2,1)S(1)}, bf16[160,1024]{1,0:T(8,128)(2,1)}, u32[]{:S(2)}) copy-start(bf16[160,1024]{1,0:T(8,128)(2,1)} %param.2) | copy-start | bytes 983044
  0.0 28.6 %copy-start.1 = (bf16[160,1024]{1,0:T(8,128)(2,1)S(1)}, bf16[160,1024]{1,0:T(8,128)(2,1)}, u32[]{:S(2)}) copy-start(bf16[160,1024]{1,0:T(8,128)(2,1)} %param.3) | copy-start | bytes 983044
  0.0 6.3 %collective-permute-start = (bf16[160,1024]{1,0:T(8,128)(2,1)}, bf16[160,1024]{1,0:T(8,128)(2,1)S(1)}, u32[]{:S(2)}, u32[]{:S(2)}) collective-permute-start(bf16[160,1024]{1,0:T(8,128)(2,1)} %param.2), channel_id=1, source_target_pairs={{0,16},{16,0},{1,17},{17,1},{2,18},{18,2},{3,19},{19,3},{4,20},{20... | collective-permute-start | bytes 983048 | tf_op jit(solution)/shard_map/ppermute | solution.py:20
  2.1 12.1 %collective-permute-start.1 = (bf16[160,1024]{1,0:T(8,128)(2,1)}, bf16[160,1024]{1,0:T(8,128)(2,1)S(1)}, u32[]{:S(2)}, u32[]{:S(2)}) collective-permute-start(bf16[160,1024]{1,0:T(8,128)(2,1)} %param.2), channel_id=1, source_target_pairs={{0,1},{1,2},{2,3},{3,4},{4,5},{5,6},{6,7},{7,0},{16,16},{17,17},{1... | collective-permute-start | bytes 983048 | tf_op jit(solution)/shard_map/ppermute | solution.py:165
  6.4 13.3 %collective-permute-start.3 = (bf16[160,1024]{1,0:T(8,128)(2,1)S(1)}, bf16[160,1024]{1,0:T(8,128)(2,1)S(1)}, u32[]{:S(2)}, u32[]{:S(2)}) collective-permute-start(bf16[160,1024]{1,0:T(8,128)(2,1)S(1)} %collective-permute-done), channel_id=1, source_target_pairs={{0,1},{1,2},{2,3},{3,4},{4,5},{5,6},{6,7},{7,0},{16,16},{17,17},{1... | collective-permute-start | bytes 983048 | tf_op jit(solution)/shard_map/ppermute | solution.py:169
  11.8 16.9 %collective-permute-start.5 = (bf16[320,1024]{1,0:T(8,128)(2,1)S(1)}, bf16[320,1024]{1,0:T(8,128)(2,1)S(1)}, u32[]{:S(2)}, u32[]{:S(2)}) collective-permute-start(bf16[320,1024]{1,0:T(8,128)(2,1)S(1)} %pad_maximum_fusion.1), channel_id=1, source_target_pairs={{0,8},{8,0},{1,9},{9,1},{2,10},{10,2},{3,11},{11,3},{4,12},{12,4},... | collective-permute-start | bytes 1966088 | tf_op jit(solution)/shard_map/ppermute | solution.py:20
  14.1 10.7 %collective-permute-start.2 = (bf16[160,1024]{1,0:T(8,128)(2,1)S(1)}, bf16[160,1024]{1,0:T(8,128)(2,1)S(1)}, u32[]{:S(2)}, u32[]{:S(2)}) collective-permute-start(bf16[160,1024]{1,0:T(8,128)(2,1)S(1)} %collective-permute-done.1), channel_id=1, source_target_pairs={{0,1},{1,2},{2,3},{3,4},{4,5},{5,6},{6,7},{7,0},{16,23},{17,16},{1... | collective-permute-start | bytes 983048 | tf_op jit(solution)/shard_map/ppermute | solution.py:172
  19.6 9.0 %collective-permute-start.4 = (bf16[160,1024]{1,0:T(8,128)(2,1)S(1)}, bf16[160,1024]{1,0:T(8,128)(2,1)S(1)}, u32[]{:S(2)}, u32[]{:S(2)}) collective-permute-start(bf16[160,1024]{1,0:T(8,128)(2,1)S(1)} %collective-permute-done.3), channel_id=1, source_target_pairs={{0,1},{1,2},{2,3},{3,4},{4,5},{5,6},{6,7},{7,0},{16,23},{17,16},{1... | collective-permute-start | bytes 983048 | tf_op jit(solution)/shard_map/ppermute | solution.py:173
  28.8 15.4 %collective-permute-start.7 = (bf16[640,1024]{1,0:T(8,128)(2,1)S(1)}, bf16[640,1024]{1,0:T(8,128)(2,1)S(1)}, u32[]{:S(2)}, u32[]{:S(2)}) collective-permute-start(bf16[640,1024]{1,0:T(8,128)(2,1)S(1)} %pad_maximum_fusion), channel_id=1, source_target_pairs={{0,16},{16,0},{1,17},{17,1},{2,18},{18,2},{3,19},{19,3},{4,20},{20... | collective-permute-start | bytes 3932168 | tf_op jit(solution)/shard_map/ppermute | solution.py:20
  30.8 9.9 %collective-permute-start.8 = (bf16[160,1024]{1,0:T(8,128)(2,1)S(1)}, bf16[160,1024]{1,0:T(8,128)(2,1)S(1)}, u32[]{:S(2)}, u32[]{:S(2)}) collective-permute-start(bf16[160,1024]{1,0:T(8,128)(2,1)S(1)} %collective-permute-done.4), channel_id=1, source_target_pairs={{0,1},{1,2},{2,3},{3,4},{4,5},{5,6},{6,7},{7,0},{16,23},{17,16},{1... | collective-permute-start | bytes 983048 | tf_op jit(solution)/shard_map/ppermute | solution.py:186
  34.3 9.9 %collective-permute-start.6 = (bf16[160,1024]{1,0:T(8,128)(2,1)S(1)}, bf16[160,1024]{1,0:T(8,128)(2,1)S(1)}, u32[]{:S(2)}, u32[]{:S(2)}) collective-permute-start(bf16[160,1024]{1,0:T(8,128)(2,1)S(1)} %collective-permute-done.2), channel_id=1, source_target_pairs={{0,1},{1,2},{2,3},{3,4},{4,5},{5,6},{6,7},{7,0},{16,23},{17,16},{1... | collective-permute-start | bytes 983048 | tf_op jit(solution)/shard_map/ppermute | solution.py:185
  40.7 14.8 %collective-permute-start.10 = (bf16[160,1024]{1,0:T(8,128)(2,1)S(1)}, bf16[160,1024]{1,0:T(8,128)(2,1)S(1)}, u32[]{:S(2)}, u32[]{:S(2)}) collective-permute-start(bf16[160,1024]{1,0:T(8,128)(2,1)S(1)} %collective-permute-done.8), channel_id=1, source_target_pairs={{0,1},{1,2},{2,3},{3,4},{4,5},{5,6},{6,7},{7,0},{16,23},{17,16},{1... | collective-permute-start | bytes 983048 | tf_op jit(solution)/shard_map/ppermute | solution.py:189
  44.8 10.2 %collective-permute-start.9 = (bf16[160,1024]{1,0:T(8,128)(2,1)S(1)}, bf16[160,1024]{1,0:T(8,128)(2,1)S(1)}, u32[]{:S(2)}, u32[]{:S(2)}) collective-permute-start(bf16[160,1024]{1,0:T(8,128)(2,1)S(1)} %collective-permute-done.6), channel_id=1, source_target_pairs={{0,1},{1,2},{2,3},{3,4},{4,5},{5,6},{6,7},{7,0},{16,23},{17,16},{1... | collective-permute-start | bytes 983048 | tf_op jit(solution)/shard_map/ppermute | solution.py:188
  100.5 13.0 %all-to-all-start.2 = ((f32[4,40,320]{2,1,0:T(8,128)}), f32[4,40,320]{2,1,0:T(8,128)S(1)}, u32[]{:S(2)}, u32[]{:S(2)}) async-start(f32[4,40,320]{2,1,0:T(8,128)} %broadcast_in_dim.36), calls=%async_computation.2 | async-start | bytes 491520 | tf_op jit(solution)/shard_map/all_to_all | solution.py:24
  103.9 14.2 %collective-permute-start.11 = (f32[40,320]{1,0:T(8,128)S(1)}, f32[40,320]{1,0:T(8,128)S(1)}, u32[]{:S(2)}, u32[]{:S(2)}) collective-permute-start(f32[40,320]{1,0:T(8,128)S(1)} %pad_maximum_fusion.3), channel_id=1, source_target_pairs={{0,7},{1,32},{2,65},{3,98},{4,131},{5,164},{6,197},{7,230},{8,15},... | collective-permute-start | bytes 153608 | tf_op jit(solution)/shard_map/ppermute | solution.py:221
  114.6 13.1 %all-to-all-start.3 = ((f32[4,40,1280]{2,1,0:T(8,128)}), f32[4,40,1280]{2,1,0:T(8,128)S(1)}, u32[]{:S(2)}, u32[]{:S(2)}) async-start(f32[4,40,1280]{2,1,0:T(8,128)} %broadcast_in_dim.37), calls=%async_computation.3 | async-start | bytes 1638400 | tf_op jit(solution)/shard_map/all_to_all | solution.py:24
  118.1 6.1 %collective-permute-start.12 = (f32[40,320]{1,0:T(8,128)S(1)}, f32[40,320]{1,0:T(8,128)S(1)}, u32[]{:S(2)}, u32[]{:S(2)}) collective-permute-start(f32[40,320]{1,0:T(8,128)S(1)} %collective-permute-done.11), channel_id=1, source_target_pairs={{0,8},{8,0},{1,9},{9,1},{2,10},{10,2},{3,11},{11,3},{4,12},{12,4},... | collective-permute-start | bytes 153608 | tf_op jit(solution)/shard_map/ppermute | solution.py:20

commit v15 on v14

--- a/solution.py
+++ b/solution.py
@@ -184,7 +184,7 @@
     columns_there = shift(columns, "c", 2, 1)
     here.append(lax.ppermute(here[1], ("c", "z"), later))
     there.append(lax.ppermute(there[1], ("c", "z"), later))
-    here[2], columns_there = lax.optimization_barrier((here[2], columns_there))
+    there[2], columns_there = lax.optimization_barrier((there[2], columns_there))
     here.append(lax.ppermute(here[2], ("c", "z"), later))
     there.append(lax.ppermute(there[2], ("c", "z"), later))
     partial = jnp.zeros((4, rows, 4 * rows), jnp.float32)

time: 186 us -> 187 us (level)
  starting transfers between devices: 49.8 us -> 53.2 us
  blocking collectives: 93.2 us -> 91.3 us
    ppermute x1, waiting for transfers between devices: 4.4 us -> 0.01 us  [body(): here.append(lax.ppermute(here[2], ('c', 'z'), later))]
    ppermute x1, waiting for transfers between devices: 3.04 us -> 0.39 us  [body(): there.append(lax.ppermute(there[1], ('c', 'z'), later))]
    ppermute x1, waiting for transfers between devices: 0.01 us -> 2.34 us  [body(): there.append(lax.ppermute(there[2], ('c', 'z'), later))]
    all_to_all x2, blocking collectives: 45.9 us -> 43.9 us  [body(): got = lax.all_to_all(sent, FEAT, 0, 0)]
where the time goes in v15:
time: 187 us; the launch traced here: 186 us
  blocking collectives  91.3 us (49%)
  starting transfers between devices  53.2 us (28%)
  waiting for transfers between devices  24.3 us (13%)
  Pallas kernels  6.09 us (3%)
  matrix products  4.64 us (2%)
  other arithmetic  3.56 us (2%)
  local copies, waits for them, and re-layouts  2.5 us (1%)
    all_to_all x2, blocking collectives, body(): got = lax.all_to_all(sent, FEAT, 0, 0)  43.9 us
    all_to_all x1, blocking collectives, body(): partial = jnp.sum(lax.all_to_all(partial, 'x', 0, 0), 0)  23.4 us
    all_to_all x1, blocking collectives, body(): own = lax.all_to_all(jnp.stack(packed), ('yh', 'yl'), 0, 0)  19 us
    all_to_all x2, waiting for transfers between devices, spread(): lax.all_to_all(jnp.broadcast_to(array[None], (count,) + array.shape), axe...  10.2 us
    ppermute x4, starting transfers between devices, shift(): lax.ppermute(array, axis, [(i, (i + step) % size) for i in range(size)])  9.2 us
    all_to_all x2, starting transfers between devices, spread(): lax.all_to_all(jnp.broadcast_to(array[None], (count,) + array.shape), axe...  6.89 us
    ppermute x1, starting transfers between devices, body(): here.append(lax.ppermute(here[0], ('c', 'z'), later))  5.49 us
    ppermute x1, waiting for transfers between devices, body(): there.append(lax.ppermute(there[0], ('c', 'z'), later))  5.21 us
  transfers between devices with their start and end apart: 15, of which 8 were waited for; matrix products, arithmetic and copies ran while one was open for 4% of the time, Pallas kernels for 0%

profile of v15, /device:TPU:72, one launch (start us, length us, event | category | flops | bytes accessed | tf_op | source)
XLA Modules:
  0.0 186.0 jit_solution(3926994113347959784)
XLA Ops:
  1.9 4.3 %collective-permute-start.1 = (bf16[160,1024]{1,0:T(8,128)(2,1)}, bf16[160,1024]{1,0:T(8,128)(2,1)S(1)}, u32[]{:S(2)}, u32[]{:S(2)}) collective-permute-start(bf16[160,1024]{1,0:T(8,128)(2,1)} %param.2), channel_id=1, source_target_pairs={{0,1},{1,2},{2,3},{3,4},{4,5},{5,6},{6,7},{7,0},{16,16},{17,17},{1... | collective-permute-start | bytes 983048 | tf_op jit(solution)/shard_map/ppermute | solution.py:165
  7.3 2.4 %collective-permute-start.5 = (bf16[320,1024]{1,0:T(8,128)(2,1)S(1)}, bf16[320,1024]{1,0:T(8,128)(2,1)S(1)}, u32[]{:S(2)}, u32[]{:S(2)}) collective-permute-start(bf16[320,1024]{1,0:T(8,128)(2,1)S(1)} %pad_maximum_fusion.1), channel_id=1, source_target_pairs={{0,8},{8,0},{1,9},{9,1},{2,10},{10,2},{3,11},{11,3},{4,12},{12,4},... | collective-permute-start | bytes 1966088 | tf_op jit(solution)/shard_map/ppermute | solution.py:20
  9.7 4.3 %collective-permute-start.3 = (bf16[160,1024]{1,0:T(8,128)(2,1)S(1)}, bf16[160,1024]{1,0:T(8,128)(2,1)S(1)}, u32[]{:S(2)}, u32[]{:S(2)}) collective-permute-start(bf16[160,1024]{1,0:T(8,128)(2,1)S(1)} %collective-permute-done), channel_id=1, source_target_pairs={{0,1},{1,2},{2,3},{3,4},{4,5},{5,6},{6,7},{7,0},{16,16},{17,17},{1... | collective-permute-start | bytes 983048 | tf_op jit(solution)/shard_map/ppermute | solution.py:169
  14.0 5.5 %collective-permute-start.2 = (bf16[160,1024]{1,0:T(8,128)(2,1)S(1)}, bf16[160,1024]{1,0:T(8,128)(2,1)S(1)}, u32[]{:S(2)}, u32[]{:S(2)}) collective-permute-start(bf16[160,1024]{1,0:T(8,128)(2,1)S(1)} %collective-permute-done.1), channel_id=1, source_target_pairs={{0,1},{1,2},{2,3},{3,4},{4,5},{5,6},{6,7},{7,0},{16,23},{17,16},{1... | collective-permute-start | bytes 983048 | tf_op jit(solution)/shard_map/ppermute | solution.py:172
  19.5 4.5 %collective-permute-start.4 = (bf16[160,1024]{1,0:T(8,128)(2,1)S(1)}, bf16[160,1024]{1,0:T(8,128)(2,1)S(1)}, u32[]{:S(2)}, u32[]{:S(2)}) collective-permute-start(bf16[160,1024]{1,0:T(8,128)(2,1)S(1)} %collective-permute-done.3), channel_id=1, source_target_pairs={{0,1},{1,2},{2,3},{3,4},{4,5},{5,6},{6,7},{7,0},{16,23},{17,16},{1... | collective-permute-start | bytes 983048 | tf_op jit(solution)/shard_map/ppermute | solution.py:173
  24.7 5.2 %collective-permute-done.4 = bf16[160,1024]{1,0:T(8,128)(2,1)S(1)} collective-permute-done((bf16[160,1024]{1,0:T(8,128)(2,1)S(1)}, bf16[160,1024]{1,0:T(8,128)(2,1)S(1)}, u32[]{:S(2)}, u32[]{:S(2)}) %collective-permute-start.4) | collective-permute-done | bytes 327712 | tf_op jit(solution)/shard_map/ppermute | solution.py:173
  33.1 3.1 %collective-permute-start.8 = (bf16[160,1024]{1,0:T(8,128)(2,1)S(1)}, bf16[160,1024]{1,0:T(8,128)(2,1)S(1)}, u32[]{:S(2)}, u32[]{:S(2)}) collective-permute-start(bf16[160,1024]{1,0:T(8,128)(2,1)S(1)} %collective-permute-done.2), channel_id=1, source_target_pairs={{0,1},{1,2},{2,3},{3,4},{4,5},{5,6},{6,7},{7,0},{16,23},{17,16},{1... | collective-permute-start | bytes 983048 | tf_op jit(solution)/shard_map/ppermute | solution.py:185
  36.2 4.6 %collective-permute-start.6 = (bf16[160,1024]{1,0:T(8,128)(2,1)S(1)}, bf16[160,1024]{1,0:T(8,128)(2,1)S(1)}, u32[]{:S(2)}, u32[]{:S(2)}) collective-permute-start(bf16[160,1024]{1,0:T(8,128)(2,1)S(1)} %collective-permute-done.4), channel_id=1, source_target_pairs={{0,1},{1,2},{2,3},{3,4},{4,5},{5,6},{6,7},{7,0},{16,23},{17,16},{1... | collective-permute-start | bytes 983048 | tf_op jit(solution)/shard_map/ppermute | solution.py:186
  40.8 2.5 %collective-permute-done.8 = bf16[160,1024]{1,0:T(8,128)(2,1)S(1)} collective-permute-done((bf16[160,1024]{1,0:T(8,128)(2,1)S(1)}, bf16[160,1024]{1,0:T(8,128)(2,1)S(1)}, u32[]{:S(2)}, u32[]{:S(2)}) %collective-permute-start.8) | collective-permute-done | bytes 327712 | tf_op jit(solution)/shard_map/ppermute | solution.py:185
  43.3 3.1 %collective-permute-start.9 = (bf16[160,1024]{1,0:T(8,128)(2,1)S(1)}, bf16[160,1024]{1,0:T(8,128)(2,1)S(1)}, u32[]{:S(2)}, u32[]{:S(2)}) collective-permute-start(bf16[160,1024]{1,0:T(8,128)(2,1)S(1)} %collective-permute-done.8), channel_id=1, source_target_pairs={{0,1},{1,2},{2,3},{3,4},{4,5},{5,6},{6,7},{7,0},{16,23},{17,16},{1... | collective-permute-start | bytes 983048 | tf_op jit(solution)/shard_map/ppermute | solution.py:188
  46.8 4.2 %collective-permute-start.10 = (bf16[160,1024]{1,0:T(8,128)(2,1)S(1)}, bf16[160,1024]{1,0:T(8,128)(2,1)S(1)}, u32[]{:S(2)}, u32[]{:S(2)}) collective-permute-start(bf16[160,1024]{1,0:T(8,128)(2,1)S(1)} %collective-permute-done.6), channel_id=1, source_target_pairs={{0,1},{1,2},{2,3},{3,4},{4,5},{5,6},{6,7},{7,0},{16,23},{17,16},{1... | collective-permute-start | bytes 983048 | tf_op jit(solution)/shard_map/ppermute | solution.py:189
  58.2 23.4 %all_to_all.35 = f32[4,160,640]{2,1,0:T(8,128)S(1)} all-to-all(f32[4,160,640]{2,1,0:T(8,128)S(1)} %fusion.3), channel_id=1, replica_groups=mesh['yh'=4,'x'=4,'c'=2,'yl'=2,'z'=8] {'x'}, dimensions={0} | all-to-all | bytes 3276800 | tf_op jit(solution)/shard_map/all_to_all | solution.py:198
  82.7 19.0 %all_to_all.36 = f32[8,40,320]{2,1,0:T(8,128)S(1)} all-to-all(f32[8,40,320]{2,1,0:T(8,128)S(1)} %fusion.15), channel_id=1, replica_groups=mesh['yh'=4,'x'=4,'c'=2,'yl'=2,'z'=8] {'yh','yl'}, dimensions={0} | all-to-all | bytes 819200 | tf_op jit(solution)/shard_map/all_to_all | solution.py:217
  102.6 3.4 %all-to-all-start.2 = ((f32[4,40,320]{2,1,0:T(8,128)}), f32[4,40,320]{2,1,0:T(8,128)S(1)}, u32[]{:S(2)}, u32[]{:S(2)}) async-start(f32[4,40,320]{2,1,0:T(8,128)} %broadcast_in_dim.36), calls=%async_computation.2 | async-start | bytes 491520 | tf_op jit(solution)/shard_map/all_to_all | solution.py:24
  106.1 3.6 %collective-permute-start.11 = (f32[40,320]{1,0:T(8,128)S(1)}, f32[40,320]{1,0:T(8,128)S(1)}, u32[]{:S(2)}, u32[]{:S(2)}) collective-permute-start(f32[40,320]{1,0:T(8,128)S(1)} %pad_maximum_fusion.3), channel_id=1, source_target_pairs={{0,7},{1,32},{2,65},{3,98},{4,131},{5,164},{6,197},{7,230},{8,15},... | collective-permute-start | bytes 153608 | tf_op jit(solution)/shard_map/ppermute | solution.py:221
  109.7 5.9 %all-to-all-done.2 = f32[4,40,320]{2,1,0:T(8,128)S(1)} async-done(((f32[4,40,320]{2,1,0:T(8,128)}), f32[4,40,320]{2,1,0:T(8,128)S(1)}, u32[]{:S(2)}, u32[]{:S(2)}) %all-to-all-start.2) | async-done | bytes 204832 | tf_op jit(solution)/shard_map/all_to_all | solution.py:24
  116.8 3.5 %all-to-all-start.3 = ((f32[4,40,1280]{2,1,0:T(8,128)}), f32[4,40,1280]{2,1,0:T(8,128)S(1)}, u32[]{:S(2)}, u32[]{:S(2)}) async-start(f32[4,40,1280]{2,1,0:T(8,128)} %broadcast_in_dim.37), calls=%async_computation.3 | async-start | bytes 1638400 | tf_op jit(solution)/shard_map/all_to_all | solution.py:24
  120.3 3.0 %collective-permute-start.12 = (f32[40,320]{1,0:T(8,128)S(1)}, f32[40,320]{1,0:T(8,128)S(1)}, u32[]{:S(2)}, u32[]{:S(2)}) collective-permute-start(f32[40,320]{1,0:T(8,128)S(1)} %collective-permute-done.11), channel_id=1, source_target_pairs={{0,8},{8,0},{1,9},{9,1},{2,10},{10,2},{3,11},{11,3},{4,12},{12,4},... | collective-permute-start | bytes 153608 | tf_op jit(solution)/shard_map/ppermute | solution.py:20
  123.4 3.0 %collective-permute-done.12 = f32[40,320]{1,0:T(8,128)S(1)} collective-permute-done((f32[40,320]{1,0:T(8,128)S(1)}, f32[40,320]{1,0:T(8,128)S(1)}, u32[]{:S(2)}, u32[]{:S(2)}) %collective-permute-start.12) | collective-permute-done | bytes 51232 | tf_op jit(solution)/shard_map/ppermute | solution.py:20
  126.6 4.3 %all-to-all-done.3 = f32[4,40,1280]{2,1,0:T(8,128)S(1)} async-done(((f32[4,40,1280]{2,1,0:T(8,128)}), f32[4,40,1280]{2,1,0:T(8,128)S(1)}, u32[]{:S(2)}, u32[]{:S(2)}) %all-to-all-start.3) | async-done | bytes 819232 | tf_op jit(solution)/shard_map/all_to_all | solution.py:24
  131.0 5.0 %all_to_all.37 = f32[2,4,40,1280]{3,2,1,0:T(8,128)S(1)} all-to-all(f32[2,4,40,1280]{3,2,1,0:T(8,128)S(1)} %broadcast_in_dim.38), channel_id=1, replica_groups=mesh['yh'=4,'x'=4,'c'=2,'yl'=2,'z'=8] {'c'}, dimensions={0} | all-to-all | bytes 3276800 | tf_op jit(solution)/shard_map/all_to_all | solution.py:24
  137.8 24.1 %all_to_all.38.got = bf16[16,40,384]{2,1,0:T(8,128)(2,1)S(1)} all-to-all(bf16[16,40,384]{2,1,0:T(8,128)(2,1)S(1)} %get-tuple-element.28), channel_id=1, replica_groups=mesh['yh'=4,'x'=4,'c'=2,'yl'=2,'z'=8] {'yl','z'}, dimensions={0} | all-to-all | bytes 983040 | tf_op jit(solution)/shard_map/all_to_all | solution.py:250
  163.8 19.8 %all_to_all.39.got = bf16[16,40,384]{2,1,0:T(8,128)(2,1)S(1)} all-to-all(bf16[16,40,384]{2,1,0:T(8,128)(2,1)S(1)} %get-tuple-element.31), channel_id=1, replica_groups=mesh['yh'=4,'x'=4,'c'=2,'yl'=2,'z'=8] {'yl','z'}, dimensions={0} | all-to-all | bytes 983040 | tf_op jit(solution)/shard_map/all_to_all | solution.py:259
  183.5 2.5 %shard_map.30 = f32[160,80]{1,0:T(8,128)} custom-call(s32[2]{0:T(128)S(1)} %pad_add_fusion.place, bf16[16,40,384]{2,1,0:T(8,128)(2,1)S(1)} %all_to_all.39.got, bf16[2560,160]{1,0:T(8,128)(2,1)S(1)} %get-tuple-element.29.high, bf16[2560,160]{1,0:T(8,128)(2,1)S(1)} %get-tuple-element.30.low, f32[40,320]{1,0:T(8,128)S(1)} %fusion.16.target.target_in, ...), custom_call_target="tpu_custom_call" | custom-call | tf_op jit(solution)/shard_map/pallas_call | solution.py:260
  (50 shorter events, 21.6 us)
Async XLA Ops:
  0.0 6.2 %collective-permute-start = (bf16[160,1024]{1,0:T(8,128)(2,1)}, bf16[160,1024]{1,0:T(8,128)(2,1)S(1)}, u32[]{:S(2)}, u32[]{:S(2)}) collective-permute-start(bf16[160,1024]{1,0:T(8,128)(2,1)} %param.2), channel_id=1, source_target_pairs={{0,16},{16,0},{1,17},{17,1},{2,18},{18,2},{3,19},{19,3},{4,20},{20... | collective-permute-start | bytes 983048 | tf_op jit(solution)/shard_map/ppermute | solution.py:20
  1.9 12.1 %collective-permute-start.1 = (bf16[160,1024]{1,0:T(8,128)(2,1)}, bf16[160,1024]{1,0:T(8,128)(2,1)S(1)}, u32[]{:S(2)}, u32[]{:S(2)}) collective-permute-start(bf16[160,1024]{1,0:T(8,128)(2,1)} %param.2), channel_id=1, source_target_pairs={{0,1},{1,2},{2,3},{3,4},{4,5},{5,6},{6,7},{7,0},{16,16},{17,17},{1... | collective-permute-start | bytes 983048 | tf_op jit(solution)/shard_map/ppermute | solution.py:165
  7.3 17.4 %collective-permute-start.5 = (bf16[320,1024]{1,0:T(8,128)(2,1)S(1)}, bf16[320,1024]{1,0:T(8,128)(2,1)S(1)}, u32[]{:S(2)}, u32[]{:S(2)}) collective-permute-start(bf16[320,1024]{1,0:T(8,128)(2,1)S(1)} %pad_maximum_fusion.1), channel_id=1, source_target_pairs={{0,8},{8,0},{1,9},{9,1},{2,10},{10,2},{3,11},{11,3},{4,12},{12,4},... | collective-permute-start | bytes 1966088 | tf_op jit(solution)/shard_map/ppermute | solution.py:20
  9.7 9.8 %collective-permute-start.3 = (bf16[160,1024]{1,0:T(8,128)(2,1)S(1)}, bf16[160,1024]{1,0:T(8,128)(2,1)S(1)}, u32[]{:S(2)}, u32[]{:S(2)}) collective-permute-start(bf16[160,1024]{1,0:T(8,128)(2,1)S(1)} %collective-permute-done), channel_id=1, source_target_pairs={{0,1},{1,2},{2,3},{3,4},{4,5},{5,6},{6,7},{7,0},{16,16},{17,17},{1... | collective-permute-start | bytes 983048 | tf_op jit(solution)/shard_map/ppermute | solution.py:169
  14.0 10.7 %collective-permute-start.2 = (bf16[160,1024]{1,0:T(8,128)(2,1)S(1)}, bf16[160,1024]{1,0:T(8,128)(2,1)S(1)}, u32[]{:S(2)}, u32[]{:S(2)}) collective-permute-start(bf16[160,1024]{1,0:T(8,128)(2,1)S(1)} %collective-permute-done.1), channel_id=1, source_target_pairs={{0,1},{1,2},{2,3},{3,4},{4,5},{5,6},{6,7},{7,0},{16,23},{17,16},{1... | collective-permute-start | bytes 983048 | tf_op jit(solution)/shard_map/ppermute | solution.py:172
  19.5 10.4 %collective-permute-start.4 = (bf16[160,1024]{1,0:T(8,128)(2,1)S(1)}, bf16[160,1024]{1,0:T(8,128)(2,1)S(1)}, u32[]{:S(2)}, u32[]{:S(2)}) collective-permute-start(bf16[160,1024]{1,0:T(8,128)(2,1)S(1)} %collective-permute-done.3), channel_id=1, source_target_pairs={{0,1},{1,2},{2,3},{3,4},{4,5},{5,6},{6,7},{7,0},{16,23},{17,16},{1... | collective-permute-start | bytes 983048 | tf_op jit(solution)/shard_map/ppermute | solution.py:173
  31.2 15.6 %collective-permute-start.7 = (bf16[640,1024]{1,0:T(8,128)(2,1)S(1)}, bf16[640,1024]{1,0:T(8,128)(2,1)S(1)}, u32[]{:S(2)}, u32[]{:S(2)}) collective-permute-start(bf16[640,1024]{1,0:T(8,128)(2,1)S(1)} %pad_maximum_fusion), channel_id=1, source_target_pairs={{0,16},{16,0},{1,17},{17,1},{2,18},{18,2},{3,19},{19,3},{4,20},{20... | collective-permute-start | bytes 3932168 | tf_op jit(solution)/shard_map/ppermute | solution.py:20
  33.1 10.2 %collective-permute-start.8 = (bf16[160,1024]{1,0:T(8,128)(2,1)S(1)}, bf16[160,1024]{1,0:T(8,128)(2,1)S(1)}, u32[]{:S(2)}, u32[]{:S(2)}) collective-permute-start(bf16[160,1024]{1,0:T(8,128)(2,1)S(1)} %collective-permute-done.2), channel_id=1, source_target_pairs={{0,1},{1,2},{2,3},{3,4},{4,5},{5,6},{6,7},{7,0},{16,23},{17,16},{1... | collective-permute-start | bytes 983048 | tf_op jit(solution)/shard_map/ppermute | solution.py:185
  36.2 10.6 %collective-permute-start.6 = (bf16[160,1024]{1,0:T(8,128)(2,1)S(1)}, bf16[160,1024]{1,0:T(8,128)(2,1)S(1)}, u32[]{:S(2)}, u32[]{:S(2)}) collective-permute-start(bf16[160,1024]{1,0:T(8,128)(2,1)S(1)} %collective-permute-done.4), channel_id=1, source_target_pairs={{0,1},{1,2},{2,3},{3,4},{4,5},{5,6},{6,7},{7,0},{16,23},{17,16},{1... | collective-permute-start | bytes 983048 | tf_op jit(solution)/shard_map/ppermute | solution.py:186
  43.3 14.3 %collective-permute-start.9 = (bf16[160,1024]{1,0:T(8,128)(2,1)S(1)}, bf16[160,1024]{1,0:T(8,128)(2,1)S(1)}, u32[]{:S(2)}, u32[]{:S(2)}) collective-permute-start(bf16[160,1024]{1,0:T(8,128)(2,1)S(1)} %collective-permute-done.8), channel_id=1, source_target_pairs={{0,1},{1,2},{2,3},{3,4},{4,5},{5,6},{6,7},{7,0},{16,23},{17,16},{1... | collective-permute-start | bytes 983048 | tf_op jit(solution)/shard_map/ppermute | solution.py:188
  46.8 10.2 %collective-permute-start.10 = (bf16[160,1024]{1,0:T(8,128)(2,1)S(1)}, bf16[160,1024]{1,0:T(8,128)(2,1)S(1)}, u32[]{:S(2)}, u32[]{:S(2)}) collective-permute-start(bf16[160,1024]{1,0:T(8,128)(2,1)S(1)} %collective-permute-done.6), channel_id=1, source_target_pairs={{0,1},{1,2},{2,3},{3,4},{4,5},{5,6},{6,7},{7,0},{16,23},{17,16},{1... | collective-permute-start | bytes 983048 | tf_op jit(solution)/shard_map/ppermute | solution.py:189
  102.6 13.0 %all-to-all-start.2 = ((f32[4,40,320]{2,1,0:T(8,128)}), f32[4,40,320]{2,1,0:T(8,128)S(1)}, u32[]{:S(2)}, u32[]{:S(2)}) async-start(f32[4,40,320]{2,1,0:T(8,128)} %broadcast_in_dim.36), calls=%async_computation.2 | async-start | bytes 491520 | tf_op jit(solution)/shard_map/all_to_all | solution.py:24
  106.1 14.2 %collective-permute-start.11 = (f32[40,320]{1,0:T(8,128)S(1)}, f32[40,320]{1,0:T(8,128)S(1)}, u32[]{:S(2)}, u32[]{:S(2)}) collective-permute-start(f32[40,320]{1,0:T(8,128)S(1)} %pad_maximum_fusion.3), channel_id=1, source_target_pairs={{0,7},{1,32},{2,65},{3,98},{4,131},{5,164},{6,197},{7,230},{8,15},... | collective-permute-start | bytes 153608 | tf_op jit(solution)/shard_map/ppermute | solution.py:221
  116.8 14.1 %all-to-all-start.3 = ((f32[4,40,1280]{2,1,0:T(8,128)}), f32[4,40,1280]{2,1,0:T(8,128)S(1)}, u32[]{:S(2)}, u32[]{:S(2)}) async-start(f32[4,40,1280]{2,1,0:T(8,128)} %broadcast_in_dim.37), calls=%async_computation.3 | async-start | bytes 1638400 | tf_op jit(solution)/shard_map/all_to_all | solution.py:24
  120.3 6.1 %collective-permute-start.12 = (f32[40,320]{1,0:T(8,128)S(1)}, f32[40,320]{1,0:T(8,128)S(1)}, u32[]{:S(2)}, u32[]{:S(2)}) collective-permute-start(f32[40,320]{1,0:T(8,128)S(1)} %collective-permute-done.11), channel_id=1, source_target_pairs={{0,8},{8,0},{1,9},{9,1},{2,10},{10,2},{3,11},{11,3},{4,12},{12,4},... | collective-permute-start | bytes 153608 | tf_op jit(solution)/shard_map/ppermute | solution.py:20
